TPU v7x, 32 devices: a whole 2x2x4 slice. The times are simulated.
32 devices in a mesh: seq: 8 (over z, y), exp: 4 (over x, core).
Axes of the slice: x: 2, y: 2, z: 4, core: 2. Of those that a mesh axis runs over, the one named last changes fastest.
Arguments:
- residual: bfloat16 [1024, 6144], P('exp', 'seq'), may hold values from -8 to 8
- query: bfloat16 [1024, 8192], P('seq', 'exp'), may hold values from -6 to 6
- key_in: bfloat16 [1024, 8192], P('seq', 'exp'), may hold values from -6 to 6
- value_in: bfloat16 [1024, 8192], P('seq', 'exp'), may hold values from -0.75 to 0.75
- gate_in: bfloat16 [1024, 8192], P('seq', 'exp'), may hold values from -6 to 6
- log_decay: float32 [1024, 64], P('seq', 'exp'), may hold values from -2 to 0
- state_in: float32 [64, 128, 128], P('exp'), may hold values from -12 to 12
- attn_gain: float32 [8192], P('exp'), may hold values from 0.1 to 1.9
- w_out: bfloat16 [8192, 6144], P('exp', 'seq'), may hold values from -0.0625 to 0.0625
- moe_gain: float32 [6144], P('seq'), may hold values from 0.1 to 1.9
- router: float32 [6144, 32], P('seq'), may hold values from -0.078125 to 0.078125
- w_gate: bfloat16 [4, 9216, 6144], P('exp', 'seq'), may hold values from -0.078125 to 0.078125
- w_up: bfloat16 [4, 9216, 6144], P('exp', 'seq'), may hold values from -0.078125 to 0.078125
- w_down: bfloat16 [4, 9216, 6144], P('exp', None, 'seq'), may hold values from -0.09375 to 0.09375
- expert_ids: int32 [1024, 2], P('exp'), may hold values from 0 to 31, all different within a row; in each aligned block of 256 rows (0 to 255, 256 to 511, ...) at most 20 rows name the same one
- keep_counts: int32 [32], replicated, may hold values from 16 to 79
Outputs:
- layer_out: bfloat16 [1024, 6144], P('exp', 'seq')
- final_state: float32 [64, 128, 128], P('exp', 'seq')
Inputs may be any that keep to these rules, and one draw needn't show every extreme that they name: `expert_ids`: each row names 2 different experts. Among the rows of one device no expert is named more than 20 times, a bound that some block reaches.
All inputs are finite; a program needn't handle non-finite values.
Results may differ from a plain program's by a relative error of at most 0.014.
Values may be sent and summed in bfloat16 or wider, within the bound.
No kernel may reach another device: no remote copies, remote signals or barrier semaphores. Data moves between devices by JAX's collectives and lax.ppermute only.
A program may use at most 128 MiB of HBM per device.

v0:
```python
import jax
import jax.numpy as jnp
from jax import lax
from jax.sharding import PartitionSpec as P

D = 6144


epsilon = 1e-05
highest = lax.Precision.HIGHEST


def entering(x, axis, join, neutral):
    place = lax.axis_index(axis)
    gathered = jax.tree.map(
        lambda a, kind: lax.all_gather(a.astype(kind), axis), x, (jnp.bfloat16, jnp.bfloat16)
    )
    state = jax.tree.map(lambda a, e: jnp.zeros_like(a) + jnp.asarray(e, a.dtype), x, neutral)

    def one(lap, state):
        return join(
            state,
            jax.tree.map(
                lambda a, own: lax.dynamic_index_in_dim(a, lap, 0, False).astype(own.dtype),
                gathered,
                x,
            ),
        )

    return lax.fori_loop(0, place, one, state)


def broadcast(value, axis, source):
    kept = jnp.where(lax.axis_index(axis) == source, value, 0).astype(value.dtype)
    return lax.psum(kept, axis)


def entering_2(part, axis, combine, identity):
    place = lax.axis_index(axis)
    gathered = lax.all_gather(part, axis)
    state = jnp.zeros_like(part) + jnp.asarray(identity, part.dtype)

    def one(lap, state):
        return combine(state, lax.dynamic_index_in_dim(gathered, lap, 0, False))

    return lax.fori_loop(0, place, one, state)


def block_terms(act_query, act_key, val_rows, log_rows):
    running_log = jnp.cumsum(log_rows, axis=0)
    block_log = running_log[-1]
    length = log_rows.shape[0]
    causal_mask = (jnp.arange(length)[:, None] >= jnp.arange(length)[None, :])[None]
    flipped = jnp.transpose(running_log)
    log_gap = flipped[:, :, None] - flipped[:, None, :]
    decay_rows = jnp.where(causal_mask, jnp.exp(jnp.where(causal_mask, log_gap, 0.0)), 0.0)
    scores = jnp.einsum("thd,shd->hts", act_query, act_key, precision=highest)
    local_part = jnp.einsum("hts,shd->thd", scores * decay_rows, val_rows, precision=highest)
    tail_decay = jnp.exp(block_log[None, :] - running_log)
    update = jnp.einsum(
        "shd,she->hde", act_key * tail_decay[:, :, None], val_rows, precision=highest
    )
    return (local_part, running_log, block_log, update)


def from_state(act_query, running_log, state_carry):
    return jnp.einsum(
        "thd,hde->the", act_query * jnp.exp(running_log)[:, :, None], state_carry, precision=highest
    )


def join_states(earlier, later_part):
    return (
        earlier[0] + later_part[0],
        jnp.exp(later_part[0])[:, None, None] * earlier[1] + later_part[1],
    )


def add_counts(earlier, later_counts):
    return earlier + later_counts


def local(
    residual,
    query,
    key_in,
    value_in,
    gate_in,
    log_decay,
    state_in,
    attn_gain,
    w_out,
    moe_gain,
    router,
    w_gate,
    w_up,
    w_down,
    expert_ids,
    keep_counts,
):
    tok_rows, head_width = query.shape
    head_count = log_decay.shape[1]
    head_size = head_width // head_count
    act_query = jax.nn.silu(query.astype(jnp.float32)).reshape(tok_rows, head_count, head_size)
    act_key = jax.nn.silu(key_in.astype(jnp.float32)).reshape(tok_rows, head_count, head_size)
    val_rows = value_in.astype(jnp.float32).reshape(tok_rows, head_count, head_size)
    local_part, running_log, block_log, update = block_terms(
        act_query, act_key, val_rows, log_decay
    )
    segments = lax.axis_size("seq")
    position = lax.axis_index("seq")
    row_share = head_size // segments
    identity_pair = (jnp.zeros_like(block_log), jnp.zeros_like(update))
    before_log, before_state = entering((block_log, update), "seq", join_states, identity_pair)
    incoming = jnp.exp(before_log)[:, None, None] * state_in + before_state
    through = jnp.exp(block_log)[:, None, None] * incoming + update
    last_whole = broadcast(through.astype(jnp.bfloat16), "seq", segments - 1).astype(through.dtype)
    final_rows = lax.dynamic_slice_in_dim(last_whole, position * row_share, row_share, 1)
    outputs = local_part + from_state(act_query, running_log, incoming)
    square_mean = jnp.mean(outputs * outputs, axis=2, keepdims=True)
    normed = outputs * lax.rsqrt(square_mean + epsilon) * attn_gain.reshape(head_count, head_size)
    heads_mixed = (
        normed.reshape(tok_rows, head_width) * jax.nn.sigmoid(gate_in.astype(jnp.float32))
    ).astype(jnp.bfloat16)
    gathered = lax.all_gather(heads_mixed, "seq", axis=0, tiled=True)
    block_rows = residual.shape[0]
    projected = lax.psum_scatter(
        jnp.dot(gathered, w_out, preferred_element_type=jnp.float32).astype(jnp.bfloat16),
        "exp",
        scatter_dimension=0,
        tiled=True,
    ).astype(jnp.float32)
    after_attn = residual.astype(jnp.float32) + projected
    experts_all = router.shape[1]
    logit_part = jnp.dot(after_attn * moe_gain, router, precision=highest)
    choose = (
        expert_ids[:, :, None] == jnp.arange(experts_all, dtype=jnp.int32)[None, None, :]
    ).astype(jnp.float32)
    chosen_part = jnp.einsum("tke,te->tk", choose, logit_part, precision=highest)
    squares, chosen = lax.psum((jnp.sum(after_attn * after_attn, axis=1), chosen_part), "seq")
    inv_rms = lax.rsqrt(squares / D + epsilon)
    chosen = chosen * inv_rms[:, None]
    gate_probs = jnp.stack(
        [jax.nn.sigmoid(chosen[:, 0] - chosen[:, 1]), jax.nn.sigmoid(chosen[:, 1] - chosen[:, 0])],
        axis=1,
    )
    routed_in = (after_attn * inv_rms[:, None] * moe_gain).astype(jnp.bfloat16)
    lanes = lax.axis_size("exp")
    window = w_gate.shape[0] * lanes
    capacity = 5 * block_rows * lanes // (2 * lanes * experts_all)
    top_count = expert_ids.shape[1]
    flat_ids = expert_ids.reshape(block_rows * top_count)
    onehot = (flat_ids[:, None] == jnp.arange(window, dtype=jnp.int32)[None, :]).astype(jnp.int32)
    local_rank = jnp.sum((jnp.cumsum(onehot, axis=0) - onehot) * onehot, axis=1)
    before = entering_2(jnp.sum(onehot, axis=0), "exp", add_counts, jnp.zeros((window,), jnp.int32))
    global_rank = local_rank + jnp.sum(before[None, :] * onehot, axis=1)
    limits = jnp.sum(keep_counts[None, :window] * onehot, axis=1)
    is_kept = (flat_ids < window) & (global_rank < limits)
    slot_hot = ((local_rank[:, None] == jnp.arange(capacity)[None, :]) & is_kept[:, None]).astype(
        jnp.int32
    )
    assign_int = onehot[:, :, None] * slot_hot[:, None, :]
    assign_table = assign_int.astype(jnp.bfloat16)
    token_table = jnp.sum(
        assign_int.reshape(block_rows, top_count, window, capacity), axis=1
    ).astype(jnp.bfloat16)
    sending = jnp.einsum(
        "tec,td->ecd", token_table, routed_in, preferred_element_type=jnp.float32
    ).astype(jnp.bfloat16)
    arrived = lax.all_to_all(sending, "exp", split_axis=0, concat_axis=1, tiled=True)
    contract_dims = (((1,), (1,)), ((), ()))
    portion = lax.all_gather(arrived, "seq", axis=2, tiled=True)
    gate_cols = w_gate[0]
    up_cols = w_up[0]
    gate_add = lax.dot_general(
        portion[0], gate_cols, contract_dims, preferred_element_type=jnp.float32
    )
    up_add = lax.dot_general(portion[0], up_cols, contract_dims, preferred_element_type=jnp.float32)
    hidden = (jax.nn.silu(gate_add) * up_add).astype(jnp.bfloat16)
    down_rows = w_down[0]
    result = jnp.dot(
        lax.all_gather(hidden, "seq", axis=1, tiled=True),
        down_rows,
        preferred_element_type=jnp.float32,
    )
    expert_out = result.astype(jnp.bfloat16)[None]
    returned = lax.all_to_all(expert_out, "exp", split_axis=1, concat_axis=0, tiled=True)
    picked = jnp.einsum(
        "aec,ecd->ad", assign_table, returned, preferred_element_type=jnp.float32
    ).reshape(block_rows, top_count, -1)
    weight = jnp.where(is_kept.reshape(block_rows, top_count), gate_probs, 0.0)
    expert_sum = jnp.sum(picked * weight[:, :, None], axis=1)
    return ((after_attn + expert_sum).astype(jnp.bfloat16), final_rows)


def solution(mesh):
    in_specs = (
        P("exp", "seq"),
        P("seq", "exp"),
        P("seq", "exp"),
        P("seq", "exp"),
        P("seq", "exp"),
        P("seq", "exp"),
        P("exp", None, None),
        P("exp"),
        P("exp", "seq"),
        P("seq"),
        P("seq", None),
        P("exp", "seq", None),
        P("exp", "seq", None),
        P("exp", None, "seq"),
        P("exp", None),
        P(),
    )
    out_specs = (P("exp", "seq"), P("exp", "seq", None))
    return jax.shard_map(local, mesh=mesh, in_specs=in_specs, out_specs=out_specs, check_vma=False)
```

profile of v0, /device:TPU:0, one launch (start us, length us, event | category | flops | bytes accessed | tf_op | source)
XLA Modules:
  0.0 446.0 jit_solution(14622574727578191917)
XLA Ops:
  7.2 2.5 convert_multiply_fusion
  9.7 2.5 copy.134
  12.2 0.8 copy.104
  13.3 3.2 fusion.59
  16.7 22.4 %all-gather.2 = bf16[8,1,16]{2,1,0:T(2,128)(2,1)S(1)} all-gather(bf16[1,1,16]{2,1,0:T(2,128)(2,1)S(1)} %convert_bitcast_fusion), channel_id=1, replica_groups=mesh['seq'=8,'exp'=4] {'seq'}, dimensions={0}, use_global_device_ids=true | all-gather | bytes 288 | tf_op jit(solution)/shard_map/all_gather | solution.py:16
  39.2 2.9 convolution_multiply_fusion
  42.1 2.2 convolution_bitcast_fusion.1
  44.3 48.5 %all-gather.11.cloned.1.call-done = bf16[128,128,128]{2,1,0:T(8,128)(2,1)} async-done(((bf16[16,128,128]{2,1,0:T(8,128)(2,1)}), bf16[128,128,128]{2,1,0:T(8,128)(2,1)}) %all-gather.11.cloned.1.call-update) | async-done | bytes 4194320 | tf_op jit(solution)/shard_map/all_gather | solution.py:16
  92.8 1.1 broadcast_in_dim.29
  93.9 4.3 multiply_reduce_fusion
  98.2 1.4 multiply_multiply_fusion
  99.6 2.6 copy.114
  102.1 2.4 multiply_convert_fusion
  104.7 89.3 %all-gather.7.cloned.1.call-done = bf16[1024,2048]{1,0:T(8,128)(2,1)} async-done(((bf16[128,2048]{1,0:T(8,128)(2,1)}), bf16[1024,2048]{1,0:T(8,128)(2,1)}) %all-gather.7.cloned.1.call-update) | async-done | bytes 4194320 | tf_op jit(solution)/shard_map/all_gather | solution.py:125
  193.9 6.8 %convolution_convert_fusion = bf16[1024,768]{1,0:T(8,128)(2,1)} fusion(bf16[1024,2048]{1,0:T(8,128)(2,1)} %all-gather.7.cloned.1.call-done, bf16[2048,768]{1,0:T(8,128)(2,1)S(1)} %copy-done), kind=kOutput, calls=%fused_computation.13 | convolution fusion | flops 3222011904 | bytes 8912896 | tf_op jit(solution)/shard_map/dot_general | solution.py:128
  201.2 0.6 dynamic-slice
  202.6 0.2 dynamic-update-slice
  202.9 4.9 %all-reduce = s32[16]{0:T(128)S(1)} all-reduce(s32[16]{0:T(128)S(1)} %dynamic-update-slice), channel_id=3, replica_groups=mesh['seq'=8,'exp'=4] {'exp'}, use_global_device_ids=true, to_apply=%add | all-reduce | flops 16 | bytes 128
  207.8 1.2 reduce-window.6
  209.6 0.7 select_reduce_fusion.1
  211.1 16.3 %reduce-scatter.2.cloned.1.call-done = bf16[256,768]{1,0:T(8,128)(2,1)} async-done(((bf16[1024,768]{1,0:T(8,128)(2,1)}), bf16[256,768]{1,0:T(8,128)(2,1)}) %reduce-scatter.2.cloned.1.call-update) | async-done | bytes 393232 | tf_op jit(solution)/shard_map/reduce_scatter | solution.py:127
  227.3 1.8 fusion.34
  229.1 0.9 fusion.48
  230.1 1.2 multiply_reduce_fusion.1
  231.3 21.4 %all-reduce.1 = (f32[256]{0:T(256)S(1)}, f32[256,2]{0,1:T(2,128)S(1)}) all-reduce(f32[256]{0:T(256)S(1)} %multiply_reduce_fusion.1, f32[256,2]{0,1:T(2,128)S(1)} %copy.130), channel_id=1, replica_groups=mesh['seq'=8,'exp'=4] {'seq'}, use_global_device_ids=true, to_apply=%region_15.16 | all-reduce | flops 768 | bytes 6144 | tf_op jit(solution)/shard_map/psum | solution.py:140
  252.7 0.6 maximum_select_fusion
  253.4 0.5 copy-done.7
  253.9 1.3 convolution_convert_fusion.1
  255.2 7.2 %all_to_all.24 = bf16[4,20,768]{2,1,0:T(8,128)(2,1)S(1)} all-to-all(bf16[4,20,768]{2,1,0:T(8,128)(2,1)S(1)} %convolution_convert_fusion.1), channel_id=1, replica_groups=mesh['seq'=8,'exp'=4] {'exp'}, dimensions={0} | all-to-all | bytes 245760 | tf_op jit(solution)/shard_map/all_to_all | solution.py:170
  262.4 32.6 %all_gather.31 = bf16[1,80,6144]{2,1,0:T(8,128)(2,1)S(1)} all-gather(bf16[1,80,768]{2,1,0:T(8,128)(2,1)S(1)} %all_to_all.9), channel_id=1, replica_groups=mesh['seq'=8,'exp'=4] {'seq'}, dimensions={2}, use_global_device_ids=true | all-gather | bytes 1105920 | tf_op jit(solution)/shard_map/all_gather | solution.py:172
  295.0 9.4 %fusion.4 = f32[80,1152]{1,0:T(8,128)S(1)} fusion(bf16[1,1152,6144]{2,1,0:T(8,128)(2,1)} %param.31, bf16[1,80,6144]{2,1,0:T(8,128)(2,1)S(1)} %all_gather.31), kind=kOutput, calls=%fused_computation.9 | convolution fusion | flops 1132462080 | bytes 15507456 | tf_op jit(solution)/shard_map/dot_general | solution.py:175
  304.4 10.2 %fusion.9 = bf16[80,1152]{1,0:T(8,128)(2,1)} fusion(bf16[1,1152,6144]{2,1,0:T(8,128)(2,1)} %param.32, bf16[1,80,6144]{2,1,0:T(8,128)(2,1)S(1)} %all_gather.31, f32[80,1152]{1,0:T(8,128)S(1)} %fusion.4), kind=kOutput, calls=%fused_computation.12 | convolution fusion | flops 1133015040 | bytes 15691776 | tf_op jit(solution)/shard_map/dot_general | solution.py:178
  314.8 0.7 fusion.58
  315.5 2.3 fusion.36
  317.8 36.9 %all-gather.9.cloned.1.call-done = bf16[80,9216]{1,0:T(8,128)(2,1)} async-done(((bf16[80,1152]{1,0:T(8,128)(2,1)}), bf16[80,9216]{1,0:T(8,128)(2,1)}) %all-gather.9.cloned.1.call-update) | async-done | bytes 1474576 | tf_op jit(solution)/shard_map/all_gather | solution.py:182
  354.7 8.1 %fusion.17 = bf16[1,80,768]{2,1,0:T(8,128)(2,1)S(1)} fusion(bf16[80,9216]{1,0:T(8,128)(2,1)} %all-gather.9.cloned.1.call-done, bf16[1,9216,768]{2,1,0:T(8,128)(2,1)} %param.33), kind=kOutput, calls=%fused_computation.26 | convolution fusion | flops 1132523520 | bytes 15753216 | tf_op jit(solution)/shard_map/dot_general | solution.py:181
  362.9 0.9 copy.164
  363.7 0.6 broadcast.139
  364.3 3.0 reduce.6
  367.3 1.6 reshape.243
  368.9 3.9 all-to-all-start.1
  372.8 56.3 %all-reduce.4.cloned.1.call-done = bf16[16,128,128]{2,1,0:T(8,128)(2,1)} async-done(((bf16[16,128,128]{2,1,0:T(8,128)(2,1)}), bf16[16,128,128]{2,1,0:T(8,128)(2,1)}) %all-reduce.4.cloned.1.call-update) | async-done | bytes 524304 | tf_op jit(solution)/shard_map/psum | solution.py:35
  429.2 1.5 dynamic-slice_convert_fusion
  430.7 1.7 reshape.244
  432.4 2.3 bitcast_reduce_fusion
  434.6 1.6 reshape.236
  436.2 1.4 fusion.12
  437.6 1.9 add_convert_fusion.1
  (80 shorter events, 2.9 us)
Async XLA Ops:
  7.2 186.8 %copy-start = (bf16[2048,768]{1,0:T(8,128)(2,1)S(1)}, bf16[2048,768]{1,0:T(8,128)(2,1)}, u32[]{:S(2)}) copy-start(bf16[2048,768]{1,0:T(8,128)(2,1)} %param.28) | copy-start | bytes 9437188
  7.2 85.6 %all-gather.11.cloned.1.call-start = ((), (), s32[]{:S(2)}) async-start(), calls=%async_computation.7 | async-start | bytes 4718592 | tf_op jit(solution)/shard_map/all_gather | solution.py:16
  13.2 28.9 %copy-start.6 = (f32[128,16]{1,0:T(8,128)}, f32[128,16]{1,0:T(8,128)S(1)}, u32[]{:S(2)}) copy-start(f32[128,16]{1,0:T(8,128)S(1)} %reduce_window_sum.26) | copy-start | bytes 24580
  16.5 177.4 %all-gather.7.cloned.1.call-start = ((), (), s32[]{:S(2)}) async-start(), calls=%async_computation.3 | async-start | bytes 4718592 | tf_op jit(solution)/shard_map/all_gather | solution.py:125
  16.7 25.4 %copy-start.5 = (bf16[128,2048]{1,0:T(8,128)(2,1)S(1)}, bf16[128,2048]{1,0:T(8,128)(2,1)}, u32[]{:S(2)}) copy-start(bf16[128,2048]{1,0:T(8,128)(2,1)} %param.23) | copy-start | bytes 1572868
  93.9 4.3 copy-start.9
  93.9 5.7 %copy-start.12 = (f32[16]{0:T(128)}, f32[16]{0:T(128)S(1)}, u32[]{:S(2)}) copy-start(f32[16]{0:T(128)S(1)} %exp.60) | copy-start | bytes 196
  104.6 96.2 %copy-start.8 = (s32[256,2]{0,1:T(2,128)S(1)}, s32[256,2]{0,1:T(2,128)}, u32[]{:S(2)}) copy-start(s32[256,2]{0,1:T(2,128)} %param.34) | copy-start | bytes 6148
  104.6 96.6 %copy-start.14 = (u32[32]{0:T(128)S(1)}, u32[32]{0:T(128)}, u32[]{:S(2)}) copy-start(u32[32]{0:T(128)} %constant.77) | copy-start | bytes 388
  104.6 122.7 %copy-start.4 = (bf16[256,768]{1,0:T(8,128)(2,1)S(1)}, bf16[256,768]{1,0:T(8,128)(2,1)}, u32[]{:S(2)}) copy-start(bf16[256,768]{1,0:T(8,128)(2,1)} %param.20) | copy-start | bytes 1179652
  104.6 122.7 %copy-start.10 = (f32[768]{0:T(1024)S(1)}, f32[768]{0:T(1024)}, u32[]{:S(2)}) copy-start(f32[768]{0:T(1024)} %param.29) | copy-start | bytes 9220
  104.6 122.7 %reduce-scatter.2.cloned.1.call-start = ((), (), s32[]{:S(2)}) async-start(), calls=%async_computation.4 | async-start | bytes 1966080 | tf_op jit(solution)/shard_map/reduce_scatter | solution.py:127
  200.7 154.0 %all-gather.9.cloned.1.call-start = ((), (), s32[]{:S(2)}) async-start(), calls=%async_computation.5 | async-start | bytes 1658880 | tf_op jit(solution)/shard_map/all_gather | solution.py:182
  253.3 0.6 copy-start.7
  304.4 11.0 %copy-start.2 = (f32[16,128,128]{2,1,0:T(8,128)S(1)}, f32[16,128,128]{2,1,0:T(8,128)}, u32[]{:S(2)}) copy-start(f32[16,128,128]{2,1,0:T(8,128)} %get-tuple-element.60) | copy-start | bytes 3145732
  304.4 11.0 %copy-start.3 = (f32[16,128,128]{2,1,0:T(8,128)S(1)}, f32[16,128,128]{2,1,0:T(8,128)}, u32[]{:S(2)}) copy-start(f32[16,128,128]{2,1,0:T(8,128)} %get-tuple-element.96) | copy-start | bytes 3145732
  304.4 11.0 %copy-start.13 = (f32[16]{0:T(128)S(1)}, f32[16]{0:T(128)}, u32[]{:S(2)}) copy-start(f32[16]{0:T(128)} %copy-done.12) | copy-start | bytes 196
  314.7 114.5 %all-reduce.4.cloned.1.call-start = ((), (), s32[]{:S(2)}) async-start(), calls=%async_computation.6 | async-start | bytes 1048576 | tf_op jit(solution)/shard_map/psum | solution.py:35
  317.8 118.4 %copy-start.11 = (f32[256,2]{0,1:T(2,128)S(1)}, f32[256,2]{0,1:T(2,128)}, u32[]{:S(2)}) copy-start(f32[256,2]{0,1:T(2,128)} %get-tuple-element.87) | copy-start | bytes 6148
  354.7 84.8 %copy-start.1 = (bf16[2048,768]{1,0:T(8,128)(2,1)S(1)}, bf16[2048,768]{1,0:T(8,128)(2,1)}, u32[]{:S(2)}) copy-start(bf16[2048,768]{1,0:T(8,128)(2,1)} %param.28) | copy-start | bytes 9437188
  368.9 61.8 %all-to-all-start.1 = ((bf16[4,2,7680]{2,1,0:T(2,128)(2,1)}), bf16[4,2,7680]{2,1,0:T(2,128)(2,1)}, u32[]{:S(2)}, u32[]{:S(2)}) async-start(bf16[4,2,7680]{2,1,0:T(2,128)(2,1)} %reshape.243), calls=%async_computation.2 | async-start | bytes 245760 | tf_op jit(solution)/shard_map/all_to_all | solution.py:187
Sparse Core Ops, SparseCore 0:
  16.7 76.1 all-gather.10
  104.7 89.1 all-gather.6
  200.9 26.4 reduce-scatter.1
  314.8 39.8 all-gather.8
  358.4 70.7 all-reduce.3
where the time goes:
time: 447 us; the launch traced here: 446 us
  waiting for transfers between devices  247 us (55%)
  blocking collectives  88.4 us (20%)
  matrix products  51.6 us (12%)
  other arithmetic  20.3 us (5%)
  local copies, waits for them, and re-layouts  19.4 us (4%)
  between operations  14.7 us (3%)
    all_gather x1, waiting for transfers between devices, local(): gathered = lax.all_gather(heads_mixed, 'seq', axis=0, tiled=True)  89.3 us
    psum x1, waiting for transfers between devices, broadcast(): return lax.psum(kept, axis)  56.3 us
    all_gather x1, waiting for transfers between devices, entering(): lax.all_gather(a.astype(kind), axis)  48.5 us
    all_gather x1, waiting for transfers between devices, local(): lax.all_gather(hidden, 'seq', axis=1, tiled=True)  36.9 us
    all_gather x1, blocking collectives, local(): portion = lax.all_gather(arrived, 'seq', axis=2, tiled=True)  32.6 us
    all_gather x1, blocking collectives, entering(): lax.all_gather(a.astype(kind), axis)  22.4 us
    psum x1, blocking collectives, local(): lax.psum((jnp.sum(after_attn * after_attn, axis=1), chosen_part), 'seq')  21.4 us
    reduce_scatter x1, waiting for transfers between devices, local(): lax.psum_scatter(jnp.dot(gathered, w_out, preferred_element_type=jnp.floa...  16.3 us
  transfers between devices with their start and end apart: 6, of which 5 were waited for; matrix products, arithmetic and copies ran while one was open for 6% of the time, Pallas kernels for 0%

commit v1 on v0

v1 whole, which is shorter than its diff:
```python
import functools
import jax
import jax.numpy as jnp
from jax import lax
from jax.experimental import pallas as pl
from jax.experimental.pallas import tpu as pltpu
from jax.sharding import PartitionSpec as P

EPS = 1e-05
F32 = jnp.float32
BF16 = jnp.bfloat16
I32 = jnp.int32
HIGHEST = lax.Precision.HIGHEST
NT = (((1,), (1,)), ((), ()))
TN = (((0,), (0,)), ((), ()))
NN = (((1,), (0,)), ((), ()))


def mm(a, b, dims=NN, precision=None):
    return lax.dot_general(a, b, dims, precision=precision, preferred_element_type=F32)


def sigmoid(v):
    return 1.0 / (1.0 + jnp.exp(-v))


def bit_reversed(p, bits):
    r = 0
    for b in range(bits):
        r = r * 2 + ((p >> b) & 1)
    return r


def whole(shape):
    return pl.BlockSpec(tuple(shape), lambda i, s: (0,) * len(shape))


def call(kernel, place, operands, outs, scratch=(), flops=0, limit=40):
    arrays, specs, moved = [], [], 0
    for item in operands:
        array, spec = item if isinstance(item, tuple) else (item, whole(item.shape))
        arrays.append(array)
        specs.append(spec)
        moved += array.size * array.dtype.itemsize
    moved += sum(o.size * o.dtype.itemsize for o in outs)
    return pl.pallas_call(
        kernel,
        out_shape=list(outs),
        grid_spec=pltpu.PrefetchScalarGridSpec(
            num_scalar_prefetch=1,
            grid=(1,),
            in_specs=specs,
            out_specs=[whole(o.shape) for o in outs],
            scratch_shapes=list(scratch),
        ),
        compiler_params=pltpu.CompilerParams(vmem_limit_bytes=limit * 1024 * 1024),
        cost_estimate=pl.CostEstimate(flops=flops, bytes_accessed=moved, transcendentals=0),
    )(place, *arrays)


def sds(shape, dtype):
    return jax.ShapeDtypeStruct(tuple(shape), dtype)


def pieces(x):
    hi = x.astype(BF16)
    rest = x - hi.astype(F32)
    mid = rest.astype(BF16)
    return hi, mid, (rest - mid.astype(F32)).astype(BF16)


def pack_kernel(s, k, v, q, g, kv, qg):
    kv[0] = k[...]
    kv[1] = v[...]
    qg[0] = q[...]
    qg[1] = g[...]


def update_kernel(nz, ny, heads, hd, s, *refs):
    z, y = s[0], s[1]
    n = ny - 1
    k_own, v_own = refs[0], refs[1]
    kv = refs[2 : 2 + n]
    logs = refs[2 + n : 2 + n + ny]
    outs = refs[2 + n + ny : 2 + n + ny + nz]
    c_row, c_col, log_all, state, tail = refs[2 + n + ny + nz :]
    tok = k_own.shape[0]
    total_tok = tok * ny
    share = hd // nz
    for d in range(ny):
        at = pl.multiple_of(lax.rem(y + ny - d, ny) * tok, tok)
        log_all[:, pl.ds(at, tok)] = logs[d][...]
    rows = lax.broadcasted_iota(I32, (total_tok, total_tok), 0)
    cols = lax.broadcasted_iota(I32, (total_tok, total_tok), 1)
    c_row[...] = mm(log_all[...], (rows <= cols).astype(F32), precision=HIGHEST)
    c_col[...] = mm((rows >= cols).astype(F32), log_all[...], NT, precision=HIGHEST)
    total = c_row[:, total_tok - 1 : total_tok]
    for h in range(heads):
        add = None
        for d in range(ny):
            at = pl.multiple_of(lax.rem(y + ny - d, ny) * tok, tok)
            lanes = slice(h * hd, (h + 1) * hd)
            key = (k_own[:, lanes] if d == 0 else kv[d - 1][0, :, lanes]).astype(F32)
            val = v_own[:, lanes] if d == 0 else kv[d - 1][1, :, lanes]
            decay = jnp.exp(total[h : h + 1, :] - c_col[pl.ds(at, tok), h : h + 1])
            weighted = (key * sigmoid(key) * decay).astype(BF16)
            part = mm(weighted, val, TN)
            add = part if add is None else add + part
        state[h] = add.astype(BF16)
    tail[...] = jnp.zeros_like(tail)
    hi, mid, lo = pieces(total)
    lane = lax.broadcasted_iota(I32, (heads, hd), 1)
    tail[0:heads, :] = jnp.where(
        lane == 0,
        hi.astype(F32),
        jnp.where(lane == 1, mid.astype(F32), jnp.where(lane == 2, lo.astype(F32), 0.0)),
    )
    for d in range(nz):
        at = pl.multiple_of(lax.rem(z + d, nz) * share, share)
        for h in range(heads):
            outs[d][h * share : (h + 1) * share, :] = state[h, pl.ds(at, share), :]
        outs[d][heads * share :, :] = tail[...].astype(BF16)


def prefix_kernel(nz, heads, hd, s, *refs):
    z = s[0]
    parts = refs[:nz]
    start = refs[nz]
    outs = refs[nz + 1 : 2 * nz + 1]
    final, held, entering, run = refs[2 * nz + 1 :]
    share = hd // nz
    for d in range(nz):
        held[lax.rem(z + nz - d, nz)] = parts[d][...]
    run[...] = start[...]
    for p in range(nz):
        logs = jnp.sum(held[p, heads * share :, :].astype(F32), axis=1, keepdims=True)
        keep = jnp.exp(logs)
        for h in range(heads):
            rows = slice(h * share, (h + 1) * share)
            now = run[h]
            entering[p, rows, :] = now.astype(BF16)
            run[h] = keep[h : h + 1, :] * now + held[p, rows, :].astype(F32)
    final[...] = run[...]
    for d in range(nz):
        outs[d][...] = entering[lax.rem(z + d, nz)]


def attention_kernel(nz, ny, heads, hd, s, *refs):
    z, y = s[0], s[1]
    n = ny - 1
    own = refs[:4]
    kv = refs[4 : 4 + n]
    qg = refs[4 + n : 4 + 2 * n]
    states = refs[4 + 2 * n : 4 + 2 * n + nz]
    c_row, c_col, gain, ids, tok_ids, out, chosen, qs, ks, vs, gs, state = refs[4 + 2 * n + nz :]
    tok = own[0].shape[0]
    total_tok = tok * ny
    share = hd // nz
    for d in range(ny):
        at = pl.ds(pl.multiple_of(lax.rem(y + ny - d, ny) * tok, tok), tok)
        ks[at, :] = own[0][...] if d == 0 else kv[d - 1][0]
        vs[at, :] = own[1][...] if d == 0 else kv[d - 1][1]
        qs[at, :] = own[2][...] if d == 0 else qg[d - 1][0]
        gs[at, :] = own[3][...] if d == 0 else qg[d - 1][1]
    for d in range(nz):
        at = pl.ds(pl.multiple_of(lax.rem(z + nz - d, nz) * share, share), share)
        for h in range(heads):
            state[h, at, :] = states[d][h * share : (h + 1) * share, :]
    rows = lax.broadcasted_iota(I32, (total_tok, total_tok), 0)
    cols = lax.broadcasted_iota(I32, (total_tok, total_tok), 1)
    causal = rows >= cols
    for h in range(heads):
        lanes = slice(h * hd, (h + 1) * hd)
        query = qs[:, lanes].astype(F32)
        query = query * sigmoid(query)
        key = ks[:, lanes].astype(F32)
        key = (key * sigmoid(key)).astype(BF16)
        col = c_col[:, h : h + 1]
        gap = jnp.where(causal, col - c_row[h : h + 1, :], 0.0)
        decay = jnp.where(causal, jnp.exp(gap), 0.0)
        scores = mm(query.astype(BF16), key, NT) * decay
        att = mm(scores.astype(BF16), vs[:, lanes])
        att = att + mm((query * jnp.exp(col)).astype(BF16), state[h])
        square = jnp.mean(att * att, axis=1, keepdims=True)
        gate = sigmoid(gs[:, lanes].astype(F32))
        out[:, lanes] = (att * lax.rsqrt(square + EPS) * gain[:, lanes] * gate).astype(BF16)
    pick = (ids[...] == tok_ids[0:1, :]) | (ids[...] == tok_ids[1:2, :])
    chosen[...] = mm(pick.astype(F32).astype(BF16), out[...]).astype(BF16)


def project_chosen_kernel(nz, ny, s, *refs):
    count = nz * ny
    blocks = refs[:count]
    weights = refs[count : count + ny]
    row_ids, col_ids, tok_ids, residual, keep, send, stacked = refs[count + ny :]
    rows = blocks[0].shape[0]
    total = None
    for dy in range(ny):
        for dz in range(nz):
            stacked[dz * rows : (dz + 1) * rows, :] = blocks[dy * nz + dz][...]
        part = mm(stacked[...], weights[dy][...])
        total = part if total is None else total + part
    order = (row_ids[...] == col_ids[...]).astype(F32).astype(BF16)
    mine = (row_ids[...] == tok_ids[0:1, :]) | (row_ids[...] == tok_ids[1:2, :])
    result = mm(order, total.astype(BF16)) + mm(mine.astype(F32).astype(BF16), residual[...])
    half = keep.shape[0]
    keep[...] = result[:half, :]
    send[...] = result[half:, :].astype(BF16)


def project_kernel(nz, ny, s, *refs):
    z, j = s[0], s[2]
    bits = nz.bit_length() - 1
    count = nz * ny
    blocks = refs[:count]
    weights = refs[count : count + ny]
    keep, send, stacked, sem = refs[count + ny :]
    rows = blocks[0].shape[0]
    copies = []
    for dy in range(ny):
        for dz in range(nz):
            copies.append(
                pltpu.make_async_copy(
                    blocks[dy * nz + dz], stacked.at[dy, dz], sem.at[dy * nz + dz]
                )
            )
            copies[-1].start()
    for c in copies:
        c.wait()
    for p in range(nz):
        block = lax.bitwise_xor(jnp.int32(bit_reversed(p, bits)), j)
        dz = lax.rem(z + nz - block, nz)
        total = None
        for dy in range(ny):
            part = mm(stacked[dy, dz], weights[dy][...])
            total = part if total is None else total + part
        if p < nz // 2:
            keep[p] = total.astype(BF16)
        else:
            send[p - nz // 2] = total.astype(BF16)


def rows_kernel(s, keep, received, gain, router, sign, out):
    width = gain.shape[1]
    rows = keep[...] + received[...].astype(F32)
    square = jnp.sum(rows * rows, axis=1, keepdims=True)
    scaled = rows * gain[...]
    logits = mm(scaled, router[...], precision=HIGHEST)
    gap = jnp.sum(logits * sign[...], axis=1, keepdims=True)
    out[:, :width] = scaled.astype(BF16)
    lane = lax.broadcasted_iota(I32, (rows.shape[0], 128), 1)
    stats = jnp.zeros((rows.shape[0], 128), F32)
    for at, value in ((0, square), (3, gap)):
        for k, piece in enumerate(pieces(value)):
            stats = jnp.where(lane == at + k, piece.astype(F32), stats)
    out[:, width:] = stats.astype(BF16)


def up_kernel(nz, ny, places, first, last, features, s, *refs):
    z, y = s[0], s[1]
    count = len(places)
    blocks = refs[:count]
    refs = refs[count:]
    before = () if first else refs[:3]
    refs = refs[0 if first else 3 :]
    w_gate, w_up = refs[:2]
    outs = refs[2 : 4 if last else 5]
    gate_buf, up_buf, sem = refs[4 if last else 5 :]
    width = gate_buf.shape[2]
    copies = []
    for n, (dz, dy) in enumerate(places):
        source = lax.rem(z + nz - dz, nz) * ny + lax.rem(y + ny - dy, ny)
        at = pl.ds(pl.multiple_of(source * width, 128), width)
        copies.append(
            (
                pltpu.make_async_copy(w_gate.at[0, :, at], gate_buf.at[n], sem.at[0, n]),
                pltpu.make_async_copy(w_up.at[0, :, at], up_buf.at[n], sem.at[1, n]),
            )
        )
        for c in copies[-1]:
            c.start()
    gate, up, stats = (None, None, None) if first else (b[...] for b in before)
    for n in range(count):
        rows = blocks[n][:, :width]
        part = blocks[n][:, width:].astype(F32)
        stats = part if stats is None else stats + part
        copies[n][0].wait()
        part = mm(rows, gate_buf[n], NT)
        gate = part if gate is None else gate + part
        copies[n][1].wait()
        part = mm(rows, up_buf[n], NT)
        up = part if up is None else up + part
    if not last:
        outs[0][...] = gate
        outs[1][...] = up
        outs[2][...] = stats
        return
    square = stats[:, 0:1] + stats[:, 1:2] + stats[:, 2:3]
    gap = stats[:, 3:4] + stats[:, 4:5] + stats[:, 5:6]
    inverse = lax.rsqrt(square / features + EPS)
    gate = gate * inverse
    outs[0][...] = (gate * sigmoid(gate) * (up * inverse)).astype(BF16)
    outs[1][...] = jnp.broadcast_to(sigmoid(gap * inverse), outs[1].shape)


def down_kernel(nz, ny, places, first, last, s, *refs):
    z, y = s[0], s[1]
    count = len(places)
    blocks = refs[:count]
    refs = refs[count:]
    before = None if first else refs[0]
    refs = refs[0 if first else 1 :]
    w_down = refs[0]
    refs = refs[1:]
    if last:
        weight, out_ids, row_ids = refs[:3]
        refs = refs[3:]
    outs, buf, sem = refs[:-2], refs[-2], refs[-1]
    depth = buf.shape[1]
    copies = []
    for n, (dz, dy) in enumerate(places):
        source = lax.rem(z + nz - dz, nz) * ny + lax.rem(y + ny - dy, ny)
        at = pl.ds(pl.multiple_of(source * depth, depth), depth)
        copies.append(pltpu.make_async_copy(w_down.at[0, at, :], buf.at[n], sem.at[n]))
        copies[-1].start()
    total = None if first else before[...]
    for n in range(count):
        copies[n].wait()
        part = mm(blocks[n][...], buf[n])
        total = part if total is None else total + part
    if not last:
        outs[0][...] = total
        return
    result = (total * weight[:, 0:1]).astype(BF16)
    for r, out in enumerate(outs):
        rows = out.shape[0]
        pick = out_ids[r * rows : (r + 1) * rows, :] == row_ids[...]
        out[...] = mm(pick.astype(F32).astype(BF16), result).astype(BF16)


def combine_kernel(count, s, *refs):
    returned = refs[:count]
    keep, received, residual, tok_ids, ret_ids, out, stacked = refs[count:]
    rows = returned[0].shape[0]
    for n in range(count):
        stacked[n * rows : (n + 1) * rows, :] = returned[n][...]
    pick = (tok_ids[:, 0:1] == ret_ids[...]) | (tok_ids[:, 1:2] == ret_ids[...])
    total = residual[...].astype(F32) + (keep[...].astype(F32) + received[...].astype(F32))
    total = total + mm(pick.astype(F32).astype(BF16), stacked[...])
    out[...] = total.astype(BF16)


def local(
    residual,
    query,
    key_in,
    value_in,
    gate_in,
    log_decay,
    state_in,
    attn_gain,
    w_out,
    moe_gain,
    router,
    w_gate,
    w_up,
    w_down,
    expert_ids,
    keep_counts,
):
    nz = lax.axis_size("exp")
    ny = lax.axis_size("seq") // nz
    bits = nz.bit_length() - 1
    i = lax.axis_index("seq").astype(I32)
    j = lax.axis_index("exp").astype(I32)
    z, y = i // ny, i % ny
    place = jnp.stack([z, y, j])

    tok, head_width = query.shape
    head_count, hd = state_in.shape[0], state_in.shape[2]
    heads = head_count // ny
    width = heads * hd
    block, cols = residual.shape
    features = w_gate.shape[2]
    units = w_gate.shape[1]
    experts = router.shape[1]
    cap = 5 * block * nz // (2 * nz * experts)
    slots = nz * cap

    def z_turn(a, d):
        pairs = [(p * ny + q, (p + d) % nz * ny + q) for p in range(nz) for q in range(ny)]
        return lax.ppermute(a, "seq", pairs)

    def y_turn(a, d):
        pairs = [(p * ny + q, p * ny + (q + d) % ny) for p in range(nz) for q in range(ny)]
        return lax.ppermute(a, "seq", pairs)

    def swap(a, r):
        return lax.ppermute(a, "exp", [(p, p ^ r) for p in range(nz)])

    z_order = sorted(range(1, nz), key=lambda d: (min(d, nz - d), d))

    def gather(a):
        held = {(0, 0): a}
        for d in range(1, ny):
            held[0, d] = y_turn(a, d)
        for d in z_order:
            held[d, 0] = z_turn(a, d)
        for d in z_order:
            for e in range(1, ny):
                held[d, e] = y_turn(held[d, 0], e)
        return held

    ids = jnp.transpose(expert_ids)[None]
    for b in range(bits):
        ids = jnp.concatenate([ids, swap(ids, 1 << b)], axis=0)
    ids = jnp.stack([lax.dynamic_index_in_dim(ids, p ^ j, 0, False) for p in range(nz)])
    window = jnp.arange(nz, dtype=I32)
    named = (ids[None, :, 0] == window[:, None, None]) | (ids[None, :, 1] == window[:, None, None])
    strict = (jnp.arange(block)[:, None] < jnp.arange(block)[None, :]).astype(BF16)
    rank = jnp.einsum(
        "ebt,ts->ebs", named.astype(BF16), strict, preferred_element_type=F32
    ).astype(I32)
    counts = jnp.sum(named.astype(I32), axis=2)
    earlier = jnp.sum(
        jnp.where(window[:, None] < window[None, :], 1, 0)[None] * counts[:, :, None], axis=1
    )
    kept = named & (rank + earlier[:, :, None] < keep_counts[:nz][:, None, None])
    code = jnp.where(
        kept, (window[:, None, None] * nz + window[None, :, None]) * cap + rank, -1
    )
    code_a = jnp.max(code, axis=0)
    code_b = jnp.max(jnp.where(code == code_a[None], -1, code), axis=0)
    codes = jnp.stack([code_a, code_b], axis=1)
    codes_z = lax.dynamic_index_in_dim(codes, z, 0, False)
    codes_j = lax.dynamic_index_in_dim(codes, j, 0, False)
    slot = jnp.arange(cap, dtype=I32)

    def number(e, p):
        return (e * nz + p)[..., None] * cap + slot

    back = (z - window) % nz
    col_ids = number(window[None, :], back[:, None]).reshape(nz * slots)
    turned = jnp.array([bit_reversed(p, bits) for p in range(nz)], I32) ^ j
    row_ids = number(turned[:, None], window[None, :]).reshape(nz * slots, 1)
    own_rows = number(j, window).reshape(slots)
    pad = -cap % 16
    ret_rows = slot.shape[0] + pad
    padded = functools.partial(jnp.pad, pad_width=((0, 0), (0, pad)), constant_values=-2)
    out_ids = padded(number(j, window ^ j)).reshape(nz * ret_rows, 1)
    ret_ids = padded(number(window ^ j, j)).reshape(1, nz * ret_rows)
    holds = (own_rows[:, None, None] == code_a[None]) | (own_rows[:, None, None] == code_b[None])
    other = jnp.sum(jnp.where(holds, (ids[:, 0] + ids[:, 1])[None], 0), axis=(1, 2)) - j
    every = jnp.arange(experts, dtype=I32)[None, :]
    sign = (every == j).astype(F32) - (every == other[:, None]).astype(F32)

    here = pl.BlockSpec((tok, width), lambda n, s: (0, s[1]))
    logs_t = jnp.transpose(log_decay)
    logs = [lax.dynamic_slice_in_dim(logs_t, y * heads, heads, 0)]
    kvs, qgs = [], []
    for d in range(1, ny):
        there = pl.BlockSpec((tok, width), lambda n, s, d=d: (0, lax.rem(s[1] + d, ny)))
        kv, qg = call(
            pack_kernel,
            place,
            [(key_in, there), (value_in, there), (query, there), (gate_in, there)],
            [sds((2, tok, width), BF16)] * 2,
        )
        to = (y + d) % ny
        logs.append(y_turn(lax.dynamic_slice_in_dim(logs_t, to * heads, heads, 0), d))
        kvs.append(y_turn(kv, d))
        qgs.append(y_turn(qg, d))
    share = hd // nz
    long = tok * ny
    *parts, c_row, c_col = call(
        functools.partial(update_kernel, nz, ny, heads, hd),
        place,
        [(key_in, here), (value_in, here), *kvs, *logs],
        [sds((heads * share + 16, hd), BF16)] * nz
        + [sds((heads, long), F32), sds((long, heads), F32)],
        [
            pltpu.VMEM((heads, long), F32),
            pltpu.VMEM((heads, hd, hd), BF16),
            pltpu.VMEM((16, hd), F32),
        ],
        flops=2 * long * hd * hd * heads,
    )
    parts = [parts[0]] + [z_turn(parts[d], d) for d in range(1, nz)]
    *entering, last_rows = call(
        functools.partial(prefix_kernel, nz, heads, hd),
        place,
        [*parts, (state_in, pl.BlockSpec((heads, share, hd), lambda n, s: (s[1], s[0], 0)))],
        [sds((heads * share, hd), BF16)] * nz + [sds((heads, share, hd), F32)],
        [
            pltpu.VMEM((nz, heads * share + 16, hd), BF16),
            pltpu.VMEM((nz, heads * share, hd), BF16),
            pltpu.VMEM((heads, share, hd), F32),
        ],
    )
    entering = [entering[0]] + [z_turn(entering[d], d) for d in range(1, nz)]
    mixed, chosen = call(
        functools.partial(attention_kernel, nz, ny, heads, hd),
        place,
        [
            (key_in, here),
            (value_in, here),
            (query, here),
            (gate_in, here),
            *kvs,
            *qgs,
            *entering,
            c_row,
            c_col,
            (attn_gain[None], pl.BlockSpec((1, width), lambda n, s: (0, s[1]))),
            col_ids[:slots, None],
            codes_z,
        ],
        [sds((long, width), BF16), sds((slots, width), BF16)],
        [pltpu.VMEM((long, width), BF16)] * 4 + [pltpu.VMEM((heads, hd, hd), BF16)],
        flops=4 * long * long * width,
    )
    rows = share // ny
    final_rows = jnp.zeros((head_count, rows, hd), F32)
    for d in range(ny):
        sent = lax.dynamic_slice_in_dim(last_rows, (y + d) % ny * rows, rows, 1)
        got = sent if d == 0 else y_turn(sent, d)
        final_rows = lax.dynamic_update_slice_in_dim(
            final_rows, got, (y - d) % ny * heads, 0
        )

    picked = gather(chosen)
    places = [(dz, dy) for dy in range(ny) for dz in range(nz)]
    w_parts = [
        (w_out, pl.BlockSpec((width, cols), lambda n, s, d=d: (lax.rem(s[1] + ny - d, ny), 0)))
        for d in range(ny)
    ]
    keep, send = call(
        functools.partial(project_chosen_kernel, nz, ny),
        place,
        [picked[p] for p in places]
        + w_parts
        + [row_ids, col_ids[None], codes_j, residual],
        [sds((nz * slots // 2, cols), F32), sds((nz * slots // 2, cols), BF16)],
        [pltpu.VMEM((nz * slots, width), BF16)],
        flops=2 * nz * slots * head_width * cols,
    )
    for b in range(bits):
        received = swap(send, 1 << b)
        if b < bits - 1:
            half = keep.shape[0] // 2
            send = (keep[half:] + received[half:].astype(F32)).astype(BF16)
            keep = keep[:half] + received[:half].astype(F32)
    (rows_out,) = call(
        rows_kernel,
        place,
        [keep, received, moe_gain[None], router, sign],
        [sds((slots, cols + 128), BF16)],
    )

    everything = gather(mixed)
    keep_all, send_all = call(
        functools.partial(project_kernel, nz, ny),
        place,
        [(everything[p], pl.BlockSpec(memory_space=pl.ANY)) for p in places] + w_parts,
        [sds((nz // 2, block, cols), BF16)] * 2,
        [pltpu.VMEM((ny, nz, long, width), BF16), pltpu.SemaphoreType.DMA((nz * ny,))],
        flops=2 * nz * long * head_width * cols,
    )
    for b in range(bits):
        received_all = swap(send_all, 1 << b)
        if b < bits - 1:
            half = keep_all.shape[0] // 2
            both = keep_all.astype(F32) + received_all.astype(F32)
            send_all, keep_all = both[half:].astype(BF16), both[:half].astype(BF16)

    groups = [[(0, d) for d in range(ny)], [(d, 0) for d in z_order]]
    groups.append([(d, e) for d in z_order for e in range(1, ny)])
    arrived = gather(rows_out)
    state = []
    if cols % 128:
        order = jnp.stack([(z - dz) % nz * ny + (y - dy) % ny for dz, dy in places])
        at = jnp.argsort(order)
        rows_all = jnp.take(jnp.stack([arrived[p] for p in places]), at, axis=0)
        stats = jnp.sum(rows_all[:, :, cols:].astype(F32), axis=0)
        rows_all = jnp.swapaxes(rows_all[:, :, :cols], 0, 1).reshape(slots, features)
        inverse = lax.rsqrt(jnp.sum(stats[:, :3], axis=1) / features + EPS)[:, None]
        gate = mm(rows_all, w_gate[0], NT) * inverse
        hidden = (gate * sigmoid(gate) * (mm(rows_all, w_up[0], NT) * inverse)).astype(BF16)
        weight = sigmoid(jnp.sum(stats[:, 3:6], axis=1)[:, None] * inverse)
        state = [hidden, jnp.broadcast_to(weight, (slots, 128))]
    for n, group in enumerate(groups if cols % 128 == 0 else ()):
        last = n == len(groups) - 1
        hbm = pl.BlockSpec(memory_space=pl.ANY)
        outs = [sds((slots, units), F32)] * 2 + [sds((slots, 128), F32)]
        if last:
            outs = [sds((slots, units), BF16), sds((slots, 128), F32)]
        state = call(
            functools.partial(up_kernel, nz, ny, group, n == 0, last, features),
            place,
            [arrived[p] for p in group] + list(state) + [(w_gate, hbm), (w_up, hbm)],
            outs,
            [pltpu.VMEM((len(group), units, cols), BF16)] * 2
            + [pltpu.SemaphoreType.DMA((2, len(group)))],
            flops=4 * len(group) * slots * units * cols,
        )
    hidden, weight = state
    arrived = gather(hidden)
    state = []
    for n, group in enumerate(groups):
        last = n == len(groups) - 1
        outs = [sds((slots, cols), F32)]
        if last:
            outs = [sds((ret_rows, cols), BF16)] * nz
        state = call(
            functools.partial(down_kernel, nz, ny, group, n == 0, last),
            place,
            [arrived[p] for p in group]
            + list(state)
            + [(w_down, pl.BlockSpec(memory_space=pl.ANY))]
            + ([weight, out_ids, own_rows[None]] if last else []),
            outs,
            [
                pltpu.VMEM((len(group), units, cols), BF16),
                pltpu.SemaphoreType.DMA((len(group),)),
            ],
            flops=2 * len(group) * slots * units * cols,
        )
    returned = [state[0]] + [swap(state[r], r) for r in range(1, nz)]
    (layer_out,) = call(
        functools.partial(combine_kernel, nz),
        place,
        returned
        + [keep_all[0], received_all[0], residual, jnp.transpose(codes_j), ret_ids],
        [sds((block, cols), BF16)],
        [pltpu.VMEM((nz * ret_rows, cols), BF16)],
    )
    return layer_out, final_rows


def solution(mesh):
    in_specs = (
        P("exp", "seq"),
        P("seq", "exp"),
        P("seq", "exp"),
        P("seq", "exp"),
        P("seq", "exp"),
        P("seq", "exp"),
        P("exp", None, None),
        P("exp"),
        P("exp", "seq"),
        P("seq"),
        P("seq", None),
        P("exp", "seq", None),
        P("exp", "seq", None),
        P("exp", None, "seq"),
        P("exp", None),
        P(),
    )
    out_specs = (P("exp", "seq"), P("exp", "seq", None))
    return jax.shard_map(local, mesh=mesh, in_specs=in_specs, out_specs=out_specs, check_vma=False)
```

time: 447 us -> 235 us (0.53)
  waiting for transfers between devices: 247 us -> 95 us
  blocking collectives: 88.4 us -> 0 us
  starting transfers between devices: 4.14 us -> 60.8 us
  matrix products: 51.6 us -> 0.82 us
  Pallas kernels: 0 us -> 48.7 us
  other arithmetic: 20.3 us -> 6.58 us
  between operations: 14.7 us -> 1.2 us
    all_gather x3 -> x0, waiting for transfers between devices: 175 us -> none  [the longest x1 89.3 us: local(): gathered = lax.all_gather(heads_mixed, 'seq', axis=0, tiled=True)]
    ppermute x0 -> x47, waiting for transfers between devices: none -> 95 us  [the longest x18 49.1 us: z_turn(): return lax.ppermute(a, 'seq', pairs)]
    ppermute x0 -> x47, starting transfers between devices: none -> 60.8 us  [the longest x18 34.2 us: z_turn(): return lax.ppermute(a, 'seq', pairs)]
    psum x1 -> x0, waiting for transfers between devices: 56.3 us -> none  [broadcast(): return lax.psum(kept, axis)]
    all_gather x2 -> x0, blocking collectives: 55 us -> none  [the longest x1 32.6 us: local(): portion = lax.all_gather(arrived, 'seq', axis=2, tiled=True)]
    dot_general x10 -> x1, matrix products: 49.8 us -> 0.82 us  [local(): jnp.einsum('ebt,ts->ebs', named.astype(BF16), strict, preferred_element_t...]
    pallas_call x0 -> x14, Pallas kernels: none -> 48.7 us  [call(): pl.pallas_call(kernel, out_shape=list(outs), grid_spec=pltpu.PrefetchScal...]
    psum x1 -> x0, blocking collectives: 21.4 us -> none  [local(): lax.psum((jnp.sum(after_attn * after_attn, axis=1), chosen_part), 'seq')]
  transfers between devices with their start and end apart: 6 -> 47, of which waited for: 5 -> 23; matrix products, arithmetic and copies ran while one was open for 6% -> 7% of each run, Pallas kernels for 0% -> 18%
where the time goes in v1:
time: 235 us; the launch traced here: 234 us
  waiting for transfers between devices  95 us (40%)
  starting transfers between devices  60.8 us (26%)
  Pallas kernels  48.7 us (21%)
  local copies, waits for them, and re-layouts  21.1 us (9%)
  other arithmetic  6.58 us (3%)
    ppermute x18, waiting for transfers between devices, z_turn(): return lax.ppermute(a, 'seq', pairs)  49.1 us
    pallas_call x14, Pallas kernels, call(): pl.pallas_call(kernel, out_shape=list(outs), grid_spec=pltpu.PrefetchScal...  48.7 us
    ppermute x20, waiting for transfers between devices, y_turn(): return lax.ppermute(a, 'seq', pairs)  41.1 us
    ppermute x18, starting transfers between devices, z_turn(): return lax.ppermute(a, 'seq', pairs)  34.2 us
    ppermute x20, starting transfers between devices, y_turn(): return lax.ppermute(a, 'seq', pairs)  19 us
    unnamed x78, local copies, waits for them, and re-layouts  13.9 us
    ppermute x9, starting transfers between devices, swap(): return lax.ppermute(a, 'exp', [(p, p ^ r) for p in range(nz)])  7.54 us
    ppermute x9, waiting for transfers between devices, swap(): return lax.ppermute(a, 'exp', [(p, p ^ r) for p in range(nz)])  4.87 us
  transfers between devices with their start and end apart: 47, of which 23 were waited for; matrix products, arithmetic and copies ran while one was open for 7% of the time, Pallas kernels for 18%

profile of v1, /device:TPU:0, one launch (start us, length us, event | category | flops | bytes accessed | tf_op | source)
XLA Modules:
  0.0 234.2 jit_solution(3957072594207276260)
XLA Ops:
  1.9 2.6 %collective-permute-start.2 = (f32[8,128]{1,0:T(8,128)S(1)}, f32[8,128]{1,0:T(8,128)S(1)}, u32[]{:S(2)}, u32[]{:S(2)}) collective-permute-start(f32[8,128]{1,0:T(8,128)S(1)} %get-tuple-element.80), channel_id=1, source_target_pairs={{0,4},{4,0},{8,12},{12,8},{16,20},{20,16},{24,28},{28,24},{1,5},{5... | collective-permute-start | bytes 12296 | tf_op jit(solution)/shard_map/ppermute | solution.py:396
  10.1 2.0 collective-permute-start.1
  14.8 1.5 collective-permute-start.10
  20.7 4.2 %collective-permute-done.refs_2_.refs_4_ = bf16[2,128,1024]{2,1,0:T(8,128)(2,1)S(1)} collective-permute-done((bf16[2,128,1024]{2,1,0:T(8,128)(2,1)S(1)}, bf16[2,128,1024]{2,1,0:T(8,128)(2,1)S(1)}, u32[]{:S(2)}, u32[]{:S(2)}) %collective-permute-start) | collective-permute-done | bytes 524320 | tf_op jit(solution)/shard_map/ppermute | solution.py:396
  26.9 2.1 shard_map.177
  29.8 1.6 collective-permute-start.3
  31.4 2.6 %collective-permute-start.4 = (bf16[272,128]{1,0:T(8,128)(2,1)S(1)}, bf16[272,128]{1,0:T(8,128)(2,1)S(1)}, u32[]{:S(2)}, u32[]{:S(2)}) collective-permute-start(bf16[272,128]{1,0:T(8,128)(2,1)S(1)} %get-tuple-element.37), channel_id=1, source_target_pairs={{0,16},{4,20},{8,24},{12,28},{16,0},{20,4},{24,8},{28,12},{1,17},{... | collective-permute-start | bytes 208904 | tf_op jit(solution)/shard_map/ppermute | solution.py:392
  36.5 1.7 collective-permute-done.4.refs_2_
  42.0 2.6 %collective-permute-start.7 = (bf16[256,128]{1,0:T(8,128)(2,1)S(1)}, bf16[256,128]{1,0:T(8,128)(2,1)S(1)}, u32[]{:S(2)}, u32[]{:S(2)}) collective-permute-start(bf16[256,128]{1,0:T(8,128)(2,1)S(1)} %get-tuple-element.41), channel_id=1, source_target_pairs={{0,16},{4,20},{8,24},{12,28},{16,0},{20,4},{24,8},{28,12},{1,17},{... | collective-permute-start | bytes 196616 | tf_op jit(solution)/shard_map/ppermute | solution.py:392
  45.2 2.3 collective-permute-done.6.refs_7_
  50.3 4.8 %shard_map.179 = (bf16[256,1024]{1,0:T(8,128)(2,1)S(1)}, bf16[80,1024]{1,0:T(8,128)(2,1)}) custom-call(s32[3]{0:T(128)S(1)} %pad_add_fusion.3.s, bf16[128,2048]{1,0:T(8,128)(2,1)S(1)} %copy-done.3, bf16[128,2048]{1,0:T(8,128)(2,1)S(1)} %copy-done.6, bf16[128,2048]{1,0:T(8,128)(2,1)S(1)} %copy-done.8, bf16[128,2048]{1,0:T(8,128)(2,1)S(1)} %copy-done.10, ...), custom_call_target="tpu_custom_call" | custom-call | flops 268435456 | bytes 4122944 | tf_op jit(solution)/shard_map/pallas_call | solution.py:46
  56.7 2.3 collective-permute-start.12
  62.4 2.9 %collective-permute-done.11.refs_1_ = bf16[80,1024]{1,0:T(8,128)(2,1)} collective-permute-done((bf16[80,1024]{1,0:T(8,128)(2,1)}, bf16[80,1024]{1,0:T(8,128)(2,1)}, u32[]{:S(2)}, u32[]{:S(2)}) %collective-permute-start.11) | collective-permute-done | bytes 163872 | tf_op jit(solution)/shard_map/ppermute | solution.py:392
  65.3 3.2 %collective-permute-start.39 = (bf16[256,1024]{1,0:T(8,128)(2,1)}, bf16[256,1024]{1,0:T(8,128)(2,1)}, u32[]{:S(2)}, u32[]{:S(2)}) collective-permute-start(bf16[256,1024]{1,0:T(8,128)(2,1)} %copy-done.22), channel_id=1, source_target_pairs={{0,24},{4,28},{8,0},{12,4},{16,8},{20,12},{24,16},{28,20},{1,25},{... | collective-permute-start | bytes 1572872 | tf_op jit(solution)/shard_map/ppermute | solution.py:392
  68.5 18.9 %collective-permute-done.12.refs_2_ = bf16[80,1024]{1,0:T(8,128)(2,1)} collective-permute-done((bf16[80,1024]{1,0:T(8,128)(2,1)}, bf16[80,1024]{1,0:T(8,128)(2,1)}, u32[]{:S(2)}, u32[]{:S(2)}) %collective-permute-start.12) | collective-permute-done | bytes 163872 | tf_op jit(solution)/shard_map/ppermute | solution.py:392
  87.7 1.8 collective-permute-start.15
  90.9 1.5 add.336.refs_10_
  92.4 1.8 copy.37.router
  97.5 1.8 collective-permute-start.17
  100.0 2.8 %collective-permute-done.16.refs_6_ = bf16[80,1024]{1,0:T(8,128)(2,1)S(1)} collective-permute-done((bf16[80,1024]{1,0:T(8,128)(2,1)}, bf16[80,1024]{1,0:T(8,128)(2,1)S(1)}, u32[]{:S(2)}, u32[]{:S(2)}) %collective-permute-start.16) | collective-permute-done | bytes 163872 | tf_op jit(solution)/shard_map/ppermute | solution.py:396
  103.0 1.5 collective-permute-done.17.refs_7_
  105.5 3.7 %shard_map.180 = (f32[160,768]{1,0:T(8,128)S(1)}, bf16[160,768]{1,0:T(8,128)(2,1)S(1)}) custom-call(s32[3]{0:T(128)S(1)} %pad_add_fusion.3.s, bf16[80,1024]{1,0:T(8,128)(2,1)} %get-tuple-element.45.refs_0_, bf16[80,1024]{1,0:T(8,128)(2,1)} %collective-permute-done.11.refs_1_, bf16[80,1024]{1,0:T(8,128)(2,1)} %collective-permute-done.12.refs_2_, ...), custom_call_target="tpu_custom_call" | custom-call | flops 1006632960 | bytes 8737280 | tf_op jit(solution)/shard_map/pallas_call | solution.py:46
  109.6 1.8 collective-permute-start.42
  111.9 1.8 collective-permute-start.19
  113.7 10.5 %collective-permute-done.41.refs_5_ = bf16[256,1024]{1,0:T(8,128)(2,1)S(1)} collective-permute-done((bf16[256,1024]{1,0:T(8,128)(2,1)}, bf16[256,1024]{1,0:T(8,128)(2,1)S(1)}, u32[]{:S(2)}, u32[]{:S(2)}) %collective-permute-start.41) | collective-permute-done | bytes 524320 | tf_op jit(solution)/shard_map/ppermute | solution.py:396
  124.3 11.2 %collective-permute-done.42.refs_6_ = bf16[256,1024]{1,0:T(8,128)(2,1)S(1)} collective-permute-done((bf16[256,1024]{1,0:T(8,128)(2,1)}, bf16[256,1024]{1,0:T(8,128)(2,1)S(1)}, u32[]{:S(2)}, u32[]{:S(2)}) %collective-permute-start.42) | collective-permute-done | bytes 524320 | tf_op jit(solution)/shard_map/ppermute | solution.py:396
  135.5 10.8 %collective-permute-done.43.refs_7_ = bf16[256,1024]{1,0:T(8,128)(2,1)S(1)} collective-permute-done((bf16[256,1024]{1,0:T(8,128)(2,1)}, bf16[256,1024]{1,0:T(8,128)(2,1)S(1)}, u32[]{:S(2)}, u32[]{:S(2)}) %collective-permute-start.43) | collective-permute-done | bytes 524320 | tf_op jit(solution)/shard_map/ppermute | solution.py:396
  146.3 5.5 %shard_map.188 = (bf16[2,256,768]{2,1,0:T(8,128)(2,1)S(1)}, bf16[2,256,768]{2,1,0:T(8,128)(2,1)S(1)}) custom-call(s32[3]{0:T(128)S(1)} %pad_add_fusion.3.s, bf16[256,1024]{1,0:T(8,128)(2,1)S(1)} %copy-done.23, bf16[256,1024]{1,0:T(8,128)(2,1)} %collective-permute-done.37.refs_1_, bf16[256,1024]{1,0:T(8,128)(2,1)} %collective-permute-done.38.refs_2_, ...), custom_call_target="tpu_custom_call" | custom-call | flops 3221225472 | bytes 12058624 | tf_op jit(solution)/shard_map/pallas_call | solution.py:46
  153.0 9.4 %collective-permute-start.20 = (bf16[80,896]{1,0:T(8,128)(2,1)S(1)}, bf16[80,896]{1,0:T(8,128)(2,1)S(1)}, u32[]{:S(2)}, u32[]{:S(2)}) collective-permute-start(bf16[80,896]{1,0:T(8,128)(2,1)S(1)} %shard_map.181.refs_0_), channel_id=1, source_target_pairs={{0,8},{4,12},{8,16},{12,20},{16,24},{20,28},{24,0},{28,4},{1,9},{5... | collective-permute-start | bytes 430088 | tf_op jit(solution)/shard_map/ppermute | solution.py:392
  162.4 1.5 collective-permute-start.24
  164.6 1.9 collective-permute-done.20.refs_0_
  167.2 2.4 %collective-permute-done.22.refs_1_ = bf16[80,896]{1,0:T(8,128)(2,1)S(1)} collective-permute-done((bf16[80,896]{1,0:T(8,128)(2,1)S(1)}, bf16[80,896]{1,0:T(8,128)(2,1)S(1)}, u32[]{:S(2)}, u32[]{:S(2)}) %collective-permute-start.22) | collective-permute-done | bytes 143392 | tf_op jit(solution)/shard_map/ppermute | solution.py:392
  170.3 3.9 %collective-permute-done.24.refs_2_ = bf16[80,896]{1,0:T(8,128)(2,1)S(1)} collective-permute-done((bf16[80,896]{1,0:T(8,128)(2,1)S(1)}, bf16[80,896]{1,0:T(8,128)(2,1)S(1)}, u32[]{:S(2)}, u32[]{:S(2)}) %collective-permute-start.24) | collective-permute-done | bytes 143392 | tf_op jit(solution)/shard_map/ppermute | solution.py:392
  175.0 5.6 %shard_map.182 = (f32[80,1152]{1,0:T(8,128)S(1)}, f32[80,1152]{1,0:T(8,128)S(1)}, f32[80,128]{1,0:T(8,128)S(1)}) custom-call(s32[3]{0:T(128)S(1)} %pad_add_fusion.3.s, bf16[80,896]{1,0:T(8,128)(2,1)S(1)} %shard_map.181.refs_0_, bf16[80,896]{1,0:T(8,128)(2,1)S(1)} %collective-permute-done.26.refs_1_, bf16[1,1152,6144]{2,1,0:T(8,128)(2,1)} %refs_6_.4, ...), custom_call_target="tpu_custom_call" | custom-call | flops 566231040 | bytes 29376512 | tf_op jit(solution)/shard_map/pallas_call | solution.py:46
  180.6 5.8 %shard_map.183 = (f32[80,1152]{1,0:T(8,128)S(1)}, f32[80,1152]{1,0:T(8,128)S(1)}, f32[80,128]{1,0:T(8,128)S(1)}) custom-call(s32[3]{0:T(128)S(1)} %pad_add_fusion.3.s, bf16[80,896]{1,0:T(8,128)(2,1)S(1)} %collective-permute-done.20.refs_0_, bf16[80,896]{1,0:T(8,128)(2,1)S(1)} %collective-permute-done.22.refs_1_, ...), custom_call_target="tpu_custom_call" | custom-call | flops 849346560 | bytes 30298112 | tf_op jit(solution)/shard_map/pallas_call | solution.py:46
  186.4 5.8 %shard_map.184 = (bf16[80,1152]{1,0:T(8,128)(2,1)S(1)}, f32[80,128]{1,0:T(8,128)S(1)}) custom-call(s32[3]{0:T(128)S(1)} %pad_add_fusion.3.s, bf16[80,896]{1,0:T(8,128)(2,1)S(1)} %collective-permute-done.21.refs_0_, bf16[80,896]{1,0:T(8,128)(2,1)S(1)} %collective-permute-done.23.refs_1_, bf16[80,896]{1,0:T(8,128)(2,1)S(1)} %collective-permute-done.25.refs_2_, ...), custom_call_target="tpu_custom_call" | custom-call | flops 849346560 | bytes 29745152 | tf_op jit(solution)/shard_map/pallas_call | solution.py:46
  192.2 1.4 collective-permute-start.33
  193.6 1.4 collective-permute-start.27
  195.1 2.8 %collective-permute-start.29 = (bf16[80,1152]{1,0:T(8,128)(2,1)S(1)}, bf16[80,1152]{1,0:T(8,128)(2,1)S(1)}, u32[]{:S(2)}, u32[]{:S(2)}) collective-permute-start(bf16[80,1152]{1,0:T(8,128)(2,1)S(1)} %get-tuple-element.54.refs_0_), channel_id=1, source_target_pairs={{0,24},{4,28},{8,0},{12,4},{16,8},{20,12},{24,16},{28,20},{1,25},{... | collective-permute-start | bytes 552968 | tf_op jit(solution)/shard_map/ppermute | solution.py:392
  198.8 1.7 collective-permute-start.45
  200.6 2.9 %collective-permute-done.27.refs_0_ = bf16[80,1152]{1,0:T(8,128)(2,1)S(1)} collective-permute-done((bf16[80,1152]{1,0:T(8,128)(2,1)S(1)}, bf16[80,1152]{1,0:T(8,128)(2,1)S(1)}, u32[]{:S(2)}, u32[]{:S(2)}) %collective-permute-start.27) | collective-permute-done | bytes 184352 | tf_op jit(solution)/shard_map/ppermute | solution.py:392
  205.5 8.4 %collective-permute-done.31.refs_2_ = bf16[80,1152]{1,0:T(8,128)(2,1)S(1)} collective-permute-done((bf16[80,1152]{1,0:T(8,128)(2,1)S(1)}, bf16[80,1152]{1,0:T(8,128)(2,1)S(1)}, u32[]{:S(2)}, u32[]{:S(2)}) %collective-permute-start.31) | collective-permute-done | bytes 184352 | tf_op jit(solution)/shard_map/ppermute | solution.py:392
  216.3 3.3 %shard_map.185.refs_3_ = f32[80,768]{1,0:T(8,128)S(1)} custom-call(s32[3]{0:T(128)S(1)} %pad_add_fusion.3.s, bf16[80,1152]{1,0:T(8,128)(2,1)S(1)} %get-tuple-element.54.refs_0_, bf16[80,1152]{1,0:T(8,128)(2,1)S(1)} %collective-permute-done.33.refs_1_, bf16[1,9216,768]{2,1,0:T(8,128)(2,1)} %refs_4_.5), custom_call_target="tpu_custom_call" | custom-call | flops 283115520 | bytes 14770176 | tf_op jit(solution)/shard_map/pallas_call | solution.py:46
  219.6 3.6 %shard_map.186.refs_3_ = f32[80,768]{1,0:T(8,128)S(1)} custom-call(s32[3]{0:T(128)S(1)} %pad_add_fusion.3.s, bf16[80,1152]{1,0:T(8,128)(2,1)S(1)} %collective-permute-done.27.refs_0_, bf16[80,1152]{1,0:T(8,128)(2,1)S(1)} %collective-permute-done.29.refs_1_, bf16[80,1152]{1,0:T(8,128)(2,1)S(1)} %collective-permute-done.31.refs_2_, ...), custom_call_target="tpu_custom_call" | custom-call | flops 424673280 | bytes 15200256 | tf_op jit(solution)/shard_map/pallas_call | solution.py:46
  223.3 3.8 %shard_map.187 = (bf16[32,768]{1,0:T(8,128)(2,1)S(1)}, bf16[32,768]{1,0:T(8,128)(2,1)S(1)}, bf16[32,768]{1,0:T(8,128)(2,1)S(1)}, bf16[32,768]{1,0:T(8,128)(2,1)S(1)}) custom-call(s32[3]{0:T(128)S(1)} %pad_add_fusion.3.s, bf16[80,1152]{1,0:T(8,128)(2,1)S(1)} %collective-permute-done.28.refs_0_, bf16[80,1152]{1,0:T(8,128)(2,1)S(1)} %collective-permute-done.30.refs_1_, ...), custom_call_target="tpu_custom_call" | custom-call | flops 424673280 | bytes 15192896 | tf_op jit(solution)/shard_map/pallas_call | solution.py:46
  227.2 1.7 collective-permute-start.35
  229.1 2.3 collective-permute-done.35.refs_2_
  232.6 1.7 shard_map.189
  (188 shorter events, 50.0 us)
Async XLA Ops:
  0.6 13.5 %collective-permute-start.9 = (s32[1,2,256]{2,1,0:T(2,128)}, s32[1,2,256]{2,1,0:T(2,128)S(1)}, u32[]{:S(2)}, u32[]{:S(2)}) collective-permute-start(s32[1,2,256]{2,1,0:T(2,128)} %bitcast.44), channel_id=1, source_target_pairs={{0,1},{1,0},{2,3},{3,2},{4,5},{5,4},{6,7},{7,6},{8,9},{9,8},{10,11... | collective-permute-start | bytes 6152 | tf_op jit(solution)/shard_map/ppermute | solution.py:399
  1.9 18.8 %collective-permute-start.2 = (f32[8,128]{1,0:T(8,128)S(1)}, f32[8,128]{1,0:T(8,128)S(1)}, u32[]{:S(2)}, u32[]{:S(2)}) collective-permute-start(f32[8,128]{1,0:T(8,128)S(1)} %get-tuple-element.80), channel_id=1, source_target_pairs={{0,4},{4,0},{8,12},{12,8},{16,20},{20,16},{24,28},{28,24},{1,5},{5... | collective-permute-start | bytes 12296 | tf_op jit(solution)/shard_map/ppermute | solution.py:396
  10.1 14.8 %collective-permute-start = (bf16[2,128,1024]{2,1,0:T(8,128)(2,1)S(1)}, bf16[2,128,1024]{2,1,0:T(8,128)(2,1)S(1)}, u32[]{:S(2)}, u32[]{:S(2)}) collective-permute-start(bf16[2,128,1024]{2,1,0:T(8,128)(2,1)S(1)} %get-tuple-element.33), channel_id=1, source_target_pairs={{0,4},{4,0},{8,12},{12,8},{16,20},{20,16},{24,28},{28,24},{1,5},{5... | collective-permute-start | bytes 1572872 | tf_op jit(solution)/shard_map/ppermute | solution.py:396
  10.1 35.1 %collective-permute-start.1 = (bf16[2,128,1024]{2,1,0:T(8,128)(2,1)}, bf16[2,128,1024]{2,1,0:T(8,128)(2,1)}, u32[]{:S(2)}, u32[]{:S(2)}) collective-permute-start(bf16[2,128,1024]{2,1,0:T(8,128)(2,1)} %get-tuple-element.34), channel_id=1, source_target_pairs={{0,4},{4,0},{8,12},{12,8},{16,20},{20,16},{24,28},{28,24},{1,5},{5... | collective-permute-start | bytes 1572872 | tf_op jit(solution)/shard_map/ppermute | solution.py:396
  14.8 3.6 %collective-permute-start.10 = (s32[2,2,256]{2,1,0:T(2,128)S(1)}, s32[2,2,256]{2,1,0:T(2,128)S(1)}, u32[]{:S(2)}, u32[]{:S(2)}) collective-permute-start(s32[2,2,256]{2,1,0:T(2,128)S(1)} %pad_add_fusion.2), channel_id=1, source_target_pairs={{0,2},{1,3},{2,0},{3,1},{4,6},{5,7},{6,4},{7,5},{8,10},{9,11},{10,... | collective-permute-start | bytes 12296 | tf_op jit(solution)/shard_map/ppermute | solution.py:399
  29.8 74.7 %copy-start = (bf16[2048,768]{1,0:T(8,128)(2,1)S(1)}, bf16[2048,768]{1,0:T(8,128)(2,1)}, u32[]{:S(2)}) copy-start(bf16[2048,768]{1,0:T(8,128)(2,1)} %refs_9_.3) | copy-start | bytes 9437188
  29.8 6.6 %collective-permute-start.3 = (bf16[272,128]{1,0:T(8,128)(2,1)S(1)}, bf16[272,128]{1,0:T(8,128)(2,1)S(1)}, u32[]{:S(2)}, u32[]{:S(2)}) collective-permute-start(bf16[272,128]{1,0:T(8,128)(2,1)S(1)} %get-tuple-element.36), channel_id=1, source_target_pairs={{0,8},{4,12},{8,16},{12,20},{16,24},{20,28},{24,0},{28,4},{1,9},{5... | collective-permute-start | bytes 208904 | tf_op jit(solution)/shard_map/ppermute | solution.py:392
  31.4 6.8 %collective-permute-start.4 = (bf16[272,128]{1,0:T(8,128)(2,1)S(1)}, bf16[272,128]{1,0:T(8,128)(2,1)S(1)}, u32[]{:S(2)}, u32[]{:S(2)}) collective-permute-start(bf16[272,128]{1,0:T(8,128)(2,1)S(1)} %get-tuple-element.37), channel_id=1, source_target_pairs={{0,16},{4,20},{8,24},{12,28},{16,0},{20,4},{24,8},{28,12},{1,17},{... | collective-permute-start | bytes 208904 | tf_op jit(solution)/shard_map/ppermute | solution.py:392
  34.0 4.8 %collective-permute-start.5 = (bf16[272,128]{1,0:T(8,128)(2,1)S(1)}, bf16[272,128]{1,0:T(8,128)(2,1)S(1)}, u32[]{:S(2)}, u32[]{:S(2)}) collective-permute-start(bf16[272,128]{1,0:T(8,128)(2,1)S(1)} %get-tuple-element.38), channel_id=1, source_target_pairs={{0,24},{4,28},{8,0},{12,4},{16,8},{20,12},{24,16},{28,20},{1,25},{... | collective-permute-start | bytes 208904 | tf_op jit(solution)/shard_map/ppermute | solution.py:392
  41.4 6.2 %collective-permute-start.6 = (bf16[256,128]{1,0:T(8,128)(2,1)S(1)}, bf16[256,128]{1,0:T(8,128)(2,1)S(1)}, u32[]{:S(2)}, u32[]{:S(2)}) collective-permute-start(bf16[256,128]{1,0:T(8,128)(2,1)S(1)} %get-tuple-element.40), channel_id=1, source_target_pairs={{0,8},{4,12},{8,16},{12,20},{16,24},{20,28},{24,0},{28,4},{1,9},{5... | collective-permute-start | bytes 196616 | tf_op jit(solution)/shard_map/ppermute | solution.py:392
  42.0 6.7 %collective-permute-start.7 = (bf16[256,128]{1,0:T(8,128)(2,1)S(1)}, bf16[256,128]{1,0:T(8,128)(2,1)S(1)}, u32[]{:S(2)}, u32[]{:S(2)}) collective-permute-start(bf16[256,128]{1,0:T(8,128)(2,1)S(1)} %get-tuple-element.41), channel_id=1, source_target_pairs={{0,16},{4,20},{8,24},{12,28},{16,0},{20,4},{24,8},{28,12},{1,17},{... | collective-permute-start | bytes 196616 | tf_op jit(solution)/shard_map/ppermute | solution.py:392
  44.6 4.6 %collective-permute-start.8 = (bf16[256,128]{1,0:T(8,128)(2,1)S(1)}, bf16[256,128]{1,0:T(8,128)(2,1)S(1)}, u32[]{:S(2)}, u32[]{:S(2)}) collective-permute-start(bf16[256,128]{1,0:T(8,128)(2,1)S(1)} %get-tuple-element.42), channel_id=1, source_target_pairs={{0,24},{4,28},{8,0},{12,4},{16,8},{20,12},{24,16},{28,20},{1,25},{... | collective-permute-start | bytes 196616 | tf_op jit(solution)/shard_map/ppermute | solution.py:392
  55.9 9.4 %collective-permute-start.11 = (bf16[80,1024]{1,0:T(8,128)(2,1)}, bf16[80,1024]{1,0:T(8,128)(2,1)}, u32[]{:S(2)}, u32[]{:S(2)}) collective-permute-start(bf16[80,1024]{1,0:T(8,128)(2,1)} %get-tuple-element.45.refs_0_), channel_id=1, source_target_pairs={{0,8},{4,12},{8,16},{12,20},{16,24},{20,28},{24,0},{28,4},{1,9},{5... | collective-permute-start | bytes 491528 | tf_op jit(solution)/shard_map/ppermute | solution.py:392
  56.7 30.7 %collective-permute-start.12 = (bf16[80,1024]{1,0:T(8,128)(2,1)}, bf16[80,1024]{1,0:T(8,128)(2,1)}, u32[]{:S(2)}, u32[]{:S(2)}) collective-permute-start(bf16[80,1024]{1,0:T(8,128)(2,1)} %get-tuple-element.45.refs_0_), channel_id=1, source_target_pairs={{0,16},{4,20},{8,24},{12,28},{16,0},{20,4},{24,8},{28,12},{1,17},{... | collective-permute-start | bytes 491528 | tf_op jit(solution)/shard_map/ppermute | solution.py:392
  59.0 28.6 %collective-permute-start.13 = (bf16[80,1024]{1,0:T(8,128)(2,1)}, bf16[80,1024]{1,0:T(8,128)(2,1)}, u32[]{:S(2)}, u32[]{:S(2)}) collective-permute-start(bf16[80,1024]{1,0:T(8,128)(2,1)} %get-tuple-element.45.refs_0_), channel_id=1, source_target_pairs={{0,24},{4,28},{8,0},{12,4},{16,8},{20,12},{24,16},{28,20},{1,25},{... | collective-permute-start | bytes 491528 | tf_op jit(solution)/shard_map/ppermute | solution.py:392
  60.4 48.9 %collective-permute-start.37 = (bf16[256,1024]{1,0:T(8,128)(2,1)}, bf16[256,1024]{1,0:T(8,128)(2,1)}, u32[]{:S(2)}, u32[]{:S(2)}) collective-permute-start(bf16[256,1024]{1,0:T(8,128)(2,1)} %copy-done.22), channel_id=1, source_target_pairs={{0,8},{4,12},{8,16},{12,20},{16,24},{20,28},{24,0},{28,4},{1,9},{5... | collective-permute-start | bytes 1572872 | tf_op jit(solution)/shard_map/ppermute | solution.py:392
  61.7 47.9 %collective-permute-start.38 = (bf16[256,1024]{1,0:T(8,128)(2,1)}, bf16[256,1024]{1,0:T(8,128)(2,1)}, u32[]{:S(2)}, u32[]{:S(2)}) collective-permute-start(bf16[256,1024]{1,0:T(8,128)(2,1)} %copy-done.22), channel_id=1, source_target_pairs={{0,16},{4,20},{8,24},{12,28},{16,0},{20,4},{24,8},{28,12},{1,17},{... | collective-permute-start | bytes 1572872 | tf_op jit(solution)/shard_map/ppermute | solution.py:392
  65.3 46.1 %collective-permute-start.39 = (bf16[256,1024]{1,0:T(8,128)(2,1)}, bf16[256,1024]{1,0:T(8,128)(2,1)}, u32[]{:S(2)}, u32[]{:S(2)}) collective-permute-start(bf16[256,1024]{1,0:T(8,128)(2,1)} %copy-done.22), channel_id=1, source_target_pairs={{0,24},{4,28},{8,0},{12,4},{16,8},{20,12},{24,16},{28,20},{1,25},{... | collective-permute-start | bytes 1572872 | tf_op jit(solution)/shard_map/ppermute | solution.py:392
  87.4 9.8 %collective-permute-start.14 = (bf16[80,1024]{1,0:T(8,128)(2,1)}, bf16[80,1024]{1,0:T(8,128)(2,1)}, u32[]{:S(2)}, u32[]{:S(2)}) collective-permute-start(bf16[80,1024]{1,0:T(8,128)(2,1)} %get-tuple-element.45.refs_0_), channel_id=1, source_target_pairs={{0,4},{4,0},{8,12},{12,8},{16,20},{20,16},{24,28},{28,24},{1,5},{5... | collective-permute-start | bytes 491528 | tf_op jit(solution)/shard_map/ppermute | solution.py:396
  87.7 9.9 %collective-permute-start.15 = (bf16[80,1024]{1,0:T(8,128)(2,1)}, bf16[80,1024]{1,0:T(8,128)(2,1)}, u32[]{:S(2)}, u32[]{:S(2)}) collective-permute-start(bf16[80,1024]{1,0:T(8,128)(2,1)} %collective-permute-done.11.refs_1_), channel_id=1, source_target_pairs={{0,4},{4,0},{8,12},{12,8},{16,20},{20,16},{24,28},{28,24},{1,5},{5... | collective-permute-start | bytes 491528 | tf_op jit(solution)/shard_map/ppermute | solution.py:396
  97.2 5.6 %collective-permute-start.16 = (bf16[80,1024]{1,0:T(8,128)(2,1)}, bf16[80,1024]{1,0:T(8,128)(2,1)S(1)}, u32[]{:S(2)}, u32[]{:S(2)}) collective-permute-start(bf16[80,1024]{1,0:T(8,128)(2,1)} %collective-permute-done.12.refs_2_), channel_id=1, source_target_pairs={{0,4},{4,0},{8,12},{12,8},{16,20},{20,16},{24,28},{28,24},{1,5},{5... | collective-permute-start | bytes 491528 | tf_op jit(solution)/shard_map/ppermute | solution.py:396
  97.5 7.0 %collective-permute-start.17 = (bf16[80,1024]{1,0:T(8,128)(2,1)}, bf16[80,1024]{1,0:T(8,128)(2,1)S(1)}, u32[]{:S(2)}, u32[]{:S(2)}) collective-permute-start(bf16[80,1024]{1,0:T(8,128)(2,1)} %collective-permute-done.13.refs_3_), channel_id=1, source_target_pairs={{0,4},{4,0},{8,12},{12,8},{16,20},{20,16},{24,28},{28,24},{1,5},{5... | collective-permute-start | bytes 491528 | tf_op jit(solution)/shard_map/ppermute | solution.py:396
  102.8 10.9 %collective-permute-start.40 = (bf16[256,1024]{1,0:T(8,128)(2,1)}, bf16[256,1024]{1,0:T(8,128)(2,1)S(1)}, u32[]{:S(2)}, u32[]{:S(2)}) collective-permute-start(bf16[256,1024]{1,0:T(8,128)(2,1)} %copy-done.22), channel_id=1, source_target_pairs={{0,4},{4,0},{8,12},{12,8},{16,20},{20,16},{24,28},{28,24},{1,5},{5... | collective-permute-start | bytes 1572872 | tf_op jit(solution)/shard_map/ppermute | solution.py:396
  109.2 2.7 %collective-permute-start.18 = (bf16[160,768]{1,0:T(8,128)(2,1)S(1)}, bf16[160,768]{1,0:T(8,128)(2,1)S(1)}, u32[]{:S(2)}, u32[]{:S(2)}) collective-permute-start(bf16[160,768]{1,0:T(8,128)(2,1)S(1)} %get-tuple-element.47), channel_id=1, source_target_pairs={{0,1},{1,0},{2,3},{3,2},{4,5},{5,4},{6,7},{7,6},{8,9},{9,8},{10,11... | collective-permute-start | bytes 737288 | tf_op jit(solution)/shard_map/ppermute | solution.py:399
  109.3 15.0 %collective-permute-start.41 = (bf16[256,1024]{1,0:T(8,128)(2,1)}, bf16[256,1024]{1,0:T(8,128)(2,1)S(1)}, u32[]{:S(2)}, u32[]{:S(2)}) collective-permute-start(bf16[256,1024]{1,0:T(8,128)(2,1)} %collective-permute-done.37.refs_1_), channel_id=1, source_target_pairs={{0,4},{4,0},{8,12},{12,8},{16,20},{20,16},{24,28},{28,24},{1,5},{5... | collective-permute-start | bytes 1572872 | tf_op jit(solution)/shard_map/ppermute | solution.py:396
  109.6 25.9 %collective-permute-start.42 = (bf16[256,1024]{1,0:T(8,128)(2,1)}, bf16[256,1024]{1,0:T(8,128)(2,1)S(1)}, u32[]{:S(2)}, u32[]{:S(2)}) collective-permute-start(bf16[256,1024]{1,0:T(8,128)(2,1)} %collective-permute-done.38.refs_2_), channel_id=1, source_target_pairs={{0,4},{4,0},{8,12},{12,8},{16,20},{20,16},{24,28},{28,24},{1,5},{5... | collective-permute-start | bytes 1572872 | tf_op jit(solution)/shard_map/ppermute | solution.py:396
  111.4 34.9 %collective-permute-start.43 = (bf16[256,1024]{1,0:T(8,128)(2,1)}, bf16[256,1024]{1,0:T(8,128)(2,1)S(1)}, u32[]{:S(2)}, u32[]{:S(2)}) collective-permute-start(bf16[256,1024]{1,0:T(8,128)(2,1)} %collective-permute-done.39.refs_3_), channel_id=1, source_target_pairs={{0,4},{4,0},{8,12},{12,8},{16,20},{20,16},{24,28},{28,24},{1,5},{5... | collective-permute-start | bytes 1572872 | tf_op jit(solution)/shard_map/ppermute | solution.py:396
  111.9 40.1 %collective-permute-start.19 = (bf16[80,768]{1,0:T(8,128)(2,1)S(1)}, bf16[80,768]{1,0:T(8,128)(2,1)S(1)}, u32[]{:S(2)}, u32[]{:S(2)}) collective-permute-start(bf16[80,768]{1,0:T(8,128)(2,1)S(1)} %get-tuple-element.68), channel_id=1, source_target_pairs={{0,2},{1,3},{2,0},{3,1},{4,6},{5,7},{6,4},{7,5},{8,10},{9,11},{10,... | collective-permute-start | bytes 368648 | tf_op jit(solution)/shard_map/ppermute | solution.py:399
  151.8 46.7 %collective-permute-start.44 = (bf16[2,256,768]{2,1,0:T(8,128)(2,1)S(1)}, bf16[2,256,768]{2,1,0:T(8,128)(2,1)S(1)}, u32[]{:S(2)}, u32[]{:S(2)}) collective-permute-start(bf16[2,256,768]{2,1,0:T(8,128)(2,1)S(1)} %get-tuple-element.62), channel_id=1, source_target_pairs={{0,1},{1,0},{2,3},{3,2},{4,5},{5,4},{6,7},{7,6},{8,9},{9,8},{10,11... | collective-permute-start | bytes 2359304 | tf_op jit(solution)/shard_map/ppermute | solution.py:399
  153.0 13.5 %collective-permute-start.20 = (bf16[80,896]{1,0:T(8,128)(2,1)S(1)}, bf16[80,896]{1,0:T(8,128)(2,1)S(1)}, u32[]{:S(2)}, u32[]{:S(2)}) collective-permute-start(bf16[80,896]{1,0:T(8,128)(2,1)S(1)} %shard_map.181.refs_0_), channel_id=1, source_target_pairs={{0,8},{4,12},{8,16},{12,20},{16,24},{20,28},{24,0},{28,4},{1,9},{5... | collective-permute-start | bytes 430088 | tf_op jit(solution)/shard_map/ppermute | solution.py:392
  162.4 7.2 %collective-permute-start.22 = (bf16[80,896]{1,0:T(8,128)(2,1)S(1)}, bf16[80,896]{1,0:T(8,128)(2,1)S(1)}, u32[]{:S(2)}, u32[]{:S(2)}) collective-permute-start(bf16[80,896]{1,0:T(8,128)(2,1)S(1)} %shard_map.181.refs_0_), channel_id=1, source_target_pairs={{0,24},{4,28},{8,0},{12,4},{16,8},{20,12},{24,16},{28,20},{1,25},{... | collective-permute-start | bytes 430088 | tf_op jit(solution)/shard_map/ppermute | solution.py:392
  162.4 11.8 %collective-permute-start.24 = (bf16[80,896]{1,0:T(8,128)(2,1)S(1)}, bf16[80,896]{1,0:T(8,128)(2,1)S(1)}, u32[]{:S(2)}, u32[]{:S(2)}) collective-permute-start(bf16[80,896]{1,0:T(8,128)(2,1)S(1)} %shard_map.181.refs_0_), channel_id=1, source_target_pairs={{0,16},{4,20},{8,24},{12,28},{16,0},{20,4},{24,8},{28,12},{1,17},{... | collective-permute-start | bytes 430088 | tf_op jit(solution)/shard_map/ppermute | solution.py:392
  164.0 11.0 %collective-permute-start.26 = (bf16[80,896]{1,0:T(8,128)(2,1)S(1)}, bf16[80,896]{1,0:T(8,128)(2,1)S(1)}, u32[]{:S(2)}, u32[]{:S(2)}) collective-permute-start(bf16[80,896]{1,0:T(8,128)(2,1)S(1)} %shard_map.181.refs_0_), channel_id=1, source_target_pairs={{0,4},{4,0},{8,12},{12,8},{16,20},{20,16},{24,28},{28,24},{1,5},{5... | collective-permute-start | bytes 430088 | tf_op jit(solution)/shard_map/ppermute | solution.py:396
  166.5 19.9 %collective-permute-start.21 = (bf16[80,896]{1,0:T(8,128)(2,1)S(1)}, bf16[80,896]{1,0:T(8,128)(2,1)S(1)}, u32[]{:S(2)}, u32[]{:S(2)}) collective-permute-start(bf16[80,896]{1,0:T(8,128)(2,1)S(1)} %collective-permute-done.20.refs_0_), channel_id=1, source_target_pairs={{0,4},{4,0},{8,12},{12,8},{16,20},{20,16},{24,28},{28,24},{1,5},{5... | collective-permute-start | bytes 430088 | tf_op jit(solution)/shard_map/ppermute | solution.py:396
  169.6 16.7 %collective-permute-start.23 = (bf16[80,896]{1,0:T(8,128)(2,1)S(1)}, bf16[80,896]{1,0:T(8,128)(2,1)S(1)}, u32[]{:S(2)}, u32[]{:S(2)}) collective-permute-start(bf16[80,896]{1,0:T(8,128)(2,1)S(1)} %collective-permute-done.22.refs_1_), channel_id=1, source_target_pairs={{0,4},{4,0},{8,12},{12,8},{16,20},{20,16},{24,28},{28,24},{1,5},{5... | collective-permute-start | bytes 430088 | tf_op jit(solution)/shard_map/ppermute | solution.py:396
  174.2 12.1 %collective-permute-start.25 = (bf16[80,896]{1,0:T(8,128)(2,1)S(1)}, bf16[80,896]{1,0:T(8,128)(2,1)S(1)}, u32[]{:S(2)}, u32[]{:S(2)}) collective-permute-start(bf16[80,896]{1,0:T(8,128)(2,1)S(1)} %collective-permute-done.24.refs_2_), channel_id=1, source_target_pairs={{0,4},{4,0},{8,12},{12,8},{16,20},{20,16},{24,28},{28,24},{1,5},{5... | collective-permute-start | bytes 430088 | tf_op jit(solution)/shard_map/ppermute | solution.py:396
  192.2 22.6 %collective-permute-start.33 = (bf16[80,1152]{1,0:T(8,128)(2,1)S(1)}, bf16[80,1152]{1,0:T(8,128)(2,1)S(1)}, u32[]{:S(2)}, u32[]{:S(2)}) collective-permute-start(bf16[80,1152]{1,0:T(8,128)(2,1)S(1)} %get-tuple-element.54.refs_0_), channel_id=1, source_target_pairs={{0,4},{4,0},{8,12},{12,8},{16,20},{20,16},{24,28},{28,24},{1,5},{5... | collective-permute-start | bytes 552968 | tf_op jit(solution)/shard_map/ppermute | solution.py:396
  193.6 9.9 %collective-permute-start.27 = (bf16[80,1152]{1,0:T(8,128)(2,1)S(1)}, bf16[80,1152]{1,0:T(8,128)(2,1)S(1)}, u32[]{:S(2)}, u32[]{:S(2)}) collective-permute-start(bf16[80,1152]{1,0:T(8,128)(2,1)S(1)} %get-tuple-element.54.refs_0_), channel_id=1, source_target_pairs={{0,8},{4,12},{8,16},{12,20},{16,24},{20,28},{24,0},{28,4},{1,9},{5... | collective-permute-start | bytes 552968 | tf_op jit(solution)/shard_map/ppermute | solution.py:392
  195.1 9.6 %collective-permute-start.29 = (bf16[80,1152]{1,0:T(8,128)(2,1)S(1)}, bf16[80,1152]{1,0:T(8,128)(2,1)S(1)}, u32[]{:S(2)}, u32[]{:S(2)}) collective-permute-start(bf16[80,1152]{1,0:T(8,128)(2,1)S(1)} %get-tuple-element.54.refs_0_), channel_id=1, source_target_pairs={{0,24},{4,28},{8,0},{12,4},{16,8},{20,12},{24,16},{28,20},{1,25},{... | collective-permute-start | bytes 552968 | tf_op jit(solution)/shard_map/ppermute | solution.py:392
  197.9 16.0 %collective-permute-start.31 = (bf16[80,1152]{1,0:T(8,128)(2,1)S(1)}, bf16[80,1152]{1,0:T(8,128)(2,1)S(1)}, u32[]{:S(2)}, u32[]{:S(2)}) collective-permute-start(bf16[80,1152]{1,0:T(8,128)(2,1)S(1)} %get-tuple-element.54.refs_0_), channel_id=1, source_target_pairs={{0,16},{4,20},{8,24},{12,28},{16,0},{20,4},{24,8},{28,12},{1,17},{... | collective-permute-start | bytes 552968 | tf_op jit(solution)/shard_map/ppermute | solution.py:392
  198.8 33.8 %collective-permute-start.45 = (bf16[1,256,768]{2,1,0:T(8,128)(2,1)S(1)}, bf16[1,256,768]{2,1,0:T(8,128)(2,1)S(1)}, u32[]{:S(2)}, u32[]{:S(2)}) collective-permute-start(bf16[1,256,768]{2,1,0:T(8,128)(2,1)S(1)} %get-tuple-element.66), channel_id=1, source_target_pairs={{0,2},{1,3},{2,0},{3,1},{4,6},{5,7},{6,4},{7,5},{8,10},{9,11},{10,... | collective-permute-start | bytes 1179656 | tf_op jit(solution)/shard_map/ppermute | solution.py:399
  203.5 19.8 %collective-permute-start.28 = (bf16[80,1152]{1,0:T(8,128)(2,1)S(1)}, bf16[80,1152]{1,0:T(8,128)(2,1)S(1)}, u32[]{:S(2)}, u32[]{:S(2)}) collective-permute-start(bf16[80,1152]{1,0:T(8,128)(2,1)S(1)} %collective-permute-done.27.refs_0_), channel_id=1, source_target_pairs={{0,4},{4,0},{8,12},{12,8},{16,20},{20,16},{24,28},{28,24},{1,5},{5... | collective-permute-start | bytes 552968 | tf_op jit(solution)/shard_map/ppermute | solution.py:396
  204.6 18.6 %collective-permute-start.30 = (bf16[80,1152]{1,0:T(8,128)(2,1)S(1)}, bf16[80,1152]{1,0:T(8,128)(2,1)S(1)}, u32[]{:S(2)}, u32[]{:S(2)}) collective-permute-start(bf16[80,1152]{1,0:T(8,128)(2,1)S(1)} %collective-permute-done.29.refs_1_), channel_id=1, source_target_pairs={{0,4},{4,0},{8,12},{12,8},{16,20},{20,16},{24,28},{28,24},{1,5},{5... | collective-permute-start | bytes 552968 | tf_op jit(solution)/shard_map/ppermute | solution.py:396
  213.9 9.4 %collective-permute-start.32 = (bf16[80,1152]{1,0:T(8,128)(2,1)S(1)}, bf16[80,1152]{1,0:T(8,128)(2,1)S(1)}, u32[]{:S(2)}, u32[]{:S(2)}) collective-permute-start(bf16[80,1152]{1,0:T(8,128)(2,1)S(1)} %collective-permute-done.31.refs_2_), channel_id=1, source_target_pairs={{0,4},{4,0},{8,12},{12,8},{16,20},{20,16},{24,28},{28,24},{1,5},{5... | collective-permute-start | bytes 552968 | tf_op jit(solution)/shard_map/ppermute | solution.py:396
  214.9 14.2 %collective-permute-start.46 = (f32[8,16,128]{2,1,0:T(8,128)S(1)}, f32[8,16,128]{2,1,0:T(8,128)S(1)}, u32[]{:S(2)}, u32[]{:S(2)}) collective-permute-start(f32[8,16,128]{2,1,0:T(8,128)S(1)} %get-tuple-element.70), channel_id=1, source_target_pairs={{0,4},{4,0},{8,12},{12,8},{16,20},{20,16},{24,28},{28,24},{1,5},{5... | collective-permute-start | bytes 196616 | tf_op jit(solution)/shard_map/ppermute | solution.py:396
  227.1 2.0 collective-permute-start.34
  227.2 4.2 %collective-permute-start.35 = (bf16[32,768]{1,0:T(8,128)(2,1)S(1)}, bf16[32,768]{1,0:T(8,128)(2,1)S(1)}, u32[]{:S(2)}, u32[]{:S(2)}) collective-permute-start(bf16[32,768]{1,0:T(8,128)(2,1)S(1)} %get-tuple-element.58), channel_id=1, source_target_pairs={{0,2},{1,3},{2,0},{3,1},{4,6},{5,7},{6,4},{7,5},{8,10},{9,11},{10,... | collective-permute-start | bytes 147464 | tf_op jit(solution)/shard_map/ppermute | solution.py:399
  228.9 3.7 %collective-permute-start.36 = (bf16[32,768]{1,0:T(8,128)(2,1)S(1)}, bf16[32,768]{1,0:T(8,128)(2,1)S(1)}, u32[]{:S(2)}, u32[]{:S(2)}) collective-permute-start(bf16[32,768]{1,0:T(8,128)(2,1)S(1)} %get-tuple-element.59), channel_id=1, source_target_pairs={{0,3},{1,2},{2,1},{3,0},{4,7},{5,6},{6,5},{7,4},{8,11},{9,10},{10,... | collective-permute-start | bytes 147464 | tf_op jit(solution)/shard_map/ppermute | solution.py:399
  (37 other events, 540.2 us)

commit v2 on v1

v2 whole, which is shorter than its diff:
```python
import functools
import jax
import jax.numpy as jnp
import numpy as np
from jax import lax
from jax.experimental import pallas as pl
from jax.experimental.pallas import tpu as pltpu
from jax.sharding import PartitionSpec as P

EPS = 1e-05
F32 = jnp.float32
BF16 = jnp.bfloat16
I32 = jnp.int32
HIGHEST = lax.Precision.HIGHEST
NT = (((1,), (1,)), ((), ()))
TN = (((0,), (0,)), ((), ()))
NN = (((1,), (0,)), ((), ()))


def mm(a, b, dims=NN, precision=None):
    return lax.dot_general(a, b, dims, precision=precision, preferred_element_type=F32)


def sigmoid(v):
    return 1.0 / (1.0 + jnp.exp(-v))


def bit_reversed(p, bits):
    r = 0
    for b in range(bits):
        r = r * 2 + ((p >> b) & 1)
    return r


def whole(shape):
    return pl.BlockSpec(tuple(shape), lambda i, s: (0,) * len(shape))


def call(kernel, place, operands, outs, scratch=(), flops=0, limit=40, out_any=False):
    arrays, specs, moved = [], [], 0
    for item in operands:
        array, spec = item if isinstance(item, tuple) else (item, whole(item.shape))
        arrays.append(array)
        specs.append(spec)
        moved += array.size * array.dtype.itemsize
    moved += sum(o.size * o.dtype.itemsize for o in outs)
    return pl.pallas_call(
        kernel,
        out_shape=list(outs),
        grid_spec=pltpu.PrefetchScalarGridSpec(
            num_scalar_prefetch=1,
            grid=(1,),
            in_specs=specs,
            out_specs=[
                pl.BlockSpec(memory_space=pl.ANY) if out_any else whole(o.shape) for o in outs
            ],
            scratch_shapes=list(scratch),
        ),
        compiler_params=pltpu.CompilerParams(vmem_limit_bytes=limit * 1024 * 1024),
        cost_estimate=pl.CostEstimate(flops=flops, bytes_accessed=moved, transcendentals=0),
    )(place, *arrays)


def hbm(array):
    return (array, pl.BlockSpec(memory_space=pltpu.HBM))


def anywhere(array):
    return (array, pl.BlockSpec(memory_space=pl.ANY))


def run_copies(pairs, sem):
    copies = [pltpu.make_async_copy(a, b, sem.at[n]) for n, (a, b) in enumerate(pairs)]
    for c in copies:
        c.start()
    return copies


def one_hot(mask):
    return mask.astype(F32).astype(BF16)


def turned_back(z, back, nz):
    return jnp.where(z < back, z - back + nz, z - back)


def sds(shape, dtype):
    return jax.ShapeDtypeStruct(tuple(shape), dtype)


def pieces(x):
    hi = x.astype(BF16)
    rest = x - hi.astype(F32)
    mid = rest.astype(BF16)
    return hi, mid, (rest - mid.astype(F32)).astype(BF16)


def routing_kernel(nz, cap, own_rows, s, *refs):
    keep = refs[0]
    given = refs[1 : nz + 1]
    base, codes, sign, ids = refs[nz + 1 :]
    j = s[2]
    block = given[0].shape[1]
    for r in range(nz):
        ids[lax.bitwise_xor(j, r)] = given[r][...]
    rows = lax.broadcasted_iota(I32, (block, block), 0)
    cols = lax.broadcasted_iota(I32, (block, block), 1)
    strict = one_hot(rows < cols)
    own = base[...] + j * (nz * cap)
    earlier = [jnp.zeros((1, 1), I32) for _ in range(nz)]
    other = jnp.zeros((own_rows, 1), I32)
    place = lax.broadcasted_iota(I32, (16, block), 0)
    for b in range(nz):
        first, second = ids[b, 0:1, :], ids[b, 1:2, :]
        named = ((place == first) | (place == second)) & (place < nz)
        ranks = mm(one_hot(named), strict).astype(I32)
        slots = []
        for e in range(nz):
            hit = (first == e) | (second == e)
            rank = ranks[e : e + 1, :]
            kept = hit & (rank + earlier[e] < keep[e])
            slots.append(jnp.where(kept, (e * nz + b) * cap + rank, -1))
            earlier[e] = earlier[e] + jnp.sum(hit.astype(I32), axis=1, keepdims=True)
        top = functools.reduce(jnp.maximum, slots)
        rest = functools.reduce(jnp.maximum, [jnp.where(c == top, -1, c) for c in slots])
        codes[b, 0:1, :] = top
        codes[b, 1:2, :] = rest
        holds = (own == top) | (own == rest)
        other = other + jnp.sum(jnp.where(holds, first + second, 0), axis=1, keepdims=True)
    every = lax.broadcasted_iota(I32, sign.shape, 1)
    sign[...] = (every == j).astype(F32) - (every == other - j).astype(F32)


def pack_kernel(away, ny, width, s, a, b, out, sem):
    at = pl.multiple_of(lax.rem(s[1] + away, ny) * width, 128)
    for c in run_copies([(x.at[:, pl.ds(at, width)], out.at[n]) for n, x in enumerate((a, b))], sem):
        c.wait()


def update_kernel(nz, ny, heads, hd, s, *refs):
    z, y = s[0], s[1]
    n = ny - 1
    k_arg, v_arg = refs[0], refs[1]
    kv = refs[2 : 2 + n]
    logs = refs[2 + n : 2 + n + ny]
    outs = refs[2 + n + ny : 2 + n + ny + nz]
    c_row, c_col, log_all, state, tail, own, sem = refs[2 + n + ny + nz :]
    tok = k_arg.shape[0]
    total_tok = tok * ny
    share = hd // nz
    mine = pl.ds(pl.multiple_of(y * heads * hd, 128), heads * hd)
    copies = run_copies([(x.at[:, mine], own.at[m]) for m, x in enumerate((k_arg, v_arg))], sem)
    for d in range(ny):
        at = pl.multiple_of(lax.rem(y + ny - d, ny) * tok, tok)
        log_all[:, pl.ds(at, tok)] = logs[d][pl.ds(y * heads, heads), :]
    rows = lax.broadcasted_iota(I32, (total_tok, total_tok), 0)
    cols = lax.broadcasted_iota(I32, (total_tok, total_tok), 1)
    c_row[...] = mm(log_all[...], (rows <= cols).astype(F32), precision=HIGHEST)
    c_col[...] = mm((rows >= cols).astype(F32), log_all[...], NT, precision=HIGHEST)
    total = c_row[:, total_tok - 1 : total_tok]
    for c in copies:
        c.wait()
    for h in range(heads):
        add = None
        for d in range(ny):
            at = pl.multiple_of(lax.rem(y + ny - d, ny) * tok, tok)
            lanes = slice(h * hd, (h + 1) * hd)
            pair = own if d == 0 else kv[d - 1]
            key = pair[0, :, lanes].astype(F32)
            decay = jnp.exp(total[h : h + 1, :] - c_col[pl.ds(at, tok), h : h + 1])
            weighted = (key * sigmoid(key) * decay).astype(BF16)
            part = mm(weighted, pair[1, :, lanes], TN)
            add = part if add is None else add + part
        state[h] = add.astype(BF16)
    tail[...] = jnp.zeros_like(tail)
    hi, mid, lo = pieces(total)
    lane = lax.broadcasted_iota(I32, (heads, hd), 1)
    tail[0:heads, :] = jnp.where(
        lane == 0,
        hi.astype(F32),
        jnp.where(lane == 1, mid.astype(F32), jnp.where(lane == 2, lo.astype(F32), 0.0)),
    )
    for d in range(nz):
        at = pl.multiple_of(lax.rem(z + d, nz) * share, share)
        for h in range(heads):
            outs[d][h * share : (h + 1) * share, :] = state[h, pl.ds(at, share), :]
        outs[d][heads * share :, :] = tail[...].astype(BF16)


def prefix_kernel(nz, heads, hd, s, *refs):
    z, y = s[0], s[1]
    parts = refs[:nz]
    start = refs[nz]
    outs = refs[nz + 1 : 2 * nz + 1]
    final, held, entering, run, sem = refs[2 * nz + 1 :]
    share = hd // nz
    source = start.at[
        pl.ds(y * heads, heads), pl.ds(pl.multiple_of(z * share, share), share), :
    ]
    copies = run_copies([(source, run)], sem)
    for d in range(nz):
        held[lax.rem(z + nz - d, nz)] = parts[d][...]
    copies[0].wait()
    for p in range(nz):
        logs = jnp.sum(held[p, heads * share :, :].astype(F32), axis=1, keepdims=True)
        keep = jnp.exp(logs)
        for h in range(heads):
            rows = slice(h * share, (h + 1) * share)
            now = run[h]
            entering[p, rows, :] = now.astype(BF16)
            run[h] = keep[h : h + 1, :] * now + held[p, rows, :].astype(F32)
    final[...] = run[...]
    for d in range(nz):
        outs[d][...] = entering[lax.rem(z + d, nz)]


def attention_kernel(nz, ny, heads, hd, s, *refs):
    z, y = s[0], s[1]
    n = ny - 1
    args = refs[:4]
    kv = refs[4 : 4 + n]
    qg = refs[4 + n : 4 + 2 * n]
    states = refs[4 + 2 * n : 4 + 2 * n + nz]
    c_row, c_col, gain, out, ks, vs, qs, gs, state, sem = refs[4 + 2 * n + nz :]
    tok = args[0].shape[0]
    total_tok = tok * ny
    share = hd // nz
    mine = pl.ds(pl.multiple_of(y * heads * hd, 128), heads * hd)
    moves = []
    for d in range(ny):
        at = pl.ds(pl.multiple_of(lax.rem(y + ny - d, ny) * tok, tok), tok)
        for m, to in enumerate((ks, vs, qs, gs)):
            if d == 0:
                source = args[m].at[:, mine]
            else:
                source = (kv if m < 2 else qg)[d - 1].at[m % 2]
            moves.append((source, to.at[at, :]))
    copies = run_copies(moves, sem)
    for d in range(nz):
        at = pl.ds(pl.multiple_of(lax.rem(z + nz - d, nz) * share, share), share)
        for h in range(heads):
            state[h, at, :] = states[d][h * share : (h + 1) * share, :]
    rows = lax.broadcasted_iota(I32, (total_tok, total_tok), 0)
    cols = lax.broadcasted_iota(I32, (total_tok, total_tok), 1)
    causal = rows >= cols
    for c in copies:
        c.wait()
    for h in range(heads):
        lanes = slice(h * hd, (h + 1) * hd)
        query = qs[:, lanes].astype(F32)
        query = query * sigmoid(query)
        key = ks[:, lanes].astype(F32)
        key = (key * sigmoid(key)).astype(BF16)
        col = c_col[:, h : h + 1]
        gap = jnp.where(causal, col - c_row[h : h + 1, :], 0.0)
        decay = jnp.where(causal, jnp.exp(gap), 0.0)
        scores = mm(query.astype(BF16), key, NT) * decay
        att = mm(scores.astype(BF16), vs[:, lanes])
        att = att + mm((query * jnp.exp(col)).astype(BF16), state[h])
        square = jnp.mean(att * att, axis=1, keepdims=True)
        gate = sigmoid(gs[:, lanes].astype(F32))
        out[:, lanes] = (att * lax.rsqrt(square + EPS) * gain[:, lanes] * gate).astype(BF16)


def project_kernel(nz, ny, cap, dzs, last, s, *refs):
    z, j = s[0], s[2]
    bits = nz.bit_length() - 1
    parts = [len(p) for p in dzs.values()]
    count = sum(parts) * ny
    blocks = refs[:count]
    weights = refs[count : count + ny]
    r_ids, b_ids, codes = refs[count + ny : count + ny + 3]
    refs = refs[count + ny + 3 :]
    if last:
        done, sums, residual = refs[:3]
        keep, send, keep_all, send_all, stacked, own, sem = refs[3:]
    else:
        done, sums, stacked, sem = refs
    rows = stacked.shape[2]
    moves = []
    at = 0
    for dy in range(ny):
        for n, (dz, pieces_of) in enumerate(dzs.items()):
            first = 0
            for _ in pieces_of:
                size = blocks[at].shape[0]
                moves.append((blocks[at], stacked.at[dy, n, pl.ds(first, size)]))
                first += size
                at += 1
    if last:
        moves.append((residual, own))
    copies = run_copies(moves, sem)
    ids = lax.bitwise_xor(r_ids[...], j) * (nz * cap) + b_ids[...]
    pick = lambda b: one_hot((ids == codes[b, 0:1, :]) | (ids == codes[b, 1:2, :]))
    total_rows = sums[...] if last else None
    for c in copies:
        c.wait()
    projected = {}
    for n, dz in enumerate(dzs):
        total = None
        for dy in range(ny):
            part = mm(stacked[dy, n], weights[dy][...])
            total = part if total is None else total + part
        projected[dz] = total.astype(BF16)
        part = mm(pick(lax.rem(z + nz - dz, nz)), projected[dz])
        total_rows = part if total_rows is None else total_rows + part
    if not last:
        for n, dz in enumerate(dzs):
            done[n] = projected[dz]
        sums[...] = total_rows
        return
    total_rows = total_rows + mm(pick(j), own[...])
    half = keep.shape[0]
    keep[...] = total_rows[:half, :]
    send[...] = total_rows[half:, :].astype(BF16)
    before = [dz for dz in range(nz) if dz not in dzs]
    for p in range(nz):
        block = lax.bitwise_xor(jnp.int32(bit_reversed(p, bits)), j)
        away = lax.rem(z + nz - block, nz)
        to = keep_all.at[p] if p < nz // 2 else send_all.at[p - nz // 2]
        for dz in range(nz):

            @pl.when(away == dz)
            def _(dz=dz):
                to[...] = projected[dz] if dz in dzs else done[before.index(dz)]


def rows_kernel(s, keep, received, gain, router_t, sign, out):
    width = gain.shape[1]
    rows = keep[...] + received[...].astype(F32)
    square = jnp.sum(rows * rows, axis=1, keepdims=True)
    scaled = rows * gain[...]
    logits = mm(scaled, router_t[...], NT, precision=HIGHEST)
    gap = jnp.sum(logits * sign[...], axis=1, keepdims=True)
    out[:, :width] = scaled.astype(BF16)
    lane = lax.broadcasted_iota(I32, (rows.shape[0], 128), 1)
    stats = jnp.zeros((rows.shape[0], 128), F32)
    for at, value in ((0, square), (3, gap)):
        for k, piece in enumerate(pieces(value)):
            stats = jnp.where(lane == at + k, piece.astype(F32), stats)
    out[:, width:] = stats.astype(BF16)


def up_kernel(nz, ny, places, first, last, features, s, *refs):
    z, y = s[0], s[1]
    count = len(places)
    blocks = refs[:count]
    refs = refs[count:]
    before = () if first else refs[:3]
    refs = refs[0 if first else 3 :]
    w_gate, w_up = refs[:2]
    outs = refs[2 : 4 if last else 5]
    gate_buf, up_buf, sem = refs[4 if last else 5 :]
    width = gate_buf.shape[2]
    copies = []
    for n, (dz, dy) in enumerate(places):
        source = lax.rem(z + nz - dz, nz) * ny + lax.rem(y + ny - dy, ny)
        at = pl.ds(pl.multiple_of(source * width, 128), width)
        copies.append(
            (
                pltpu.make_async_copy(w_gate.at[0, :, at], gate_buf.at[n], sem.at[0, n]),
                pltpu.make_async_copy(w_up.at[0, :, at], up_buf.at[n], sem.at[1, n]),
            )
        )
        for c in copies[-1]:
            c.start()
    gate, up, stats = (None, None, None) if first else (b[...] for b in before)
    for n in range(count):
        rows = blocks[n][:, :width]
        part = blocks[n][:, width:].astype(F32)
        stats = part if stats is None else stats + part
        copies[n][0].wait()
        part = mm(rows, gate_buf[n], NT)
        gate = part if gate is None else gate + part
        copies[n][1].wait()
        part = mm(rows, up_buf[n], NT)
        up = part if up is None else up + part
    if not last:
        outs[0][...] = gate
        outs[1][...] = up
        outs[2][...] = stats
        return
    square = stats[:, 0:1] + stats[:, 1:2] + stats[:, 2:3]
    gap = stats[:, 3:4] + stats[:, 4:5] + stats[:, 5:6]
    inverse = lax.rsqrt(square / features + EPS)
    gate = gate * inverse
    outs[0][...] = (gate * sigmoid(gate) * (up * inverse)).astype(BF16)
    outs[1][...] = jnp.broadcast_to(sigmoid(gap * inverse), outs[1].shape)


def down_kernel(nz, ny, cap, places, first, last, s, *refs):
    z, y, j = s[0], s[1], s[2]
    count = len(places)
    blocks = refs[:count]
    refs = refs[count:]
    before = None if first else refs[0]
    refs = refs[0 if first else 1 :]
    w_down = refs[0]
    refs = refs[1:]
    if last:
        weight, out_base, row_base = refs[:3]
        refs = refs[3:]
    outs, buf, sem = refs[:-2], refs[-2], refs[-1]
    depth = buf.shape[1]
    copies = []
    for n, (dz, dy) in enumerate(places):
        source = lax.rem(z + nz - dz, nz) * ny + lax.rem(y + ny - dy, ny)
        at = pl.ds(pl.multiple_of(source * depth, depth), depth)
        copies.append(pltpu.make_async_copy(w_down.at[0, at, :], buf.at[n], sem.at[n]))
        copies[-1].start()
    total = None if first else before[...]
    for n in range(count):
        copies[n].wait()
        part = mm(blocks[n][...], buf[n])
        total = part if total is None else total + part
    if not last:
        outs[0][...] = total
        return
    result = (total * weight[:, 0:1]).astype(BF16)
    for r, out in enumerate(outs):
        wanted = out_base[...] + lax.bitwise_xor(j, r) * cap
        out[...] = mm(one_hot(wanted == row_base[...]), result).astype(BF16)


def combine_kernel(nz, cap, s, *refs):
    j = s[2]
    returned = refs[:nz]
    keep, received, residual, codes, ret_r, ret_base, out, stacked, own, sem = refs[nz:]
    copies = run_copies([(residual, own)], sem)
    rows = returned[0].shape[0]
    for n in range(nz):
        stacked[n * rows : (n + 1) * rows, :] = returned[n][...]
    ids = lax.bitwise_xor(ret_r[...], j) * (nz * cap) + ret_base[...] + j * cap
    pick = (ids == codes[j, 0:1, :]) | (ids == codes[j, 1:2, :])
    added = mm(one_hot(pick), stacked[...], TN)
    copies[0].wait()
    total = own[...].astype(F32) + (keep[...].astype(F32) + received[...].astype(F32))
    out[...] = (total + added).astype(BF16)


def local(
    residual,
    query,
    key_in,
    value_in,
    gate_in,
    log_decay,
    state_in,
    attn_gain,
    w_out,
    moe_gain,
    router,
    w_gate,
    w_up,
    w_down,
    expert_ids,
    keep_counts,
):
    nz = lax.axis_size("exp")
    ny = lax.axis_size("seq") // nz
    bits = nz.bit_length() - 1
    i = lax.axis_index("seq").astype(I32)
    j = lax.axis_index("exp").astype(I32)
    z, y = i // ny, i % ny
    place = jnp.stack([z, y, j])

    tok, head_width = query.shape
    head_count, hd = state_in.shape[0], state_in.shape[2]
    heads = head_count // ny
    width = heads * hd
    block, cols = residual.shape
    features = w_gate.shape[2]
    units = w_gate.shape[1]
    experts = router.shape[1]
    cap = 5 * block * nz // (2 * nz * experts)
    slots = nz * cap

    def z_turn(a, d):
        pairs = [(p * ny + q, (p + d) % nz * ny + q) for p in range(nz) for q in range(ny)]
        return lax.ppermute(a, "seq", pairs)

    def y_turn(a, d):
        pairs = [(p * ny + q, p * ny + (q + d) % ny) for p in range(nz) for q in range(ny)]
        return lax.ppermute(a, "seq", pairs)

    def swap(a, r):
        return lax.ppermute(a, "exp", [(p, p ^ r) for p in range(nz)])

    z_order = sorted(range(1, nz), key=lambda d: (min(d, nz - d), d))
    near = [d for d in z_order if min(d, nz - d) == 1]
    distant = [d for d in z_order if d not in near]
    places = [(dz, dy) for dy in range(ny) for dz in range(nz)]

    def behind(values, events):
        return list(lax.optimization_barrier((tuple(values), tuple(events)))[0])

    def gather(a):
        held = {(0, 0): a}
        for d in range(1, ny):
            held[0, d] = y_turn(a, d)
        for d in z_order:
            held[d, 0] = z_turn(a, d)
        for d in z_order:
            for e in range(1, ny):
                held[d, e] = y_turn(held[d, 0], e)
        return held

    slot = np.arange(cap)
    row_r = np.repeat([bit_reversed(p, bits) for p in range(nz)], slots).astype(np.int32)[:, None]
    row_base = np.tile((np.arange(nz)[:, None] * cap + slot).reshape(slots), nz)
    row_base = row_base.astype(np.int32)[:, None]
    own_base = row_base[:slots]
    ret_rows = cap + -cap % 16
    padded = np.where(np.arange(ret_rows) < cap, np.arange(ret_rows), -(10**8)).astype(np.int32)
    ret_r = np.repeat(np.arange(nz), ret_rows).astype(np.int32)[:, None]
    ret_base = np.tile(padded, nz)[:, None]

    hand = [pltpu.SemaphoreType.DMA((2,))]
    logs_t = jnp.transpose(log_decay)
    logs, kvs, qgs = [logs_t], [], []
    for d in range(1, ny):
        pack = functools.partial(pack_kernel, d, ny, width)
        out = [sds((2, tok, width), BF16)]
        (kv,) = call(pack, place, [hbm(key_in), hbm(value_in)], out, hand, out_any=True)
        kvs.append(y_turn(kv, d))
        logs.append(y_turn(logs_t, d))
        (qg,) = call(pack, place, [hbm(query), hbm(gate_in)], out, hand, out_any=True)
        qgs.append(y_turn(qg, d))
    ids = jnp.transpose(expert_ids)
    codes, sign = call(
        functools.partial(routing_kernel, nz, cap, slots),
        place,
        [(keep_counts, pl.BlockSpec(memory_space=pltpu.SMEM))]
        + [ids]
        + [swap(ids, r) for r in range(1, nz)]
        + [own_base],
        [sds((nz, 2, block), I32), sds((slots, experts), F32)],
        [pltpu.VMEM((nz, 2, block), I32)],
    )
    attn_gain_2, moe_gain_2, router_t = attn_gain[None], moe_gain[None], jnp.transpose(router)
    kvs = behind(kvs, [codes, sign, attn_gain_2, moe_gain_2])
    share = hd // nz
    long = tok * ny
    *parts, c_row, c_col = call(
        functools.partial(update_kernel, nz, ny, heads, hd),
        place,
        [hbm(key_in), hbm(value_in), *kvs, *logs],
        [sds((heads * share + 16, hd), BF16)] * nz
        + [sds((heads, long), F32), sds((long, heads), F32)],
        [
            pltpu.VMEM((heads, long), F32),
            pltpu.VMEM((heads, hd, hd), BF16),
            pltpu.VMEM((16, hd), F32),
            pltpu.VMEM((2, tok, width), BF16),
            pltpu.SemaphoreType.DMA((2,)),
        ],
        flops=2 * long * hd * hd * heads,
    )
    parts = [parts[0]] + [z_turn(parts[d], d) for d in range(1, nz)]
    *entering, last_rows = call(
        functools.partial(prefix_kernel, nz, heads, hd),
        place,
        [*parts, hbm(state_in)],
        [sds((heads * share, hd), BF16)] * nz + [sds((heads, share, hd), F32)],
        [
            pltpu.VMEM((nz, heads * share + 16, hd), BF16),
            pltpu.VMEM((nz, heads * share, hd), BF16),
            pltpu.VMEM((heads, share, hd), F32),
            pltpu.SemaphoreType.DMA((1,)),
        ],
    )
    entering = [entering[0]] + [z_turn(entering[d], d) for d in range(1, nz)]
    (mixed,) = call(
        functools.partial(attention_kernel, nz, ny, heads, hd),
        place,
        [
            hbm(key_in),
            hbm(value_in),
            hbm(query),
            hbm(gate_in),
            *[anywhere(x) for x in kvs],
            *[anywhere(x) for x in qgs],
            *entering,
            c_row,
            c_col,
            (attn_gain_2, pl.BlockSpec((1, width), lambda n, s: (0, s[1]))),
        ],
        [sds((long, width), BF16)],
        [pltpu.VMEM((long, width), BF16)] * 4
        + [pltpu.VMEM((heads, hd, hd), BF16), pltpu.SemaphoreType.DMA((4 * ny,))],
        flops=4 * long * long * width,
    )

    def across(blocks):
        return [[y_turn(x, e) for x in blocks] for e in range(1, ny)]

    held = {0: [[mixed]] + across([mixed])}
    for d in near:
        held[d] = [[z_turn(mixed, d)]]
    free = behind([mixed], [held[d][0][0] for d in near])[0]
    for d in near:
        held[d] += across(held[d][0])
    halves = [free[: long // 2], free[long // 2 :]]
    for d in distant:
        held[d] = [[z_turn(x, d) for x in halves]]
    for d in distant:
        held[d] += across(held[d][0])
    w_parts = [
        (w_out, pl.BlockSpec((width, cols), lambda n, s, d=d: (lax.rem(s[1] + ny - d, ny), 0)))
        for d in range(ny)
    ]
    given = []
    for group in ([0] + near, distant):
        last = group is distant
        dzs = {d: held[d][0] for d in group}
        blocks = [x for dy in range(ny) for d in group for x in held[d][dy]]
        half = nz * slots // 2
        outs = [sds((len(group), block, cols), BF16), sds((nz * slots, cols), F32)]
        if last:
            outs = [sds((half, cols), F32), sds((half, cols), BF16)]
            outs += [sds((nz // 2, block, cols), BF16)] * 2
        given = call(
            functools.partial(project_kernel, nz, ny, cap, dzs, last),
            place,
            [anywhere(x) for x in blocks]
            + w_parts
            + [row_r, row_base, codes]
            + list(given)
            + ([hbm(residual)] if last else []),
            outs,
            [pltpu.VMEM((ny, len(group), long, width), BF16)]
            + ([pltpu.VMEM((block, cols), BF16)] if last else [])
            + [pltpu.SemaphoreType.DMA((len(blocks) + 1,))],
            flops=2 * len(group) * long * head_width * cols,
        )
    keep, send, keep_all, send_all = given
    for b in range(bits):
        received = swap(send, 1 << b)
        if b < bits - 1:
            part = keep.shape[0] // 2
            send = (keep[part:] + received[part:].astype(F32)).astype(BF16)
            keep = keep[:part] + received[:part].astype(F32)
    (rows_out,) = call(
        rows_kernel,
        place,
        [keep, received, moe_gain_2, router_t, sign],
        [sds((slots, cols + 128), BF16)],
    )
    send_all = behind([send_all], [rows_out])[0]
    for b in range(bits):
        received_all = swap(send_all, 1 << b)
        if b < bits - 1:
            n = keep_all.shape[0] // 2
            both = keep_all.astype(F32) + received_all.astype(F32)
            send_all, keep_all = both[n:].astype(BF16), both[:n].astype(BF16)
    rows = share // ny
    last_rows = behind([last_rows], [rows_out])[0]
    final_rows = jnp.zeros((head_count, rows, hd), F32)
    for d in range(ny):
        sent = lax.dynamic_slice_in_dim(last_rows, (y + d) % ny * rows, rows, 1)
        got = sent if d == 0 else y_turn(sent, d)
        final_rows = lax.dynamic_update_slice_in_dim(
            final_rows, got, (y - d) % ny * heads, 0
        )

    groups = [[(0, d) for d in range(ny)], [(d, 0) for d in z_order]]
    groups.append([(d, e) for d in z_order for e in range(1, ny)])
    arrived = gather(rows_out)
    state = []
    if cols % 128:
        order = jnp.stack([(z - dz) % nz * ny + (y - dy) % ny for dz, dy in places])
        at = jnp.argsort(order)
        rows_all = jnp.take(jnp.stack([arrived[p] for p in places]), at, axis=0)
        stats = jnp.sum(rows_all[:, :, cols:].astype(F32), axis=0)
        rows_all = jnp.swapaxes(rows_all[:, :, :cols], 0, 1).reshape(slots, features)
        inverse = lax.rsqrt(jnp.sum(stats[:, :3], axis=1) / features + EPS)[:, None]
        gate = mm(rows_all, w_gate[0], NT) * inverse
        hidden = (gate * sigmoid(gate) * (mm(rows_all, w_up[0], NT) * inverse)).astype(BF16)
        weight = sigmoid(jnp.sum(stats[:, 3:6], axis=1)[:, None] * inverse)
        state = [hidden, jnp.broadcast_to(weight, (slots, 128))]
    for n, group in enumerate(groups if cols % 128 == 0 else ()):
        last = n == len(groups) - 1
        outs = [sds((slots, units), F32)] * 2 + [sds((slots, 128), F32)]
        if last:
            outs = [sds((slots, units), BF16), sds((slots, 128), F32)]
        state = call(
            functools.partial(up_kernel, nz, ny, group, n == 0, last, features),
            place,
            [arrived[p] for p in group] + list(state) + [anywhere(w_gate), anywhere(w_up)],
            outs,
            [pltpu.VMEM((len(group), units, cols), BF16)] * 2
            + [pltpu.SemaphoreType.DMA((2, len(group)))],
            flops=4 * len(group) * slots * units * cols,
        )
    hidden, weight = state
    arrived = gather(hidden)
    state = []
    for n, group in enumerate(groups):
        last = n == len(groups) - 1
        outs = [sds((slots, cols), F32)]
        if last:
            outs = [sds((ret_rows, cols), BF16)] * nz
        state = call(
            functools.partial(down_kernel, nz, ny, cap, group, n == 0, last),
            place,
            [arrived[p] for p in group]
            + list(state)
            + [anywhere(w_down)]
            + ([weight, padded[:, None], own_base.T] if last else []),
            outs,
            [
                pltpu.VMEM((len(group), units, cols), BF16),
                pltpu.SemaphoreType.DMA((len(group),)),
            ],
            flops=2 * len(group) * slots * units * cols,
        )
    returned = [state[0]] + [swap(state[r], r) for r in range(1, nz)]
    (layer_out,) = call(
        functools.partial(combine_kernel, nz, cap),
        place,
        returned + [keep_all[0], received_all[0], hbm(residual), codes, ret_r, ret_base],
        [sds((block, cols), BF16)],
        [
            pltpu.VMEM((nz * ret_rows, cols), BF16),
            pltpu.VMEM((block, cols), BF16),
            pltpu.SemaphoreType.DMA((1,)),
        ],
    )
    return layer_out, final_rows


def solution(mesh):
    in_specs = (
        P("exp", "seq"),
        P("seq", "exp"),
        P("seq", "exp"),
        P("seq", "exp"),
        P("seq", "exp"),
        P("seq", "exp"),
        P("exp", None, None),
        P("exp"),
        P("exp", "seq"),
        P("seq"),
        P("seq", None),
        P("exp", "seq", None),
        P("exp", "seq", None),
        P("exp", None, "seq"),
        P("exp", None),
        P(),
    )
    out_specs = (P("exp", "seq"), P("exp", "seq", None))
    return jax.shard_map(local, mesh=mesh, in_specs=in_specs, out_specs=out_specs, check_vma=False)
```

time: 235 us -> 198 us (0.84)
  local copies, waits for them, and re-layouts: 21.1 us -> 4.39 us
  starting transfers between devices: 60.8 us -> 53.8 us
  other arithmetic: 6.58 us -> 0.34 us
  waiting for transfers between devices: 95 us -> 90.1 us
    ppermute x20 -> x17, waiting for transfers between devices: 41.1 us -> 16.6 us  [y_turn(): return lax.ppermute(a, 'seq', pairs)]
    ppermute x18 -> x16, waiting for transfers between devices: 49.1 us -> 62.7 us  [z_turn(): return lax.ppermute(a, 'seq', pairs)]
    ppermute x18 -> x16, starting transfers between devices: 34.2 us -> 23.9 us  [z_turn(): return lax.ppermute(a, 'seq', pairs)]
    unnamed x78 -> x50, local copies, waits for them, and re-layouts: 13.9 us -> 4.27 us
    ppermute x9 -> x10, waiting for transfers between devices: 4.87 us -> 10.8 us  [swap(): return lax.ppermute(a, 'exp', [(p, p ^ r) for p in range(nz)])]
    ppermute x20 -> x17, starting transfers between devices: 19 us -> 22.2 us  [y_turn(): return lax.ppermute(a, 'seq', pairs)]
    add x4 -> x0, local copies, waits for them, and re-layouts: 2.93 us -> none  [number(): return (e * nz + p)[..., None] * cap + slot]
    pallas_call x14 -> x16, Pallas kernels: 48.7 us -> 47.9 us  [call(): pl.pallas_call(kernel, out_shape=list(outs), grid_spec=pltpu.PrefetchScal...]
  transfers between devices with their start and end apart: 47 -> 43, of which waited for: 23 -> 22; matrix products, arithmetic and copies ran while one was open for 7% -> 0% of each run, Pallas kernels for 18% -> 19%
where the time goes in v2:
time: 198 us
  waiting for transfers between devices  90.1 us (46%)
  starting transfers between devices  53.8 us (27%)
  Pallas kernels  47.9 us (24%)
  local copies, waits for them, and re-layouts  4.39 us (2%)
    ppermute x16, waiting for transfers between devices, z_turn(): return lax.ppermute(a, 'seq', pairs)  62.7 us
    pallas_call x16, Pallas kernels, call(): pl.pallas_call(kernel, out_shape=list(outs), grid_spec=pltpu.PrefetchScal...  47.9 us
    ppermute x16, starting transfers between devices, z_turn(): return lax.ppermute(a, 'seq', pairs)  23.9 us
    ppermute x17, starting transfers between devices, y_turn(): return lax.ppermute(a, 'seq', pairs)  22.2 us
    ppermute x17, waiting for transfers between devices, y_turn(): return lax.ppermute(a, 'seq', pairs)  16.6 us
    ppermute x10, waiting for transfers between devices, swap(): return lax.ppermute(a, 'exp', [(p, p ^ r) for p in range(nz)])  10.8 us
    ppermute x10, starting transfers between devices, swap(): return lax.ppermute(a, 'exp', [(p, p ^ r) for p in range(nz)])  7.69 us
    unnamed x50, local copies, waits for them, and re-layouts  4.27 us
  transfers between devices with their start and end apart: 43, of which 22 were waited for; matrix products, arithmetic and copies ran while one was open for 0% of the time, Pallas kernels for 19%

profile of v2, /device:TPU:0, one launch (start us, length us, event | category | flops | bytes accessed | tf_op | source)
XLA Modules:
  0.0 197.9 jit_solution(13638782937477264546)
XLA Ops:
  3.5 3.0 %collective-permute-start = (bf16[2,128,1024]{2,1,0:T(8,128)(2,1)S(1)}, bf16[2,128,1024]{2,1,0:T(8,128)(2,1)S(1)}, u32[]{:S(2)}, u32[]{:S(2)}) collective-permute-start(bf16[2,128,1024]{2,1,0:T(8,128)(2,1)S(1)} %shard_map.230), channel_id=1, source_target_pairs={{0,4},{4,0},{8,12},{12,8},{16,20},{20,16},{24,28},{28,24},{1,5},{5... | collective-permute-start | bytes 1572872 | tf_op jit(solution)/shard_map/ppermute | solution.py:484
  9.3 2.0 %collective-permute-start.5 = (f32[16,128]{1,0:T(8,128)S(1)}, f32[16,128]{1,0:T(8,128)S(1)}, u32[]{:S(2)}, u32[]{:S(2)}) collective-permute-start(f32[16,128]{1,0:T(8,128)S(1)} %bitcast.12), channel_id=1, source_target_pairs={{0,4},{4,0},{8,12},{12,8},{16,20},{20,16},{24,28},{28,24},{1,5},{5... | collective-permute-start | bytes 24584 | tf_op jit(solution)/shard_map/ppermute | solution.py:484
  17.3 2.0 collective-permute-done.refs_2_.refs_4_
  19.3 10.6 %collective-permute-done.5.refs_4_ = f32[16,128]{1,0:T(8,128)S(1)} collective-permute-done((f32[16,128]{1,0:T(8,128)S(1)}, f32[16,128]{1,0:T(8,128)S(1)}, u32[]{:S(2)}, u32[]{:S(2)}) %collective-permute-start.5) | collective-permute-done | bytes 8224 | tf_op jit(solution)/shard_map/ppermute | solution.py:484
  29.9 3.0 %shard_map.233 = (bf16[272,128]{1,0:T(8,128)(2,1)S(1)}, bf16[272,128]{1,0:T(8,128)(2,1)S(1)}, bf16[272,128]{1,0:T(8,128)(2,1)S(1)}, bf16[272,128]{1,0:T(8,128)(2...) custom-call(s32[3]{0:T(128)S(1)} %pad_add_fusion.s, bf16[128,2048]{1,0:T(8,128)(2,1)S(1)} %copy-done.2, ...), custom_call_target="tpu_custom_call" | custom-call | flops 67108864 | bytes 1884160 | tf_op jit(solution)/shard_map/pallas_call | solution.py:47
  32.9 1.9 collective-permute-start.6
  34.7 2.6 %collective-permute-start.7 = (bf16[272,128]{1,0:T(8,128)(2,1)S(1)}, bf16[272,128]{1,0:T(8,128)(2,1)S(1)}, u32[]{:S(2)}, u32[]{:S(2)}) collective-permute-start(bf16[272,128]{1,0:T(8,128)(2,1)S(1)} %get-tuple-element.42), channel_id=1, source_target_pairs={{0,16},{4,20},{8,24},{12,28},{16,0},{20,4},{24,8},{28,12},{1,17},{... | collective-permute-start | bytes 208904 | tf_op jit(solution)/shard_map/ppermute | solution.py:480
  39.8 2.1 %collective-permute-done.7.refs_2_ = bf16[272,128]{1,0:T(8,128)(2,1)S(1)} collective-permute-done((bf16[272,128]{1,0:T(8,128)(2,1)S(1)}, bf16[272,128]{1,0:T(8,128)(2,1)S(1)}, u32[]{:S(2)}, u32[]{:S(2)}) %collective-permute-start.7) | collective-permute-done | bytes 69664 | tf_op jit(solution)/shard_map/ppermute | solution.py:480
  43.4 2.9 %collective-permute-start.11 = (bf16[256,128]{1,0:T(8,128)(2,1)S(1)}, bf16[256,128]{1,0:T(8,128)(2,1)S(1)}, u32[]{:S(2)}, u32[]{:S(2)}) collective-permute-start(bf16[256,128]{1,0:T(8,128)(2,1)S(1)} %get-tuple-element.47), channel_id=1, source_target_pairs={{0,24},{4,28},{8,0},{12,4},{16,8},{20,12},{24,16},{28,20},{1,25},{... | collective-permute-start | bytes 196616 | tf_op jit(solution)/shard_map/ppermute | solution.py:480
  46.4 2.4 %collective-permute-done.10.refs_8_ = bf16[256,128]{1,0:T(8,128)(2,1)S(1)} collective-permute-done((bf16[256,128]{1,0:T(8,128)(2,1)S(1)}, bf16[256,128]{1,0:T(8,128)(2,1)S(1)}, u32[]{:S(2)}, u32[]{:S(2)}) %collective-permute-start.10) | collective-permute-done | bytes 65568 | tf_op jit(solution)/shard_map/ppermute | solution.py:480
  48.7 3.7 %collective-permute-done.9.refs_7_ = bf16[256,128]{1,0:T(8,128)(2,1)S(1)} collective-permute-done((bf16[256,128]{1,0:T(8,128)(2,1)S(1)}, bf16[256,128]{1,0:T(8,128)(2,1)S(1)}, u32[]{:S(2)}, u32[]{:S(2)}) %collective-permute-start.9) | collective-permute-done | bytes 65568 | tf_op jit(solution)/shard_map/ppermute | solution.py:480
  52.4 3.4 %shard_map.235.refs_0_ = bf16[256,1024]{1,0:T(8,128)(2,1)S(1)} custom-call(s32[3]{0:T(128)S(1)} %pad_add_fusion.s, bf16[128,2048]{1,0:T(8,128)(2,1)S(1)} %copy-done.2, bf16[128,2048]{1,0:T(8,128)(2,1)S(1)} %copy-done.4, bf16[128,2048]{1,0:T(8,128)(2,1)S(1)} %copy-done.6, bf16[128,2048]{1,0:T(8,128)(2,1)S(1)} %copy-done.8, ...), custom_call_target="tpu_custom_call" | custom-call | flops 268435456 | bytes 3956736 | tf_op jit(solution)/shard_map/pallas_call | solution.py:47
  55.9 3.8 %collective-permute-start.13 = (bf16[256,1024]{1,0:T(8,128)(2,1)S(1)}, bf16[256,1024]{1,0:T(8,128)(2,1)S(1)}, u32[]{:S(2)}, u32[]{:S(2)}) collective-permute-start(bf16[256,1024]{1,0:T(8,128)(2,1)S(1)} %shard_map.235.refs_0_), channel_id=1, source_target_pairs={{0,24},{4,28},{8,0},{12,4},{16,8},{20,12},{24,16},{28,20},{1,25},{... | collective-permute-start | bytes 1572872 | tf_op jit(solution)/shard_map/ppermute | solution.py:480
  61.2 11.3 %collective-permute-done.12.refs_1_ = bf16[256,1024]{1,0:T(8,128)(2,1)S(1)} collective-permute-done((bf16[256,1024]{1,0:T(8,128)(2,1)S(1)}, bf16[256,1024]{1,0:T(8,128)(2,1)S(1)}, u32[]{:S(2)}, u32[]{:S(2)}) %collective-permute-start.12) | collective-permute-done | bytes 524320 | tf_op jit(solution)/shard_map/ppermute | solution.py:480
  72.6 6.2 %collective-permute-done.13.refs_2_ = bf16[256,1024]{1,0:T(8,128)(2,1)S(1)} collective-permute-done((bf16[256,1024]{1,0:T(8,128)(2,1)S(1)}, bf16[256,1024]{1,0:T(8,128)(2,1)S(1)}, u32[]{:S(2)}, u32[]{:S(2)}) %collective-permute-start.13) | collective-permute-done | bytes 524320 | tf_op jit(solution)/shard_map/ppermute | solution.py:480
  78.8 1.5 collective-permute-start.19
  80.9 2.4 %collective-permute-start.14 = (bf16[128,1024]{1,0:T(8,128)(2,1)S(1)}, bf16[128,1024]{1,0:T(8,128)(2,1)S(1)}, u32[]{:S(2)}, u32[]{:S(2)}) collective-permute-start(bf16[128,1024]{1,0:T(8,128)(2,1)S(1)} %get-tuple-element.77), channel_id=1, source_target_pairs={{0,16},{4,20},{8,24},{12,28},{16,0},{20,4},{24,8},{28,12},{1,17},{... | collective-permute-start | bytes 786440 | tf_op jit(solution)/shard_map/ppermute | solution.py:480
  83.9 14.1 %collective-permute-done.14.refs_0_ = bf16[128,1024]{1,0:T(8,128)(2,1)S(1)} collective-permute-done((bf16[128,1024]{1,0:T(8,128)(2,1)S(1)}, bf16[128,1024]{1,0:T(8,128)(2,1)S(1)}, u32[]{:S(2)}, u32[]{:S(2)}) %collective-permute-start.14) | collective-permute-done | bytes 262176 | tf_op jit(solution)/shard_map/ppermute | solution.py:480
  98.0 1.5 collective-permute-start.16
  99.5 4.0 %collective-permute-done.15.refs_1_ = bf16[128,1024]{1,0:T(8,128)(2,1)S(1)} collective-permute-done((bf16[128,1024]{1,0:T(8,128)(2,1)S(1)}, bf16[128,1024]{1,0:T(8,128)(2,1)S(1)}, u32[]{:S(2)}, u32[]{:S(2)}) %collective-permute-start.15) | collective-permute-done | bytes 262176 | tf_op jit(solution)/shard_map/ppermute | solution.py:480
  103.5 1.5 collective-permute-start.17
  105.1 4.1 %shard_map.236 = (bf16[3,256,768]{2,1,0:T(8,128)(2,1)S(1)}, f32[320,768]{1,0:T(8,128)S(1)}) custom-call(s32[3]{0:T(128)S(1)} %pad_add_fusion.s, bf16[256,1024]{1,0:T(8,128)(2,1)S(1)} %shard_map.235.refs_0_, bf16[256,1024]{1,0:T(8,128)(2,1)S(1)} %collective-permute-done.12.refs_1_, bf16[256,1024]{1,0:T(8,128)(2,1)S(1)} %collective-permute-done.13.refs_2_, ...), custom_call_target="tpu_custom_call" | custom-call | flops 2415919104 | bytes 11610624 | tf_op jit(solution)/shard_map/pallas_call | solution.py:47
  109.2 4.1 %collective-permute-done.17.refs_3_ = bf16[128,1024]{1,0:T(8,128)(2,1)S(1)} collective-permute-done((bf16[128,1024]{1,0:T(8,128)(2,1)S(1)}, bf16[128,1024]{1,0:T(8,128)(2,1)S(1)}, u32[]{:S(2)}, u32[]{:S(2)}) %collective-permute-start.17) | collective-permute-done | bytes 262176 | tf_op jit(solution)/shard_map/ppermute | solution.py:484
  113.3 3.0 %shard_map.237 = (f32[160,768]{1,0:T(8,128)S(1)}, bf16[160,768]{1,0:T(8,128)(2,1)S(1)}, bf16[2,256,768]{2,1,0:T(8,128)(2,1)S(1)}, bf16[2,256,768]{2,1,0:T(8,128)(2,1)S(1)}) custom-call(s32[3]{0:T(128)S(1)} %pad_add_fusion.s, bf16[128,1024]{1,0:T(8,128)(2,1)S(1)} %collective-permute-done.14.refs_0_, bf16[128,1024]{1,0:T(8,128)(2,1)S(1)} %collective-permute-done.15.refs_1_, ...), custom_call_target="tpu_custom_call" | custom-call | flops 805306368 | bytes 12216832 | tf_op jit(solution)/shard_map/pallas_call | solution.py:47
  116.4 1.5 collective-permute-done.21
  118.0 1.6 collective-permute-start.22
  119.5 3.8 %collective-permute-done.22.received = bf16[80,768]{1,0:T(8,128)(2,1)S(1)} collective-permute-done((bf16[80,768]{1,0:T(8,128)(2,1)S(1)}, bf16[80,768]{1,0:T(8,128)(2,1)S(1)}, u32[]{:S(2)}, u32[]{:S(2)}) %collective-permute-start.22) | collective-permute-done | bytes 122912 | tf_op jit(solution)/shard_map/ppermute | solution.py:487
  124.5 3.8 %collective-permute-start.25 = (bf16[80,896]{1,0:T(8,128)(2,1)S(1)}, bf16[80,896]{1,0:T(8,128)(2,1)S(1)}, u32[]{:S(2)}, u32[]{:S(2)}) collective-permute-start(bf16[80,896]{1,0:T(8,128)(2,1)S(1)} %shard_map.238.refs_0_), channel_id=1, source_target_pairs={{0,24},{4,28},{8,0},{12,4},{16,8},{20,12},{24,16},{28,20},{1,25},{... | collective-permute-start | bytes 430088 | tf_op jit(solution)/shard_map/ppermute | solution.py:480
  128.3 1.5 collective-permute-start.29
  129.9 3.0 %collective-permute-done.23.refs_0_ = bf16[80,896]{1,0:T(8,128)(2,1)S(1)} collective-permute-done((bf16[80,896]{1,0:T(8,128)(2,1)S(1)}, bf16[80,896]{1,0:T(8,128)(2,1)S(1)}, u32[]{:S(2)}, u32[]{:S(2)}) %collective-permute-start.23) | collective-permute-done | bytes 143392 | tf_op jit(solution)/shard_map/ppermute | solution.py:480
  132.9 1.5 collective-permute-start.24
  135.2 5.4 %collective-permute-done.27.refs_2_ = bf16[80,896]{1,0:T(8,128)(2,1)S(1)} collective-permute-done((bf16[80,896]{1,0:T(8,128)(2,1)S(1)}, bf16[80,896]{1,0:T(8,128)(2,1)S(1)}, u32[]{:S(2)}, u32[]{:S(2)}) %collective-permute-start.27) | collective-permute-done | bytes 143392 | tf_op jit(solution)/shard_map/ppermute | solution.py:480
  140.6 1.6 collective-permute-start.28
  142.2 5.6 %shard_map.239 = (f32[80,1152]{1,0:T(8,128)S(1)}, f32[80,1152]{1,0:T(8,128)S(1)}, f32[80,128]{1,0:T(8,128)S(1)}) custom-call(s32[3]{0:T(128)S(1)} %pad_add_fusion.s, bf16[80,896]{1,0:T(8,128)(2,1)S(1)} %shard_map.238.refs_0_, bf16[80,896]{1,0:T(8,128)(2,1)S(1)} %collective-permute-done.29.refs_1_, bf16[1,1152,6144]{2,1,0:T(8,128)(2,1)} %refs_6_.8, ...), custom_call_target="tpu_custom_call" | custom-call | flops 566231040 | bytes 29376512 | tf_op jit(solution)/shard_map/pallas_call | solution.py:47
  147.8 5.8 %shard_map.240 = (f32[80,1152]{1,0:T(8,128)S(1)}, f32[80,1152]{1,0:T(8,128)S(1)}, f32[80,128]{1,0:T(8,128)S(1)}) custom-call(s32[3]{0:T(128)S(1)} %pad_add_fusion.s, bf16[80,896]{1,0:T(8,128)(2,1)S(1)} %collective-permute-done.23.refs_0_, bf16[80,896]{1,0:T(8,128)(2,1)S(1)} %collective-permute-done.25.refs_1_, ...), custom_call_target="tpu_custom_call" | custom-call | flops 849346560 | bytes 30298112 | tf_op jit(solution)/shard_map/pallas_call | solution.py:47
  153.6 5.8 %shard_map.241 = (bf16[80,1152]{1,0:T(8,128)(2,1)S(1)}, f32[80,128]{1,0:T(8,128)S(1)}) custom-call(s32[3]{0:T(128)S(1)} %pad_add_fusion.s, bf16[80,896]{1,0:T(8,128)(2,1)S(1)} %collective-permute-done.24.refs_0_, bf16[80,896]{1,0:T(8,128)(2,1)S(1)} %collective-permute-done.26.refs_1_, bf16[80,896]{1,0:T(8,128)(2,1)S(1)} %collective-permute-done.28.refs_2_, ...), custom_call_target="tpu_custom_call" | custom-call | flops 849346560 | bytes 29745152 | tf_op jit(solution)/shard_map/pallas_call | solution.py:47
  159.9 3.8 %collective-permute-start.32 = (bf16[80,1152]{1,0:T(8,128)(2,1)S(1)}, bf16[80,1152]{1,0:T(8,128)(2,1)S(1)}, u32[]{:S(2)}, u32[]{:S(2)}) collective-permute-start(bf16[80,1152]{1,0:T(8,128)(2,1)S(1)} %get-tuple-element.61.refs_0_), channel_id=1, source_target_pairs={{0,24},{4,28},{8,0},{12,4},{16,8},{20,12},{24,16},{28,20},{1,25},{... | collective-permute-start | bytes 552968 | tf_op jit(solution)/shard_map/ppermute | solution.py:480
  164.0 1.6 collective-permute-start.41
  165.6 3.7 %collective-permute-done.30.refs_0_ = bf16[80,1152]{1,0:T(8,128)(2,1)S(1)} collective-permute-done((bf16[80,1152]{1,0:T(8,128)(2,1)S(1)}, bf16[80,1152]{1,0:T(8,128)(2,1)S(1)}, u32[]{:S(2)}, u32[]{:S(2)}) %collective-permute-start.30) | collective-permute-done | bytes 184352 | tf_op jit(solution)/shard_map/ppermute | solution.py:480
  169.3 1.6 collective-permute-start.31
  171.7 5.5 %collective-permute-done.34.refs_2_ = bf16[80,1152]{1,0:T(8,128)(2,1)S(1)} collective-permute-done((bf16[80,1152]{1,0:T(8,128)(2,1)S(1)}, bf16[80,1152]{1,0:T(8,128)(2,1)S(1)}, u32[]{:S(2)}, u32[]{:S(2)}) %collective-permute-start.34) | collective-permute-done | bytes 184352 | tf_op jit(solution)/shard_map/ppermute | solution.py:480
  177.2 1.6 collective-permute-start.35
  179.4 3.3 %shard_map.242.refs_3_ = f32[80,768]{1,0:T(8,128)S(1)} custom-call(s32[3]{0:T(128)S(1)} %pad_add_fusion.s, bf16[80,1152]{1,0:T(8,128)(2,1)S(1)} %get-tuple-element.61.refs_0_, bf16[80,1152]{1,0:T(8,128)(2,1)S(1)} %collective-permute-done.36.refs_1_, bf16[1,9216,768]{2,1,0:T(8,128)(2,1)} %refs_4_.7), custom_call_target="tpu_custom_call" | custom-call | flops 283115520 | bytes 14770176 | tf_op jit(solution)/shard_map/pallas_call | solution.py:47
  182.7 3.6 %shard_map.243.refs_3_ = f32[80,768]{1,0:T(8,128)S(1)} custom-call(s32[3]{0:T(128)S(1)} %pad_add_fusion.s, bf16[80,1152]{1,0:T(8,128)(2,1)S(1)} %collective-permute-done.30.refs_0_, bf16[80,1152]{1,0:T(8,128)(2,1)S(1)} %collective-permute-done.32.refs_1_, bf16[80,1152]{1,0:T(8,128)(2,1)S(1)} %collective-permute-done.34.refs_2_, ...), custom_call_target="tpu_custom_call" | custom-call | flops 424673280 | bytes 15200256 | tf_op jit(solution)/shard_map/pallas_call | solution.py:47
  186.4 3.9 %shard_map.244 = (bf16[32,768]{1,0:T(8,128)(2,1)S(1)}, bf16[32,768]{1,0:T(8,128)(2,1)S(1)}, bf16[32,768]{1,0:T(8,128)(2,1)S(1)}, bf16[32,768]{1,0:T(8,128)(2,1)S(1)}) custom-call(s32[3]{0:T(128)S(1)} %pad_add_fusion.s, bf16[80,1152]{1,0:T(8,128)(2,1)S(1)} %collective-permute-done.31.refs_0_, bf16[80,1152]{1,0:T(8,128)(2,1)S(1)} %collective-permute-done.33.refs_1_, ...), custom_call_target="tpu_custom_call" | custom-call | flops 424673280 | bytes 15192512 | tf_op jit(solution)/shard_map/pallas_call | solution.py:47
  190.4 1.6 collective-permute-start.38
  192.3 2.3 %collective-permute-done.38.refs_2_ = bf16[32,768]{1,0:T(8,128)(2,1)S(1)} collective-permute-done((bf16[32,768]{1,0:T(8,128)(2,1)S(1)}, bf16[32,768]{1,0:T(8,128)(2,1)S(1)}, u32[]{:S(2)}, u32[]{:S(2)}) %collective-permute-start.38) | collective-permute-done | bytes 49184 | tf_op jit(solution)/shard_map/ppermute | solution.py:487
  195.7 2.0 %shard_map.245 = bf16[256,768]{1,0:T(8,128)(2,1)} custom-call(s32[3]{0:T(128)S(1)} %pad_add_fusion.s, bf16[32,768]{1,0:T(8,128)(2,1)S(1)} %get-tuple-element.63.refs_0_, bf16[32,768]{1,0:T(8,128)(2,1)S(1)} %collective-permute-done.37.refs_1_, bf16[32,768]{1,0:T(8,128)(2,1)S(1)} %collective-permute-done.38.refs_2_, ...), custom_call_target="tpu_custom_call" | custom-call | bytes 1778688 | tf_op jit(solution)/shard_map/pallas_call | solution.py:47
  (113 shorter events, 24.0 us)
Async XLA Ops:
  0.7 51.7 %copy-start.19 = (f32[2048]{0:T(1024)S(1)}, f32[2048]{0:T(1024)}, u32[]{:S(2)}) copy-start(f32[2048]{0:T(1024)} %param.30) | copy-start | bytes 24580
  2.9 49.5 %copy-start.6 = (bf16[128,2048]{1,0:T(8,128)(2,1)S(1)}, bf16[128,2048]{1,0:T(8,128)(2,1)}, u32[]{:S(2)}) copy-start(bf16[128,2048]{1,0:T(8,128)(2,1)} %refs_2_.3) | copy-start | bytes 1572868
  3.5 15.8 %collective-permute-start = (bf16[2,128,1024]{2,1,0:T(8,128)(2,1)S(1)}, bf16[2,128,1024]{2,1,0:T(8,128)(2,1)S(1)}, u32[]{:S(2)}, u32[]{:S(2)}) collective-permute-start(bf16[2,128,1024]{2,1,0:T(8,128)(2,1)S(1)} %shard_map.230), channel_id=1, source_target_pairs={{0,4},{4,0},{8,12},{12,8},{16,20},{20,16},{24,28},{28,24},{1,5},{5... | collective-permute-start | bytes 1572872 | tf_op jit(solution)/shard_map/ppermute | solution.py:484
  9.2 37.1 %collective-permute-start.4 = (bf16[2,128,1024]{2,1,0:T(8,128)(2,1)S(1)}, bf16[2,128,1024]{2,1,0:T(8,128)(2,1)S(1)}, u32[]{:S(2)}, u32[]{:S(2)}) collective-permute-start(bf16[2,128,1024]{2,1,0:T(8,128)(2,1)S(1)} %shard_map.232), channel_id=1, source_target_pairs={{0,4},{4,0},{8,12},{12,8},{16,20},{20,16},{24,28},{28,24},{1,5},{5... | collective-permute-start | bytes 1572872 | tf_op jit(solution)/shard_map/ppermute | solution.py:484
  9.3 20.5 %collective-permute-start.5 = (f32[16,128]{1,0:T(8,128)S(1)}, f32[16,128]{1,0:T(8,128)S(1)}, u32[]{:S(2)}, u32[]{:S(2)}) collective-permute-start(f32[16,128]{1,0:T(8,128)S(1)} %bitcast.12), channel_id=1, source_target_pairs={{0,4},{4,0},{8,12},{12,8},{16,20},{20,16},{24,28},{28,24},{1,5},{5... | collective-permute-start | bytes 24584 | tf_op jit(solution)/shard_map/ppermute | solution.py:484
  11.3 1.5 collective-permute-start.1
  11.3 3.6 %collective-permute-start.2 = (s32[2,256]{1,0:T(2,128)S(1)}, s32[2,256]{1,0:T(2,128)S(1)}, u32[]{:S(2)}, u32[]{:S(2)}) collective-permute-start(s32[2,256]{1,0:T(2,128)S(1)} %bitcast.16), channel_id=1, source_target_pairs={{0,2},{1,3},{2,0},{3,1},{4,6},{5,7},{6,4},{7,5},{8,10},{9,11},{10,... | collective-permute-start | bytes 6152 | tf_op jit(solution)/shard_map/ppermute | solution.py:487
  12.8 3.0 %collective-permute-start.3 = (s32[2,256]{1,0:T(2,128)S(1)}, s32[2,256]{1,0:T(2,128)S(1)}, u32[]{:S(2)}, u32[]{:S(2)}) collective-permute-start(s32[2,256]{1,0:T(2,128)S(1)} %bitcast.17), channel_id=1, source_target_pairs={{0,3},{1,2},{2,1},{3,0},{4,7},{5,6},{6,5},{7,4},{8,11},{9,10},{10,... | collective-permute-start | bytes 6152 | tf_op jit(solution)/shard_map/ppermute | solution.py:487
  32.9 6.9 %collective-permute-start.6 = (bf16[272,128]{1,0:T(8,128)(2,1)S(1)}, bf16[272,128]{1,0:T(8,128)(2,1)S(1)}, u32[]{:S(2)}, u32[]{:S(2)}) collective-permute-start(bf16[272,128]{1,0:T(8,128)(2,1)S(1)} %get-tuple-element.41), channel_id=1, source_target_pairs={{0,8},{4,12},{8,16},{12,20},{16,24},{20,28},{24,0},{28,4},{1,9},{5... | collective-permute-start | bytes 208904 | tf_op jit(solution)/shard_map/ppermute | solution.py:480
  34.7 7.1 %collective-permute-start.7 = (bf16[272,128]{1,0:T(8,128)(2,1)S(1)}, bf16[272,128]{1,0:T(8,128)(2,1)S(1)}, u32[]{:S(2)}, u32[]{:S(2)}) collective-permute-start(bf16[272,128]{1,0:T(8,128)(2,1)S(1)} %get-tuple-element.42), channel_id=1, source_target_pairs={{0,16},{4,20},{8,24},{12,28},{16,0},{20,4},{24,8},{28,12},{1,17},{... | collective-permute-start | bytes 208904 | tf_op jit(solution)/shard_map/ppermute | solution.py:480
  37.3 4.7 %collective-permute-start.8 = (bf16[272,128]{1,0:T(8,128)(2,1)S(1)}, bf16[272,128]{1,0:T(8,128)(2,1)S(1)}, u32[]{:S(2)}, u32[]{:S(2)}) collective-permute-start(bf16[272,128]{1,0:T(8,128)(2,1)S(1)} %get-tuple-element.43), channel_id=1, source_target_pairs={{0,24},{4,28},{8,0},{12,4},{16,8},{20,12},{24,16},{28,20},{1,25},{... | collective-permute-start | bytes 208904 | tf_op jit(solution)/shard_map/ppermute | solution.py:480
  42.0 63.0 %copy-start = (bf16[2048,768]{1,0:T(8,128)(2,1)S(1)}, bf16[2048,768]{1,0:T(8,128)(2,1)}, u32[]{:S(2)}) copy-start(bf16[2048,768]{1,0:T(8,128)(2,1)} %refs_5_.2) | copy-start | bytes 9437188
  42.0 63.0 %copy-start.11 = (s32[320,1]{1,0:T(8,128)S(1)}, s32[320,1]{1,0:T(8,128)}, u32[]{:S(2)}) copy-start(s32[320,1]{1,0:T(8,128)} %constant.73.clone.refs_8_.refs_6_) | copy-start | bytes 3844
  42.0 63.0 %copy-start.12 = (s32[320,1]{1,0:T(8,128)S(1)}, s32[320,1]{1,0:T(8,128)}, u32[]{:S(2)}) copy-start(s32[320,1]{1,0:T(8,128)} %constant.74.clone.refs_9_.refs_7_) | copy-start | bytes 3844
  42.8 5.9 %collective-permute-start.10 = (bf16[256,128]{1,0:T(8,128)(2,1)S(1)}, bf16[256,128]{1,0:T(8,128)(2,1)S(1)}, u32[]{:S(2)}, u32[]{:S(2)}) collective-permute-start(bf16[256,128]{1,0:T(8,128)(2,1)S(1)} %get-tuple-element.46), channel_id=1, source_target_pairs={{0,16},{4,20},{8,24},{12,28},{16,0},{20,4},{24,8},{28,12},{1,17},{... | collective-permute-start | bytes 196616 | tf_op jit(solution)/shard_map/ppermute | solution.py:480
  43.4 5.3 %collective-permute-start.11 = (bf16[256,128]{1,0:T(8,128)(2,1)S(1)}, bf16[256,128]{1,0:T(8,128)(2,1)S(1)}, u32[]{:S(2)}, u32[]{:S(2)}) collective-permute-start(bf16[256,128]{1,0:T(8,128)(2,1)S(1)} %get-tuple-element.47), channel_id=1, source_target_pairs={{0,24},{4,28},{8,0},{12,4},{16,8},{20,12},{24,16},{28,20},{1,25},{... | collective-permute-start | bytes 196616 | tf_op jit(solution)/shard_map/ppermute | solution.py:480
  46.4 6.1 %collective-permute-start.9 = (bf16[256,128]{1,0:T(8,128)(2,1)S(1)}, bf16[256,128]{1,0:T(8,128)(2,1)S(1)}, u32[]{:S(2)}, u32[]{:S(2)}) collective-permute-start(bf16[256,128]{1,0:T(8,128)(2,1)S(1)} %get-tuple-element.45), channel_id=1, source_target_pairs={{0,8},{4,12},{8,16},{12,20},{16,24},{20,28},{24,0},{28,4},{1,9},{5... | collective-permute-start | bytes 196616 | tf_op jit(solution)/shard_map/ppermute | solution.py:480
  55.9 16.7 %collective-permute-start.12 = (bf16[256,1024]{1,0:T(8,128)(2,1)S(1)}, bf16[256,1024]{1,0:T(8,128)(2,1)S(1)}, u32[]{:S(2)}, u32[]{:S(2)}) collective-permute-start(bf16[256,1024]{1,0:T(8,128)(2,1)S(1)} %shard_map.235.refs_0_), channel_id=1, source_target_pairs={{0,8},{4,12},{8,16},{12,20},{16,24},{20,28},{24,0},{28,4},{1,9},{5... | collective-permute-start | bytes 1572872 | tf_op jit(solution)/shard_map/ppermute | solution.py:480
  55.9 22.9 %collective-permute-start.13 = (bf16[256,1024]{1,0:T(8,128)(2,1)S(1)}, bf16[256,1024]{1,0:T(8,128)(2,1)S(1)}, u32[]{:S(2)}, u32[]{:S(2)}) collective-permute-start(bf16[256,1024]{1,0:T(8,128)(2,1)S(1)} %shard_map.235.refs_0_), channel_id=1, source_target_pairs={{0,24},{4,28},{8,0},{12,4},{16,8},{20,12},{24,16},{28,20},{1,25},{... | collective-permute-start | bytes 1572872 | tf_op jit(solution)/shard_map/ppermute | solution.py:480
  59.7 45.3 %collective-permute-start.18 = (bf16[256,1024]{1,0:T(8,128)(2,1)S(1)}, bf16[256,1024]{1,0:T(8,128)(2,1)S(1)}, u32[]{:S(2)}, u32[]{:S(2)}) collective-permute-start(bf16[256,1024]{1,0:T(8,128)(2,1)S(1)} %shard_map.235.refs_0_), channel_id=1, source_target_pairs={{0,4},{4,0},{8,12},{12,8},{16,20},{20,16},{24,28},{28,24},{1,5},{5... | collective-permute-start | bytes 1572872 | tf_op jit(solution)/shard_map/ppermute | solution.py:484
  78.8 26.2 %collective-permute-start.19 = (bf16[256,1024]{1,0:T(8,128)(2,1)S(1)}, bf16[256,1024]{1,0:T(8,128)(2,1)S(1)}, u32[]{:S(2)}, u32[]{:S(2)}) collective-permute-start(bf16[256,1024]{1,0:T(8,128)(2,1)S(1)} %collective-permute-done.12.refs_1_), channel_id=1, source_target_pairs={{0,4},{4,0},{8,12},{12,8},{16,20},{20,16},{24,28},{28,24},{1,5},{5... | collective-permute-start | bytes 1572872 | tf_op jit(solution)/shard_map/ppermute | solution.py:484
  80.4 24.7 %collective-permute-start.20 = (bf16[256,1024]{1,0:T(8,128)(2,1)S(1)}, bf16[256,1024]{1,0:T(8,128)(2,1)S(1)}, u32[]{:S(2)}, u32[]{:S(2)}) collective-permute-start(bf16[256,1024]{1,0:T(8,128)(2,1)S(1)} %collective-permute-done.13.refs_2_), channel_id=1, source_target_pairs={{0,4},{4,0},{8,12},{12,8},{16,20},{20,16},{24,28},{28,24},{1,5},{5... | collective-permute-start | bytes 1572872 | tf_op jit(solution)/shard_map/ppermute | solution.py:484
  80.9 17.1 %collective-permute-start.14 = (bf16[128,1024]{1,0:T(8,128)(2,1)S(1)}, bf16[128,1024]{1,0:T(8,128)(2,1)S(1)}, u32[]{:S(2)}, u32[]{:S(2)}) collective-permute-start(bf16[128,1024]{1,0:T(8,128)(2,1)S(1)} %get-tuple-element.77), channel_id=1, source_target_pairs={{0,16},{4,20},{8,24},{12,28},{16,0},{20,4},{24,8},{28,12},{1,17},{... | collective-permute-start | bytes 786440 | tf_op jit(solution)/shard_map/ppermute | solution.py:480
  83.3 20.2 %collective-permute-start.15 = (bf16[128,1024]{1,0:T(8,128)(2,1)S(1)}, bf16[128,1024]{1,0:T(8,128)(2,1)S(1)}, u32[]{:S(2)}, u32[]{:S(2)}) collective-permute-start(bf16[128,1024]{1,0:T(8,128)(2,1)S(1)} %get-tuple-element.76), channel_id=1, source_target_pairs={{0,16},{4,20},{8,24},{12,28},{16,0},{20,4},{24,8},{28,12},{1,17},{... | collective-permute-start | bytes 786440 | tf_op jit(solution)/shard_map/ppermute | solution.py:480
  98.0 11.2 %collective-permute-start.16 = (bf16[128,1024]{1,0:T(8,128)(2,1)S(1)}, bf16[128,1024]{1,0:T(8,128)(2,1)S(1)}, u32[]{:S(2)}, u32[]{:S(2)}) collective-permute-start(bf16[128,1024]{1,0:T(8,128)(2,1)S(1)} %collective-permute-done.14.refs_0_), channel_id=1, source_target_pairs={{0,4},{4,0},{8,12},{12,8},{16,20},{20,16},{24,28},{28,24},{1,5},{5... | collective-permute-start | bytes 786440 | tf_op jit(solution)/shard_map/ppermute | solution.py:484
  103.5 9.8 %collective-permute-start.17 = (bf16[128,1024]{1,0:T(8,128)(2,1)S(1)}, bf16[128,1024]{1,0:T(8,128)(2,1)S(1)}, u32[]{:S(2)}, u32[]{:S(2)}) collective-permute-start(bf16[128,1024]{1,0:T(8,128)(2,1)S(1)} %collective-permute-done.15.refs_1_), channel_id=1, source_target_pairs={{0,4},{4,0},{8,12},{12,8},{16,20},{20,16},{24,28},{28,24},{1,5},{5... | collective-permute-start | bytes 786440 | tf_op jit(solution)/shard_map/ppermute | solution.py:484
  116.3 1.6 collective-permute-start.21
  118.0 5.4 %collective-permute-start.22 = (bf16[80,768]{1,0:T(8,128)(2,1)S(1)}, bf16[80,768]{1,0:T(8,128)(2,1)S(1)}, u32[]{:S(2)}, u32[]{:S(2)}) collective-permute-start(bf16[80,768]{1,0:T(8,128)(2,1)S(1)} %get-tuple-element.74), channel_id=1, source_target_pairs={{0,2},{1,3},{2,0},{3,1},{4,6},{5,7},{6,4},{7,5},{8,10},{9,11},{10,... | collective-permute-start | bytes 368648 | tf_op jit(solution)/shard_map/ppermute | solution.py:487
  124.4 39.4 %collective-permute-start.40 = (bf16[2,256,768]{2,1,0:T(8,128)(2,1)S(1)}, bf16[2,256,768]{2,1,0:T(8,128)(2,1)S(1)}, u32[]{:S(2)}, u32[]{:S(2)}) collective-permute-start(bf16[2,256,768]{2,1,0:T(8,128)(2,1)S(1)} %get-tuple-element.69), channel_id=1, source_target_pairs={{0,1},{1,0},{2,3},{3,2},{4,5},{5,4},{6,7},{7,6},{8,9},{9,8},{10,11... | collective-permute-start | bytes 2359304 | tf_op jit(solution)/shard_map/ppermute | solution.py:487
  124.4 8.5 %collective-permute-start.23 = (bf16[80,896]{1,0:T(8,128)(2,1)S(1)}, bf16[80,896]{1,0:T(8,128)(2,1)S(1)}, u32[]{:S(2)}, u32[]{:S(2)}) collective-permute-start(bf16[80,896]{1,0:T(8,128)(2,1)S(1)} %shard_map.238.refs_0_), channel_id=1, source_target_pairs={{0,8},{4,12},{8,16},{12,20},{16,24},{20,28},{24,0},{28,4},{1,9},{5... | collective-permute-start | bytes 430088 | tf_op jit(solution)/shard_map/ppermute | solution.py:480
  124.5 9.9 %collective-permute-start.25 = (bf16[80,896]{1,0:T(8,128)(2,1)S(1)}, bf16[80,896]{1,0:T(8,128)(2,1)S(1)}, u32[]{:S(2)}, u32[]{:S(2)}) collective-permute-start(bf16[80,896]{1,0:T(8,128)(2,1)S(1)} %shard_map.238.refs_0_), channel_id=1, source_target_pairs={{0,24},{4,28},{8,0},{12,4},{16,8},{20,12},{24,16},{28,20},{1,25},{... | collective-permute-start | bytes 430088 | tf_op jit(solution)/shard_map/ppermute | solution.py:480
  128.3 12.3 %collective-permute-start.27 = (bf16[80,896]{1,0:T(8,128)(2,1)S(1)}, bf16[80,896]{1,0:T(8,128)(2,1)S(1)}, u32[]{:S(2)}, u32[]{:S(2)}) collective-permute-start(bf16[80,896]{1,0:T(8,128)(2,1)S(1)} %shard_map.238.refs_0_), channel_id=1, source_target_pairs={{0,16},{4,20},{8,24},{12,28},{16,0},{20,4},{24,8},{28,12},{1,17},{... | collective-permute-start | bytes 430088 | tf_op jit(solution)/shard_map/ppermute | solution.py:480
  128.3 13.9 %collective-permute-start.29 = (bf16[80,896]{1,0:T(8,128)(2,1)S(1)}, bf16[80,896]{1,0:T(8,128)(2,1)S(1)}, u32[]{:S(2)}, u32[]{:S(2)}) collective-permute-start(bf16[80,896]{1,0:T(8,128)(2,1)S(1)} %shard_map.238.refs_0_), channel_id=1, source_target_pairs={{0,4},{4,0},{8,12},{12,8},{16,20},{20,16},{24,28},{28,24},{1,5},{5... | collective-permute-start | bytes 430088 | tf_op jit(solution)/shard_map/ppermute | solution.py:484
  132.9 20.7 %collective-permute-start.24 = (bf16[80,896]{1,0:T(8,128)(2,1)S(1)}, bf16[80,896]{1,0:T(8,128)(2,1)S(1)}, u32[]{:S(2)}, u32[]{:S(2)}) collective-permute-start(bf16[80,896]{1,0:T(8,128)(2,1)S(1)} %collective-permute-done.23.refs_0_), channel_id=1, source_target_pairs={{0,4},{4,0},{8,12},{12,8},{16,20},{20,16},{24,28},{28,24},{1,5},{5... | collective-permute-start | bytes 430088 | tf_op jit(solution)/shard_map/ppermute | solution.py:484
  134.4 19.2 %collective-permute-start.26 = (bf16[80,896]{1,0:T(8,128)(2,1)S(1)}, bf16[80,896]{1,0:T(8,128)(2,1)S(1)}, u32[]{:S(2)}, u32[]{:S(2)}) collective-permute-start(bf16[80,896]{1,0:T(8,128)(2,1)S(1)} %collective-permute-done.25.refs_1_), channel_id=1, source_target_pairs={{0,4},{4,0},{8,12},{12,8},{16,20},{20,16},{24,28},{28,24},{1,5},{5... | collective-permute-start | bytes 430088 | tf_op jit(solution)/shard_map/ppermute | solution.py:484
  140.6 13.0 %collective-permute-start.28 = (bf16[80,896]{1,0:T(8,128)(2,1)S(1)}, bf16[80,896]{1,0:T(8,128)(2,1)S(1)}, u32[]{:S(2)}, u32[]{:S(2)}) collective-permute-start(bf16[80,896]{1,0:T(8,128)(2,1)S(1)} %collective-permute-done.27.refs_2_), channel_id=1, source_target_pairs={{0,4},{4,0},{8,12},{12,8},{16,20},{20,16},{24,28},{28,24},{1,5},{5... | collective-permute-start | bytes 430088 | tf_op jit(solution)/shard_map/ppermute | solution.py:484
  159.4 19.5 %collective-permute-start.36 = (bf16[80,1152]{1,0:T(8,128)(2,1)S(1)}, bf16[80,1152]{1,0:T(8,128)(2,1)S(1)}, u32[]{:S(2)}, u32[]{:S(2)}) collective-permute-start(bf16[80,1152]{1,0:T(8,128)(2,1)S(1)} %get-tuple-element.61.refs_0_), channel_id=1, source_target_pairs={{0,4},{4,0},{8,12},{12,8},{16,20},{20,16},{24,28},{28,24},{1,5},{5... | collective-permute-start | bytes 552968 | tf_op jit(solution)/shard_map/ppermute | solution.py:484
  159.9 9.4 %collective-permute-start.30 = (bf16[80,1152]{1,0:T(8,128)(2,1)S(1)}, bf16[80,1152]{1,0:T(8,128)(2,1)S(1)}, u32[]{:S(2)}, u32[]{:S(2)}) collective-permute-start(bf16[80,1152]{1,0:T(8,128)(2,1)S(1)} %get-tuple-element.61.refs_0_), channel_id=1, source_target_pairs={{0,8},{4,12},{8,16},{12,20},{16,24},{20,28},{24,0},{28,4},{1,9},{5... | collective-permute-start | bytes 552968 | tf_op jit(solution)/shard_map/ppermute | solution.py:480
  159.9 10.9 %collective-permute-start.32 = (bf16[80,1152]{1,0:T(8,128)(2,1)S(1)}, bf16[80,1152]{1,0:T(8,128)(2,1)S(1)}, u32[]{:S(2)}, u32[]{:S(2)}) collective-permute-start(bf16[80,1152]{1,0:T(8,128)(2,1)S(1)} %get-tuple-element.61.refs_0_), channel_id=1, source_target_pairs={{0,24},{4,28},{8,0},{12,4},{16,8},{20,12},{24,16},{28,20},{1,25},{... | collective-permute-start | bytes 552968 | tf_op jit(solution)/shard_map/ppermute | solution.py:480
  163.7 13.5 %collective-permute-start.34 = (bf16[80,1152]{1,0:T(8,128)(2,1)S(1)}, bf16[80,1152]{1,0:T(8,128)(2,1)S(1)}, u32[]{:S(2)}, u32[]{:S(2)}) collective-permute-start(bf16[80,1152]{1,0:T(8,128)(2,1)S(1)} %get-tuple-element.61.refs_0_), channel_id=1, source_target_pairs={{0,16},{4,20},{8,24},{12,28},{16,0},{20,4},{24,8},{28,12},{1,17},{... | collective-permute-start | bytes 552968 | tf_op jit(solution)/shard_map/ppermute | solution.py:480
  164.0 31.6 %collective-permute-start.41 = (bf16[1,256,768]{2,1,0:T(8,128)(2,1)S(1)}, bf16[1,256,768]{2,1,0:T(8,128)(2,1)S(1)}, u32[]{:S(2)}, u32[]{:S(2)}) collective-permute-start(bf16[1,256,768]{2,1,0:T(8,128)(2,1)S(1)} %get-tuple-element.72), channel_id=1, source_target_pairs={{0,2},{1,3},{2,0},{3,1},{4,6},{5,7},{6,4},{7,5},{8,10},{9,11},{10,... | collective-permute-start | bytes 1179656 | tf_op jit(solution)/shard_map/ppermute | solution.py:487
  169.3 17.1 %collective-permute-start.31 = (bf16[80,1152]{1,0:T(8,128)(2,1)S(1)}, bf16[80,1152]{1,0:T(8,128)(2,1)S(1)}, u32[]{:S(2)}, u32[]{:S(2)}) collective-permute-start(bf16[80,1152]{1,0:T(8,128)(2,1)S(1)} %collective-permute-done.30.refs_0_), channel_id=1, source_target_pairs={{0,4},{4,0},{8,12},{12,8},{16,20},{20,16},{24,28},{28,24},{1,5},{5... | collective-permute-start | bytes 552968 | tf_op jit(solution)/shard_map/ppermute | solution.py:484
  170.9 15.5 %collective-permute-start.33 = (bf16[80,1152]{1,0:T(8,128)(2,1)S(1)}, bf16[80,1152]{1,0:T(8,128)(2,1)S(1)}, u32[]{:S(2)}, u32[]{:S(2)}) collective-permute-start(bf16[80,1152]{1,0:T(8,128)(2,1)S(1)} %collective-permute-done.32.refs_1_), channel_id=1, source_target_pairs={{0,4},{4,0},{8,12},{12,8},{16,20},{20,16},{24,28},{28,24},{1,5},{5... | collective-permute-start | bytes 552968 | tf_op jit(solution)/shard_map/ppermute | solution.py:484
  177.2 9.2 %collective-permute-start.35 = (bf16[80,1152]{1,0:T(8,128)(2,1)S(1)}, bf16[80,1152]{1,0:T(8,128)(2,1)S(1)}, u32[]{:S(2)}, u32[]{:S(2)}) collective-permute-start(bf16[80,1152]{1,0:T(8,128)(2,1)S(1)} %collective-permute-done.34.refs_2_), channel_id=1, source_target_pairs={{0,4},{4,0},{8,12},{12,8},{16,20},{20,16},{24,28},{28,24},{1,5},{5... | collective-permute-start | bytes 552968 | tf_op jit(solution)/shard_map/ppermute | solution.py:484
  178.9 13.4 %collective-permute-start.42 = (f32[8,16,128]{2,1,0:T(8,128)S(1)}, f32[8,16,128]{2,1,0:T(8,128)S(1)}, u32[]{:S(2)}, u32[]{:S(2)}) collective-permute-start(f32[8,16,128]{2,1,0:T(8,128)S(1)} %get-tuple-element.78), channel_id=1, source_target_pairs={{0,4},{4,0},{8,12},{12,8},{16,20},{20,16},{24,28},{28,24},{1,5},{5... | collective-permute-start | bytes 196616 | tf_op jit(solution)/shard_map/ppermute | solution.py:484
  190.3 2.0 collective-permute-start.37
  190.4 4.2 %collective-permute-start.38 = (bf16[32,768]{1,0:T(8,128)(2,1)S(1)}, bf16[32,768]{1,0:T(8,128)(2,1)S(1)}, u32[]{:S(2)}, u32[]{:S(2)}) collective-permute-start(bf16[32,768]{1,0:T(8,128)(2,1)S(1)} %get-tuple-element.65), channel_id=1, source_target_pairs={{0,2},{1,3},{2,0},{3,1},{4,6},{5,7},{6,4},{7,5},{8,10},{9,11},{10,... | collective-permute-start | bytes 147464 | tf_op jit(solution)/shard_map/ppermute | solution.py:487
  191.9 3.7 %collective-permute-start.39 = (bf16[32,768]{1,0:T(8,128)(2,1)S(1)}, bf16[32,768]{1,0:T(8,128)(2,1)S(1)}, u32[]{:S(2)}, u32[]{:S(2)}) collective-permute-start(bf16[32,768]{1,0:T(8,128)(2,1)S(1)} %get-tuple-element.66), channel_id=1, source_target_pairs={{0,3},{1,2},{2,1},{3,0},{4,7},{5,6},{6,5},{7,4},{8,11},{9,10},{10,... | collective-permute-start | bytes 147464 | tf_op jit(solution)/shard_map/ppermute | solution.py:487
  (20 other events, 269.6 us)

commit v3 on v2

--- a/solution.py
+++ b/solution.py
@@ -36,7 +36,7 @@
     return pl.BlockSpec(tuple(shape), lambda i, s: (0,) * len(shape))
 
 
-def call(kernel, place, operands, outs, scratch=(), flops=0, limit=40, out_any=False):
+def call(kernel, place, operands, outs, scratch=(), flops=0, limit=40):
     arrays, specs, moved = [], [], 0
     for item in operands:
         array, spec = item if isinstance(item, tuple) else (item, whole(item.shape))
@@ -51,9 +51,7 @@
             num_scalar_prefetch=1,
             grid=(1,),
             in_specs=specs,
-            out_specs=[
-                pl.BlockSpec(memory_space=pl.ANY) if out_any else whole(o.shape) for o in outs
-            ],
+            out_specs=[whole(o.shape) for o in outs],
             scratch_shapes=list(scratch),
         ),
         compiler_params=pltpu.CompilerParams(vmem_limit_bytes=limit * 1024 * 1024),
@@ -131,10 +129,9 @@
     sign[...] = (every == j).astype(F32) - (every == other - j).astype(F32)
 
 
-def pack_kernel(away, ny, width, s, a, b, out, sem):
-    at = pl.multiple_of(lax.rem(s[1] + away, ny) * width, 128)
-    for c in run_copies([(x.at[:, pl.ds(at, width)], out.at[n]) for n, x in enumerate((a, b))], sem):
-        c.wait()
+def pack_kernel(s, a, b, out):
+    out[0] = a[...]
+    out[1] = b[...]
 
 
 def update_kernel(nz, ny, heads, hd, s, *refs):
@@ -362,7 +359,7 @@
                 pltpu.make_async_copy(w_up.at[0, :, at], up_buf.at[n], sem.at[1, n]),
             )
         )
-        for c in copies[-1]:
+        for c in copies[-1] if n < 2 else ():
             c.start()
     gate, up, stats = (None, None, None) if first else (b[...] for b in before)
     for n in range(count):
@@ -370,6 +367,9 @@
         part = blocks[n][:, width:].astype(F32)
         stats = part if stats is None else stats + part
         copies[n][0].wait()
+        if n + 2 < count:
+            for c in copies[n + 2]:
+                c.start()
         part = mm(rows, gate_buf[n], NT)
         gate = part if gate is None else gate + part
         copies[n][1].wait()
@@ -407,10 +407,13 @@
         source = lax.rem(z + nz - dz, nz) * ny + lax.rem(y + ny - dy, ny)
         at = pl.ds(pl.multiple_of(source * depth, depth), depth)
         copies.append(pltpu.make_async_copy(w_down.at[0, at, :], buf.at[n], sem.at[n]))
-        copies[-1].start()
+        if n < 3:
+            copies[-1].start()
     total = None if first else before[...]
     for n in range(count):
         copies[n].wait()
+        if n + 3 < count:
+            copies[n + 3].start()
         part = mm(blocks[n][...], buf[n])
         total = part if total is None else total + part
     if not last:
@@ -494,16 +497,30 @@
     def behind(values, events):
         return list(lax.optimization_barrier((tuple(values), tuple(events)))[0])
 
-    def gather(a):
+    def gather_z(a):
         held = {(0, 0): a}
         for d in range(1, ny):
             held[0, d] = y_turn(a, d)
         for d in z_order:
             held[d, 0] = z_turn(a, d)
+        return held
+
+    def gather_y(held, events):
         for d in z_order:
+            x = held[d, 0] = behind([held[d, 0]], events)[0]
             for e in range(1, ny):
-                held[d, e] = y_turn(held[d, 0], e)
-        return held
+                held[d, e] = y_turn(x, e)
+
+    def stages(run, a):
+        arrived = gather_z(a)
+        state = run(0, groups[0], arrived, [])
+        gather_y(arrived, state)
+        for n in (1, 2):
+            state = run(n, groups[n], arrived, state)
+        return state
+
+    groups = [[(0, 0)], [(0, d) for d in range(1, ny)] + [(d, 0) for d in z_order]]
+    groups.append([(d, e) for d in z_order for e in range(1, ny)])
 
     slot = np.arange(cap)
     row_r = np.repeat([bit_reversed(p, bits) for p in range(nz)], slots).astype(np.int32)[:, None]
@@ -515,17 +532,15 @@
     ret_r = np.repeat(np.arange(nz), ret_rows).astype(np.int32)[:, None]
     ret_base = np.tile(padded, nz)[:, None]
 
-    hand = [pltpu.SemaphoreType.DMA((2,))]
     logs_t = jnp.transpose(log_decay)
     logs, kvs, qgs = [logs_t], [], []
     for d in range(1, ny):
-        pack = functools.partial(pack_kernel, d, ny, width)
+        there = pl.BlockSpec((tok, width), lambda n, s, d=d: (0, lax.rem(s[1] + d, ny)))
         out = [sds((2, tok, width), BF16)]
-        (kv,) = call(pack, place, [hbm(key_in), hbm(value_in)], out, hand, out_any=True)
+        (kv,) = call(pack_kernel, place, [(key_in, there), (value_in, there)], out, limit=60)
         kvs.append(y_turn(kv, d))
         logs.append(y_turn(logs_t, d))
-        (qg,) = call(pack, place, [hbm(query), hbm(gate_in)], out, hand, out_any=True)
-        qgs.append(y_turn(qg, d))
+        qgs += call(pack_kernel, place, [(query, there), (gate_in, there)], out, limit=60)
     ids = jnp.transpose(expert_ids)
     codes, sign = call(
         functools.partial(routing_kernel, nz, cap, slots),
@@ -538,7 +553,8 @@
         [pltpu.VMEM((nz, 2, block), I32)],
     )
     attn_gain_2, moe_gain_2, router_t = attn_gain[None], moe_gain[None], jnp.transpose(router)
-    kvs = behind(kvs, [codes, sign, attn_gain_2, moe_gain_2])
+    prepared = [codes, sign, attn_gain_2, moe_gain_2]
+    qgs = [y_turn(qg, d + 1) for d, qg in enumerate(behind(qgs, kvs + logs + prepared))]
     share = hd // nz
     long = tok * ny
     *parts, c_row, c_col = call(
@@ -554,7 +570,8 @@
             pltpu.VMEM((2, tok, width), BF16),
             pltpu.SemaphoreType.DMA((2,)),
         ],
-        flops=2 * long * hd * hd * heads,
+        limit=40,
+            flops=2 * long * hd * hd * heads,
     )
     parts = [parts[0]] + [z_turn(parts[d], d) for d in range(1, nz)]
     *entering, last_rows = call(
@@ -588,7 +605,8 @@
         [sds((long, width), BF16)],
         [pltpu.VMEM((long, width), BF16)] * 4
         + [pltpu.VMEM((heads, hd, hd), BF16), pltpu.SemaphoreType.DMA((4 * ny,))],
-        flops=4 * long * long * width,
+        limit=40,
+            flops=4 * long * long * width,
     )
 
     def across(blocks):
@@ -631,6 +649,7 @@
             [pltpu.VMEM((ny, len(group), long, width), BF16)]
             + ([pltpu.VMEM((block, cols), BF16)] if last else [])
             + [pltpu.SemaphoreType.DMA((len(blocks) + 1,))],
+            limit=40,
             flops=2 * len(group) * long * head_width * cols,
         )
     keep, send, keep_all, send_all = given
@@ -663,44 +682,28 @@
             final_rows, got, (y - d) % ny * heads, 0
         )
 
-    groups = [[(0, d) for d in range(ny)], [(d, 0) for d in z_order]]
-    groups.append([(d, e) for d in z_order for e in range(1, ny)])
-    arrived = gather(rows_out)
-    state = []
-    if cols % 128:
-        order = jnp.stack([(z - dz) % nz * ny + (y - dy) % ny for dz, dy in places])
-        at = jnp.argsort(order)
-        rows_all = jnp.take(jnp.stack([arrived[p] for p in places]), at, axis=0)
-        stats = jnp.sum(rows_all[:, :, cols:].astype(F32), axis=0)
-        rows_all = jnp.swapaxes(rows_all[:, :, :cols], 0, 1).reshape(slots, features)
-        inverse = lax.rsqrt(jnp.sum(stats[:, :3], axis=1) / features + EPS)[:, None]
-        gate = mm(rows_all, w_gate[0], NT) * inverse
-        hidden = (gate * sigmoid(gate) * (mm(rows_all, w_up[0], NT) * inverse)).astype(BF16)
-        weight = sigmoid(jnp.sum(stats[:, 3:6], axis=1)[:, None] * inverse)
-        state = [hidden, jnp.broadcast_to(weight, (slots, 128))]
-    for n, group in enumerate(groups if cols % 128 == 0 else ()):
+    def up(n, group, arrived, state):
         last = n == len(groups) - 1
         outs = [sds((slots, units), F32)] * 2 + [sds((slots, 128), F32)]
         if last:
             outs = [sds((slots, units), BF16), sds((slots, 128), F32)]
-        state = call(
+        return call(
             functools.partial(up_kernel, nz, ny, group, n == 0, last, features),
             place,
             [arrived[p] for p in group] + list(state) + [anywhere(w_gate), anywhere(w_up)],
             outs,
             [pltpu.VMEM((len(group), units, cols), BF16)] * 2
             + [pltpu.SemaphoreType.DMA((2, len(group)))],
+            limit=40,
             flops=4 * len(group) * slots * units * cols,
         )
-    hidden, weight = state
-    arrived = gather(hidden)
-    state = []
-    for n, group in enumerate(groups):
+
+    def down(n, group, arrived, state):
         last = n == len(groups) - 1
         outs = [sds((slots, cols), F32)]
         if last:
             outs = [sds((ret_rows, cols), BF16)] * nz
-        state = call(
+        return call(
             functools.partial(down_kernel, nz, ny, cap, group, n == 0, last),
             place,
             [arrived[p] for p in group]
@@ -712,8 +715,26 @@
                 pltpu.VMEM((len(group), units, cols), BF16),
                 pltpu.SemaphoreType.DMA((len(group),)),
             ],
+            limit=40,
             flops=2 * len(group) * slots * units * cols,
         )
+
+    if cols % 128:
+        arrived = gather_z(rows_out)
+        gather_y(arrived, [])
+        order = jnp.stack([(z - dz) % nz * ny + (y - dy) % ny for dz, dy in places])
+        at = jnp.argsort(order)
+        rows_all = jnp.take(jnp.stack([arrived[p] for p in places]), at, axis=0)
+        stats = jnp.sum(rows_all[:, :, cols:].astype(F32), axis=0)
+        rows_all = jnp.swapaxes(rows_all[:, :, :cols], 0, 1).reshape(slots, features)
+        inverse = lax.rsqrt(jnp.sum(stats[:, :3], axis=1) / features + EPS)[:, None]
+        gate = mm(rows_all, w_gate[0], NT) * inverse
+        hidden = (gate * sigmoid(gate) * (mm(rows_all, w_up[0], NT) * inverse)).astype(BF16)
+        weight = sigmoid(jnp.sum(stats[:, 3:6], axis=1)[:, None] * inverse)
+        weight = jnp.broadcast_to(weight, (slots, 128))
+    else:
+        hidden, weight = stages(up, rows_out)
+    state = stages(down, hidden)
     returned = [state[0]] + [swap(state[r], r) for r in range(1, nz)]
     (layer_out,) = call(
         functools.partial(combine_kernel, nz, cap),

time: 198 us -> 188 us (0.949)
  waiting for transfers between devices: 90.1 us -> 81.2 us
  starting transfers between devices: 53.8 us -> 48.1 us
  local copies, waits for them, and re-layouts: 4.39 us -> 6.69 us
  Pallas kernels: 47.9 us -> 49.9 us
    ppermute x16, waiting for transfers between devices: 62.7 us -> 55.5 us  [z_turn(): return lax.ppermute(a, 'seq', pairs)]
    ppermute x17, starting transfers between devices: 22.2 us -> 16.1 us  [y_turn(): return lax.ppermute(a, 'seq', pairs)]
    ppermute x10, waiting for transfers between devices: 10.8 us -> 8.72 us  [swap(): return lax.ppermute(a, 'exp', [(p, p ^ r) for p in range(nz)])]
    unnamed x50 -> x44, local copies, waits for them, and re-layouts: 4.27 us -> 5.13 us
  transfers between devices with their start and end apart: 43 -> 43, of which waited for: 22 -> 23; matrix products, arithmetic and copies ran while one was open for 0% -> 1% of each run, Pallas kernels for 19% -> 20%
where the time goes in v3:
time: 188 us
  waiting for transfers between devices  81.2 us (43%)
  Pallas kernels  49.9 us (27%)
  starting transfers between devices  48.1 us (26%)
  local copies, waits for them, and re-layouts  6.69 us (4%)
    ppermute x16, waiting for transfers between devices, z_turn(): return lax.ppermute(a, 'seq', pairs)  55.5 us
    pallas_call x16, Pallas kernels, call(): pl.pallas_call(kernel, out_shape=list(outs), grid_spec=pltpu.PrefetchScal...  49.9 us
    ppermute x16, starting transfers between devices, z_turn(): return lax.ppermute(a, 'seq', pairs)  24.8 us
    ppermute x17, waiting for transfers between devices, y_turn(): return lax.ppermute(a, 'seq', pairs)  17 us
    ppermute x17, starting transfers between devices, y_turn(): return lax.ppermute(a, 'seq', pairs)  16.1 us
    ppermute x10, waiting for transfers between devices, swap(): return lax.ppermute(a, 'exp', [(p, p ^ r) for p in range(nz)])  8.72 us
    ppermute x10, starting transfers between devices, swap(): return lax.ppermute(a, 'exp', [(p, p ^ r) for p in range(nz)])  7.24 us
    unnamed x44, local copies, waits for them, and re-layouts  5.13 us
  transfers between devices with their start and end apart: 43, of which 23 were waited for; matrix products, arithmetic and copies ran while one was open for 1% of the time, Pallas kernels for 20%

profile of v3, /device:TPU:0, one launch (start us, length us, event | category | flops | bytes accessed | tf_op | source)
XLA Modules:
  0.0 188.0 jit_solution(12090154576614317609)
XLA Ops:
  1.4 2.7 %shard_map.230 = bf16[2,128,1024]{2,1,0:T(8,128)(2,1)} custom-call(s32[3]{0:T(128)} %pad_add_fusion.s, bf16[128,2048]{1,0:T(8,128)(2,1)} %refs_0_.5, bf16[128,2048]{1,0:T(8,128)(2,1)} %refs_1_.5), custom_call_target="tpu_custom_call" | custom-call | bytes 1572864 | tf_op jit(solution)/shard_map/pallas_call | solution.py:47
  4.1 3.0 %collective-permute-start = (bf16[2,128,1024]{2,1,0:T(8,128)(2,1)}, bf16[2,128,1024]{2,1,0:T(8,128)(2,1)S(1)}, u32[]{:S(2)}, u32[]{:S(2)}) collective-permute-start(bf16[2,128,1024]{2,1,0:T(8,128)(2,1)} %shard_map.230), channel_id=1, source_target_pairs={{0,4},{4,0},{8,12},{12,8},{16,20},{20,16},{24,28},{28,24},{1,5},{5... | collective-permute-start | bytes 1572872 | tf_op jit(solution)/shard_map/ppermute | solution.py:487
  7.1 2.0 %collective-permute-start.3 = (s32[2,256]{1,0:T(2,128)}, s32[2,256]{1,0:T(2,128)S(1)}, u32[]{:S(2)}, u32[]{:S(2)}) collective-permute-start(s32[2,256]{1,0:T(2,128)} %bitcast.16), channel_id=1, source_target_pairs={{0,2},{1,3},{2,0},{3,1},{4,6},{5,7},{6,4},{7,5},{8,10},{9,11},{10,... | collective-permute-start | bytes 6152 | tf_op jit(solution)/shard_map/ppermute | solution.py:490
  9.9 2.5 %shard_map.231 = bf16[2,128,1024]{2,1,0:T(8,128)(2,1)} custom-call(s32[3]{0:T(128)} %pad_add_fusion.s, bf16[128,2048]{1,0:T(8,128)(2,1)} %refs_2_.2, bf16[128,2048]{1,0:T(8,128)(2,1)} %refs_3_.1), custom_call_target="tpu_custom_call" | custom-call | bytes 1572864 | tf_op jit(solution)/shard_map/pallas_call | solution.py:47
  13.9 5.4 %collective-permute-done.1.refs_4_ = f32[16,128]{1,0:T(8,128)S(1)} collective-permute-done((f32[16,128]{1,0:T(8,128)}, f32[16,128]{1,0:T(8,128)S(1)}, u32[]{:S(2)}, u32[]{:S(2)}) %collective-permute-start.1) | collective-permute-done | bytes 8224 | tf_op jit(solution)/shard_map/ppermute | solution.py:487
  19.4 1.7 collective-permute-start.5
  21.1 3.0 %shard_map.233 = (bf16[272,128]{1,0:T(8,128)(2,1)S(1)}, bf16[272,128]{1,0:T(8,128)(2,1)S(1)}, bf16[272,128]{1,0:T(8,128)(2,1)S(1)}, bf16[272,128]{1,0:T(8,128)(2...) custom-call(s32[3]{0:T(128)S(1)} %copy-done.10, bf16[128,2048]{1,0:T(8,128)(2,1)S(1)} %copy-done.2, ...), custom_call_target="tpu_custom_call" | custom-call | flops 67108864 | bytes 1884160 | tf_op jit(solution)/shard_map/pallas_call | solution.py:47
  24.1 1.6 collective-permute-start.6
  25.7 2.6 %collective-permute-start.7 = (bf16[272,128]{1,0:T(8,128)(2,1)S(1)}, bf16[272,128]{1,0:T(8,128)(2,1)S(1)}, u32[]{:S(2)}, u32[]{:S(2)}) collective-permute-start(bf16[272,128]{1,0:T(8,128)(2,1)S(1)} %get-tuple-element.48), channel_id=1, source_target_pairs={{0,16},{4,20},{8,24},{12,28},{16,0},{20,4},{24,8},{28,12},{1,17},{... | collective-permute-start | bytes 208904 | tf_op jit(solution)/shard_map/ppermute | solution.py:483
  30.9 1.7 collective-permute-done.7.refs_2_
  34.4 2.6 %collective-permute-start.11 = (bf16[256,128]{1,0:T(8,128)(2,1)S(1)}, bf16[256,128]{1,0:T(8,128)(2,1)S(1)}, u32[]{:S(2)}, u32[]{:S(2)}) collective-permute-start(bf16[256,128]{1,0:T(8,128)(2,1)S(1)} %get-tuple-element.53), channel_id=1, source_target_pairs={{0,24},{4,28},{8,0},{12,4},{16,8},{20,12},{24,16},{28,20},{1,25},{... | collective-permute-start | bytes 196616 | tf_op jit(solution)/shard_map/ppermute | solution.py:483
  37.2 2.7 %collective-permute-done.10.refs_8_ = bf16[256,128]{1,0:T(8,128)(2,1)S(1)} collective-permute-done((bf16[256,128]{1,0:T(8,128)(2,1)S(1)}, bf16[256,128]{1,0:T(8,128)(2,1)S(1)}, u32[]{:S(2)}, u32[]{:S(2)}) %collective-permute-start.10) | collective-permute-done | bytes 65568 | tf_op jit(solution)/shard_map/ppermute | solution.py:483
  39.9 3.2 %collective-permute-done.9.refs_7_ = bf16[256,128]{1,0:T(8,128)(2,1)S(1)} collective-permute-done((bf16[256,128]{1,0:T(8,128)(2,1)S(1)}, bf16[256,128]{1,0:T(8,128)(2,1)S(1)}, u32[]{:S(2)}, u32[]{:S(2)}) %collective-permute-start.9) | collective-permute-done | bytes 65568 | tf_op jit(solution)/shard_map/ppermute | solution.py:483
  43.1 3.4 %shard_map.235.refs_0_ = bf16[256,1024]{1,0:T(8,128)(2,1)S(1)} custom-call(s32[3]{0:T(128)S(1)} %copy-done.10, bf16[128,2048]{1,0:T(8,128)(2,1)S(1)} %copy-done.2, bf16[128,2048]{1,0:T(8,128)(2,1)S(1)} %copy-done.3, bf16[128,2048]{1,0:T(8,128)(2,1)S(1)} %copy-done.4, bf16[128,2048]{1,0:T(8,128)(2,1)S(1)} %copy-done.5, ...), custom_call_target="tpu_custom_call" | custom-call | flops 268435456 | bytes 3956736 | tf_op jit(solution)/shard_map/pallas_call | solution.py:47
  46.6 3.8 %collective-permute-start.13 = (bf16[256,1024]{1,0:T(8,128)(2,1)S(1)}, bf16[256,1024]{1,0:T(8,128)(2,1)S(1)}, u32[]{:S(2)}, u32[]{:S(2)}) collective-permute-start(bf16[256,1024]{1,0:T(8,128)(2,1)S(1)} %shard_map.235.refs_0_), channel_id=1, source_target_pairs={{0,24},{4,28},{8,0},{12,4},{16,8},{20,12},{24,16},{28,20},{1,25},{... | collective-permute-start | bytes 1572872 | tf_op jit(solution)/shard_map/ppermute | solution.py:483
  51.0 12.3 %collective-permute-done.12.refs_1_ = bf16[256,1024]{1,0:T(8,128)(2,1)S(1)} collective-permute-done((bf16[256,1024]{1,0:T(8,128)(2,1)S(1)}, bf16[256,1024]{1,0:T(8,128)(2,1)S(1)}, u32[]{:S(2)}, u32[]{:S(2)}) %collective-permute-start.12) | collective-permute-done | bytes 524320 | tf_op jit(solution)/shard_map/ppermute | solution.py:483
  63.3 6.4 %collective-permute-done.13.refs_2_ = bf16[256,1024]{1,0:T(8,128)(2,1)S(1)} collective-permute-done((bf16[256,1024]{1,0:T(8,128)(2,1)S(1)}, bf16[256,1024]{1,0:T(8,128)(2,1)S(1)}, u32[]{:S(2)}, u32[]{:S(2)}) %collective-permute-start.13) | collective-permute-done | bytes 524320 | tf_op jit(solution)/shard_map/ppermute | solution.py:483
  70.2 1.5 collective-permute-start.20
  71.8 2.4 %collective-permute-start.14 = (bf16[128,1024]{1,0:T(8,128)(2,1)S(1)}, bf16[128,1024]{1,0:T(8,128)(2,1)S(1)}, u32[]{:S(2)}, u32[]{:S(2)}) collective-permute-start(bf16[128,1024]{1,0:T(8,128)(2,1)S(1)} %get-tuple-element.89), channel_id=1, source_target_pairs={{0,16},{4,20},{8,24},{12,28},{16,0},{20,4},{24,8},{28,12},{1,17},{... | collective-permute-start | bytes 786440 | tf_op jit(solution)/shard_map/ppermute | solution.py:483
  74.8 14.1 %collective-permute-done.14.refs_0_ = bf16[128,1024]{1,0:T(8,128)(2,1)S(1)} collective-permute-done((bf16[128,1024]{1,0:T(8,128)(2,1)S(1)}, bf16[128,1024]{1,0:T(8,128)(2,1)S(1)}, u32[]{:S(2)}, u32[]{:S(2)}) %collective-permute-start.14) | collective-permute-done | bytes 262176 | tf_op jit(solution)/shard_map/ppermute | solution.py:483
  89.4 5.0 %collective-permute-done.15.refs_1_ = bf16[128,1024]{1,0:T(8,128)(2,1)S(1)} collective-permute-done((bf16[128,1024]{1,0:T(8,128)(2,1)S(1)}, bf16[128,1024]{1,0:T(8,128)(2,1)S(1)}, u32[]{:S(2)}, u32[]{:S(2)}) %collective-permute-start.15) | collective-permute-done | bytes 262176 | tf_op jit(solution)/shard_map/ppermute | solution.py:483
  95.0 4.1 %shard_map.236 = (bf16[3,256,768]{2,1,0:T(8,128)(2,1)S(1)}, f32[320,768]{1,0:T(8,128)S(1)}) custom-call(s32[3]{0:T(128)S(1)} %copy-done.10, bf16[256,1024]{1,0:T(8,128)(2,1)S(1)} %shard_map.235.refs_0_, bf16[256,1024]{1,0:T(8,128)(2,1)S(1)} %collective-permute-done.12.refs_1_, bf16[256,1024]{1,0:T(8,128)(2,1)S(1)} %collective-permute-done.13.refs_2_, ...), custom_call_target="tpu_custom_call" | custom-call | flops 2415919104 | bytes 11610624 | tf_op jit(solution)/shard_map/pallas_call | solution.py:47
  100.0 4.1 %collective-permute-done.17.refs_3_ = bf16[128,1024]{1,0:T(8,128)(2,1)S(1)} collective-permute-done((bf16[128,1024]{1,0:T(8,128)(2,1)S(1)}, bf16[128,1024]{1,0:T(8,128)(2,1)S(1)}, u32[]{:S(2)}, u32[]{:S(2)}) %collective-permute-start.17) | collective-permute-done | bytes 262176 | tf_op jit(solution)/shard_map/ppermute | solution.py:487
  104.2 3.0 %shard_map.237 = (f32[160,768]{1,0:T(8,128)S(1)}, bf16[160,768]{1,0:T(8,128)(2,1)S(1)}, bf16[2,256,768]{2,1,0:T(8,128)(2,1)S(1)}, bf16[2,256,768]{2,1,0:T(8,128)(2,1)S(1)}) custom-call(s32[3]{0:T(128)S(1)} %copy-done.10, bf16[128,1024]{1,0:T(8,128)(2,1)S(1)} %collective-permute-done.14.refs_0_, bf16[128,1024]{1,0:T(8,128)(2,1)S(1)} %collective-permute-done.15.refs_1_, ...), custom_call_target="tpu_custom_call" | custom-call | flops 805306368 | bytes 12216832 | tf_op jit(solution)/shard_map/pallas_call | solution.py:47
  107.3 1.5 collective-permute-done.21
  108.8 1.6 collective-permute-start.22
  110.4 3.9 %collective-permute-done.22.received = bf16[80,768]{1,0:T(8,128)(2,1)S(1)} collective-permute-done((bf16[80,768]{1,0:T(8,128)(2,1)S(1)}, bf16[80,768]{1,0:T(8,128)(2,1)S(1)}, u32[]{:S(2)}, u32[]{:S(2)}) %collective-permute-start.22) | collective-permute-done | bytes 122912 | tf_op jit(solution)/shard_map/ppermute | solution.py:490
  119.2 3.5 %shard_map.239 = (f32[80,1152]{1,0:T(8,128)S(1)}, f32[80,1152]{1,0:T(8,128)S(1)}, f32[80,128]{1,0:T(8,128)S(1)}) custom-call(s32[3]{0:T(128)S(1)} %copy-done.10, bf16[80,896]{1,0:T(8,128)(2,1)S(1)} %shard_map.238.refs_0_, bf16[1,1152,6144]{2,1,0:T(8,128)(2,1)} %refs_6_.6, bf16[1,1152,6144]{2,1,0:T(8,128)(2,1)} %refs_7_.7), custom_call_target="tpu_custom_call" | custom-call | flops 283115520 | bytes 29233152 | tf_op jit(solution)/shard_map/pallas_call | solution.py:47
  122.7 2.3 %collective-permute-done.27.refs_3_ = bf16[80,896]{1,0:T(8,128)(2,1)S(1)} collective-permute-done((bf16[80,896]{1,0:T(8,128)(2,1)S(1)}, bf16[80,896]{1,0:T(8,128)(2,1)S(1)}, u32[]{:S(2)}, u32[]{:S(2)}) %collective-permute-start.27) | collective-permute-done | bytes 143392 | tf_op jit(solution)/shard_map/ppermute | solution.py:483
  125.0 3.6 %collective-permute-done.25.refs_2_ = bf16[80,896]{1,0:T(8,128)(2,1)S(1)} collective-permute-done((bf16[80,896]{1,0:T(8,128)(2,1)S(1)}, bf16[80,896]{1,0:T(8,128)(2,1)S(1)}, u32[]{:S(2)}, u32[]{:S(2)}) %collective-permute-start.25) | collective-permute-done | bytes 143392 | tf_op jit(solution)/shard_map/ppermute | solution.py:483
  129.2 1.5 collective-permute-start.26
  131.2 7.0 %shard_map.240 = (f32[80,1152]{1,0:T(8,128)S(1)}, f32[80,1152]{1,0:T(8,128)S(1)}, f32[80,128]{1,0:T(8,128)S(1)}) custom-call(s32[3]{0:T(128)S(1)} %copy-done.10, bf16[80,896]{1,0:T(8,128)(2,1)S(1)} %collective-permute-done.29.refs_0_, bf16[80,896]{1,0:T(8,128)(2,1)S(1)} %collective-permute-done.23.refs_1_, ...), custom_call_target="tpu_custom_call" | custom-call | flops 1132462080 | bytes 30441472 | tf_op jit(solution)/shard_map/pallas_call | solution.py:47
  138.3 1.5 collective-permute-done.24.refs_0_
  139.9 5.9 %shard_map.241 = (bf16[80,1152]{1,0:T(8,128)(2,1)S(1)}, f32[80,128]{1,0:T(8,128)S(1)}) custom-call(s32[3]{0:T(128)S(1)} %copy-done.10, bf16[80,896]{1,0:T(8,128)(2,1)S(1)} %collective-permute-done.24.refs_0_, bf16[80,896]{1,0:T(8,128)(2,1)S(1)} %collective-permute-done.26.refs_1_, bf16[80,896]{1,0:T(8,128)(2,1)S(1)} %collective-permute-done.28.refs_2_, ...), custom_call_target="tpu_custom_call" | custom-call | flops 849346560 | bytes 29745152 | tf_op jit(solution)/shard_map/pallas_call | solution.py:47
  145.7 3.6 %collective-permute-start.34 = (bf16[80,1152]{1,0:T(8,128)(2,1)S(1)}, bf16[80,1152]{1,0:T(8,128)(2,1)S(1)}, u32[]{:S(2)}, u32[]{:S(2)}) collective-permute-start(bf16[80,1152]{1,0:T(8,128)(2,1)S(1)} %get-tuple-element.70.refs_0_), channel_id=1, source_target_pairs={{0,16},{4,20},{8,24},{12,28},{16,0},{20,4},{24,8},{28,12},{1,17},{... | collective-permute-start | bytes 552968 | tf_op jit(solution)/shard_map/ppermute | solution.py:483
  149.4 2.0 %collective-permute-start.32 = (bf16[80,1152]{1,0:T(8,128)(2,1)S(1)}, bf16[80,1152]{1,0:T(8,128)(2,1)S(1)}, u32[]{:S(2)}, u32[]{:S(2)}) collective-permute-start(bf16[80,1152]{1,0:T(8,128)(2,1)S(1)} %get-tuple-element.70.refs_0_), channel_id=1, source_target_pairs={{0,24},{4,28},{8,0},{12,4},{16,8},{20,12},{24,16},{28,20},{1,25},{... | collective-permute-start | bytes 552968 | tf_op jit(solution)/shard_map/ppermute | solution.py:483
  152.4 1.5 collective-permute-start.41
  154.4 5.0 %copy-done = bf16[1,9216,768]{2,1,0:T(8,128)(2,1)S(1)} copy-done((bf16[1,9216,768]{2,1,0:T(8,128)(2,1)S(1)}, bf16[1,9216,768]{2,1,0:T(8,128)(2,1)}, u32[]{:S(2)}) %copy-start) | copy-done | bytes 14155800
  160.8 2.4 %collective-permute-done.30.refs_1_ = bf16[80,1152]{1,0:T(8,128)(2,1)S(1)} collective-permute-done((bf16[80,1152]{1,0:T(8,128)(2,1)S(1)}, bf16[80,1152]{1,0:T(8,128)(2,1)S(1)}, u32[]{:S(2)}, u32[]{:S(2)}) %collective-permute-start.30) | collective-permute-done | bytes 184352 | tf_op jit(solution)/shard_map/ppermute | solution.py:483
  163.7 1.5 collective-permute-start.33
  165.8 1.6 collective-permute-start.42
  167.3 4.4 %shard_map.243.refs_3_ = f32[80,768]{1,0:T(8,128)S(1)} custom-call(s32[3]{0:T(128)S(1)} %copy-done.10, bf16[80,1152]{1,0:T(8,128)(2,1)S(1)} %collective-permute-done.36.refs_0_, bf16[80,1152]{1,0:T(8,128)(2,1)S(1)} %collective-permute-done.30.refs_1_, bf16[80,1152]{1,0:T(8,128)(2,1)S(1)} %collective-permute-done.32.refs_2_, ...), custom_call_target="tpu_custom_call" | custom-call | flops 566231040 | bytes 15384576 | tf_op jit(solution)/shard_map/pallas_call | solution.py:47
  171.7 2.9 %collective-permute-done.33.refs_1_ = bf16[80,1152]{1,0:T(8,128)(2,1)S(1)} collective-permute-done((bf16[80,1152]{1,0:T(8,128)(2,1)S(1)}, bf16[80,1152]{1,0:T(8,128)(2,1)S(1)}, u32[]{:S(2)}, u32[]{:S(2)}) %collective-permute-start.33) | collective-permute-done | bytes 184352 | tf_op jit(solution)/shard_map/ppermute | solution.py:487
  174.6 2.0 %collective-permute-done.31.refs_0_ = bf16[80,1152]{1,0:T(8,128)(2,1)S(1)} collective-permute-done((bf16[80,1152]{1,0:T(8,128)(2,1)S(1)}, bf16[80,1152]{1,0:T(8,128)(2,1)S(1)}, u32[]{:S(2)}, u32[]{:S(2)}) %collective-permute-start.31) | collective-permute-done | bytes 184352 | tf_op jit(solution)/shard_map/ppermute | solution.py:487
  176.6 3.8 %shard_map.244 = (bf16[32,768]{1,0:T(8,128)(2,1)S(1)}, bf16[32,768]{1,0:T(8,128)(2,1)S(1)}, bf16[32,768]{1,0:T(8,128)(2,1)S(1)}, bf16[32,768]{1,0:T(8,128)(2,1)S(1)}) custom-call(s32[3]{0:T(128)S(1)} %copy-done.10, bf16[80,1152]{1,0:T(8,128)(2,1)S(1)} %collective-permute-done.31.refs_0_, bf16[80,1152]{1,0:T(8,128)(2,1)S(1)} %collective-permute-done.33.refs_1_, ...), custom_call_target="tpu_custom_call" | custom-call | flops 424673280 | bytes 15192512 | tf_op jit(solution)/shard_map/pallas_call | solution.py:47
  180.5 1.5 collective-permute-start.38
  182.4 2.3 %collective-permute-done.38.refs_2_ = bf16[32,768]{1,0:T(8,128)(2,1)S(1)} collective-permute-done((bf16[32,768]{1,0:T(8,128)(2,1)S(1)}, bf16[32,768]{1,0:T(8,128)(2,1)S(1)}, u32[]{:S(2)}, u32[]{:S(2)}) %collective-permute-start.38) | collective-permute-done | bytes 49184 | tf_op jit(solution)/shard_map/ppermute | solution.py:490
  185.8 2.0 %shard_map.245 = bf16[256,768]{1,0:T(8,128)(2,1)} custom-call(s32[3]{0:T(128)S(1)} %copy-done.10, bf16[32,768]{1,0:T(8,128)(2,1)S(1)} %get-tuple-element.75.refs_0_, bf16[32,768]{1,0:T(8,128)(2,1)S(1)} %collective-permute-done.37.refs_1_, bf16[32,768]{1,0:T(8,128)(2,1)S(1)} %collective-permute-done.38.refs_2_, ...), custom_call_target="tpu_custom_call" | custom-call | bytes 1778688 | tf_op jit(solution)/shard_map/pallas_call | solution.py:47
  (107 shorter events, 23.0 us)
Async XLA Ops:
  0.7 42.4 %copy-start.4 = (bf16[128,2048]{1,0:T(8,128)(2,1)S(1)}, bf16[128,2048]{1,0:T(8,128)(2,1)}, u32[]{:S(2)}) copy-start(bf16[128,2048]{1,0:T(8,128)(2,1)} %refs_2_.2) | copy-start | bytes 1572868
  0.7 42.4 %copy-start.5 = (bf16[128,2048]{1,0:T(8,128)(2,1)S(1)}, bf16[128,2048]{1,0:T(8,128)(2,1)}, u32[]{:S(2)}) copy-start(bf16[128,2048]{1,0:T(8,128)(2,1)} %refs_3_.1) | copy-start | bytes 1572868
  4.1 15.3 %collective-permute-start = (bf16[2,128,1024]{2,1,0:T(8,128)(2,1)}, bf16[2,128,1024]{2,1,0:T(8,128)(2,1)S(1)}, u32[]{:S(2)}, u32[]{:S(2)}) collective-permute-start(bf16[2,128,1024]{2,1,0:T(8,128)(2,1)} %shard_map.230), channel_id=1, source_target_pairs={{0,4},{4,0},{8,12},{12,8},{16,20},{20,16},{24,28},{28,24},{1,5},{5... | collective-permute-start | bytes 1572872 | tf_op jit(solution)/shard_map/ppermute | solution.py:487
  7.0 12.3 %collective-permute-start.1 = (f32[16,128]{1,0:T(8,128)}, f32[16,128]{1,0:T(8,128)S(1)}, u32[]{:S(2)}, u32[]{:S(2)}) collective-permute-start(f32[16,128]{1,0:T(8,128)} %bitcast.12), channel_id=1, source_target_pairs={{0,4},{4,0},{8,12},{12,8},{16,20},{20,16},{24,28},{28,24},{1,5},{5... | collective-permute-start | bytes 24584 | tf_op jit(solution)/shard_map/ppermute | solution.py:487
  7.1 5.3 %collective-permute-start.2 = (s32[2,256]{1,0:T(2,128)}, s32[2,256]{1,0:T(2,128)S(1)}, u32[]{:S(2)}, u32[]{:S(2)}) collective-permute-start(s32[2,256]{1,0:T(2,128)} %bitcast.15), channel_id=1, source_target_pairs={{0,1},{1,0},{2,3},{3,2},{4,5},{5,4},{6,7},{7,6},{8,9},{9,8},{10,11... | collective-permute-start | bytes 6152 | tf_op jit(solution)/shard_map/ppermute | solution.py:490
  7.1 5.3 %collective-permute-start.3 = (s32[2,256]{1,0:T(2,128)}, s32[2,256]{1,0:T(2,128)S(1)}, u32[]{:S(2)}, u32[]{:S(2)}) collective-permute-start(s32[2,256]{1,0:T(2,128)} %bitcast.16), channel_id=1, source_target_pairs={{0,2},{1,3},{2,0},{3,1},{4,6},{5,7},{6,4},{7,5},{8,10},{9,11},{10,... | collective-permute-start | bytes 6152 | tf_op jit(solution)/shard_map/ppermute | solution.py:490
  9.0 3.4 %collective-permute-start.4 = (s32[2,256]{1,0:T(2,128)}, s32[2,256]{1,0:T(2,128)S(1)}, u32[]{:S(2)}, u32[]{:S(2)}) collective-permute-start(s32[2,256]{1,0:T(2,128)} %bitcast.17), channel_id=1, source_target_pairs={{0,3},{1,2},{2,1},{3,0},{4,7},{5,6},{6,5},{7,4},{8,11},{9,10},{10,... | collective-permute-start | bytes 6152 | tf_op jit(solution)/shard_map/ppermute | solution.py:490
  19.4 23.8 %collective-permute-start.5 = (bf16[2,128,1024]{2,1,0:T(8,128)(2,1)}, bf16[2,128,1024]{2,1,0:T(8,128)(2,1)S(1)}, u32[]{:S(2)}, u32[]{:S(2)}) collective-permute-start(bf16[2,128,1024]{2,1,0:T(8,128)(2,1)} %shard_map.231), channel_id=1, source_target_pairs={{0,4},{4,0},{8,12},{12,8},{16,20},{20,16},{24,28},{28,24},{1,5},{5... | collective-permute-start | bytes 1572872 | tf_op jit(solution)/shard_map/ppermute | solution.py:487
  24.1 6.8 %collective-permute-start.6 = (bf16[272,128]{1,0:T(8,128)(2,1)S(1)}, bf16[272,128]{1,0:T(8,128)(2,1)S(1)}, u32[]{:S(2)}, u32[]{:S(2)}) collective-permute-start(bf16[272,128]{1,0:T(8,128)(2,1)S(1)} %get-tuple-element.47), channel_id=1, source_target_pairs={{0,8},{4,12},{8,16},{12,20},{16,24},{20,28},{24,0},{28,4},{1,9},{5... | collective-permute-start | bytes 208904 | tf_op jit(solution)/shard_map/ppermute | solution.py:483
  25.7 6.9 %collective-permute-start.7 = (bf16[272,128]{1,0:T(8,128)(2,1)S(1)}, bf16[272,128]{1,0:T(8,128)(2,1)S(1)}, u32[]{:S(2)}, u32[]{:S(2)}) collective-permute-start(bf16[272,128]{1,0:T(8,128)(2,1)S(1)} %get-tuple-element.48), channel_id=1, source_target_pairs={{0,16},{4,20},{8,24},{12,28},{16,0},{20,4},{24,8},{28,12},{1,17},{... | collective-permute-start | bytes 208904 | tf_op jit(solution)/shard_map/ppermute | solution.py:483
  28.3 4.8 %collective-permute-start.8 = (bf16[272,128]{1,0:T(8,128)(2,1)S(1)}, bf16[272,128]{1,0:T(8,128)(2,1)S(1)}, u32[]{:S(2)}, u32[]{:S(2)}) collective-permute-start(bf16[272,128]{1,0:T(8,128)(2,1)S(1)} %get-tuple-element.49), channel_id=1, source_target_pairs={{0,24},{4,28},{8,0},{12,4},{16,8},{20,12},{24,16},{28,20},{1,25},{... | collective-permute-start | bytes 208904 | tf_op jit(solution)/shard_map/ppermute | solution.py:483
  33.1 61.8 %copy-start.1 = (bf16[2048,768]{1,0:T(8,128)(2,1)S(1)}, bf16[2048,768]{1,0:T(8,128)(2,1)}, u32[]{:S(2)}) copy-start(bf16[2048,768]{1,0:T(8,128)(2,1)} %refs_5_.3) | copy-start | bytes 9437188
  33.1 61.8 %copy-start.8 = (s32[320,1]{1,0:T(8,128)S(1)}, s32[320,1]{1,0:T(8,128)}, u32[]{:S(2)}) copy-start(s32[320,1]{1,0:T(8,128)} %constant.73.clone.refs_8_.refs_6_) | copy-start | bytes 3844
  33.1 61.8 %copy-start.9 = (s32[320,1]{1,0:T(8,128)S(1)}, s32[320,1]{1,0:T(8,128)}, u32[]{:S(2)}) copy-start(s32[320,1]{1,0:T(8,128)} %constant.74.clone.refs_9_.refs_7_) | copy-start | bytes 3844
  33.9 6.0 %collective-permute-start.10 = (bf16[256,128]{1,0:T(8,128)(2,1)S(1)}, bf16[256,128]{1,0:T(8,128)(2,1)S(1)}, u32[]{:S(2)}, u32[]{:S(2)}) collective-permute-start(bf16[256,128]{1,0:T(8,128)(2,1)S(1)} %get-tuple-element.52), channel_id=1, source_target_pairs={{0,16},{4,20},{8,24},{12,28},{16,0},{20,4},{24,8},{28,12},{1,17},{... | collective-permute-start | bytes 196616 | tf_op jit(solution)/shard_map/ppermute | solution.py:483
  34.4 5.5 %collective-permute-start.11 = (bf16[256,128]{1,0:T(8,128)(2,1)S(1)}, bf16[256,128]{1,0:T(8,128)(2,1)S(1)}, u32[]{:S(2)}, u32[]{:S(2)}) collective-permute-start(bf16[256,128]{1,0:T(8,128)(2,1)S(1)} %get-tuple-element.53), channel_id=1, source_target_pairs={{0,24},{4,28},{8,0},{12,4},{16,8},{20,12},{24,16},{28,20},{1,25},{... | collective-permute-start | bytes 196616 | tf_op jit(solution)/shard_map/ppermute | solution.py:483
  37.1 6.1 %collective-permute-start.9 = (bf16[256,128]{1,0:T(8,128)(2,1)S(1)}, bf16[256,128]{1,0:T(8,128)(2,1)S(1)}, u32[]{:S(2)}, u32[]{:S(2)}) collective-permute-start(bf16[256,128]{1,0:T(8,128)(2,1)S(1)} %get-tuple-element.51), channel_id=1, source_target_pairs={{0,8},{4,12},{8,16},{12,20},{16,24},{20,28},{24,0},{28,4},{1,9},{5... | collective-permute-start | bytes 196616 | tf_op jit(solution)/shard_map/ppermute | solution.py:483
  46.6 16.7 %collective-permute-start.12 = (bf16[256,1024]{1,0:T(8,128)(2,1)S(1)}, bf16[256,1024]{1,0:T(8,128)(2,1)S(1)}, u32[]{:S(2)}, u32[]{:S(2)}) collective-permute-start(bf16[256,1024]{1,0:T(8,128)(2,1)S(1)} %shard_map.235.refs_0_), channel_id=1, source_target_pairs={{0,8},{4,12},{8,16},{12,20},{16,24},{20,28},{24,0},{28,4},{1,9},{5... | collective-permute-start | bytes 1572872 | tf_op jit(solution)/shard_map/ppermute | solution.py:483
  46.6 23.1 %collective-permute-start.13 = (bf16[256,1024]{1,0:T(8,128)(2,1)S(1)}, bf16[256,1024]{1,0:T(8,128)(2,1)S(1)}, u32[]{:S(2)}, u32[]{:S(2)}) collective-permute-start(bf16[256,1024]{1,0:T(8,128)(2,1)S(1)} %shard_map.235.refs_0_), channel_id=1, source_target_pairs={{0,24},{4,28},{8,0},{12,4},{16,8},{20,12},{24,16},{28,20},{1,25},{... | collective-permute-start | bytes 1572872 | tf_op jit(solution)/shard_map/ppermute | solution.py:483
  50.4 44.5 %collective-permute-start.18 = (bf16[256,1024]{1,0:T(8,128)(2,1)S(1)}, bf16[256,1024]{1,0:T(8,128)(2,1)S(1)}, u32[]{:S(2)}, u32[]{:S(2)}) collective-permute-start(bf16[256,1024]{1,0:T(8,128)(2,1)S(1)} %shard_map.235.refs_0_), channel_id=1, source_target_pairs={{0,4},{4,0},{8,12},{12,8},{16,20},{20,16},{24,28},{28,24},{1,5},{5... | collective-permute-start | bytes 1572872 | tf_op jit(solution)/shard_map/ppermute | solution.py:487
  69.7 25.2 %collective-permute-start.19 = (bf16[256,1024]{1,0:T(8,128)(2,1)S(1)}, bf16[256,1024]{1,0:T(8,128)(2,1)S(1)}, u32[]{:S(2)}, u32[]{:S(2)}) collective-permute-start(bf16[256,1024]{1,0:T(8,128)(2,1)S(1)} %collective-permute-done.12.refs_1_), channel_id=1, source_target_pairs={{0,4},{4,0},{8,12},{12,8},{16,20},{20,16},{24,28},{28,24},{1,5},{5... | collective-permute-start | bytes 1572872 | tf_op jit(solution)/shard_map/ppermute | solution.py:487
  70.2 24.7 %collective-permute-start.20 = (bf16[256,1024]{1,0:T(8,128)(2,1)S(1)}, bf16[256,1024]{1,0:T(8,128)(2,1)S(1)}, u32[]{:S(2)}, u32[]{:S(2)}) collective-permute-start(bf16[256,1024]{1,0:T(8,128)(2,1)S(1)} %collective-permute-done.13.refs_2_), channel_id=1, source_target_pairs={{0,4},{4,0},{8,12},{12,8},{16,20},{20,16},{24,28},{28,24},{1,5},{5... | collective-permute-start | bytes 1572872 | tf_op jit(solution)/shard_map/ppermute | solution.py:487
  71.8 17.1 %collective-permute-start.14 = (bf16[128,1024]{1,0:T(8,128)(2,1)S(1)}, bf16[128,1024]{1,0:T(8,128)(2,1)S(1)}, u32[]{:S(2)}, u32[]{:S(2)}) collective-permute-start(bf16[128,1024]{1,0:T(8,128)(2,1)S(1)} %get-tuple-element.89), channel_id=1, source_target_pairs={{0,16},{4,20},{8,24},{12,28},{16,0},{20,4},{24,8},{28,12},{1,17},{... | collective-permute-start | bytes 786440 | tf_op jit(solution)/shard_map/ppermute | solution.py:483
  74.2 20.2 %collective-permute-start.15 = (bf16[128,1024]{1,0:T(8,128)(2,1)S(1)}, bf16[128,1024]{1,0:T(8,128)(2,1)S(1)}, u32[]{:S(2)}, u32[]{:S(2)}) collective-permute-start(bf16[128,1024]{1,0:T(8,128)(2,1)S(1)} %get-tuple-element.88), channel_id=1, source_target_pairs={{0,16},{4,20},{8,24},{12,28},{16,0},{20,4},{24,8},{28,12},{1,17},{... | collective-permute-start | bytes 786440 | tf_op jit(solution)/shard_map/ppermute | solution.py:483
  88.9 11.2 %collective-permute-start.16 = (bf16[128,1024]{1,0:T(8,128)(2,1)S(1)}, bf16[128,1024]{1,0:T(8,128)(2,1)S(1)}, u32[]{:S(2)}, u32[]{:S(2)}) collective-permute-start(bf16[128,1024]{1,0:T(8,128)(2,1)S(1)} %collective-permute-done.14.refs_0_), channel_id=1, source_target_pairs={{0,4},{4,0},{8,12},{12,8},{16,20},{20,16},{24,28},{28,24},{1,5},{5... | collective-permute-start | bytes 786440 | tf_op jit(solution)/shard_map/ppermute | solution.py:487
  94.4 9.8 %collective-permute-start.17 = (bf16[128,1024]{1,0:T(8,128)(2,1)S(1)}, bf16[128,1024]{1,0:T(8,128)(2,1)S(1)}, u32[]{:S(2)}, u32[]{:S(2)}) collective-permute-start(bf16[128,1024]{1,0:T(8,128)(2,1)S(1)} %collective-permute-done.15.refs_1_), channel_id=1, source_target_pairs={{0,4},{4,0},{8,12},{12,8},{16,20},{20,16},{24,28},{28,24},{1,5},{5... | collective-permute-start | bytes 786440 | tf_op jit(solution)/shard_map/ppermute | solution.py:487
  107.2 1.6 collective-permute-start.21
  108.8 5.4 %collective-permute-start.22 = (bf16[80,768]{1,0:T(8,128)(2,1)S(1)}, bf16[80,768]{1,0:T(8,128)(2,1)S(1)}, u32[]{:S(2)}, u32[]{:S(2)}) collective-permute-start(bf16[80,768]{1,0:T(8,128)(2,1)S(1)} %get-tuple-element.86), channel_id=1, source_target_pairs={{0,2},{1,3},{2,0},{3,1},{4,6},{5,7},{6,4},{7,5},{8,10},{9,11},{10,... | collective-permute-start | bytes 368648 | tf_op jit(solution)/shard_map/ppermute | solution.py:490
  115.2 36.2 %collective-permute-start.40 = (bf16[2,256,768]{2,1,0:T(8,128)(2,1)S(1)}, bf16[2,256,768]{2,1,0:T(8,128)(2,1)S(1)}, u32[]{:S(2)}, u32[]{:S(2)}) collective-permute-start(bf16[2,256,768]{2,1,0:T(8,128)(2,1)S(1)} %get-tuple-element.81), channel_id=1, source_target_pairs={{0,1},{1,0},{2,3},{3,2},{4,5},{5,4},{6,7},{7,6},{8,9},{9,8},{10,11... | collective-permute-start | bytes 2359304 | tf_op jit(solution)/shard_map/ppermute | solution.py:490
  115.3 9.7 %collective-permute-start.27 = (bf16[80,896]{1,0:T(8,128)(2,1)S(1)}, bf16[80,896]{1,0:T(8,128)(2,1)S(1)}, u32[]{:S(2)}, u32[]{:S(2)}) collective-permute-start(bf16[80,896]{1,0:T(8,128)(2,1)S(1)} %shard_map.238.refs_0_), channel_id=1, source_target_pairs={{0,16},{4,20},{8,24},{12,28},{16,0},{20,4},{24,8},{28,12},{1,17},{... | collective-permute-start | bytes 430088 | tf_op jit(solution)/shard_map/ppermute | solution.py:483
  116.7 12.0 %collective-permute-start.25 = (bf16[80,896]{1,0:T(8,128)(2,1)S(1)}, bf16[80,896]{1,0:T(8,128)(2,1)S(1)}, u32[]{:S(2)}, u32[]{:S(2)}) collective-permute-start(bf16[80,896]{1,0:T(8,128)(2,1)S(1)} %shard_map.238.refs_0_), channel_id=1, source_target_pairs={{0,24},{4,28},{8,0},{12,4},{16,8},{20,12},{24,16},{28,20},{1,25},{... | collective-permute-start | bytes 430088 | tf_op jit(solution)/shard_map/ppermute | solution.py:483
  117.3 11.3 %collective-permute-start.23 = (bf16[80,896]{1,0:T(8,128)(2,1)S(1)}, bf16[80,896]{1,0:T(8,128)(2,1)S(1)}, u32[]{:S(2)}, u32[]{:S(2)}) collective-permute-start(bf16[80,896]{1,0:T(8,128)(2,1)S(1)} %shard_map.238.refs_0_), channel_id=1, source_target_pairs={{0,8},{4,12},{8,16},{12,20},{16,24},{20,28},{24,0},{28,4},{1,9},{5... | collective-permute-start | bytes 430088 | tf_op jit(solution)/shard_map/ppermute | solution.py:483
  118.7 12.5 %collective-permute-start.29 = (bf16[80,896]{1,0:T(8,128)(2,1)S(1)}, bf16[80,896]{1,0:T(8,128)(2,1)S(1)}, u32[]{:S(2)}, u32[]{:S(2)}) collective-permute-start(bf16[80,896]{1,0:T(8,128)(2,1)S(1)} %shard_map.238.refs_0_), channel_id=1, source_target_pairs={{0,4},{4,0},{8,12},{12,8},{16,20},{20,16},{24,28},{28,24},{1,5},{5... | collective-permute-start | bytes 430088 | tf_op jit(solution)/shard_map/ppermute | solution.py:487
  128.6 9.6 %collective-permute-start.28 = (bf16[80,896]{1,0:T(8,128)(2,1)S(1)}, bf16[80,896]{1,0:T(8,128)(2,1)S(1)}, u32[]{:S(2)}, u32[]{:S(2)}) collective-permute-start(bf16[80,896]{1,0:T(8,128)(2,1)S(1)} %collective-permute-done.27.refs_3_), channel_id=1, source_target_pairs={{0,4},{4,0},{8,12},{12,8},{16,20},{20,16},{24,28},{28,24},{1,5},{5... | collective-permute-start | bytes 430088 | tf_op jit(solution)/shard_map/ppermute | solution.py:487
  129.2 9.2 %collective-permute-start.26 = (bf16[80,896]{1,0:T(8,128)(2,1)S(1)}, bf16[80,896]{1,0:T(8,128)(2,1)S(1)}, u32[]{:S(2)}, u32[]{:S(2)}) collective-permute-start(bf16[80,896]{1,0:T(8,128)(2,1)S(1)} %collective-permute-done.25.refs_2_), channel_id=1, source_target_pairs={{0,4},{4,0},{8,12},{12,8},{16,20},{20,16},{24,28},{28,24},{1,5},{5... | collective-permute-start | bytes 430088 | tf_op jit(solution)/shard_map/ppermute | solution.py:487
  130.7 9.2 %collective-permute-start.24 = (bf16[80,896]{1,0:T(8,128)(2,1)S(1)}, bf16[80,896]{1,0:T(8,128)(2,1)S(1)}, u32[]{:S(2)}, u32[]{:S(2)}) collective-permute-start(bf16[80,896]{1,0:T(8,128)(2,1)S(1)} %collective-permute-done.23.refs_1_), channel_id=1, source_target_pairs={{0,4},{4,0},{8,12},{12,8},{16,20},{20,16},{24,28},{28,24},{1,5},{5... | collective-permute-start | bytes 430088 | tf_op jit(solution)/shard_map/ppermute | solution.py:487
  145.7 15.0 %collective-permute-start.34 = (bf16[80,1152]{1,0:T(8,128)(2,1)S(1)}, bf16[80,1152]{1,0:T(8,128)(2,1)S(1)}, u32[]{:S(2)}, u32[]{:S(2)}) collective-permute-start(bf16[80,1152]{1,0:T(8,128)(2,1)S(1)} %get-tuple-element.70.refs_0_), channel_id=1, source_target_pairs={{0,16},{4,20},{8,24},{12,28},{16,0},{20,4},{24,8},{28,12},{1,17},{... | collective-permute-start | bytes 552968 | tf_op jit(solution)/shard_map/ppermute | solution.py:483
  149.4 11.4 %collective-permute-start.32 = (bf16[80,1152]{1,0:T(8,128)(2,1)S(1)}, bf16[80,1152]{1,0:T(8,128)(2,1)S(1)}, u32[]{:S(2)}, u32[]{:S(2)}) collective-permute-start(bf16[80,1152]{1,0:T(8,128)(2,1)S(1)} %get-tuple-element.70.refs_0_), channel_id=1, source_target_pairs={{0,24},{4,28},{8,0},{12,4},{16,8},{20,12},{24,16},{28,20},{1,25},{... | collective-permute-start | bytes 552968 | tf_op jit(solution)/shard_map/ppermute | solution.py:483
  151.4 11.7 %collective-permute-start.30 = (bf16[80,1152]{1,0:T(8,128)(2,1)S(1)}, bf16[80,1152]{1,0:T(8,128)(2,1)S(1)}, u32[]{:S(2)}, u32[]{:S(2)}) collective-permute-start(bf16[80,1152]{1,0:T(8,128)(2,1)S(1)} %get-tuple-element.70.refs_0_), channel_id=1, source_target_pairs={{0,8},{4,12},{8,16},{12,20},{16,24},{20,28},{24,0},{28,4},{1,9},{5... | collective-permute-start | bytes 552968 | tf_op jit(solution)/shard_map/ppermute | solution.py:483
  152.4 33.4 %collective-permute-start.41 = (bf16[1,256,768]{2,1,0:T(8,128)(2,1)}, bf16[1,256,768]{2,1,0:T(8,128)(2,1)S(1)}, u32[]{:S(2)}, u32[]{:S(2)}) collective-permute-start(bf16[1,256,768]{2,1,0:T(8,128)(2,1)} %get-tuple-element.84), channel_id=1, source_target_pairs={{0,2},{1,3},{2,0},{3,1},{4,6},{5,7},{6,4},{7,5},{8,10},{9,11},{10,... | collective-permute-start | bytes 1179656 | tf_op jit(solution)/shard_map/ppermute | solution.py:490
  153.9 11.9 %collective-permute-start.36 = (bf16[80,1152]{1,0:T(8,128)(2,1)S(1)}, bf16[80,1152]{1,0:T(8,128)(2,1)S(1)}, u32[]{:S(2)}, u32[]{:S(2)}) collective-permute-start(bf16[80,1152]{1,0:T(8,128)(2,1)S(1)} %get-tuple-element.70.refs_0_), channel_id=1, source_target_pairs={{0,4},{4,0},{8,12},{12,8},{16,20},{20,16},{24,28},{28,24},{1,5},{5... | collective-permute-start | bytes 552968 | tf_op jit(solution)/shard_map/ppermute | solution.py:487
  163.1 8.6 %collective-permute-start.35 = (bf16[80,1152]{1,0:T(8,128)(2,1)S(1)}, bf16[80,1152]{1,0:T(8,128)(2,1)S(1)}, u32[]{:S(2)}, u32[]{:S(2)}) collective-permute-start(bf16[80,1152]{1,0:T(8,128)(2,1)S(1)} %collective-permute-done.34.refs_3_), channel_id=1, source_target_pairs={{0,4},{4,0},{8,12},{12,8},{16,20},{20,16},{24,28},{28,24},{1,5},{5... | collective-permute-start | bytes 552968 | tf_op jit(solution)/shard_map/ppermute | solution.py:487
  163.7 10.9 %collective-permute-start.33 = (bf16[80,1152]{1,0:T(8,128)(2,1)S(1)}, bf16[80,1152]{1,0:T(8,128)(2,1)S(1)}, u32[]{:S(2)}, u32[]{:S(2)}) collective-permute-start(bf16[80,1152]{1,0:T(8,128)(2,1)S(1)} %collective-permute-done.32.refs_2_), channel_id=1, source_target_pairs={{0,4},{4,0},{8,12},{12,8},{16,20},{20,16},{24,28},{28,24},{1,5},{5... | collective-permute-start | bytes 552968 | tf_op jit(solution)/shard_map/ppermute | solution.py:487
  165.2 11.4 %collective-permute-start.31 = (bf16[80,1152]{1,0:T(8,128)(2,1)S(1)}, bf16[80,1152]{1,0:T(8,128)(2,1)S(1)}, u32[]{:S(2)}, u32[]{:S(2)}) collective-permute-start(bf16[80,1152]{1,0:T(8,128)(2,1)S(1)} %collective-permute-done.30.refs_1_), channel_id=1, source_target_pairs={{0,4},{4,0},{8,12},{12,8},{16,20},{20,16},{24,28},{28,24},{1,5},{5... | collective-permute-start | bytes 552968 | tf_op jit(solution)/shard_map/ppermute | solution.py:487
  165.8 16.6 %collective-permute-start.42 = (f32[8,16,128]{2,1,0:T(8,128)S(1)}, f32[8,16,128]{2,1,0:T(8,128)S(1)}, u32[]{:S(2)}, u32[]{:S(2)}) collective-permute-start(f32[8,16,128]{2,1,0:T(8,128)S(1)} %get-tuple-element.90), channel_id=1, source_target_pairs={{0,4},{4,0},{8,12},{12,8},{16,20},{20,16},{24,28},{28,24},{1,5},{5... | collective-permute-start | bytes 196616 | tf_op jit(solution)/shard_map/ppermute | solution.py:487
  180.4 2.0 %collective-permute-start.37 = (bf16[32,768]{1,0:T(8,128)(2,1)S(1)}, bf16[32,768]{1,0:T(8,128)(2,1)S(1)}, u32[]{:S(2)}, u32[]{:S(2)}) collective-permute-start(bf16[32,768]{1,0:T(8,128)(2,1)S(1)} %get-tuple-element.76), channel_id=1, source_target_pairs={{0,1},{1,0},{2,3},{3,2},{4,5},{5,4},{6,7},{7,6},{8,9},{9,8},{10,11... | collective-permute-start | bytes 147464 | tf_op jit(solution)/shard_map/ppermute | solution.py:490
  180.5 4.2 %collective-permute-start.38 = (bf16[32,768]{1,0:T(8,128)(2,1)S(1)}, bf16[32,768]{1,0:T(8,128)(2,1)S(1)}, u32[]{:S(2)}, u32[]{:S(2)}) collective-permute-start(bf16[32,768]{1,0:T(8,128)(2,1)S(1)} %get-tuple-element.77), channel_id=1, source_target_pairs={{0,2},{1,3},{2,0},{3,1},{4,6},{5,7},{6,4},{7,5},{8,10},{9,11},{10,... | collective-permute-start | bytes 147464 | tf_op jit(solution)/shard_map/ppermute | solution.py:490
  182.1 3.7 %collective-permute-start.39 = (bf16[32,768]{1,0:T(8,128)(2,1)S(1)}, bf16[32,768]{1,0:T(8,128)(2,1)S(1)}, u32[]{:S(2)}, u32[]{:S(2)}) collective-permute-start(bf16[32,768]{1,0:T(8,128)(2,1)S(1)} %get-tuple-element.78), channel_id=1, source_target_pairs={{0,3},{1,2},{2,1},{3,0},{4,7},{5,6},{6,5},{7,4},{8,11},{9,10},{10,... | collective-permute-start | bytes 147464 | tf_op jit(solution)/shard_map/ppermute | solution.py:490
  (17 other events, 273.0 us)

commit v4 on v3

--- a/solution.py
+++ b/solution.py
@@ -36,7 +36,7 @@
     return pl.BlockSpec(tuple(shape), lambda i, s: (0,) * len(shape))
 
 
-def call(kernel, place, operands, outs, scratch=(), flops=0, limit=40):
+def call(kernel, place, operands, outs, scratch=(), flops=0, limit=40, held=0):
     arrays, specs, moved = [], [], 0
     for item in operands:
         array, spec = item if isinstance(item, tuple) else (item, whole(item.shape))
@@ -51,7 +51,10 @@
             num_scalar_prefetch=1,
             grid=(1,),
             in_specs=specs,
-            out_specs=[whole(o.shape) for o in outs],
+            out_specs=[
+                pl.BlockSpec(memory_space=pltpu.VMEM) if n >= len(outs) - held else whole(o.shape)
+                for n, o in enumerate(outs)
+            ],
             scratch_shapes=list(scratch),
         ),
         compiler_params=pltpu.CompilerParams(vmem_limit_bytes=limit * 1024 * 1024),
@@ -338,47 +341,66 @@
     out[:, width:] = stats.astype(BF16)
 
 
-def up_kernel(nz, ny, places, first, last, features, s, *refs):
-    z, y = s[0], s[1]
+def source_of(s, nz, ny, place):
+    z = lax.rem(s[0] + nz - place[0], nz)
+    return z * ny + lax.rem(s[1] + ny - place[1], ny)
+
+
+def throttled(copies, n, depth):
+    if n < 0:
+        for c in copies[:depth]:
+            c.start()
+        return
+    copies[n].wait()
+    if n + depth < len(copies):
+        copies[n + depth].start()
+
+
+def up_kernel(nz, ny, places, ahead, first, last, features, s, *refs):
     count = len(places)
     blocks = refs[:count]
     refs = refs[count:]
     before = () if first else refs[:3]
     refs = refs[0 if first else 3 :]
-    w_gate, w_up = refs[:2]
-    outs = refs[2 : 4 if last else 5]
-    gate_buf, up_buf, sem = refs[4 if last else 5 :]
-    width = gate_buf.shape[2]
+    weights = refs[:2]
+    refs = refs[2:]
+    if last:
+        outs, buffers, sem = refs[:2], refs[2:4], refs[4]
+    elif ahead:
+        outs, kept, buffers, sem = refs[:3], refs[3:5], refs[5:7], refs[7]
+    else:
+        outs, buffers, sem = refs[:3], refs[3:5], refs[5]
+    width = blocks[0].shape[1] - 128
+
     copies = []
-    for n, (dz, dy) in enumerate(places):
-        source = lax.rem(z + nz - dz, nz) * ny + lax.rem(y + ny - dy, ny)
-        at = pl.ds(pl.multiple_of(source * width, 128), width)
-        copies.append(
-            (
-                pltpu.make_async_copy(w_gate.at[0, :, at], gate_buf.at[n], sem.at[0, n]),
-                pltpu.make_async_copy(w_up.at[0, :, at], up_buf.at[n], sem.at[1, n]),
-            )
-        )
-        for c in copies[-1] if n < 2 else ():
-            c.start()
+    if True:
+        jobs = [(p, buffers, n) for n, p in enumerate(places)]
+        jobs += [(p, kept, n) for n, p in enumerate(ahead)]
+        for p, to, n in jobs:
+            lanes = pl.ds(pl.multiple_of(source_of(s, nz, ny, p) * width, 128), width)
+            for m in range(2):
+                source = weights[m].at[0, :, lanes]
+                copies.append(pltpu.make_async_copy(source, to[m].at[n], sem.at[len(copies)]))
+        throttled(copies, -1, 4)
     gate, up, stats = (None, None, None) if first else (b[...] for b in before)
     for n in range(count):
         rows = blocks[n][:, :width]
         part = blocks[n][:, width:].astype(F32)
         stats = part if stats is None else stats + part
-        copies[n][0].wait()
-        if n + 2 < count:
-            for c in copies[n + 2]:
-                c.start()
-        part = mm(rows, gate_buf[n], NT)
+        if True:
+            throttled(copies, 2 * n, 4)
+        part = mm(rows, buffers[0][n], NT)
         gate = part if gate is None else gate + part
-        copies[n][1].wait()
-        part = mm(rows, up_buf[n], NT)
+        if True:
+            throttled(copies, 2 * n + 1, 4)
+        part = mm(rows, buffers[1][n], NT)
         up = part if up is None else up + part
     if not last:
         outs[0][...] = gate
         outs[1][...] = up
         outs[2][...] = stats
+        for n in range(2 * count, len(copies)):
+            throttled(copies, n, 4)
         return
     square = stats[:, 0:1] + stats[:, 1:2] + stats[:, 2:3]
     gap = stats[:, 3:4] + stats[:, 4:5] + stats[:, 5:6]
@@ -388,8 +410,8 @@
     outs[1][...] = jnp.broadcast_to(sigmoid(gap * inverse), outs[1].shape)
 
 
-def down_kernel(nz, ny, cap, places, first, last, s, *refs):
-    z, y, j = s[0], s[1], s[2]
+def down_kernel(nz, ny, cap, places, ahead, first, last, s, *refs):
+    j = s[2]
     count = len(places)
     blocks = refs[:count]
     refs = refs[count:]
@@ -397,27 +419,32 @@
     refs = refs[0 if first else 1 :]
     w_down = refs[0]
     refs = refs[1:]
+    depth = blocks[0].shape[1]
+    copies = []
     if last:
         weight, out_base, row_base = refs[:3]
-        refs = refs[3:]
-    outs, buf, sem = refs[:-2], refs[-2], refs[-1]
-    depth = buf.shape[1]
-    copies = []
-    for n, (dz, dy) in enumerate(places):
-        source = lax.rem(z + nz - dz, nz) * ny + lax.rem(y + ny - dy, ny)
-        at = pl.ds(pl.multiple_of(source * depth, depth), depth)
-        copies.append(pltpu.make_async_copy(w_down.at[0, at, :], buf.at[n], sem.at[n]))
-        if n < 3:
-            copies[-1].start()
+        outs, buf = refs[3:], w_down
+    else:
+        outs = refs[:1]
+        kept = refs[1] if ahead else None
+        buf, sem = refs[-2:]
+        jobs = [(p, buf, n) for n, p in enumerate(places)]
+        jobs += [(p, kept, n) for n, p in enumerate(ahead)]
+        for p, to, n in jobs:
+            at = pl.ds(pl.multiple_of(source_of(s, nz, ny, p) * depth, depth), depth)
+            source = w_down.at[0, at, :]
+            copies.append(pltpu.make_async_copy(source, to.at[n], sem.at[len(copies)]))
+        throttled(copies, -1, 3)
     total = None if first else before[...]
     for n in range(count):
-        copies[n].wait()
-        if n + 3 < count:
-            copies[n + 3].start()
+        if not last:
+            throttled(copies, n, 3)
         part = mm(blocks[n][...], buf[n])
         total = part if total is None else total + part
     if not last:
         outs[0][...] = total
+        for n in range(count, len(copies)):
+            throttled(copies, n, 3)
         return
     result = (total * weight[:, 0:1]).astype(BF16)
     for r, out in enumerate(outs):
@@ -615,7 +642,7 @@
     held = {0: [[mixed]] + across([mixed])}
     for d in near:
         held[d] = [[z_turn(mixed, d)]]
-    free = behind([mixed], [held[d][0][0] for d in near])[0]
+    free = behind([mixed], [held[near[0]][0][0]])[0]
     for d in near:
         held[d] += across(held[d][0])
     halves = [free[: long // 2], free[long // 2 :]]
@@ -682,43 +709,60 @@
             final_rows, got, (y - d) % ny * heads, 0
         )
 
+    in_vmem = pl.BlockSpec(memory_space=pltpu.VMEM)
+
     def up(n, group, arrived, state):
-        last = n == len(groups) - 1
+        first, last = n == 0, n == len(groups) - 1
+        ahead = []
         outs = [sds((slots, units), F32)] * 2 + [sds((slots, 128), F32)]
+        outs += [sds((len(ahead), units, cols), BF16)] * (2 if ahead else 0)
+        weights = [anywhere(w_gate), anywhere(w_up)]
         if last:
             outs = [sds((slots, units), BF16), sds((slots, 128), F32)]
-        return call(
-            functools.partial(up_kernel, nz, ny, group, n == 0, last, features),
+        state = call(
+            functools.partial(up_kernel, nz, ny, group, ahead, first, last, features),
             place,
-            [arrived[p] for p in group] + list(state) + [anywhere(w_gate), anywhere(w_up)],
+            [arrived[p] for p in group] + list(state) + weights,
             outs,
             [pltpu.VMEM((len(group), units, cols), BF16)] * 2
-            + [pltpu.SemaphoreType.DMA((2, len(group)))],
+            + [pltpu.SemaphoreType.DMA((2 * (len(group) + len(ahead)),))],
             limit=40,
             flops=4 * len(group) * slots * units * cols,
+            held=2 if ahead else 0,
         )
+        if ahead:
+            fetched["up"] = state[3:]
+        return state[:3]
 
     def down(n, group, arrived, state):
-        last = n == len(groups) - 1
+        first, last = n == 0, n == len(groups) - 1
+        ahead = groups[-1] if first else []
         outs = [sds((slots, cols), F32)]
+        outs += [sds((len(ahead), units, cols), BF16)] if ahead else []
+        weights = [anywhere(w_down)]
         if last:
             outs = [sds((ret_rows, cols), BF16)] * nz
-        return call(
-            functools.partial(down_kernel, nz, ny, cap, group, n == 0, last),
+            weights = [(fetched["down"], in_vmem), weight, padded[:, None], own_base.T]
+        state = call(
+            functools.partial(down_kernel, nz, ny, cap, group, ahead, first, last),
             place,
-            [arrived[p] for p in group]
-            + list(state)
-            + [anywhere(w_down)]
-            + ([weight, padded[:, None], own_base.T] if last else []),
+            [arrived[p] for p in group] + list(state) + weights,
             outs,
-            [
+            []
+            if last
+            else [
                 pltpu.VMEM((len(group), units, cols), BF16),
-                pltpu.SemaphoreType.DMA((len(group),)),
+                pltpu.SemaphoreType.DMA((len(group) + len(ahead),)),
             ],
             limit=40,
             flops=2 * len(group) * slots * units * cols,
+            held=1 if ahead else 0,
         )
-
+        if ahead:
+            fetched["down"] = state[1]
+        return state if last else state[:1]
+
+    fetched = {}
     if cols % 128:
         arrived = gather_z(rows_out)
         gather_y(arrived, [])

time: 188 us -> 184 us (0.979)
  waiting for transfers between devices: 81.2 us -> 74 us
  starting transfers between devices: 48.1 us -> 52.2 us
  local copies, waits for them, and re-layouts: 6.69 us -> 4.04 us
    ppermute x17, waiting for transfers between devices: 17 us -> 13.1 us  [y_turn(): return lax.ppermute(a, 'seq', pairs)]
    ppermute x17, starting transfers between devices: 16.1 us -> 20 us  [y_turn(): return lax.ppermute(a, 'seq', pairs)]
    ppermute x16, waiting for transfers between devices: 55.5 us -> 52.2 us  [z_turn(): return lax.ppermute(a, 'seq', pairs)]
    unnamed x44 -> x48, local copies, waits for them, and re-layouts: 5.13 us -> 2.48 us
  transfers between devices with their start and end apart: 43 -> 43, of which waited for: 23 -> 22; matrix products, arithmetic and copies ran while one was open for 1% -> 1% of each run, Pallas kernels for 20% -> 21%
where the time goes in v4:
time: 184 us; the launch traced here: 183 us
  waiting for transfers between devices  74 us (40%)
  starting transfers between devices  52.2 us (28%)
  Pallas kernels  50.8 us (28%)
  local copies, waits for them, and re-layouts  4.04 us (2%)
    ppermute x16, waiting for transfers between devices, z_turn(): return lax.ppermute(a, 'seq', pairs)  52.2 us
    pallas_call x16, Pallas kernels, call(): pl.pallas_call(kernel, out_shape=list(outs), grid_spec=pltpu.PrefetchScal...  50.8 us
    ppermute x16, starting transfers between devices, z_turn(): return lax.ppermute(a, 'seq', pairs)  25.2 us
    ppermute x17, starting transfers between devices, y_turn(): return lax.ppermute(a, 'seq', pairs)  20 us
    ppermute x17, waiting for transfers between devices, y_turn(): return lax.ppermute(a, 'seq', pairs)  13.1 us
    ppermute x10, waiting for transfers between devices, swap(): return lax.ppermute(a, 'exp', [(p, p ^ r) for p in range(nz)])  8.73 us
    ppermute x10, starting transfers between devices, swap(): return lax.ppermute(a, 'exp', [(p, p ^ r) for p in range(nz)])  7.01 us
  transfers between devices with their start and end apart: 43, of which 22 were waited for; matrix products, arithmetic and copies ran while one was open for 1% of the time, Pallas kernels for 21%

profile of v4, /device:TPU:0, one launch (start us, length us, event | category | flops | bytes accessed | tf_op | source)
XLA Modules:
  0.0 183.1 jit_solution(3351056825945413303)
XLA Ops:
  1.4 2.7 %shard_map.230 = bf16[2,128,1024]{2,1,0:T(8,128)(2,1)} custom-call(s32[3]{0:T(128)} %pad_add_fusion.s, bf16[128,2048]{1,0:T(8,128)(2,1)} %refs_0_.5, bf16[128,2048]{1,0:T(8,128)(2,1)} %refs_1_.5), custom_call_target="tpu_custom_call" | custom-call | bytes 1572864 | tf_op jit(solution)/shard_map/pallas_call | solution.py:47
  4.0 3.0 %collective-permute-start = (bf16[2,128,1024]{2,1,0:T(8,128)(2,1)}, bf16[2,128,1024]{2,1,0:T(8,128)(2,1)S(1)}, u32[]{:S(2)}, u32[]{:S(2)}) collective-permute-start(bf16[2,128,1024]{2,1,0:T(8,128)(2,1)} %shard_map.230), channel_id=1, source_target_pairs={{0,4},{4,0},{8,12},{12,8},{16,20},{20,16},{24,28},{28,24},{1,5},{5... | collective-permute-start | bytes 1572872 | tf_op jit(solution)/shard_map/ppermute | solution.py:514
  9.8 2.5 %shard_map.231 = bf16[2,128,1024]{2,1,0:T(8,128)(2,1)} custom-call(s32[3]{0:T(128)} %pad_add_fusion.s, bf16[128,2048]{1,0:T(8,128)(2,1)} %refs_2_.2, bf16[128,2048]{1,0:T(8,128)(2,1)} %refs_3_.1), custom_call_target="tpu_custom_call" | custom-call | bytes 1572864 | tf_op jit(solution)/shard_map/pallas_call | solution.py:47
  12.4 1.5 shard_map.232
  13.9 5.4 %collective-permute-done.1.refs_4_ = f32[16,128]{1,0:T(8,128)S(1)} collective-permute-done((f32[16,128]{1,0:T(8,128)}, f32[16,128]{1,0:T(8,128)S(1)}, u32[]{:S(2)}, u32[]{:S(2)}) %collective-permute-start.1) | collective-permute-done | bytes 8224 | tf_op jit(solution)/shard_map/ppermute | solution.py:514
  19.3 1.7 collective-permute-start.5
  21.1 3.0 %shard_map.233 = (bf16[272,128]{1,0:T(8,128)(2,1)S(1)}, bf16[272,128]{1,0:T(8,128)(2,1)S(1)}, bf16[272,128]{1,0:T(8,128)(2,1)S(1)}, bf16[272,128]{1,0:T(8,128)(2...) custom-call(s32[3]{0:T(128)S(1)} %copy-done.10, bf16[128,2048]{1,0:T(8,128)(2,1)S(1)} %copy-done.2, ...), custom_call_target="tpu_custom_call" | custom-call | flops 67108864 | bytes 1884160 | tf_op jit(solution)/shard_map/pallas_call | solution.py:47
  24.1 1.6 collective-permute-start.6
  25.7 2.6 %collective-permute-start.7 = (bf16[272,128]{1,0:T(8,128)(2,1)S(1)}, bf16[272,128]{1,0:T(8,128)(2,1)S(1)}, u32[]{:S(2)}, u32[]{:S(2)}) collective-permute-start(bf16[272,128]{1,0:T(8,128)(2,1)S(1)} %get-tuple-element.50), channel_id=1, source_target_pairs={{0,16},{4,20},{8,24},{12,28},{16,0},{20,4},{24,8},{28,12},{1,17},{... | collective-permute-start | bytes 208904 | tf_op jit(solution)/shard_map/ppermute | solution.py:510
  30.9 1.7 collective-permute-done.7.refs_2_
  34.6 2.5 %collective-permute-start.10 = (bf16[256,128]{1,0:T(8,128)(2,1)S(1)}, bf16[256,128]{1,0:T(8,128)(2,1)S(1)}, u32[]{:S(2)}, u32[]{:S(2)}) collective-permute-start(bf16[256,128]{1,0:T(8,128)(2,1)S(1)} %get-tuple-element.54), channel_id=1, source_target_pairs={{0,16},{4,20},{8,24},{12,28},{16,0},{20,4},{24,8},{28,12},{1,17},{... | collective-permute-start | bytes 196616 | tf_op jit(solution)/shard_map/ppermute | solution.py:510
  37.7 2.3 %collective-permute-done.9.refs_7_ = bf16[256,128]{1,0:T(8,128)(2,1)S(1)} collective-permute-done((bf16[256,128]{1,0:T(8,128)(2,1)S(1)}, bf16[256,128]{1,0:T(8,128)(2,1)S(1)}, u32[]{:S(2)}, u32[]{:S(2)}) %collective-permute-start.9) | collective-permute-done | bytes 65568 | tf_op jit(solution)/shard_map/ppermute | solution.py:510
  41.9 3.4 %shard_map.235.refs_0_ = bf16[256,1024]{1,0:T(8,128)(2,1)S(1)} custom-call(s32[3]{0:T(128)S(1)} %copy-done.10, bf16[128,2048]{1,0:T(8,128)(2,1)S(1)} %copy-done.2, bf16[128,2048]{1,0:T(8,128)(2,1)S(1)} %copy-done.3, bf16[128,2048]{1,0:T(8,128)(2,1)S(1)} %copy-done.4, bf16[128,2048]{1,0:T(8,128)(2,1)S(1)} %copy-done.5, ...), custom_call_target="tpu_custom_call" | custom-call | flops 268435456 | bytes 3956736 | tf_op jit(solution)/shard_map/pallas_call | solution.py:47
  46.1 3.1 %collective-permute-start.17 = (bf16[256,1024]{1,0:T(8,128)(2,1)S(1)}, bf16[256,1024]{1,0:T(8,128)(2,1)S(1)}, u32[]{:S(2)}, u32[]{:S(2)}) collective-permute-start(bf16[256,1024]{1,0:T(8,128)(2,1)S(1)} %shard_map.235.refs_0_), channel_id=1, source_target_pairs={{0,24},{4,28},{8,0},{12,4},{16,8},{20,12},{24,16},{28,20},{1,25},{... | collective-permute-start | bytes 1572872 | tf_op jit(solution)/shard_map/ppermute | solution.py:510
  49.8 12.2 %collective-permute-done.12.refs_1_ = bf16[256,1024]{1,0:T(8,128)(2,1)S(1)} collective-permute-done((bf16[256,1024]{1,0:T(8,128)(2,1)S(1)}, bf16[256,1024]{1,0:T(8,128)(2,1)S(1)}, u32[]{:S(2)}, u32[]{:S(2)}) %collective-permute-start.12) | collective-permute-done | bytes 524320 | tf_op jit(solution)/shard_map/ppermute | solution.py:510
  62.6 5.1 %collective-permute-done.17.refs_2_ = bf16[256,1024]{1,0:T(8,128)(2,1)S(1)} collective-permute-done((bf16[256,1024]{1,0:T(8,128)(2,1)S(1)}, bf16[256,1024]{1,0:T(8,128)(2,1)S(1)}, u32[]{:S(2)}, u32[]{:S(2)}) %collective-permute-start.17) | collective-permute-done | bytes 524320 | tf_op jit(solution)/shard_map/ppermute | solution.py:510
  69.6 1.6 collective-permute-start.13
  71.2 18.0 %collective-permute-done.14.refs_1_ = bf16[128,1024]{1,0:T(8,128)(2,1)S(1)} collective-permute-done((bf16[128,1024]{1,0:T(8,128)(2,1)S(1)}, bf16[128,1024]{1,0:T(8,128)(2,1)S(1)}, u32[]{:S(2)}, u32[]{:S(2)}) %collective-permute-start.14) | collective-permute-done | bytes 262176 | tf_op jit(solution)/shard_map/ppermute | solution.py:510
  89.2 1.4 collective-permute-start.16
  90.6 2.5 %collective-permute-done.13.refs_0_ = bf16[128,1024]{1,0:T(8,128)(2,1)S(1)} collective-permute-done((bf16[128,1024]{1,0:T(8,128)(2,1)S(1)}, bf16[128,1024]{1,0:T(8,128)(2,1)S(1)}, u32[]{:S(2)}, u32[]{:S(2)}) %collective-permute-start.13) | collective-permute-done | bytes 262176 | tf_op jit(solution)/shard_map/ppermute | solution.py:510
  93.2 1.7 collective-permute-start.15
  94.9 4.1 %shard_map.236 = (bf16[3,256,768]{2,1,0:T(8,128)(2,1)S(1)}, f32[320,768]{1,0:T(8,128)S(1)}) custom-call(s32[3]{0:T(128)S(1)} %copy-done.10, bf16[256,1024]{1,0:T(8,128)(2,1)S(1)} %shard_map.235.refs_0_, bf16[256,1024]{1,0:T(8,128)(2,1)S(1)} %collective-permute-done.12.refs_1_, bf16[256,1024]{1,0:T(8,128)(2,1)S(1)} %collective-permute-done.17.refs_2_, ...), custom_call_target="tpu_custom_call" | custom-call | flops 2415919104 | bytes 11610624 | tf_op jit(solution)/shard_map/pallas_call | solution.py:47
  99.1 2.1 %collective-permute-done.15.refs_2_ = bf16[128,1024]{1,0:T(8,128)(2,1)S(1)} collective-permute-done((bf16[128,1024]{1,0:T(8,128)(2,1)S(1)}, bf16[128,1024]{1,0:T(8,128)(2,1)S(1)}, u32[]{:S(2)}, u32[]{:S(2)}) %collective-permute-start.15) | collective-permute-done | bytes 262176 | tf_op jit(solution)/shard_map/ppermute | solution.py:514
  101.2 3.0 %shard_map.237 = (f32[160,768]{1,0:T(8,128)S(1)}, bf16[160,768]{1,0:T(8,128)(2,1)S(1)}, bf16[2,256,768]{2,1,0:T(8,128)(2,1)S(1)}, bf16[2,256,768]{2,1,0:T(8,128)(2,1)S(1)}) custom-call(s32[3]{0:T(128)S(1)} %copy-done.10, bf16[128,1024]{1,0:T(8,128)(2,1)S(1)} %collective-permute-done.13.refs_0_, bf16[128,1024]{1,0:T(8,128)(2,1)S(1)} %collective-permute-done.14.refs_1_, ...), custom_call_target="tpu_custom_call" | custom-call | flops 805306368 | bytes 12216832 | tf_op jit(solution)/shard_map/pallas_call | solution.py:47
  104.3 1.5 collective-permute-done.21
  105.9 1.5 collective-permute-start.22
  107.3 4.0 %collective-permute-done.22.received = bf16[80,768]{1,0:T(8,128)(2,1)S(1)} collective-permute-done((bf16[80,768]{1,0:T(8,128)(2,1)S(1)}, bf16[80,768]{1,0:T(8,128)(2,1)S(1)}, u32[]{:S(2)}, u32[]{:S(2)}) %collective-permute-start.22) | collective-permute-done | bytes 122912 | tf_op jit(solution)/shard_map/ppermute | solution.py:517
  112.4 1.9 %collective-permute-start.25 = (bf16[80,896]{1,0:T(8,128)(2,1)S(1)}, bf16[80,896]{1,0:T(8,128)(2,1)S(1)}, u32[]{:S(2)}, u32[]{:S(2)}) collective-permute-start(bf16[80,896]{1,0:T(8,128)(2,1)S(1)} %shard_map.238.refs_0_), channel_id=1, source_target_pairs={{0,24},{4,28},{8,0},{12,4},{16,8},{20,12},{24,16},{28,20},{1,25},{... | collective-permute-start | bytes 430088 | tf_op jit(solution)/shard_map/ppermute | solution.py:510
  114.8 1.4 collective-permute-start.29
  116.2 3.5 %shard_map.239 = (f32[80,1152]{1,0:T(8,128)S(1)}, f32[80,1152]{1,0:T(8,128)S(1)}, f32[80,128]{1,0:T(8,128)S(1)}) custom-call(s32[3]{0:T(128)S(1)} %copy-done.10, bf16[80,896]{1,0:T(8,128)(2,1)S(1)} %shard_map.238.refs_0_, bf16[1,1152,6144]{2,1,0:T(8,128)(2,1)} %refs_6_.6, bf16[1,1152,6144]{2,1,0:T(8,128)(2,1)} %refs_7_.7), custom_call_target="tpu_custom_call" | custom-call | flops 283115520 | bytes 29233152 | tf_op jit(solution)/shard_map/pallas_call | solution.py:47
  119.7 2.4 %collective-permute-done.27.refs_3_ = bf16[80,896]{1,0:T(8,128)(2,1)S(1)} collective-permute-done((bf16[80,896]{1,0:T(8,128)(2,1)S(1)}, bf16[80,896]{1,0:T(8,128)(2,1)S(1)}, u32[]{:S(2)}, u32[]{:S(2)}) %collective-permute-start.27) | collective-permute-done | bytes 143392 | tf_op jit(solution)/shard_map/ppermute | solution.py:510
  122.1 3.0 %collective-permute-done.25.refs_2_ = bf16[80,896]{1,0:T(8,128)(2,1)S(1)} collective-permute-done((bf16[80,896]{1,0:T(8,128)(2,1)S(1)}, bf16[80,896]{1,0:T(8,128)(2,1)S(1)}, u32[]{:S(2)}, u32[]{:S(2)}) %collective-permute-start.25) | collective-permute-done | bytes 143392 | tf_op jit(solution)/shard_map/ppermute | solution.py:510
  125.1 1.4 collective-permute-start.24
  127.1 1.4 collective-permute-start.28
  128.5 7.0 %shard_map.240 = (f32[80,1152]{1,0:T(8,128)S(1)}, f32[80,1152]{1,0:T(8,128)S(1)}, f32[80,128]{1,0:T(8,128)S(1)}) custom-call(s32[3]{0:T(128)S(1)} %copy-done.10, bf16[80,896]{1,0:T(8,128)(2,1)S(1)} %collective-permute-done.29.refs_0_, bf16[80,896]{1,0:T(8,128)(2,1)S(1)} %collective-permute-done.23.refs_1_, ...), custom_call_target="tpu_custom_call" | custom-call | flops 1132462080 | bytes 30441472 | tf_op jit(solution)/shard_map/pallas_call | solution.py:47
  136.5 5.9 %shard_map.241 = (bf16[80,1152]{1,0:T(8,128)(2,1)S(1)}, f32[80,128]{1,0:T(8,128)S(1)}) custom-call(s32[3]{0:T(128)S(1)} %copy-done.10, bf16[80,896]{1,0:T(8,128)(2,1)S(1)} %collective-permute-done.24.refs_0_, bf16[80,896]{1,0:T(8,128)(2,1)S(1)} %collective-permute-done.26.refs_1_, bf16[80,896]{1,0:T(8,128)(2,1)S(1)} %collective-permute-done.28.refs_2_, ...), custom_call_target="tpu_custom_call" | custom-call | flops 849346560 | bytes 29745152 | tf_op jit(solution)/shard_map/pallas_call | solution.py:47
  142.4 4.4 %collective-permute-start.34 = (bf16[80,1152]{1,0:T(8,128)(2,1)S(1)}, bf16[80,1152]{1,0:T(8,128)(2,1)S(1)}, u32[]{:S(2)}, u32[]{:S(2)}) collective-permute-start(bf16[80,1152]{1,0:T(8,128)(2,1)S(1)} %get-tuple-element.72.refs_0_), channel_id=1, source_target_pairs={{0,16},{4,20},{8,24},{12,28},{16,0},{20,4},{24,8},{28,12},{1,17},{... | collective-permute-start | bytes 552968 | tf_op jit(solution)/shard_map/ppermute | solution.py:510
  146.8 1.8 %collective-permute-start.32 = (bf16[80,1152]{1,0:T(8,128)(2,1)S(1)}, bf16[80,1152]{1,0:T(8,128)(2,1)S(1)}, u32[]{:S(2)}, u32[]{:S(2)}) collective-permute-start(bf16[80,1152]{1,0:T(8,128)(2,1)S(1)} %get-tuple-element.72.refs_0_), channel_id=1, source_target_pairs={{0,24},{4,28},{8,0},{12,4},{16,8},{20,12},{24,16},{28,20},{1,25},{... | collective-permute-start | bytes 552968 | tf_op jit(solution)/shard_map/ppermute | solution.py:510
  151.2 1.5 collective-permute-start.36
  152.7 3.9 %shard_map.242 = (f32[80,768]{1,0:T(8,128)S(1)}, bf16[3,1152,768]{2,1,0:T(8,128)(2,1)S(1)}) custom-call(s32[3]{0:T(128)S(1)} %copy-done.10, bf16[80,1152]{1,0:T(8,128)(2,1)S(1)} %get-tuple-element.72.refs_0_, bf16[1,9216,768]{2,1,0:T(8,128)(2,1)} %refs_5_.4), custom_call_target="tpu_custom_call" | custom-call | flops 141557760 | bytes 19894272 | tf_op jit(solution)/shard_map/pallas_call | solution.py:47
  156.6 2.4 %copy-done.1 = bf16[3,1152,768]{2,1,0:T(8,128)(2,1)} copy-done((bf16[3,1152,768]{2,1,0:T(8,128)(2,1)}, bf16[3,1152,768]{2,1,0:T(8,128)(2,1)S(1)}, u32[]{:S(2)}) %copy-start.1) | copy-done | bytes 5308440
  164.6 4.7 %shard_map.243.refs_3_ = f32[80,768]{1,0:T(8,128)S(1)} custom-call(s32[3]{0:T(128)S(1)} %copy-done.10, bf16[80,1152]{1,0:T(8,128)(2,1)S(1)} %collective-permute-done.36.refs_0_, bf16[80,1152]{1,0:T(8,128)(2,1)S(1)} %collective-permute-done.30.refs_1_, bf16[80,1152]{1,0:T(8,128)(2,1)S(1)} %collective-permute-done.32.refs_2_, ...), custom_call_target="tpu_custom_call" | custom-call | flops 566231040 | bytes 15384576 | tf_op jit(solution)/shard_map/pallas_call | solution.py:47
  169.3 2.5 %collective-permute-done.33.refs_1_ = bf16[80,1152]{1,0:T(8,128)(2,1)S(1)} collective-permute-done((bf16[80,1152]{1,0:T(8,128)(2,1)S(1)}, bf16[80,1152]{1,0:T(8,128)(2,1)S(1)}, u32[]{:S(2)}, u32[]{:S(2)}) %collective-permute-start.33) | collective-permute-done | bytes 184352 | tf_op jit(solution)/shard_map/ppermute | solution.py:514
  171.8 2.0 %collective-permute-done.35.refs_2_ = bf16[80,1152]{1,0:T(8,128)(2,1)S(1)} collective-permute-done((bf16[80,1152]{1,0:T(8,128)(2,1)S(1)}, bf16[80,1152]{1,0:T(8,128)(2,1)S(1)}, u32[]{:S(2)}, u32[]{:S(2)}) %collective-permute-start.35) | collective-permute-done | bytes 184352 | tf_op jit(solution)/shard_map/ppermute | solution.py:514
  173.9 1.8 shard_map.244
  175.8 1.5 collective-permute-start.38
  177.7 2.3 %collective-permute-done.38.refs_2_ = bf16[32,768]{1,0:T(8,128)(2,1)S(1)} collective-permute-done((bf16[32,768]{1,0:T(8,128)(2,1)S(1)}, bf16[32,768]{1,0:T(8,128)(2,1)S(1)}, u32[]{:S(2)}, u32[]{:S(2)}) %collective-permute-start.38) | collective-permute-done | bytes 49184 | tf_op jit(solution)/shard_map/ppermute | solution.py:517
  180.9 2.0 %shard_map.245 = bf16[256,768]{1,0:T(8,128)(2,1)} custom-call(s32[3]{0:T(128)S(1)} %copy-done.10, bf16[32,768]{1,0:T(8,128)(2,1)S(1)} %get-tuple-element.79.refs_0_, bf16[32,768]{1,0:T(8,128)(2,1)S(1)} %collective-permute-done.37.refs_1_, bf16[32,768]{1,0:T(8,128)(2,1)S(1)} %collective-permute-done.38.refs_2_, ...), custom_call_target="tpu_custom_call" | custom-call | bytes 1778688 | tf_op jit(solution)/shard_map/pallas_call | solution.py:47
  (112 shorter events, 27.2 us)
Async XLA Ops:
  0.7 41.2 %copy-start.5 = (bf16[128,2048]{1,0:T(8,128)(2,1)S(1)}, bf16[128,2048]{1,0:T(8,128)(2,1)}, u32[]{:S(2)}) copy-start(bf16[128,2048]{1,0:T(8,128)(2,1)} %refs_3_.1) | copy-start | bytes 1572868
  0.7 41.2 %copy-start.4 = (bf16[128,2048]{1,0:T(8,128)(2,1)S(1)}, bf16[128,2048]{1,0:T(8,128)(2,1)}, u32[]{:S(2)}) copy-start(bf16[128,2048]{1,0:T(8,128)(2,1)} %refs_2_.2) | copy-start | bytes 1572868
  4.0 15.3 %collective-permute-start = (bf16[2,128,1024]{2,1,0:T(8,128)(2,1)}, bf16[2,128,1024]{2,1,0:T(8,128)(2,1)S(1)}, u32[]{:S(2)}, u32[]{:S(2)}) collective-permute-start(bf16[2,128,1024]{2,1,0:T(8,128)(2,1)} %shard_map.230), channel_id=1, source_target_pairs={{0,4},{4,0},{8,12},{12,8},{16,20},{20,16},{24,28},{28,24},{1,5},{5... | collective-permute-start | bytes 1572872 | tf_op jit(solution)/shard_map/ppermute | solution.py:514
  7.0 12.3 %collective-permute-start.1 = (f32[16,128]{1,0:T(8,128)}, f32[16,128]{1,0:T(8,128)S(1)}, u32[]{:S(2)}, u32[]{:S(2)}) collective-permute-start(f32[16,128]{1,0:T(8,128)} %bitcast.14), channel_id=1, source_target_pairs={{0,4},{4,0},{8,12},{12,8},{16,20},{20,16},{24,28},{28,24},{1,5},{5... | collective-permute-start | bytes 24584 | tf_op jit(solution)/shard_map/ppermute | solution.py:514
  7.0 5.3 %collective-permute-start.4 = (s32[2,256]{1,0:T(2,128)}, s32[2,256]{1,0:T(2,128)S(1)}, u32[]{:S(2)}, u32[]{:S(2)}) collective-permute-start(s32[2,256]{1,0:T(2,128)} %bitcast.17), channel_id=1, source_target_pairs={{0,3},{1,2},{2,1},{3,0},{4,7},{5,6},{6,5},{7,4},{8,11},{9,10},{10,... | collective-permute-start | bytes 6152 | tf_op jit(solution)/shard_map/ppermute | solution.py:517
  7.9 4.5 %collective-permute-start.3 = (s32[2,256]{1,0:T(2,128)}, s32[2,256]{1,0:T(2,128)S(1)}, u32[]{:S(2)}, u32[]{:S(2)}) collective-permute-start(s32[2,256]{1,0:T(2,128)} %bitcast.18), channel_id=1, source_target_pairs={{0,2},{1,3},{2,0},{3,1},{4,6},{5,7},{6,4},{7,5},{8,10},{9,11},{10,... | collective-permute-start | bytes 6152 | tf_op jit(solution)/shard_map/ppermute | solution.py:517
  9.0 3.3 %collective-permute-start.2 = (s32[2,256]{1,0:T(2,128)}, s32[2,256]{1,0:T(2,128)S(1)}, u32[]{:S(2)}, u32[]{:S(2)}) collective-permute-start(s32[2,256]{1,0:T(2,128)} %bitcast.19), channel_id=1, source_target_pairs={{0,1},{1,0},{2,3},{3,2},{4,5},{5,4},{6,7},{7,6},{8,9},{9,8},{10,11... | collective-permute-start | bytes 6152 | tf_op jit(solution)/shard_map/ppermute | solution.py:517
  19.3 22.5 %collective-permute-start.5 = (bf16[2,128,1024]{2,1,0:T(8,128)(2,1)}, bf16[2,128,1024]{2,1,0:T(8,128)(2,1)S(1)}, u32[]{:S(2)}, u32[]{:S(2)}) collective-permute-start(bf16[2,128,1024]{2,1,0:T(8,128)(2,1)} %shard_map.231), channel_id=1, source_target_pairs={{0,4},{4,0},{8,12},{12,8},{16,20},{20,16},{24,28},{28,24},{1,5},{5... | collective-permute-start | bytes 1572872 | tf_op jit(solution)/shard_map/ppermute | solution.py:514
  24.1 6.8 %collective-permute-start.6 = (bf16[272,128]{1,0:T(8,128)(2,1)S(1)}, bf16[272,128]{1,0:T(8,128)(2,1)S(1)}, u32[]{:S(2)}, u32[]{:S(2)}) collective-permute-start(bf16[272,128]{1,0:T(8,128)(2,1)S(1)} %get-tuple-element.49), channel_id=1, source_target_pairs={{0,8},{4,12},{8,16},{12,20},{16,24},{20,28},{24,0},{28,4},{1,9},{5... | collective-permute-start | bytes 208904 | tf_op jit(solution)/shard_map/ppermute | solution.py:510
  25.7 6.9 %collective-permute-start.7 = (bf16[272,128]{1,0:T(8,128)(2,1)S(1)}, bf16[272,128]{1,0:T(8,128)(2,1)S(1)}, u32[]{:S(2)}, u32[]{:S(2)}) collective-permute-start(bf16[272,128]{1,0:T(8,128)(2,1)S(1)} %get-tuple-element.50), channel_id=1, source_target_pairs={{0,16},{4,20},{8,24},{12,28},{16,0},{20,4},{24,8},{28,12},{1,17},{... | collective-permute-start | bytes 208904 | tf_op jit(solution)/shard_map/ppermute | solution.py:510
  28.3 4.8 %collective-permute-start.8 = (bf16[272,128]{1,0:T(8,128)(2,1)S(1)}, bf16[272,128]{1,0:T(8,128)(2,1)S(1)}, u32[]{:S(2)}, u32[]{:S(2)}) collective-permute-start(bf16[272,128]{1,0:T(8,128)(2,1)S(1)} %get-tuple-element.51), channel_id=1, source_target_pairs={{0,24},{4,28},{8,0},{12,4},{16,8},{20,12},{24,16},{28,20},{1,25},{... | collective-permute-start | bytes 208904 | tf_op jit(solution)/shard_map/ppermute | solution.py:510
  33.1 61.8 %copy-start = (bf16[2048,768]{1,0:T(8,128)(2,1)S(1)}, bf16[2048,768]{1,0:T(8,128)(2,1)}, u32[]{:S(2)}) copy-start(bf16[2048,768]{1,0:T(8,128)(2,1)} %refs_5_.3) | copy-start | bytes 9437188
  33.1 61.8 %copy-start.8 = (s32[320,1]{1,0:T(8,128)S(1)}, s32[320,1]{1,0:T(8,128)}, u32[]{:S(2)}) copy-start(s32[320,1]{1,0:T(8,128)} %constant.74.clone.refs_9_.refs_7_) | copy-start | bytes 3844
  33.1 61.8 %copy-start.9 = (s32[320,1]{1,0:T(8,128)S(1)}, s32[320,1]{1,0:T(8,128)}, u32[]{:S(2)}) copy-start(s32[320,1]{1,0:T(8,128)} %constant.73.clone.refs_8_.refs_6_) | copy-start | bytes 3844
  33.9 6.2 %collective-permute-start.9 = (bf16[256,128]{1,0:T(8,128)(2,1)S(1)}, bf16[256,128]{1,0:T(8,128)(2,1)S(1)}, u32[]{:S(2)}, u32[]{:S(2)}) collective-permute-start(bf16[256,128]{1,0:T(8,128)(2,1)S(1)} %get-tuple-element.53), channel_id=1, source_target_pairs={{0,8},{4,12},{8,16},{12,20},{16,24},{20,28},{24,0},{28,4},{1,9},{5... | collective-permute-start | bytes 196616 | tf_op jit(solution)/shard_map/ppermute | solution.py:510
  34.6 6.7 %collective-permute-start.10 = (bf16[256,128]{1,0:T(8,128)(2,1)S(1)}, bf16[256,128]{1,0:T(8,128)(2,1)S(1)}, u32[]{:S(2)}, u32[]{:S(2)}) collective-permute-start(bf16[256,128]{1,0:T(8,128)(2,1)S(1)} %get-tuple-element.54), channel_id=1, source_target_pairs={{0,16},{4,20},{8,24},{12,28},{16,0},{20,4},{24,8},{28,12},{1,17},{... | collective-permute-start | bytes 196616 | tf_op jit(solution)/shard_map/ppermute | solution.py:510
  37.2 4.7 %collective-permute-start.11 = (bf16[256,128]{1,0:T(8,128)(2,1)S(1)}, bf16[256,128]{1,0:T(8,128)(2,1)S(1)}, u32[]{:S(2)}, u32[]{:S(2)}) collective-permute-start(bf16[256,128]{1,0:T(8,128)(2,1)S(1)} %get-tuple-element.55), channel_id=1, source_target_pairs={{0,24},{4,28},{8,0},{12,4},{16,8},{20,12},{24,16},{28,20},{1,25},{... | collective-permute-start | bytes 196616 | tf_op jit(solution)/shard_map/ppermute | solution.py:510
  45.3 16.7 %collective-permute-start.12 = (bf16[256,1024]{1,0:T(8,128)(2,1)S(1)}, bf16[256,1024]{1,0:T(8,128)(2,1)S(1)}, u32[]{:S(2)}, u32[]{:S(2)}) collective-permute-start(bf16[256,1024]{1,0:T(8,128)(2,1)S(1)} %shard_map.235.refs_0_), channel_id=1, source_target_pairs={{0,8},{4,12},{8,16},{12,20},{16,24},{20,28},{24,0},{28,4},{1,9},{5... | collective-permute-start | bytes 1572872 | tf_op jit(solution)/shard_map/ppermute | solution.py:510
  46.1 21.6 %collective-permute-start.17 = (bf16[256,1024]{1,0:T(8,128)(2,1)S(1)}, bf16[256,1024]{1,0:T(8,128)(2,1)S(1)}, u32[]{:S(2)}, u32[]{:S(2)}) collective-permute-start(bf16[256,1024]{1,0:T(8,128)(2,1)S(1)} %shard_map.235.refs_0_), channel_id=1, source_target_pairs={{0,24},{4,28},{8,0},{12,4},{16,8},{20,12},{24,16},{28,20},{1,25},{... | collective-permute-start | bytes 1572872 | tf_op jit(solution)/shard_map/ppermute | solution.py:510
  49.2 45.7 %collective-permute-start.18 = (bf16[256,1024]{1,0:T(8,128)(2,1)S(1)}, bf16[256,1024]{1,0:T(8,128)(2,1)S(1)}, u32[]{:S(2)}, u32[]{:S(2)}) collective-permute-start(bf16[256,1024]{1,0:T(8,128)(2,1)S(1)} %shard_map.235.refs_0_), channel_id=1, source_target_pairs={{0,4},{4,0},{8,12},{12,8},{16,20},{20,16},{24,28},{28,24},{1,5},{5... | collective-permute-start | bytes 1572872 | tf_op jit(solution)/shard_map/ppermute | solution.py:514
  62.0 32.9 %collective-permute-start.19 = (bf16[256,1024]{1,0:T(8,128)(2,1)S(1)}, bf16[256,1024]{1,0:T(8,128)(2,1)S(1)}, u32[]{:S(2)}, u32[]{:S(2)}) collective-permute-start(bf16[256,1024]{1,0:T(8,128)(2,1)S(1)} %collective-permute-done.12.refs_1_), channel_id=1, source_target_pairs={{0,4},{4,0},{8,12},{12,8},{16,20},{20,16},{24,28},{28,24},{1,5},{5... | collective-permute-start | bytes 1572872 | tf_op jit(solution)/shard_map/ppermute | solution.py:514
  67.7 27.2 %collective-permute-start.20 = (bf16[256,1024]{1,0:T(8,128)(2,1)S(1)}, bf16[256,1024]{1,0:T(8,128)(2,1)S(1)}, u32[]{:S(2)}, u32[]{:S(2)}) collective-permute-start(bf16[256,1024]{1,0:T(8,128)(2,1)S(1)} %collective-permute-done.17.refs_2_), channel_id=1, source_target_pairs={{0,4},{4,0},{8,12},{12,8},{16,20},{20,16},{24,28},{28,24},{1,5},{5... | collective-permute-start | bytes 1572872 | tf_op jit(solution)/shard_map/ppermute | solution.py:514
  68.2 21.0 %collective-permute-start.14 = (bf16[128,1024]{1,0:T(8,128)(2,1)S(1)}, bf16[128,1024]{1,0:T(8,128)(2,1)S(1)}, u32[]{:S(2)}, u32[]{:S(2)}) collective-permute-start(bf16[128,1024]{1,0:T(8,128)(2,1)S(1)} %get-tuple-element.92), channel_id=1, source_target_pairs={{0,16},{4,20},{8,24},{12,28},{16,0},{20,4},{24,8},{28,12},{1,17},{... | collective-permute-start | bytes 786440 | tf_op jit(solution)/shard_map/ppermute | solution.py:510
  69.6 23.5 %collective-permute-start.13 = (bf16[128,1024]{1,0:T(8,128)(2,1)S(1)}, bf16[128,1024]{1,0:T(8,128)(2,1)S(1)}, u32[]{:S(2)}, u32[]{:S(2)}) collective-permute-start(bf16[128,1024]{1,0:T(8,128)(2,1)S(1)} %get-tuple-element.93), channel_id=1, source_target_pairs={{0,16},{4,20},{8,24},{12,28},{16,0},{20,4},{24,8},{28,12},{1,17},{... | collective-permute-start | bytes 786440 | tf_op jit(solution)/shard_map/ppermute | solution.py:510
  89.2 9.8 %collective-permute-start.16 = (bf16[128,1024]{1,0:T(8,128)(2,1)S(1)}, bf16[128,1024]{1,0:T(8,128)(2,1)S(1)}, u32[]{:S(2)}, u32[]{:S(2)}) collective-permute-start(bf16[128,1024]{1,0:T(8,128)(2,1)S(1)} %collective-permute-done.14.refs_1_), channel_id=1, source_target_pairs={{0,4},{4,0},{8,12},{12,8},{16,20},{20,16},{24,28},{28,24},{1,5},{5... | collective-permute-start | bytes 786440 | tf_op jit(solution)/shard_map/ppermute | solution.py:514
  93.2 8.0 %collective-permute-start.15 = (bf16[128,1024]{1,0:T(8,128)(2,1)S(1)}, bf16[128,1024]{1,0:T(8,128)(2,1)S(1)}, u32[]{:S(2)}, u32[]{:S(2)}) collective-permute-start(bf16[128,1024]{1,0:T(8,128)(2,1)S(1)} %collective-permute-done.13.refs_0_), channel_id=1, source_target_pairs={{0,4},{4,0},{8,12},{12,8},{16,20},{20,16},{24,28},{28,24},{1,5},{5... | collective-permute-start | bytes 786440 | tf_op jit(solution)/shard_map/ppermute | solution.py:514
  104.3 1.6 collective-permute-start.21
  105.9 5.4 %collective-permute-start.22 = (bf16[80,768]{1,0:T(8,128)(2,1)S(1)}, bf16[80,768]{1,0:T(8,128)(2,1)S(1)}, u32[]{:S(2)}, u32[]{:S(2)}) collective-permute-start(bf16[80,768]{1,0:T(8,128)(2,1)S(1)} %get-tuple-element.90), channel_id=1, source_target_pairs={{0,2},{1,3},{2,0},{3,1},{4,6},{5,7},{6,4},{7,5},{8,10},{9,11},{10,... | collective-permute-start | bytes 368648 | tf_op jit(solution)/shard_map/ppermute | solution.py:517
  112.3 36.5 %collective-permute-start.40 = (bf16[2,256,768]{2,1,0:T(8,128)(2,1)S(1)}, bf16[2,256,768]{2,1,0:T(8,128)(2,1)S(1)}, u32[]{:S(2)}, u32[]{:S(2)}) collective-permute-start(bf16[2,256,768]{2,1,0:T(8,128)(2,1)S(1)} %get-tuple-element.85), channel_id=1, source_target_pairs={{0,1},{1,0},{2,3},{3,2},{4,5},{5,4},{6,7},{7,6},{8,9},{9,8},{10,11... | collective-permute-start | bytes 2359304 | tf_op jit(solution)/shard_map/ppermute | solution.py:517
  112.4 9.7 %collective-permute-start.27 = (bf16[80,896]{1,0:T(8,128)(2,1)S(1)}, bf16[80,896]{1,0:T(8,128)(2,1)S(1)}, u32[]{:S(2)}, u32[]{:S(2)}) collective-permute-start(bf16[80,896]{1,0:T(8,128)(2,1)S(1)} %shard_map.238.refs_0_), channel_id=1, source_target_pairs={{0,16},{4,20},{8,24},{12,28},{16,0},{20,4},{24,8},{28,12},{1,17},{... | collective-permute-start | bytes 430088 | tf_op jit(solution)/shard_map/ppermute | solution.py:510
  112.4 12.6 %collective-permute-start.25 = (bf16[80,896]{1,0:T(8,128)(2,1)S(1)}, bf16[80,896]{1,0:T(8,128)(2,1)S(1)}, u32[]{:S(2)}, u32[]{:S(2)}) collective-permute-start(bf16[80,896]{1,0:T(8,128)(2,1)S(1)} %shard_map.238.refs_0_), channel_id=1, source_target_pairs={{0,24},{4,28},{8,0},{12,4},{16,8},{20,12},{24,16},{28,20},{1,25},{... | collective-permute-start | bytes 430088 | tf_op jit(solution)/shard_map/ppermute | solution.py:510
  114.3 10.7 %collective-permute-start.23 = (bf16[80,896]{1,0:T(8,128)(2,1)S(1)}, bf16[80,896]{1,0:T(8,128)(2,1)S(1)}, u32[]{:S(2)}, u32[]{:S(2)}) collective-permute-start(bf16[80,896]{1,0:T(8,128)(2,1)S(1)} %shard_map.238.refs_0_), channel_id=1, source_target_pairs={{0,8},{4,12},{8,16},{12,20},{16,24},{20,28},{24,0},{28,4},{1,9},{5... | collective-permute-start | bytes 430088 | tf_op jit(solution)/shard_map/ppermute | solution.py:510
  114.8 13.7 %collective-permute-start.29 = (bf16[80,896]{1,0:T(8,128)(2,1)S(1)}, bf16[80,896]{1,0:T(8,128)(2,1)S(1)}, u32[]{:S(2)}, u32[]{:S(2)}) collective-permute-start(bf16[80,896]{1,0:T(8,128)(2,1)S(1)} %shard_map.238.refs_0_), channel_id=1, source_target_pairs={{0,4},{4,0},{8,12},{12,8},{16,20},{20,16},{24,28},{28,24},{1,5},{5... | collective-permute-start | bytes 430088 | tf_op jit(solution)/shard_map/ppermute | solution.py:514
  125.1 10.5 %collective-permute-start.24 = (bf16[80,896]{1,0:T(8,128)(2,1)S(1)}, bf16[80,896]{1,0:T(8,128)(2,1)S(1)}, u32[]{:S(2)}, u32[]{:S(2)}) collective-permute-start(bf16[80,896]{1,0:T(8,128)(2,1)S(1)} %collective-permute-done.23.refs_1_), channel_id=1, source_target_pairs={{0,4},{4,0},{8,12},{12,8},{16,20},{20,16},{24,28},{28,24},{1,5},{5... | collective-permute-start | bytes 430088 | tf_op jit(solution)/shard_map/ppermute | solution.py:514
  126.5 9.1 %collective-permute-start.26 = (bf16[80,896]{1,0:T(8,128)(2,1)S(1)}, bf16[80,896]{1,0:T(8,128)(2,1)S(1)}, u32[]{:S(2)}, u32[]{:S(2)}) collective-permute-start(bf16[80,896]{1,0:T(8,128)(2,1)S(1)} %collective-permute-done.25.refs_2_), channel_id=1, source_target_pairs={{0,4},{4,0},{8,12},{12,8},{16,20},{20,16},{24,28},{28,24},{1,5},{5... | collective-permute-start | bytes 430088 | tf_op jit(solution)/shard_map/ppermute | solution.py:514
  127.1 9.4 %collective-permute-start.28 = (bf16[80,896]{1,0:T(8,128)(2,1)S(1)}, bf16[80,896]{1,0:T(8,128)(2,1)S(1)}, u32[]{:S(2)}, u32[]{:S(2)}) collective-permute-start(bf16[80,896]{1,0:T(8,128)(2,1)S(1)} %collective-permute-done.27.refs_3_), channel_id=1, source_target_pairs={{0,4},{4,0},{8,12},{12,8},{16,20},{20,16},{24,28},{28,24},{1,5},{5... | collective-permute-start | bytes 430088 | tf_op jit(solution)/shard_map/ppermute | solution.py:514
  142.4 16.6 %collective-permute-start.34 = (bf16[80,1152]{1,0:T(8,128)(2,1)S(1)}, bf16[80,1152]{1,0:T(8,128)(2,1)S(1)}, u32[]{:S(2)}, u32[]{:S(2)}) collective-permute-start(bf16[80,1152]{1,0:T(8,128)(2,1)S(1)} %get-tuple-element.72.refs_0_), channel_id=1, source_target_pairs={{0,16},{4,20},{8,24},{12,28},{16,0},{20,4},{24,8},{28,12},{1,17},{... | collective-permute-start | bytes 552968 | tf_op jit(solution)/shard_map/ppermute | solution.py:510
  146.8 12.2 %collective-permute-start.32 = (bf16[80,1152]{1,0:T(8,128)(2,1)S(1)}, bf16[80,1152]{1,0:T(8,128)(2,1)S(1)}, u32[]{:S(2)}, u32[]{:S(2)}) collective-permute-start(bf16[80,1152]{1,0:T(8,128)(2,1)S(1)} %get-tuple-element.72.refs_0_), channel_id=1, source_target_pairs={{0,24},{4,28},{8,0},{12,4},{16,8},{20,12},{24,16},{28,20},{1,25},{... | collective-permute-start | bytes 552968 | tf_op jit(solution)/shard_map/ppermute | solution.py:510
  148.6 11.7 %collective-permute-start.30 = (bf16[80,1152]{1,0:T(8,128)(2,1)S(1)}, bf16[80,1152]{1,0:T(8,128)(2,1)S(1)}, u32[]{:S(2)}, u32[]{:S(2)}) collective-permute-start(bf16[80,1152]{1,0:T(8,128)(2,1)S(1)} %get-tuple-element.72.refs_0_), channel_id=1, source_target_pairs={{0,8},{4,12},{8,16},{12,20},{16,24},{20,28},{24,0},{28,4},{1,9},{5... | collective-permute-start | bytes 552968 | tf_op jit(solution)/shard_map/ppermute | solution.py:510
  149.8 31.1 %collective-permute-start.41 = (bf16[1,256,768]{2,1,0:T(8,128)(2,1)}, bf16[1,256,768]{2,1,0:T(8,128)(2,1)S(1)}, u32[]{:S(2)}, u32[]{:S(2)}) collective-permute-start(bf16[1,256,768]{2,1,0:T(8,128)(2,1)} %get-tuple-element.88), channel_id=1, source_target_pairs={{0,2},{1,3},{2,0},{3,1},{4,6},{5,7},{6,4},{7,5},{8,10},{9,11},{10,... | collective-permute-start | bytes 1179656 | tf_op jit(solution)/shard_map/ppermute | solution.py:517
  151.2 12.6 %collective-permute-start.36 = (bf16[80,1152]{1,0:T(8,128)(2,1)S(1)}, bf16[80,1152]{1,0:T(8,128)(2,1)S(1)}, u32[]{:S(2)}, u32[]{:S(2)}) collective-permute-start(bf16[80,1152]{1,0:T(8,128)(2,1)S(1)} %get-tuple-element.72.refs_0_), channel_id=1, source_target_pairs={{0,4},{4,0},{8,12},{12,8},{16,20},{20,16},{24,28},{28,24},{1,5},{5... | collective-permute-start | bytes 552968 | tf_op jit(solution)/shard_map/ppermute | solution.py:514
  160.4 8.9 %collective-permute-start.31 = (bf16[80,1152]{1,0:T(8,128)(2,1)S(1)}, bf16[80,1152]{1,0:T(8,128)(2,1)S(1)}, u32[]{:S(2)}, u32[]{:S(2)}) collective-permute-start(bf16[80,1152]{1,0:T(8,128)(2,1)S(1)} %collective-permute-done.30.refs_1_), channel_id=1, source_target_pairs={{0,4},{4,0},{8,12},{12,8},{16,20},{20,16},{24,28},{28,24},{1,5},{5... | collective-permute-start | bytes 552968 | tf_op jit(solution)/shard_map/ppermute | solution.py:514
  161.8 10.1 %collective-permute-start.33 = (bf16[80,1152]{1,0:T(8,128)(2,1)S(1)}, bf16[80,1152]{1,0:T(8,128)(2,1)S(1)}, u32[]{:S(2)}, u32[]{:S(2)}) collective-permute-start(bf16[80,1152]{1,0:T(8,128)(2,1)S(1)} %collective-permute-done.32.refs_2_), channel_id=1, source_target_pairs={{0,4},{4,0},{8,12},{12,8},{16,20},{20,16},{24,28},{28,24},{1,5},{5... | collective-permute-start | bytes 552968 | tf_op jit(solution)/shard_map/ppermute | solution.py:514
  162.4 11.4 %collective-permute-start.35 = (bf16[80,1152]{1,0:T(8,128)(2,1)S(1)}, bf16[80,1152]{1,0:T(8,128)(2,1)S(1)}, u32[]{:S(2)}, u32[]{:S(2)}) collective-permute-start(bf16[80,1152]{1,0:T(8,128)(2,1)S(1)} %collective-permute-done.34.refs_3_), channel_id=1, source_target_pairs={{0,4},{4,0},{8,12},{12,8},{16,20},{20,16},{24,28},{28,24},{1,5},{5... | collective-permute-start | bytes 552968 | tf_op jit(solution)/shard_map/ppermute | solution.py:514
  163.9 13.7 %collective-permute-start.42 = (f32[8,16,128]{2,1,0:T(8,128)S(1)}, f32[8,16,128]{2,1,0:T(8,128)S(1)}, u32[]{:S(2)}, u32[]{:S(2)}) collective-permute-start(f32[8,16,128]{2,1,0:T(8,128)S(1)} %get-tuple-element.94), channel_id=1, source_target_pairs={{0,4},{4,0},{8,12},{12,8},{16,20},{20,16},{24,28},{28,24},{1,5},{5... | collective-permute-start | bytes 196616 | tf_op jit(solution)/shard_map/ppermute | solution.py:514
  175.7 2.0 %collective-permute-start.37 = (bf16[32,768]{1,0:T(8,128)(2,1)S(1)}, bf16[32,768]{1,0:T(8,128)(2,1)S(1)}, u32[]{:S(2)}, u32[]{:S(2)}) collective-permute-start(bf16[32,768]{1,0:T(8,128)(2,1)S(1)} %get-tuple-element.80), channel_id=1, source_target_pairs={{0,1},{1,0},{2,3},{3,2},{4,5},{5,4},{6,7},{7,6},{8,9},{9,8},{10,11... | collective-permute-start | bytes 147464 | tf_op jit(solution)/shard_map/ppermute | solution.py:517
  175.8 4.2 %collective-permute-start.38 = (bf16[32,768]{1,0:T(8,128)(2,1)S(1)}, bf16[32,768]{1,0:T(8,128)(2,1)S(1)}, u32[]{:S(2)}, u32[]{:S(2)}) collective-permute-start(bf16[32,768]{1,0:T(8,128)(2,1)S(1)} %get-tuple-element.81), channel_id=1, source_target_pairs={{0,2},{1,3},{2,0},{3,1},{4,6},{5,7},{6,4},{7,5},{8,10},{9,11},{10,... | collective-permute-start | bytes 147464 | tf_op jit(solution)/shard_map/ppermute | solution.py:517
  177.2 3.7 %collective-permute-start.39 = (bf16[32,768]{1,0:T(8,128)(2,1)S(1)}, bf16[32,768]{1,0:T(8,128)(2,1)S(1)}, u32[]{:S(2)}, u32[]{:S(2)}) collective-permute-start(bf16[32,768]{1,0:T(8,128)(2,1)S(1)} %get-tuple-element.82), channel_id=1, source_target_pairs={{0,3},{1,2},{2,1},{3,0},{4,7},{5,6},{6,5},{7,4},{8,11},{9,10},{10,... | collective-permute-start | bytes 147464 | tf_op jit(solution)/shard_map/ppermute | solution.py:517
  (19 other events, 284.2 us)

commit v5 on v4

--- a/solution.py
+++ b/solution.py
@@ -99,8 +99,12 @@
 def routing_kernel(nz, cap, own_rows, s, *refs):
     keep = refs[0]
     given = refs[1 : nz + 1]
-    base, codes, sign, ids = refs[nz + 1 :]
+    base, state, codes, sign, start, ids, sem = refs[nz + 1 :]
     j = s[2]
+    heads, share, _ = start.shape
+    rows = pl.ds(pl.multiple_of(s[0] * share, share), share)
+    fetch = pltpu.make_async_copy(state.at[pl.ds(s[1] * heads, heads), rows, :], start, sem)
+    fetch.start()
     block = given[0].shape[1]
     for r in range(nz):
         ids[lax.bitwise_xor(j, r)] = given[r][...]
@@ -130,11 +134,15 @@
         other = other + jnp.sum(jnp.where(holds, first + second, 0), axis=1, keepdims=True)
     every = lax.broadcasted_iota(I32, sign.shape, 1)
     sign[...] = (every == j).astype(F32) - (every == other - j).astype(F32)
-
-
-def pack_kernel(s, a, b, out):
-    out[0] = a[...]
-    out[1] = b[...]
+    fetch.wait()
+
+
+def pack_kernel(away, ny, a, b, out, sem):
+    width = out.shape[2]
+    share = lax.rem(lax.rem(lax.axis_index("seq"), ny) + away, ny)
+    at = pl.ds(pl.multiple_of(share * width, 128), width)
+    for c in run_copies([(a.at[:, at], out.at[0]), (b.at[:, at], out.at[1])], sem):
+        c.wait()
 
 
 def update_kernel(nz, ny, heads, hd, s, *refs):
@@ -188,19 +196,15 @@
 
 
 def prefix_kernel(nz, heads, hd, s, *refs):
-    z, y = s[0], s[1]
+    z = s[0]
     parts = refs[:nz]
     start = refs[nz]
     outs = refs[nz + 1 : 2 * nz + 1]
-    final, held, entering, run, sem = refs[2 * nz + 1 :]
+    final, held, entering, run = refs[2 * nz + 1 :]
     share = hd // nz
-    source = start.at[
-        pl.ds(y * heads, heads), pl.ds(pl.multiple_of(z * share, share), share), :
-    ]
-    copies = run_copies([(source, run)], sem)
+    run[...] = start[...]
     for d in range(nz):
         held[lax.rem(z + nz - d, nz)] = parts[d][...]
-    copies[0].wait()
     for p in range(nz):
         logs = jnp.sum(held[p, heads * share :, :].astype(F32), axis=1, keepdims=True)
         keep = jnp.exp(logs)
@@ -534,7 +538,9 @@
 
     def gather_y(held, events):
         for d in z_order:
-            x = held[d, 0] = behind([held[d, 0]], events)[0]
+            x = held[d, 0]
+            if d == z_order[-1]:
+                x = held[d, 0] = behind([x], events)[0]
             for e in range(1, ny):
                 held[d, e] = y_turn(x, e)
 
@@ -562,25 +568,31 @@
     logs_t = jnp.transpose(log_decay)
     logs, kvs, qgs = [logs_t], [], []
     for d in range(1, ny):
-        there = pl.BlockSpec((tok, width), lambda n, s, d=d: (0, lax.rem(s[1] + d, ny)))
-        out = [sds((2, tok, width), BF16)]
-        (kv,) = call(pack_kernel, place, [(key_in, there), (value_in, there)], out, limit=60)
-        kvs.append(y_turn(kv, d))
+        pack = pl.pallas_call(
+            functools.partial(pack_kernel, d, ny),
+            out_shape=sds((2, tok, width), BF16),
+            in_specs=[pl.BlockSpec(memory_space=pltpu.HBM)] * 2,
+            out_specs=pl.BlockSpec(memory_space=pltpu.VMEM),
+            scratch_shapes=[pltpu.SemaphoreType.DMA((2,))],
+            compiler_params=pltpu.CompilerParams(vmem_limit_bytes=60 * 1024 * 1024),
+        )
+        kvs.append(y_turn(pack(key_in, value_in), d))
         logs.append(y_turn(logs_t, d))
-        qgs += call(pack_kernel, place, [(query, there), (gate_in, there)], out, limit=60)
+        qgs.append(pack(query, gate_in))
     ids = jnp.transpose(expert_ids)
-    codes, sign = call(
+    share = hd // nz
+    codes, sign, start = call(
         functools.partial(routing_kernel, nz, cap, slots),
         place,
         [(keep_counts, pl.BlockSpec(memory_space=pltpu.SMEM))]
         + [ids]
         + [swap(ids, r) for r in range(1, nz)]
-        + [own_base],
-        [sds((nz, 2, block), I32), sds((slots, experts), F32)],
-        [pltpu.VMEM((nz, 2, block), I32)],
+        + [own_base, hbm(state_in)],
+        [sds((nz, 2, block), I32), sds((slots, experts), F32), sds((heads, share, hd), F32)],
+        [pltpu.VMEM((nz, 2, block), I32), pltpu.SemaphoreType.DMA],
     )
     attn_gain_2, moe_gain_2, router_t = attn_gain[None], moe_gain[None], jnp.transpose(router)
-    prepared = [codes, sign, attn_gain_2, moe_gain_2]
+    prepared = [codes, sign, start, attn_gain_2, moe_gain_2]
     qgs = [y_turn(qg, d + 1) for d, qg in enumerate(behind(qgs, kvs + logs + prepared))]
     share = hd // nz
     long = tok * ny
@@ -604,13 +616,12 @@
     *entering, last_rows = call(
         functools.partial(prefix_kernel, nz, heads, hd),
         place,
-        [*parts, hbm(state_in)],
+        [*parts, start],
         [sds((heads * share, hd), BF16)] * nz + [sds((heads, share, hd), F32)],
         [
             pltpu.VMEM((nz, heads * share + 16, hd), BF16),
             pltpu.VMEM((nz, heads * share, hd), BF16),
             pltpu.VMEM((heads, share, hd), F32),
-            pltpu.SemaphoreType.DMA((1,)),
         ],
     )
     entering = [entering[0]] + [z_turn(entering[d], d) for d in range(1, nz)]

time: 184 us -> 180 us (0.978)
    pallas_call x16 -> x14, Pallas kernels: 50.8 us -> 45.2 us  [call(): pl.pallas_call(kernel, out_shape=list(outs), grid_spec=pltpu.PrefetchScal...]
    pallas_call x0 -> x2, Pallas kernels: none -> 3.87 us  [the longest x1 2.01 us: local(): kvs.append(y_turn(pack(key_in, value_in), d))]
    unnamed x48 -> x46, local copies, waits for them, and re-layouts: 2.48 us -> 3.7 us
  transfers between devices with their start and end apart: 43 -> 43, of which waited for: 22 -> 19; matrix products, arithmetic and copies ran while one was open for 1% -> 1% of each run, Pallas kernels for 21% -> 21%
where the time goes in v5:
time: 180 us
  waiting for transfers between devices  73.6 us (41%)
  starting transfers between devices  51 us (28%)
  Pallas kernels  49.1 us (27%)
  local copies, waits for them, and re-layouts  4.52 us (3%)
    ppermute x16, waiting for transfers between devices, z_turn(): return lax.ppermute(a, 'seq', pairs)  50.5 us
    pallas_call x14, Pallas kernels, call(): pl.pallas_call(kernel, out_shape=list(outs), grid_spec=pltpu.PrefetchScal...  45.2 us
    ppermute x16, starting transfers between devices, z_turn(): return lax.ppermute(a, 'seq', pairs)  25.6 us
    ppermute x17, starting transfers between devices, y_turn(): return lax.ppermute(a, 'seq', pairs)  18.5 us
    ppermute x17, waiting for transfers between devices, y_turn(): return lax.ppermute(a, 'seq', pairs)  14.3 us
    ppermute x10, waiting for transfers between devices, swap(): return lax.ppermute(a, 'exp', [(p, p ^ r) for p in range(nz)])  8.81 us
    ppermute x10, starting transfers between devices, swap(): return lax.ppermute(a, 'exp', [(p, p ^ r) for p in range(nz)])  6.86 us
    unnamed x46, local copies, waits for them, and re-layouts  3.7 us
  transfers between devices with their start and end apart: 43, of which 19 were waited for; matrix products, arithmetic and copies ran while one was open for 1% of the time, Pallas kernels for 21%

profile of v5, /device:TPU:0, one launch (start us, length us, event | category | flops | bytes accessed | tf_op | source)
XLA Modules:
  0.0 179.8 jit_solution(6951160561467816974)
XLA Ops:
  0.7 2.0 %shard_map.230 = bf16[2,128,1024]{2,1,0:T(8,128)(2,1)} custom-call(bf16[128,2048]{1,0:T(8,128)(2,1)} %refs_0_.5, bf16[128,2048]{1,0:T(8,128)(2,1)} %refs_1_.5), custom_call_target="tpu_custom_call" | custom-call | tf_op jit(solution)/shard_map/pallas_call | solution.py:579
  2.8 3.0 %collective-permute-start = (bf16[2,128,1024]{2,1,0:T(8,128)(2,1)}, bf16[2,128,1024]{2,1,0:T(8,128)(2,1)S(1)}, u32[]{:S(2)}, u32[]{:S(2)}) collective-permute-start(bf16[2,128,1024]{2,1,0:T(8,128)(2,1)} %shard_map.230), channel_id=1, source_target_pairs={{0,4},{4,0},{8,12},{12,8},{16,20},{20,16},{24,28},{28,24},{1,5},{5... | collective-permute-start | bytes 1572872 | tf_op jit(solution)/shard_map/ppermute | solution.py:518
  5.8 1.5 collective-permute-start.3
  8.7 1.9 %shard_map.231 = bf16[2,128,1024]{2,1,0:T(8,128)(2,1)} custom-call(bf16[128,2048]{1,0:T(8,128)(2,1)} %refs_2_.2, bf16[128,2048]{1,0:T(8,128)(2,1)} %refs_3_.1), custom_call_target="tpu_custom_call" | custom-call | tf_op jit(solution)/shard_map/pallas_call | solution.py:581
  11.9 1.5 shard_map.232
  13.4 4.7 %collective-permute-done.1.refs_4_ = f32[16,128]{1,0:T(8,128)S(1)} collective-permute-done((f32[16,128]{1,0:T(8,128)}, f32[16,128]{1,0:T(8,128)S(1)}, u32[]{:S(2)}, u32[]{:S(2)}) %collective-permute-start.1) | collective-permute-done | bytes 8224 | tf_op jit(solution)/shard_map/ppermute | solution.py:518
  18.1 1.7 collective-permute-start.5
  19.8 3.0 %shard_map.233 = (bf16[272,128]{1,0:T(8,128)(2,1)S(1)}, bf16[272,128]{1,0:T(8,128)(2,1)S(1)}, bf16[272,128]{1,0:T(8,128)(2,1)S(1)}, bf16[272,128]{1,0:T(8,128)(2...) custom-call(s32[3]{0:T(128)S(1)} %pad_add_fusion.s, bf16[128,2048]{1,0:T(8,128)(2,1)S(1)} %copy-done.2, ...), custom_call_target="tpu_custom_call" | custom-call | flops 67108864 | bytes 1884160 | tf_op jit(solution)/shard_map/pallas_call | solution.py:47
  22.9 1.6 collective-permute-start.6
  24.5 2.6 %collective-permute-start.7 = (bf16[272,128]{1,0:T(8,128)(2,1)S(1)}, bf16[272,128]{1,0:T(8,128)(2,1)S(1)}, u32[]{:S(2)}, u32[]{:S(2)}) collective-permute-start(bf16[272,128]{1,0:T(8,128)(2,1)S(1)} %get-tuple-element.48), channel_id=1, source_target_pairs={{0,16},{4,20},{8,24},{12,28},{16,0},{20,4},{24,8},{28,12},{1,17},{... | collective-permute-start | bytes 208904 | tf_op jit(solution)/shard_map/ppermute | solution.py:514
  29.7 1.7 collective-permute-done.7.refs_2_
  33.1 2.7 %collective-permute-start.11 = (bf16[256,128]{1,0:T(8,128)(2,1)S(1)}, bf16[256,128]{1,0:T(8,128)(2,1)S(1)}, u32[]{:S(2)}, u32[]{:S(2)}) collective-permute-start(bf16[256,128]{1,0:T(8,128)(2,1)S(1)} %get-tuple-element.53), channel_id=1, source_target_pairs={{0,24},{4,28},{8,0},{12,4},{16,8},{20,12},{24,16},{28,20},{1,25},{... | collective-permute-start | bytes 196616 | tf_op jit(solution)/shard_map/ppermute | solution.py:514
  35.9 2.7 %collective-permute-done.10.refs_8_ = bf16[256,128]{1,0:T(8,128)(2,1)S(1)} collective-permute-done((bf16[256,128]{1,0:T(8,128)(2,1)S(1)}, bf16[256,128]{1,0:T(8,128)(2,1)S(1)}, u32[]{:S(2)}, u32[]{:S(2)}) %collective-permute-start.10) | collective-permute-done | bytes 65568 | tf_op jit(solution)/shard_map/ppermute | solution.py:514
  38.6 3.2 %collective-permute-done.9.refs_7_ = bf16[256,128]{1,0:T(8,128)(2,1)S(1)} collective-permute-done((bf16[256,128]{1,0:T(8,128)(2,1)S(1)}, bf16[256,128]{1,0:T(8,128)(2,1)S(1)}, u32[]{:S(2)}, u32[]{:S(2)}) %collective-permute-start.9) | collective-permute-done | bytes 65568 | tf_op jit(solution)/shard_map/ppermute | solution.py:514
  41.8 3.4 %shard_map.235.refs_0_ = bf16[256,1024]{1,0:T(8,128)(2,1)S(1)} custom-call(s32[3]{0:T(128)S(1)} %pad_add_fusion.s, bf16[128,2048]{1,0:T(8,128)(2,1)S(1)} %copy-done.2, bf16[128,2048]{1,0:T(8,128)(2,1)S(1)} %copy-done.3, bf16[128,2048]{1,0:T(8,128)(2,1)S(1)} %copy-done.4, bf16[128,2048]{1,0:T(8,128)(2,1)S(1)} %copy-done.5, ...), custom_call_target="tpu_custom_call" | custom-call | flops 268435456 | bytes 3956736 | tf_op jit(solution)/shard_map/pallas_call | solution.py:47
  45.3 3.8 %collective-permute-start.17 = (bf16[256,1024]{1,0:T(8,128)(2,1)S(1)}, bf16[256,1024]{1,0:T(8,128)(2,1)S(1)}, u32[]{:S(2)}, u32[]{:S(2)}) collective-permute-start(bf16[256,1024]{1,0:T(8,128)(2,1)S(1)} %shard_map.235.refs_0_), channel_id=1, source_target_pairs={{0,24},{4,28},{8,0},{12,4},{16,8},{20,12},{24,16},{28,20},{1,25},{... | collective-permute-start | bytes 1572872 | tf_op jit(solution)/shard_map/ppermute | solution.py:514
  49.7 12.3 %collective-permute-done.12.refs_1_ = bf16[256,1024]{1,0:T(8,128)(2,1)S(1)} collective-permute-done((bf16[256,1024]{1,0:T(8,128)(2,1)S(1)}, bf16[256,1024]{1,0:T(8,128)(2,1)S(1)}, u32[]{:S(2)}, u32[]{:S(2)}) %collective-permute-start.12) | collective-permute-done | bytes 524320 | tf_op jit(solution)/shard_map/ppermute | solution.py:514
  62.5 5.9 %collective-permute-done.17.refs_2_ = bf16[256,1024]{1,0:T(8,128)(2,1)S(1)} collective-permute-done((bf16[256,1024]{1,0:T(8,128)(2,1)S(1)}, bf16[256,1024]{1,0:T(8,128)(2,1)S(1)}, u32[]{:S(2)}, u32[]{:S(2)}) %collective-permute-start.17) | collective-permute-done | bytes 524320 | tf_op jit(solution)/shard_map/ppermute | solution.py:514
  69.0 2.6 %collective-permute-start.13 = (bf16[128,1024]{1,0:T(8,128)(2,1)S(1)}, bf16[128,1024]{1,0:T(8,128)(2,1)S(1)}, u32[]{:S(2)}, u32[]{:S(2)}) collective-permute-start(bf16[128,1024]{1,0:T(8,128)(2,1)S(1)} %get-tuple-element.87), channel_id=1, source_target_pairs={{0,16},{4,20},{8,24},{12,28},{16,0},{20,4},{24,8},{28,12},{1,17},{... | collective-permute-start | bytes 786440 | tf_op jit(solution)/shard_map/ppermute | solution.py:514
  72.0 15.2 %collective-permute-done.13.refs_0_ = bf16[128,1024]{1,0:T(8,128)(2,1)S(1)} collective-permute-done((bf16[128,1024]{1,0:T(8,128)(2,1)S(1)}, bf16[128,1024]{1,0:T(8,128)(2,1)S(1)}, u32[]{:S(2)}, u32[]{:S(2)}) %collective-permute-start.13) | collective-permute-done | bytes 262176 | tf_op jit(solution)/shard_map/ppermute | solution.py:514
  87.9 4.6 %collective-permute-done.14.refs_1_ = bf16[128,1024]{1,0:T(8,128)(2,1)S(1)} collective-permute-done((bf16[128,1024]{1,0:T(8,128)(2,1)S(1)}, bf16[128,1024]{1,0:T(8,128)(2,1)S(1)}, u32[]{:S(2)}, u32[]{:S(2)}) %collective-permute-start.14) | collective-permute-done | bytes 262176 | tf_op jit(solution)/shard_map/ppermute | solution.py:514
  93.4 4.1 %shard_map.236 = (bf16[3,256,768]{2,1,0:T(8,128)(2,1)S(1)}, f32[320,768]{1,0:T(8,128)S(1)}) custom-call(s32[3]{0:T(128)S(1)} %pad_add_fusion.s, bf16[256,1024]{1,0:T(8,128)(2,1)S(1)} %shard_map.235.refs_0_, bf16[256,1024]{1,0:T(8,128)(2,1)S(1)} %collective-permute-done.12.refs_1_, bf16[256,1024]{1,0:T(8,128)(2,1)S(1)} %collective-permute-done.17.refs_2_, ...), custom_call_target="tpu_custom_call" | custom-call | flops 2415919104 | bytes 11610624 | tf_op jit(solution)/shard_map/pallas_call | solution.py:47
  97.6 2.8 %collective-permute-done.16.refs_3_ = bf16[128,1024]{1,0:T(8,128)(2,1)S(1)} collective-permute-done((bf16[128,1024]{1,0:T(8,128)(2,1)S(1)}, bf16[128,1024]{1,0:T(8,128)(2,1)S(1)}, u32[]{:S(2)}, u32[]{:S(2)}) %collective-permute-start.16) | collective-permute-done | bytes 262176 | tf_op jit(solution)/shard_map/ppermute | solution.py:518
  100.4 3.0 %shard_map.237 = (f32[160,768]{1,0:T(8,128)S(1)}, bf16[160,768]{1,0:T(8,128)(2,1)S(1)}, bf16[2,256,768]{2,1,0:T(8,128)(2,1)S(1)}, bf16[2,256,768]{2,1,0:T(8,128)(2,1)S(1)}) custom-call(s32[3]{0:T(128)S(1)} %pad_add_fusion.s, bf16[128,1024]{1,0:T(8,128)(2,1)S(1)} %collective-permute-done.13.refs_0_, bf16[128,1024]{1,0:T(8,128)(2,1)S(1)} %collective-permute-done.14.refs_1_, ...), custom_call_target="tpu_custom_call" | custom-call | flops 805306368 | bytes 12216832 | tf_op jit(solution)/shard_map/pallas_call | solution.py:47
  103.5 1.5 collective-permute-done.21
  105.1 1.5 collective-permute-start.22
  106.6 4.0 %collective-permute-done.22.received = bf16[80,768]{1,0:T(8,128)(2,1)S(1)} collective-permute-done((bf16[80,768]{1,0:T(8,128)(2,1)S(1)}, bf16[80,768]{1,0:T(8,128)(2,1)S(1)}, u32[]{:S(2)}, u32[]{:S(2)}) %collective-permute-start.22) | collective-permute-done | bytes 122912 | tf_op jit(solution)/shard_map/ppermute | solution.py:521
  111.6 1.7 collective-permute-start.23
  113.4 2.1 %collective-permute-start.25 = (bf16[80,896]{1,0:T(8,128)(2,1)S(1)}, bf16[80,896]{1,0:T(8,128)(2,1)S(1)}, u32[]{:S(2)}, u32[]{:S(2)}) collective-permute-start(bf16[80,896]{1,0:T(8,128)(2,1)S(1)} %shard_map.238.refs_0_), channel_id=1, source_target_pairs={{0,24},{4,28},{8,0},{12,4},{16,8},{20,12},{24,16},{28,20},{1,25},{... | collective-permute-start | bytes 430088 | tf_op jit(solution)/shard_map/ppermute | solution.py:514
  116.7 3.4 %shard_map.239 = (f32[80,1152]{1,0:T(8,128)S(1)}, f32[80,1152]{1,0:T(8,128)S(1)}, f32[80,128]{1,0:T(8,128)S(1)}) custom-call(s32[3]{0:T(128)S(1)} %pad_add_fusion.s, bf16[80,896]{1,0:T(8,128)(2,1)S(1)} %shard_map.238.refs_0_, bf16[1,1152,6144]{2,1,0:T(8,128)(2,1)} %refs_6_.8, bf16[1,1152,6144]{2,1,0:T(8,128)(2,1)} %refs_7_.7), custom_call_target="tpu_custom_call" | custom-call | flops 283115520 | bytes 29233152 | tf_op jit(solution)/shard_map/pallas_call | solution.py:47
  120.2 3.2 %collective-permute-done.27.refs_3_ = bf16[80,896]{1,0:T(8,128)(2,1)S(1)} collective-permute-done((bf16[80,896]{1,0:T(8,128)(2,1)S(1)}, bf16[80,896]{1,0:T(8,128)(2,1)S(1)}, u32[]{:S(2)}, u32[]{:S(2)}) %collective-permute-start.27) | collective-permute-done | bytes 143392 | tf_op jit(solution)/shard_map/ppermute | solution.py:514
  123.4 1.5 collective-permute-start.28
  125.5 1.5 collective-permute-start.26
  127.0 7.0 %shard_map.240 = (f32[80,1152]{1,0:T(8,128)S(1)}, f32[80,1152]{1,0:T(8,128)S(1)}, f32[80,128]{1,0:T(8,128)S(1)}) custom-call(s32[3]{0:T(128)S(1)} %pad_add_fusion.s, bf16[80,896]{1,0:T(8,128)(2,1)S(1)} %collective-permute-done.29.refs_0_, bf16[80,896]{1,0:T(8,128)(2,1)S(1)} %collective-permute-done.23.refs_1_, ...), custom_call_target="tpu_custom_call" | custom-call | flops 1132462080 | bytes 30441472 | tf_op jit(solution)/shard_map/pallas_call | solution.py:47
  135.2 5.9 %shard_map.241 = (bf16[80,1152]{1,0:T(8,128)(2,1)S(1)}, f32[80,128]{1,0:T(8,128)S(1)}) custom-call(s32[3]{0:T(128)S(1)} %pad_add_fusion.s, bf16[80,896]{1,0:T(8,128)(2,1)S(1)} %collective-permute-done.24.refs_0_, bf16[80,896]{1,0:T(8,128)(2,1)S(1)} %collective-permute-done.26.refs_1_, bf16[80,896]{1,0:T(8,128)(2,1)S(1)} %collective-permute-done.28.refs_2_, ...), custom_call_target="tpu_custom_call" | custom-call | flops 849346560 | bytes 29745152 | tf_op jit(solution)/shard_map/pallas_call | solution.py:47
  141.1 2.1 %collective-permute-start.34 = (bf16[80,1152]{1,0:T(8,128)(2,1)S(1)}, bf16[80,1152]{1,0:T(8,128)(2,1)S(1)}, u32[]{:S(2)}, u32[]{:S(2)}) collective-permute-start(bf16[80,1152]{1,0:T(8,128)(2,1)S(1)} %get-tuple-element.68.refs_0_), channel_id=1, source_target_pairs={{0,16},{4,20},{8,24},{12,28},{16,0},{20,4},{24,8},{28,12},{1,17},{... | collective-permute-start | bytes 552968 | tf_op jit(solution)/shard_map/ppermute | solution.py:514
  143.2 3.8 %collective-permute-start.32 = (bf16[80,1152]{1,0:T(8,128)(2,1)S(1)}, bf16[80,1152]{1,0:T(8,128)(2,1)S(1)}, u32[]{:S(2)}, u32[]{:S(2)}) collective-permute-start(bf16[80,1152]{1,0:T(8,128)(2,1)S(1)} %get-tuple-element.68.refs_0_), channel_id=1, source_target_pairs={{0,24},{4,28},{8,0},{12,4},{16,8},{20,12},{24,16},{28,20},{1,25},{... | collective-permute-start | bytes 552968 | tf_op jit(solution)/shard_map/ppermute | solution.py:514
  147.3 1.5 collective-permute-start.41
  150.1 3.9 %shard_map.242 = (f32[80,768]{1,0:T(8,128)S(1)}, bf16[3,1152,768]{2,1,0:T(8,128)(2,1)S(1)}) custom-call(s32[3]{0:T(128)S(1)} %pad_add_fusion.s, bf16[80,1152]{1,0:T(8,128)(2,1)S(1)} %get-tuple-element.68.refs_0_, bf16[1,9216,768]{2,1,0:T(8,128)(2,1)} %refs_5_.4), custom_call_target="tpu_custom_call" | custom-call | flops 141557760 | bytes 19894272 | tf_op jit(solution)/shard_map/pallas_call | solution.py:47
  154.0 2.4 %copy-done.1 = bf16[3,1152,768]{2,1,0:T(8,128)(2,1)} copy-done((bf16[3,1152,768]{2,1,0:T(8,128)(2,1)}, bf16[3,1152,768]{2,1,0:T(8,128)(2,1)S(1)}, u32[]{:S(2)}) %copy-start.1) | copy-done | bytes 5308440
  159.2 1.4 collective-permute-start.42
  160.6 4.4 %shard_map.243.refs_3_ = f32[80,768]{1,0:T(8,128)S(1)} custom-call(s32[3]{0:T(128)S(1)} %pad_add_fusion.s, bf16[80,1152]{1,0:T(8,128)(2,1)S(1)} %collective-permute-done.36.refs_0_, bf16[80,1152]{1,0:T(8,128)(2,1)S(1)} %collective-permute-done.30.refs_1_, bf16[80,1152]{1,0:T(8,128)(2,1)S(1)} %collective-permute-done.32.refs_2_, ...), custom_call_target="tpu_custom_call" | custom-call | flops 566231040 | bytes 15384576 | tf_op jit(solution)/shard_map/pallas_call | solution.py:47
  164.9 2.9 %collective-permute-done.31.refs_0_ = bf16[80,1152]{1,0:T(8,128)(2,1)S(1)} collective-permute-done((bf16[80,1152]{1,0:T(8,128)(2,1)S(1)}, bf16[80,1152]{1,0:T(8,128)(2,1)S(1)}, u32[]{:S(2)}, u32[]{:S(2)}) %collective-permute-start.31) | collective-permute-done | bytes 184352 | tf_op jit(solution)/shard_map/ppermute | solution.py:518
  167.9 2.6 %collective-permute-done.33.refs_1_ = bf16[80,1152]{1,0:T(8,128)(2,1)S(1)} collective-permute-done((bf16[80,1152]{1,0:T(8,128)(2,1)S(1)}, bf16[80,1152]{1,0:T(8,128)(2,1)S(1)}, u32[]{:S(2)}, u32[]{:S(2)}) %collective-permute-start.33) | collective-permute-done | bytes 184352 | tf_op jit(solution)/shard_map/ppermute | solution.py:518
  170.5 1.8 %shard_map.244 = (bf16[32,768]{1,0:T(8,128)(2,1)S(1)}, bf16[32,768]{1,0:T(8,128)(2,1)S(1)}, bf16[32,768]{1,0:T(8,128)(2,1)S(1)}, bf16[32,768]{1,0:T(8,128)(2,1)S(1)}) custom-call(s32[3]{0:T(128)S(1)} %pad_add_fusion.s, bf16[80,1152]{1,0:T(8,128)(2,1)S(1)} %collective-permute-done.31.refs_0_, bf16[80,1152]{1,0:T(8,128)(2,1)S(1)} %collective-permute-done.33.refs_1_, ...), custom_call_target="tpu_custom_call" | custom-call | flops 424673280 | bytes 6345152 | tf_op jit(solution)/shard_map/pallas_call | solution.py:47
  172.4 1.5 collective-permute-start.38
  174.3 2.3 %collective-permute-done.38.refs_2_ = bf16[32,768]{1,0:T(8,128)(2,1)S(1)} collective-permute-done((bf16[32,768]{1,0:T(8,128)(2,1)S(1)}, bf16[32,768]{1,0:T(8,128)(2,1)S(1)}, u32[]{:S(2)}, u32[]{:S(2)}) %collective-permute-start.38) | collective-permute-done | bytes 49184 | tf_op jit(solution)/shard_map/ppermute | solution.py:521
  177.6 2.1 %shard_map.245 = bf16[256,768]{1,0:T(8,128)(2,1)} custom-call(s32[3]{0:T(128)S(1)} %pad_add_fusion.s, bf16[32,768]{1,0:T(8,128)(2,1)S(1)} %get-tuple-element.73.refs_0_, bf16[32,768]{1,0:T(8,128)(2,1)S(1)} %collective-permute-done.37.refs_1_, bf16[32,768]{1,0:T(8,128)(2,1)S(1)} %collective-permute-done.38.refs_2_, ...), custom_call_target="tpu_custom_call" | custom-call | bytes 1778688 | tf_op jit(solution)/shard_map/pallas_call | solution.py:47
  (110 shorter events, 21.0 us)
Async XLA Ops:
  0.7 41.1 %copy-start.4 = (bf16[128,2048]{1,0:T(8,128)(2,1)S(1)}, bf16[128,2048]{1,0:T(8,128)(2,1)}, u32[]{:S(2)}) copy-start(bf16[128,2048]{1,0:T(8,128)(2,1)} %refs_2_.2) | copy-start | bytes 1572868
  0.7 41.1 %copy-start.5 = (bf16[128,2048]{1,0:T(8,128)(2,1)S(1)}, bf16[128,2048]{1,0:T(8,128)(2,1)}, u32[]{:S(2)}) copy-start(bf16[128,2048]{1,0:T(8,128)(2,1)} %refs_3_.1) | copy-start | bytes 1572868
  2.8 15.3 %collective-permute-start = (bf16[2,128,1024]{2,1,0:T(8,128)(2,1)}, bf16[2,128,1024]{2,1,0:T(8,128)(2,1)S(1)}, u32[]{:S(2)}, u32[]{:S(2)}) collective-permute-start(bf16[2,128,1024]{2,1,0:T(8,128)(2,1)} %shard_map.230), channel_id=1, source_target_pairs={{0,4},{4,0},{8,12},{12,8},{16,20},{20,16},{24,28},{28,24},{1,5},{5... | collective-permute-start | bytes 1572872 | tf_op jit(solution)/shard_map/ppermute | solution.py:518
  5.8 4.8 %collective-permute-start.2 = (s32[2,256]{1,0:T(2,128)}, s32[2,256]{1,0:T(2,128)S(1)}, u32[]{:S(2)}, u32[]{:S(2)}) collective-permute-start(s32[2,256]{1,0:T(2,128)} %bitcast.17), channel_id=1, source_target_pairs={{0,1},{1,0},{2,3},{3,2},{4,5},{5,4},{6,7},{7,6},{8,9},{9,8},{10,11... | collective-permute-start | bytes 6152 | tf_op jit(solution)/shard_map/ppermute | solution.py:521
  5.8 4.8 %collective-permute-start.3 = (s32[2,256]{1,0:T(2,128)}, s32[2,256]{1,0:T(2,128)S(1)}, u32[]{:S(2)}, u32[]{:S(2)}) collective-permute-start(s32[2,256]{1,0:T(2,128)} %bitcast.18), channel_id=1, source_target_pairs={{0,2},{1,3},{2,0},{3,1},{4,6},{5,7},{6,4},{7,5},{8,10},{9,11},{10,... | collective-permute-start | bytes 6152 | tf_op jit(solution)/shard_map/ppermute | solution.py:521
  7.3 3.3 %collective-permute-start.4 = (s32[2,256]{1,0:T(2,128)}, s32[2,256]{1,0:T(2,128)S(1)}, u32[]{:S(2)}, u32[]{:S(2)}) collective-permute-start(s32[2,256]{1,0:T(2,128)} %bitcast.19), channel_id=1, source_target_pairs={{0,3},{1,2},{2,1},{3,0},{4,7},{5,6},{6,5},{7,4},{8,11},{9,10},{10,... | collective-permute-start | bytes 6152 | tf_op jit(solution)/shard_map/ppermute | solution.py:521
  7.6 10.4 %collective-permute-start.1 = (f32[16,128]{1,0:T(8,128)}, f32[16,128]{1,0:T(8,128)S(1)}, u32[]{:S(2)}, u32[]{:S(2)}) collective-permute-start(f32[16,128]{1,0:T(8,128)} %bitcast.14), channel_id=1, source_target_pairs={{0,4},{4,0},{8,12},{12,8},{16,20},{20,16},{24,28},{28,24},{1,5},{5... | collective-permute-start | bytes 24584 | tf_op jit(solution)/shard_map/ppermute | solution.py:518
  18.1 23.7 %collective-permute-start.5 = (bf16[2,128,1024]{2,1,0:T(8,128)(2,1)}, bf16[2,128,1024]{2,1,0:T(8,128)(2,1)S(1)}, u32[]{:S(2)}, u32[]{:S(2)}) collective-permute-start(bf16[2,128,1024]{2,1,0:T(8,128)(2,1)} %shard_map.231), channel_id=1, source_target_pairs={{0,4},{4,0},{8,12},{12,8},{16,20},{20,16},{24,28},{28,24},{1,5},{5... | collective-permute-start | bytes 1572872 | tf_op jit(solution)/shard_map/ppermute | solution.py:518
  22.9 70.5 %copy-start = (bf16[2048,768]{1,0:T(8,128)(2,1)S(1)}, bf16[2048,768]{1,0:T(8,128)(2,1)}, u32[]{:S(2)}) copy-start(bf16[2048,768]{1,0:T(8,128)(2,1)} %refs_5_.3) | copy-start | bytes 9437188
  22.9 70.5 %copy-start.8 = (s32[320,1]{1,0:T(8,128)S(1)}, s32[320,1]{1,0:T(8,128)}, u32[]{:S(2)}) copy-start(s32[320,1]{1,0:T(8,128)} %constant.73.clone.refs_8_.refs_6_) | copy-start | bytes 3844
  22.9 70.5 %copy-start.9 = (s32[320,1]{1,0:T(8,128)S(1)}, s32[320,1]{1,0:T(8,128)}, u32[]{:S(2)}) copy-start(s32[320,1]{1,0:T(8,128)} %constant.74.clone.refs_9_.refs_7_) | copy-start | bytes 3844
  22.9 6.8 %collective-permute-start.6 = (bf16[272,128]{1,0:T(8,128)(2,1)S(1)}, bf16[272,128]{1,0:T(8,128)(2,1)S(1)}, u32[]{:S(2)}, u32[]{:S(2)}) collective-permute-start(bf16[272,128]{1,0:T(8,128)(2,1)S(1)} %get-tuple-element.47), channel_id=1, source_target_pairs={{0,8},{4,12},{8,16},{12,20},{16,24},{20,28},{24,0},{28,4},{1,9},{5... | collective-permute-start | bytes 208904 | tf_op jit(solution)/shard_map/ppermute | solution.py:514
  24.5 6.9 %collective-permute-start.7 = (bf16[272,128]{1,0:T(8,128)(2,1)S(1)}, bf16[272,128]{1,0:T(8,128)(2,1)S(1)}, u32[]{:S(2)}, u32[]{:S(2)}) collective-permute-start(bf16[272,128]{1,0:T(8,128)(2,1)S(1)} %get-tuple-element.48), channel_id=1, source_target_pairs={{0,16},{4,20},{8,24},{12,28},{16,0},{20,4},{24,8},{28,12},{1,17},{... | collective-permute-start | bytes 208904 | tf_op jit(solution)/shard_map/ppermute | solution.py:514
  27.1 4.8 %collective-permute-start.8 = (bf16[272,128]{1,0:T(8,128)(2,1)S(1)}, bf16[272,128]{1,0:T(8,128)(2,1)S(1)}, u32[]{:S(2)}, u32[]{:S(2)}) collective-permute-start(bf16[272,128]{1,0:T(8,128)(2,1)S(1)} %get-tuple-element.49), channel_id=1, source_target_pairs={{0,24},{4,28},{8,0},{12,4},{16,8},{20,12},{24,16},{28,20},{1,25},{... | collective-permute-start | bytes 208904 | tf_op jit(solution)/shard_map/ppermute | solution.py:514
  32.6 6.0 %collective-permute-start.10 = (bf16[256,128]{1,0:T(8,128)(2,1)S(1)}, bf16[256,128]{1,0:T(8,128)(2,1)S(1)}, u32[]{:S(2)}, u32[]{:S(2)}) collective-permute-start(bf16[256,128]{1,0:T(8,128)(2,1)S(1)} %get-tuple-element.52), channel_id=1, source_target_pairs={{0,16},{4,20},{8,24},{12,28},{16,0},{20,4},{24,8},{28,12},{1,17},{... | collective-permute-start | bytes 196616 | tf_op jit(solution)/shard_map/ppermute | solution.py:514
  33.1 5.5 %collective-permute-start.11 = (bf16[256,128]{1,0:T(8,128)(2,1)S(1)}, bf16[256,128]{1,0:T(8,128)(2,1)S(1)}, u32[]{:S(2)}, u32[]{:S(2)}) collective-permute-start(bf16[256,128]{1,0:T(8,128)(2,1)S(1)} %get-tuple-element.53), channel_id=1, source_target_pairs={{0,24},{4,28},{8,0},{12,4},{16,8},{20,12},{24,16},{28,20},{1,25},{... | collective-permute-start | bytes 196616 | tf_op jit(solution)/shard_map/ppermute | solution.py:514
  35.8 6.1 %collective-permute-start.9 = (bf16[256,128]{1,0:T(8,128)(2,1)S(1)}, bf16[256,128]{1,0:T(8,128)(2,1)S(1)}, u32[]{:S(2)}, u32[]{:S(2)}) collective-permute-start(bf16[256,128]{1,0:T(8,128)(2,1)S(1)} %get-tuple-element.51), channel_id=1, source_target_pairs={{0,8},{4,12},{8,16},{12,20},{16,24},{20,28},{24,0},{28,4},{1,9},{5... | collective-permute-start | bytes 196616 | tf_op jit(solution)/shard_map/ppermute | solution.py:514
  45.3 16.7 %collective-permute-start.12 = (bf16[256,1024]{1,0:T(8,128)(2,1)S(1)}, bf16[256,1024]{1,0:T(8,128)(2,1)S(1)}, u32[]{:S(2)}, u32[]{:S(2)}) collective-permute-start(bf16[256,1024]{1,0:T(8,128)(2,1)S(1)} %shard_map.235.refs_0_), channel_id=1, source_target_pairs={{0,8},{4,12},{8,16},{12,20},{16,24},{20,28},{24,0},{28,4},{1,9},{5... | collective-permute-start | bytes 1572872 | tf_op jit(solution)/shard_map/ppermute | solution.py:514
  45.3 23.1 %collective-permute-start.17 = (bf16[256,1024]{1,0:T(8,128)(2,1)S(1)}, bf16[256,1024]{1,0:T(8,128)(2,1)S(1)}, u32[]{:S(2)}, u32[]{:S(2)}) collective-permute-start(bf16[256,1024]{1,0:T(8,128)(2,1)S(1)} %shard_map.235.refs_0_), channel_id=1, source_target_pairs={{0,24},{4,28},{8,0},{12,4},{16,8},{20,12},{24,16},{28,20},{1,25},{... | collective-permute-start | bytes 1572872 | tf_op jit(solution)/shard_map/ppermute | solution.py:514
  49.1 44.2 %collective-permute-start.18 = (bf16[256,1024]{1,0:T(8,128)(2,1)S(1)}, bf16[256,1024]{1,0:T(8,128)(2,1)S(1)}, u32[]{:S(2)}, u32[]{:S(2)}) collective-permute-start(bf16[256,1024]{1,0:T(8,128)(2,1)S(1)} %shard_map.235.refs_0_), channel_id=1, source_target_pairs={{0,4},{4,0},{8,12},{12,8},{16,20},{20,16},{24,28},{28,24},{1,5},{5... | collective-permute-start | bytes 1572872 | tf_op jit(solution)/shard_map/ppermute | solution.py:518
  62.0 31.4 %collective-permute-start.19 = (bf16[256,1024]{1,0:T(8,128)(2,1)S(1)}, bf16[256,1024]{1,0:T(8,128)(2,1)S(1)}, u32[]{:S(2)}, u32[]{:S(2)}) collective-permute-start(bf16[256,1024]{1,0:T(8,128)(2,1)S(1)} %collective-permute-done.12.refs_1_), channel_id=1, source_target_pairs={{0,4},{4,0},{8,12},{12,8},{16,20},{20,16},{24,28},{28,24},{1,5},{5... | collective-permute-start | bytes 1572872 | tf_op jit(solution)/shard_map/ppermute | solution.py:518
  68.4 25.0 %collective-permute-start.20 = (bf16[256,1024]{1,0:T(8,128)(2,1)S(1)}, bf16[256,1024]{1,0:T(8,128)(2,1)S(1)}, u32[]{:S(2)}, u32[]{:S(2)}) collective-permute-start(bf16[256,1024]{1,0:T(8,128)(2,1)S(1)} %collective-permute-done.17.refs_2_), channel_id=1, source_target_pairs={{0,4},{4,0},{8,12},{12,8},{16,20},{20,16},{24,28},{28,24},{1,5},{5... | collective-permute-start | bytes 1572872 | tf_op jit(solution)/shard_map/ppermute | solution.py:518
  69.0 18.2 %collective-permute-start.13 = (bf16[128,1024]{1,0:T(8,128)(2,1)S(1)}, bf16[128,1024]{1,0:T(8,128)(2,1)S(1)}, u32[]{:S(2)}, u32[]{:S(2)}) collective-permute-start(bf16[128,1024]{1,0:T(8,128)(2,1)S(1)} %get-tuple-element.87), channel_id=1, source_target_pairs={{0,16},{4,20},{8,24},{12,28},{16,0},{20,4},{24,8},{28,12},{1,17},{... | collective-permute-start | bytes 786440 | tf_op jit(solution)/shard_map/ppermute | solution.py:514
  71.6 20.8 %collective-permute-start.14 = (bf16[128,1024]{1,0:T(8,128)(2,1)S(1)}, bf16[128,1024]{1,0:T(8,128)(2,1)S(1)}, u32[]{:S(2)}, u32[]{:S(2)}) collective-permute-start(bf16[128,1024]{1,0:T(8,128)(2,1)S(1)} %get-tuple-element.86), channel_id=1, source_target_pairs={{0,16},{4,20},{8,24},{12,28},{16,0},{20,4},{24,8},{28,12},{1,17},{... | collective-permute-start | bytes 786440 | tf_op jit(solution)/shard_map/ppermute | solution.py:514
  87.1 10.4 %collective-permute-start.15 = (bf16[128,1024]{1,0:T(8,128)(2,1)S(1)}, bf16[128,1024]{1,0:T(8,128)(2,1)S(1)}, u32[]{:S(2)}, u32[]{:S(2)}) collective-permute-start(bf16[128,1024]{1,0:T(8,128)(2,1)S(1)} %collective-permute-done.13.refs_0_), channel_id=1, source_target_pairs={{0,4},{4,0},{8,12},{12,8},{16,20},{20,16},{24,28},{28,24},{1,5},{5... | collective-permute-start | bytes 786440 | tf_op jit(solution)/shard_map/ppermute | solution.py:518
  92.4 8.0 %collective-permute-start.16 = (bf16[128,1024]{1,0:T(8,128)(2,1)S(1)}, bf16[128,1024]{1,0:T(8,128)(2,1)S(1)}, u32[]{:S(2)}, u32[]{:S(2)}) collective-permute-start(bf16[128,1024]{1,0:T(8,128)(2,1)S(1)} %collective-permute-done.14.refs_1_), channel_id=1, source_target_pairs={{0,4},{4,0},{8,12},{12,8},{16,20},{20,16},{24,28},{28,24},{1,5},{5... | collective-permute-start | bytes 786440 | tf_op jit(solution)/shard_map/ppermute | solution.py:518
  103.5 1.6 collective-permute-start.21
  105.1 5.4 %collective-permute-start.22 = (bf16[80,768]{1,0:T(8,128)(2,1)S(1)}, bf16[80,768]{1,0:T(8,128)(2,1)S(1)}, u32[]{:S(2)}, u32[]{:S(2)}) collective-permute-start(bf16[80,768]{1,0:T(8,128)(2,1)S(1)} %get-tuple-element.84), channel_id=1, source_target_pairs={{0,2},{1,3},{2,0},{3,1},{4,6},{5,7},{6,4},{7,5},{8,10},{9,11},{10,... | collective-permute-start | bytes 368648 | tf_op jit(solution)/shard_map/ppermute | solution.py:521
  111.5 35.5 %collective-permute-start.40 = (bf16[2,256,768]{2,1,0:T(8,128)(2,1)S(1)}, bf16[2,256,768]{2,1,0:T(8,128)(2,1)S(1)}, u32[]{:S(2)}, u32[]{:S(2)}) collective-permute-start(bf16[2,256,768]{2,1,0:T(8,128)(2,1)S(1)} %get-tuple-element.79), channel_id=1, source_target_pairs={{0,1},{1,0},{2,3},{3,2},{4,5},{5,4},{6,7},{7,6},{8,9},{9,8},{10,11... | collective-permute-start | bytes 2359304 | tf_op jit(solution)/shard_map/ppermute | solution.py:521
  111.6 11.9 %collective-permute-start.27 = (bf16[80,896]{1,0:T(8,128)(2,1)S(1)}, bf16[80,896]{1,0:T(8,128)(2,1)S(1)}, u32[]{:S(2)}, u32[]{:S(2)}) collective-permute-start(bf16[80,896]{1,0:T(8,128)(2,1)S(1)} %shard_map.238.refs_0_), channel_id=1, source_target_pairs={{0,16},{4,20},{8,24},{12,28},{16,0},{20,4},{24,8},{28,12},{1,17},{... | collective-permute-start | bytes 430088 | tf_op jit(solution)/shard_map/ppermute | solution.py:514
  111.6 13.3 %collective-permute-start.23 = (bf16[80,896]{1,0:T(8,128)(2,1)S(1)}, bf16[80,896]{1,0:T(8,128)(2,1)S(1)}, u32[]{:S(2)}, u32[]{:S(2)}) collective-permute-start(bf16[80,896]{1,0:T(8,128)(2,1)S(1)} %shard_map.238.refs_0_), channel_id=1, source_target_pairs={{0,8},{4,12},{8,16},{12,20},{16,24},{20,28},{24,0},{28,4},{1,9},{5... | collective-permute-start | bytes 430088 | tf_op jit(solution)/shard_map/ppermute | solution.py:514
  113.4 12.1 %collective-permute-start.25 = (bf16[80,896]{1,0:T(8,128)(2,1)S(1)}, bf16[80,896]{1,0:T(8,128)(2,1)S(1)}, u32[]{:S(2)}, u32[]{:S(2)}) collective-permute-start(bf16[80,896]{1,0:T(8,128)(2,1)S(1)} %shard_map.238.refs_0_), channel_id=1, source_target_pairs={{0,24},{4,28},{8,0},{12,4},{16,8},{20,12},{24,16},{28,20},{1,25},{... | collective-permute-start | bytes 430088 | tf_op jit(solution)/shard_map/ppermute | solution.py:514
  115.5 11.4 %collective-permute-start.29 = (bf16[80,896]{1,0:T(8,128)(2,1)S(1)}, bf16[80,896]{1,0:T(8,128)(2,1)S(1)}, u32[]{:S(2)}, u32[]{:S(2)}) collective-permute-start(bf16[80,896]{1,0:T(8,128)(2,1)S(1)} %shard_map.238.refs_0_), channel_id=1, source_target_pairs={{0,4},{4,0},{8,12},{12,8},{16,20},{20,16},{24,28},{28,24},{1,5},{5... | collective-permute-start | bytes 430088 | tf_op jit(solution)/shard_map/ppermute | solution.py:518
  123.4 10.6 %collective-permute-start.28 = (bf16[80,896]{1,0:T(8,128)(2,1)S(1)}, bf16[80,896]{1,0:T(8,128)(2,1)S(1)}, u32[]{:S(2)}, u32[]{:S(2)}) collective-permute-start(bf16[80,896]{1,0:T(8,128)(2,1)S(1)} %collective-permute-done.27.refs_3_), channel_id=1, source_target_pairs={{0,4},{4,0},{8,12},{12,8},{16,20},{20,16},{24,28},{28,24},{1,5},{5... | collective-permute-start | bytes 430088 | tf_op jit(solution)/shard_map/ppermute | solution.py:518
  125.0 9.1 %collective-permute-start.24 = (bf16[80,896]{1,0:T(8,128)(2,1)S(1)}, bf16[80,896]{1,0:T(8,128)(2,1)S(1)}, u32[]{:S(2)}, u32[]{:S(2)}) collective-permute-start(bf16[80,896]{1,0:T(8,128)(2,1)S(1)} %collective-permute-done.23.refs_1_), channel_id=1, source_target_pairs={{0,4},{4,0},{8,12},{12,8},{16,20},{20,16},{24,28},{28,24},{1,5},{5... | collective-permute-start | bytes 430088 | tf_op jit(solution)/shard_map/ppermute | solution.py:518
  125.5 9.8 %collective-permute-start.26 = (bf16[80,896]{1,0:T(8,128)(2,1)S(1)}, bf16[80,896]{1,0:T(8,128)(2,1)S(1)}, u32[]{:S(2)}, u32[]{:S(2)}) collective-permute-start(bf16[80,896]{1,0:T(8,128)(2,1)S(1)} %collective-permute-done.25.refs_2_), channel_id=1, source_target_pairs={{0,4},{4,0},{8,12},{12,8},{16,20},{20,16},{24,28},{28,24},{1,5},{5... | collective-permute-start | bytes 430088 | tf_op jit(solution)/shard_map/ppermute | solution.py:518
  141.1 15.2 %collective-permute-start.34 = (bf16[80,1152]{1,0:T(8,128)(2,1)S(1)}, bf16[80,1152]{1,0:T(8,128)(2,1)S(1)}, u32[]{:S(2)}, u32[]{:S(2)}) collective-permute-start(bf16[80,1152]{1,0:T(8,128)(2,1)S(1)} %get-tuple-element.68.refs_0_), channel_id=1, source_target_pairs={{0,16},{4,20},{8,24},{12,28},{16,0},{20,4},{24,8},{28,12},{1,17},{... | collective-permute-start | bytes 552968 | tf_op jit(solution)/shard_map/ppermute | solution.py:514
  143.2 13.9 %collective-permute-start.30 = (bf16[80,1152]{1,0:T(8,128)(2,1)S(1)}, bf16[80,1152]{1,0:T(8,128)(2,1)S(1)}, u32[]{:S(2)}, u32[]{:S(2)}) collective-permute-start(bf16[80,1152]{1,0:T(8,128)(2,1)S(1)} %get-tuple-element.68.refs_0_), channel_id=1, source_target_pairs={{0,8},{4,12},{8,16},{12,20},{16,24},{20,28},{24,0},{28,4},{1,9},{5... | collective-permute-start | bytes 552968 | tf_op jit(solution)/shard_map/ppermute | solution.py:514
  143.2 15.2 %collective-permute-start.32 = (bf16[80,1152]{1,0:T(8,128)(2,1)S(1)}, bf16[80,1152]{1,0:T(8,128)(2,1)S(1)}, u32[]{:S(2)}, u32[]{:S(2)}) collective-permute-start(bf16[80,1152]{1,0:T(8,128)(2,1)S(1)} %get-tuple-element.68.refs_0_), channel_id=1, source_target_pairs={{0,24},{4,28},{8,0},{12,4},{16,8},{20,12},{24,16},{28,20},{1,25},{... | collective-permute-start | bytes 552968 | tf_op jit(solution)/shard_map/ppermute | solution.py:514
  147.3 30.3 %collective-permute-start.41 = (bf16[1,256,768]{2,1,0:T(8,128)(2,1)S(1)}, bf16[1,256,768]{2,1,0:T(8,128)(2,1)S(1)}, u32[]{:S(2)}, u32[]{:S(2)}) collective-permute-start(bf16[1,256,768]{2,1,0:T(8,128)(2,1)S(1)} %get-tuple-element.82), channel_id=1, source_target_pairs={{0,2},{1,3},{2,0},{3,1},{4,6},{5,7},{6,4},{7,5},{8,10},{9,11},{10,... | collective-permute-start | bytes 1179656 | tf_op jit(solution)/shard_map/ppermute | solution.py:521
  148.8 10.4 %collective-permute-start.36 = (bf16[80,1152]{1,0:T(8,128)(2,1)S(1)}, bf16[80,1152]{1,0:T(8,128)(2,1)S(1)}, u32[]{:S(2)}, u32[]{:S(2)}) collective-permute-start(bf16[80,1152]{1,0:T(8,128)(2,1)S(1)} %get-tuple-element.68.refs_0_), channel_id=1, source_target_pairs={{0,4},{4,0},{8,12},{12,8},{16,20},{20,16},{24,28},{28,24},{1,5},{5... | collective-permute-start | bytes 552968 | tf_op jit(solution)/shard_map/ppermute | solution.py:518
  156.3 8.6 %collective-permute-start.35 = (bf16[80,1152]{1,0:T(8,128)(2,1)S(1)}, bf16[80,1152]{1,0:T(8,128)(2,1)S(1)}, u32[]{:S(2)}, u32[]{:S(2)}) collective-permute-start(bf16[80,1152]{1,0:T(8,128)(2,1)S(1)} %collective-permute-done.34.refs_3_), channel_id=1, source_target_pairs={{0,4},{4,0},{8,12},{12,8},{16,20},{20,16},{24,28},{28,24},{1,5},{5... | collective-permute-start | bytes 552968 | tf_op jit(solution)/shard_map/ppermute | solution.py:518
  157.1 10.8 %collective-permute-start.31 = (bf16[80,1152]{1,0:T(8,128)(2,1)S(1)}, bf16[80,1152]{1,0:T(8,128)(2,1)S(1)}, u32[]{:S(2)}, u32[]{:S(2)}) collective-permute-start(bf16[80,1152]{1,0:T(8,128)(2,1)S(1)} %collective-permute-done.30.refs_1_), channel_id=1, source_target_pairs={{0,4},{4,0},{8,12},{12,8},{16,20},{20,16},{24,28},{28,24},{1,5},{5... | collective-permute-start | bytes 552968 | tf_op jit(solution)/shard_map/ppermute | solution.py:518
  158.4 12.0 %collective-permute-start.33 = (bf16[80,1152]{1,0:T(8,128)(2,1)S(1)}, bf16[80,1152]{1,0:T(8,128)(2,1)S(1)}, u32[]{:S(2)}, u32[]{:S(2)}) collective-permute-start(bf16[80,1152]{1,0:T(8,128)(2,1)S(1)} %collective-permute-done.32.refs_2_), channel_id=1, source_target_pairs={{0,4},{4,0},{8,12},{12,8},{16,20},{20,16},{24,28},{28,24},{1,5},{5... | collective-permute-start | bytes 552968 | tf_op jit(solution)/shard_map/ppermute | solution.py:518
  159.2 15.0 %collective-permute-start.42 = (f32[8,16,128]{2,1,0:T(8,128)S(1)}, f32[8,16,128]{2,1,0:T(8,128)S(1)}, u32[]{:S(2)}, u32[]{:S(2)}) collective-permute-start(f32[8,16,128]{2,1,0:T(8,128)S(1)} %get-tuple-element.88), channel_id=1, source_target_pairs={{0,4},{4,0},{8,12},{12,8},{16,20},{20,16},{24,28},{28,24},{1,5},{5... | collective-permute-start | bytes 196616 | tf_op jit(solution)/shard_map/ppermute | solution.py:518
  172.3 2.0 %collective-permute-start.37 = (bf16[32,768]{1,0:T(8,128)(2,1)S(1)}, bf16[32,768]{1,0:T(8,128)(2,1)S(1)}, u32[]{:S(2)}, u32[]{:S(2)}) collective-permute-start(bf16[32,768]{1,0:T(8,128)(2,1)S(1)} %get-tuple-element.74), channel_id=1, source_target_pairs={{0,1},{1,0},{2,3},{3,2},{4,5},{5,4},{6,7},{7,6},{8,9},{9,8},{10,11... | collective-permute-start | bytes 147464 | tf_op jit(solution)/shard_map/ppermute | solution.py:521
  172.4 4.2 %collective-permute-start.38 = (bf16[32,768]{1,0:T(8,128)(2,1)S(1)}, bf16[32,768]{1,0:T(8,128)(2,1)S(1)}, u32[]{:S(2)}, u32[]{:S(2)}) collective-permute-start(bf16[32,768]{1,0:T(8,128)(2,1)S(1)} %get-tuple-element.75), channel_id=1, source_target_pairs={{0,2},{1,3},{2,0},{3,1},{4,6},{5,7},{6,4},{7,5},{8,10},{9,11},{10,... | collective-permute-start | bytes 147464 | tf_op jit(solution)/shard_map/ppermute | solution.py:521
  173.9 3.7 %collective-permute-start.39 = (bf16[32,768]{1,0:T(8,128)(2,1)S(1)}, bf16[32,768]{1,0:T(8,128)(2,1)S(1)}, u32[]{:S(2)}, u32[]{:S(2)}) collective-permute-start(bf16[32,768]{1,0:T(8,128)(2,1)S(1)} %get-tuple-element.76), channel_id=1, source_target_pairs={{0,3},{1,2},{2,1},{3,0},{4,7},{5,6},{6,5},{7,4},{8,11},{9,10},{10,... | collective-permute-start | bytes 147464 | tf_op jit(solution)/shard_map/ppermute | solution.py:521
  (18 other events, 235.8 us)

commit v6 on v5

--- a/solution.py
+++ b/solution.py
@@ -99,7 +99,7 @@
 def routing_kernel(nz, cap, own_rows, s, *refs):
     keep = refs[0]
     given = refs[1 : nz + 1]
-    base, state, codes, sign, start, ids, sem = refs[nz + 1 :]
+    base, state, codes, sign, spare, start, ids, sem = refs[nz + 1 :]
     j = s[2]
     heads, share, _ = start.shape
     rows = pl.ds(pl.multiple_of(s[0] * share, share), share)
@@ -114,6 +114,7 @@
     own = base[...] + j * (nz * cap)
     earlier = [jnp.zeros((1, 1), I32) for _ in range(nz)]
     other = jnp.zeros((own_rows, 1), I32)
+    taken = jnp.zeros((own_rows, 1), I32)
     place = lax.broadcasted_iota(I32, (16, block), 0)
     for b in range(nz):
         first, second = ids[b, 0:1, :], ids[b, 1:2, :]
@@ -131,9 +132,13 @@
         codes[b, 0:1, :] = top
         codes[b, 1:2, :] = rest
         holds = (own == top) | (own == rest)
+        taken = taken + jnp.sum(holds.astype(I32), axis=1, keepdims=True)
         other = other + jnp.sum(jnp.where(holds, first + second, 0), axis=1, keepdims=True)
     every = lax.broadcasted_iota(I32, sign.shape, 1)
     sign[...] = (every == j).astype(F32) - (every == other - j).astype(F32)
+    index = lax.broadcasted_iota(I32, (own_rows, 1), 0)
+    unused = jnp.min(jnp.where(taken == 0, index, own_rows), axis=0, keepdims=True)
+    spare[...] = jnp.broadcast_to((index == unused).astype(F32), spare.shape)
     fetch.wait()
 
 
@@ -329,13 +334,28 @@
                 to[...] = projected[dz] if dz in dzs else done[before.index(dz)]
 
 
-def rows_kernel(s, keep, received, gain, router_t, sign, out):
+def diagonal(rows):
+    shape = (rows, 128)
+    return lax.broadcasted_iota(I32, shape, 0) == lax.broadcasted_iota(I32, shape, 1)
+
+
+def rows_kernel(s, keep, received, gain, router_t, sign, spare, out):
     width = gain.shape[1]
     rows = keep[...] + received[...].astype(F32)
     square = jnp.sum(rows * rows, axis=1, keepdims=True)
     scaled = rows * gain[...]
     logits = mm(scaled, router_t[...], NT, precision=HIGHEST)
     gap = jnp.sum(logits * sign[...], axis=1, keepdims=True)
+    if out.shape[1] == width:
+        lines = []
+        for value in (square, gap):
+            for piece in pieces(value)[:2]:
+                spread = jnp.where(diagonal(rows.shape[0]), piece.astype(F32), 0.0)
+                lines.append(jnp.sum(spread, axis=0, keepdims=True))
+        lines.append(jnp.zeros((1, width - 128 * len(lines)), F32))
+        line = jnp.concatenate(lines, axis=1)
+        out[...] = jnp.where(spare[:, 0:1] > 0.0, line, scaled).astype(BF16)
+        return
     out[:, :width] = scaled.astype(BF16)
     lane = lax.broadcasted_iota(I32, (rows.shape[0], 128), 1)
     stats = jnp.zeros((rows.shape[0], 128), F32)
@@ -360,54 +380,43 @@
         copies[n + depth].start()
 
 
-def up_kernel(nz, ny, places, ahead, first, last, features, s, *refs):
+def up_kernel(nz, ny, places, first, last, features, s, *refs):
     count = len(places)
     blocks = refs[:count]
     refs = refs[count:]
     before = () if first else refs[:3]
     refs = refs[0 if first else 3 :]
-    weights = refs[:2]
-    refs = refs[2:]
-    if last:
-        outs, buffers, sem = refs[:2], refs[2:4], refs[4]
-    elif ahead:
-        outs, kept, buffers, sem = refs[:3], refs[3:5], refs[5:7], refs[7]
-    else:
-        outs, buffers, sem = refs[:3], refs[3:5], refs[5]
-    width = blocks[0].shape[1] - 128
-
+    weights, spare = refs[:2], refs[2]
+    outs, buffers, sem = refs[3:-3], refs[-3:-1], refs[-1]
+    slots, width = blocks[0].shape
+    is_spare = spare[:, 0:1] > 0.0
     copies = []
-    if True:
-        jobs = [(p, buffers, n) for n, p in enumerate(places)]
-        jobs += [(p, kept, n) for n, p in enumerate(ahead)]
-        for p, to, n in jobs:
-            lanes = pl.ds(pl.multiple_of(source_of(s, nz, ny, p) * width, 128), width)
-            for m in range(2):
-                source = weights[m].at[0, :, lanes]
-                copies.append(pltpu.make_async_copy(source, to[m].at[n], sem.at[len(copies)]))
-        throttled(copies, -1, 4)
+    for n, p in enumerate(places):
+        lanes = pl.ds(pl.multiple_of(source_of(s, nz, ny, p) * width, 128), width)
+        for m in range(2):
+            source = weights[m].at[0, :, lanes]
+            copies.append(pltpu.make_async_copy(source, buffers[m].at[n], sem.at[len(copies)]))
+    throttled(copies, -1, 4)
     gate, up, stats = (None, None, None) if first else (b[...] for b in before)
     for n in range(count):
-        rows = blocks[n][:, :width]
-        part = blocks[n][:, width:].astype(F32)
+        rows = blocks[n][...].astype(F32)
+        part = jnp.sum(jnp.where(is_spare, rows, 0.0), axis=0, keepdims=True)
         stats = part if stats is None else stats + part
-        if True:
-            throttled(copies, 2 * n, 4)
+        rows = jnp.where(is_spare, 0.0, rows).astype(BF16)
+        throttled(copies, 2 * n, 4)
         part = mm(rows, buffers[0][n], NT)
         gate = part if gate is None else gate + part
-        if True:
-            throttled(copies, 2 * n + 1, 4)
+        throttled(copies, 2 * n + 1, 4)
         part = mm(rows, buffers[1][n], NT)
         up = part if up is None else up + part
     if not last:
         outs[0][...] = gate
         outs[1][...] = up
         outs[2][...] = stats
-        for n in range(2 * count, len(copies)):
-            throttled(copies, n, 4)
         return
-    square = stats[:, 0:1] + stats[:, 1:2] + stats[:, 2:3]
-    gap = stats[:, 3:4] + stats[:, 4:5] + stats[:, 5:6]
+    sums = [stats[:, at : at + 128] + stats[:, at + 128 : at + 256] for at in (0, 256)]
+    sums = [jnp.where(diagonal(slots), line, 0.0) for line in sums]
+    square, gap = [jnp.sum(line, axis=1, keepdims=True) for line in sums]
     inverse = lax.rsqrt(square / features + EPS)
     gate = gate * inverse
     outs[0][...] = (gate * sigmoid(gate) * (up * inverse)).astype(BF16)
@@ -546,10 +555,11 @@
 
     def stages(run, a):
         arrived = gather_z(a)
-        state = run(0, groups[0], arrived, [])
-        gather_y(arrived, state)
-        for n in (1, 2):
-            state = run(n, groups[n], arrived, state)
+        state = []
+        for n, group in enumerate(groups):
+            state = run(n, group, [arrived[p] for p in group], state)
+            if n == 0:
+                gather_y(arrived, state)
         return state
 
     groups = [[(0, 0)], [(0, d) for d in range(1, ny)] + [(d, 0) for d in z_order]]
@@ -581,18 +591,23 @@
         qgs.append(pack(query, gate_in))
     ids = jnp.transpose(expert_ids)
     share = hd // nz
-    codes, sign, start = call(
+    codes, sign, spare, start = call(
         functools.partial(routing_kernel, nz, cap, slots),
         place,
         [(keep_counts, pl.BlockSpec(memory_space=pltpu.SMEM))]
         + [ids]
         + [swap(ids, r) for r in range(1, nz)]
         + [own_base, hbm(state_in)],
-        [sds((nz, 2, block), I32), sds((slots, experts), F32), sds((heads, share, hd), F32)],
+        [
+            sds((nz, 2, block), I32),
+            sds((slots, experts), F32),
+            sds((slots, 128), F32),
+            sds((heads, share, hd), F32),
+        ],
         [pltpu.VMEM((nz, 2, block), I32), pltpu.SemaphoreType.DMA],
     )
     attn_gain_2, moe_gain_2, router_t = attn_gain[None], moe_gain[None], jnp.transpose(router)
-    prepared = [codes, sign, start, attn_gain_2, moe_gain_2]
+    prepared = [codes, sign, spare, start, attn_gain_2, moe_gain_2]
     qgs = [y_turn(qg, d + 1) for d, qg in enumerate(behind(qgs, kvs + logs + prepared))]
     share = hd // nz
     long = tok * ny
@@ -697,11 +712,12 @@
             part = keep.shape[0] // 2
             send = (keep[part:] + received[part:].astype(F32)).astype(BF16)
             keep = keep[:part] + received[:part].astype(F32)
+    fits = cols % 128 == 0 and cols >= 512 and slots <= 128
     (rows_out,) = call(
         rows_kernel,
         place,
-        [keep, received, moe_gain_2, router_t, sign],
-        [sds((slots, cols + 128), BF16)],
+        [keep, received, moe_gain_2, router_t, sign, spare],
+        [sds((slots, cols if fits else cols + 128), BF16)],
     )
     send_all = behind([send_all], [rows_out])[0]
     for b in range(bits):
@@ -722,30 +738,23 @@
 
     in_vmem = pl.BlockSpec(memory_space=pltpu.VMEM)
 
-    def up(n, group, arrived, state):
+    def up(n, group, blocks, state):
         first, last = n == 0, n == len(groups) - 1
-        ahead = []
-        outs = [sds((slots, units), F32)] * 2 + [sds((slots, 128), F32)]
-        outs += [sds((len(ahead), units, cols), BF16)] * (2 if ahead else 0)
-        weights = [anywhere(w_gate), anywhere(w_up)]
+        outs = [sds((slots, units), F32)] * 2 + [sds((1, cols), F32)]
         if last:
             outs = [sds((slots, units), BF16), sds((slots, 128), F32)]
-        state = call(
-            functools.partial(up_kernel, nz, ny, group, ahead, first, last, features),
+        return call(
+            functools.partial(up_kernel, nz, ny, group, first, last, features),
             place,
-            [arrived[p] for p in group] + list(state) + weights,
+            blocks + list(state) + [anywhere(w_gate), anywhere(w_up), spare],
             outs,
             [pltpu.VMEM((len(group), units, cols), BF16)] * 2
-            + [pltpu.SemaphoreType.DMA((2 * (len(group) + len(ahead)),))],
+            + [pltpu.SemaphoreType.DMA((2 * len(group),))],
             limit=40,
             flops=4 * len(group) * slots * units * cols,
-            held=2 if ahead else 0,
         )
-        if ahead:
-            fetched["up"] = state[3:]
-        return state[:3]
-
-    def down(n, group, arrived, state):
+
+    def down(n, group, blocks, state):
         first, last = n == 0, n == len(groups) - 1
         ahead = groups[-1] if first else []
         outs = [sds((slots, cols), F32)]
@@ -757,7 +766,7 @@
         state = call(
             functools.partial(down_kernel, nz, ny, cap, group, ahead, first, last),
             place,
-            [arrived[p] for p in group] + list(state) + weights,
+            blocks + list(state) + weights,
             outs,
             []
             if last
@@ -774,7 +783,7 @@
         return state if last else state[:1]
 
     fetched = {}
-    if cols % 128:
+    if not fits:
         arrived = gather_z(rows_out)
         gather_y(arrived, [])
         order = jnp.stack([(z - dz) % nz * ny + (y - dy) % ny for dz, dy in places])

time: 180 us -> 178 us (0.989)
  waiting for transfers between devices: 73.6 us -> 70 us
    ppermute x17, waiting for transfers between devices: 14.3 us -> 12.2 us  [y_turn(): return lax.ppermute(a, 'seq', pairs)]
  transfers between devices with their start and end apart: 43 -> 43, of which waited for: 19 -> 18; matrix products, arithmetic and copies ran while one was open for 1% -> 1% of each run, Pallas kernels for 21% -> 21%
where the time goes in v6:
time: 178 us
  waiting for transfers between devices  70 us (39%)
  starting transfers between devices  51.6 us (29%)
  Pallas kernels  49.1 us (28%)
  local copies, waits for them, and re-layouts  5.26 us (3%)
    ppermute x16, waiting for transfers between devices, z_turn(): return lax.ppermute(a, 'seq', pairs)  49.2 us
    pallas_call x14, Pallas kernels, call(): pl.pallas_call(kernel, out_shape=list(outs), grid_spec=pltpu.PrefetchScal...  45.2 us
    ppermute x16, starting transfers between devices, z_turn(): return lax.ppermute(a, 'seq', pairs)  26.4 us
    ppermute x17, starting transfers between devices, y_turn(): return lax.ppermute(a, 'seq', pairs)  18.5 us
    ppermute x17, waiting for transfers between devices, y_turn(): return lax.ppermute(a, 'seq', pairs)  12.2 us
    ppermute x10, waiting for transfers between devices, swap(): return lax.ppermute(a, 'exp', [(p, p ^ r) for p in range(nz)])  8.51 us
    ppermute x10, starting transfers between devices, swap(): return lax.ppermute(a, 'exp', [(p, p ^ r) for p in range(nz)])  6.81 us
    unnamed x46, local copies, waits for them, and re-layouts  3.7 us
  transfers between devices with their start and end apart: 43, of which 18 were waited for; matrix products, arithmetic and copies ran while one was open for 1% of the time, Pallas kernels for 21%

profile of v6, /device:TPU:0, one launch (start us, length us, event | category | flops | bytes accessed | tf_op | source)
XLA Modules:
  0.0 177.6 jit_solution(8932705595135794143)
XLA Ops:
  0.7 2.0 %shard_map.230 = bf16[2,128,1024]{2,1,0:T(8,128)(2,1)} custom-call(bf16[128,2048]{1,0:T(8,128)(2,1)} %refs_0_.5, bf16[128,2048]{1,0:T(8,128)(2,1)} %refs_1_.5), custom_call_target="tpu_custom_call" | custom-call | tf_op jit(solution)/shard_map/pallas_call | solution.py:589
  2.8 3.0 %collective-permute-start = (bf16[2,128,1024]{2,1,0:T(8,128)(2,1)}, bf16[2,128,1024]{2,1,0:T(8,128)(2,1)S(1)}, u32[]{:S(2)}, u32[]{:S(2)}) collective-permute-start(bf16[2,128,1024]{2,1,0:T(8,128)(2,1)} %shard_map.230), channel_id=1, source_target_pairs={{0,4},{4,0},{8,12},{12,8},{16,20},{20,16},{24,28},{28,24},{1,5},{5... | collective-permute-start | bytes 1572872 | tf_op jit(solution)/shard_map/ppermute | solution.py:527
  5.8 1.5 collective-permute-start.3
  8.7 1.9 %shard_map.231 = bf16[2,128,1024]{2,1,0:T(8,128)(2,1)} custom-call(bf16[128,2048]{1,0:T(8,128)(2,1)} %refs_2_.2, bf16[128,2048]{1,0:T(8,128)(2,1)} %refs_3_.1), custom_call_target="tpu_custom_call" | custom-call | tf_op jit(solution)/shard_map/pallas_call | solution.py:591
  11.9 1.6 shard_map.232
  13.4 4.6 %collective-permute-done.1.refs_4_ = f32[16,128]{1,0:T(8,128)S(1)} collective-permute-done((f32[16,128]{1,0:T(8,128)}, f32[16,128]{1,0:T(8,128)S(1)}, u32[]{:S(2)}, u32[]{:S(2)}) %collective-permute-start.1) | collective-permute-done | bytes 8224 | tf_op jit(solution)/shard_map/ppermute | solution.py:527
  18.1 1.7 collective-permute-start.5
  19.8 3.0 %shard_map.233 = (bf16[272,128]{1,0:T(8,128)(2,1)S(1)}, bf16[272,128]{1,0:T(8,128)(2,1)S(1)}, bf16[272,128]{1,0:T(8,128)(2,1)S(1)}, bf16[272,128]{1,0:T(8,128)(2...) custom-call(s32[3]{0:T(128)S(1)} %pad_add_fusion.s, bf16[128,2048]{1,0:T(8,128)(2,1)S(1)} %copy-done.2, ...), custom_call_target="tpu_custom_call" | custom-call | flops 67108864 | bytes 1884160 | tf_op jit(solution)/shard_map/pallas_call | solution.py:47
  22.9 1.6 collective-permute-start.6
  24.5 2.6 %collective-permute-start.7 = (bf16[272,128]{1,0:T(8,128)(2,1)S(1)}, bf16[272,128]{1,0:T(8,128)(2,1)S(1)}, u32[]{:S(2)}, u32[]{:S(2)}) collective-permute-start(bf16[272,128]{1,0:T(8,128)(2,1)S(1)} %get-tuple-element.50), channel_id=1, source_target_pairs={{0,16},{4,20},{8,24},{12,28},{16,0},{20,4},{24,8},{28,12},{1,17},{... | collective-permute-start | bytes 208904 | tf_op jit(solution)/shard_map/ppermute | solution.py:523
  27.1 1.3 collective-permute-start.8
  29.7 1.7 collective-permute-done.7.refs_2_
  33.1 2.7 %collective-permute-start.11 = (bf16[256,128]{1,0:T(8,128)(2,1)S(1)}, bf16[256,128]{1,0:T(8,128)(2,1)S(1)}, u32[]{:S(2)}, u32[]{:S(2)}) collective-permute-start(bf16[256,128]{1,0:T(8,128)(2,1)S(1)} %get-tuple-element.55), channel_id=1, source_target_pairs={{0,24},{4,28},{8,0},{12,4},{16,8},{20,12},{24,16},{28,20},{1,25},{... | collective-permute-start | bytes 196616 | tf_op jit(solution)/shard_map/ppermute | solution.py:523
  35.9 2.7 %collective-permute-done.10.refs_8_ = bf16[256,128]{1,0:T(8,128)(2,1)S(1)} collective-permute-done((bf16[256,128]{1,0:T(8,128)(2,1)S(1)}, bf16[256,128]{1,0:T(8,128)(2,1)S(1)}, u32[]{:S(2)}, u32[]{:S(2)}) %collective-permute-start.10) | collective-permute-done | bytes 65568 | tf_op jit(solution)/shard_map/ppermute | solution.py:523
  38.6 3.2 %collective-permute-done.9.refs_7_ = bf16[256,128]{1,0:T(8,128)(2,1)S(1)} collective-permute-done((bf16[256,128]{1,0:T(8,128)(2,1)S(1)}, bf16[256,128]{1,0:T(8,128)(2,1)S(1)}, u32[]{:S(2)}, u32[]{:S(2)}) %collective-permute-start.9) | collective-permute-done | bytes 65568 | tf_op jit(solution)/shard_map/ppermute | solution.py:523
  41.9 3.4 %shard_map.235.refs_0_ = bf16[256,1024]{1,0:T(8,128)(2,1)S(1)} custom-call(s32[3]{0:T(128)S(1)} %pad_add_fusion.s, bf16[128,2048]{1,0:T(8,128)(2,1)S(1)} %copy-done.2, bf16[128,2048]{1,0:T(8,128)(2,1)S(1)} %copy-done.3, bf16[128,2048]{1,0:T(8,128)(2,1)S(1)} %copy-done.4, bf16[128,2048]{1,0:T(8,128)(2,1)S(1)} %copy-done.5, ...), custom_call_target="tpu_custom_call" | custom-call | flops 268435456 | bytes 3956736 | tf_op jit(solution)/shard_map/pallas_call | solution.py:47
  45.3 3.8 %collective-permute-start.17 = (bf16[256,1024]{1,0:T(8,128)(2,1)S(1)}, bf16[256,1024]{1,0:T(8,128)(2,1)S(1)}, u32[]{:S(2)}, u32[]{:S(2)}) collective-permute-start(bf16[256,1024]{1,0:T(8,128)(2,1)S(1)} %shard_map.235.refs_0_), channel_id=1, source_target_pairs={{0,24},{4,28},{8,0},{12,4},{16,8},{20,12},{24,16},{28,20},{1,25},{... | collective-permute-start | bytes 1572872 | tf_op jit(solution)/shard_map/ppermute | solution.py:523
  49.7 12.3 %collective-permute-done.12.refs_1_ = bf16[256,1024]{1,0:T(8,128)(2,1)S(1)} collective-permute-done((bf16[256,1024]{1,0:T(8,128)(2,1)S(1)}, bf16[256,1024]{1,0:T(8,128)(2,1)S(1)}, u32[]{:S(2)}, u32[]{:S(2)}) %collective-permute-start.12) | collective-permute-done | bytes 524320 | tf_op jit(solution)/shard_map/ppermute | solution.py:523
  62.5 5.9 %collective-permute-done.17.refs_2_ = bf16[256,1024]{1,0:T(8,128)(2,1)S(1)} collective-permute-done((bf16[256,1024]{1,0:T(8,128)(2,1)S(1)}, bf16[256,1024]{1,0:T(8,128)(2,1)S(1)}, u32[]{:S(2)}, u32[]{:S(2)}) %collective-permute-start.17) | collective-permute-done | bytes 524320 | tf_op jit(solution)/shard_map/ppermute | solution.py:523
  69.0 2.6 %collective-permute-start.13 = (bf16[128,1024]{1,0:T(8,128)(2,1)S(1)}, bf16[128,1024]{1,0:T(8,128)(2,1)S(1)}, u32[]{:S(2)}, u32[]{:S(2)}) collective-permute-start(bf16[128,1024]{1,0:T(8,128)(2,1)S(1)} %get-tuple-element.89), channel_id=1, source_target_pairs={{0,16},{4,20},{8,24},{12,28},{16,0},{20,4},{24,8},{28,12},{1,17},{... | collective-permute-start | bytes 786440 | tf_op jit(solution)/shard_map/ppermute | solution.py:523
  72.0 15.2 %collective-permute-done.13.refs_0_ = bf16[128,1024]{1,0:T(8,128)(2,1)S(1)} collective-permute-done((bf16[128,1024]{1,0:T(8,128)(2,1)S(1)}, bf16[128,1024]{1,0:T(8,128)(2,1)S(1)}, u32[]{:S(2)}, u32[]{:S(2)}) %collective-permute-start.13) | collective-permute-done | bytes 262176 | tf_op jit(solution)/shard_map/ppermute | solution.py:523
  87.9 4.6 %collective-permute-done.14.refs_1_ = bf16[128,1024]{1,0:T(8,128)(2,1)S(1)} collective-permute-done((bf16[128,1024]{1,0:T(8,128)(2,1)S(1)}, bf16[128,1024]{1,0:T(8,128)(2,1)S(1)}, u32[]{:S(2)}, u32[]{:S(2)}) %collective-permute-start.14) | collective-permute-done | bytes 262176 | tf_op jit(solution)/shard_map/ppermute | solution.py:523
  93.4 4.1 %shard_map.236 = (bf16[3,256,768]{2,1,0:T(8,128)(2,1)S(1)}, f32[320,768]{1,0:T(8,128)S(1)}) custom-call(s32[3]{0:T(128)S(1)} %pad_add_fusion.s, bf16[256,1024]{1,0:T(8,128)(2,1)S(1)} %shard_map.235.refs_0_, bf16[256,1024]{1,0:T(8,128)(2,1)S(1)} %collective-permute-done.12.refs_1_, bf16[256,1024]{1,0:T(8,128)(2,1)S(1)} %collective-permute-done.17.refs_2_, ...), custom_call_target="tpu_custom_call" | custom-call | flops 2415919104 | bytes 11610624 | tf_op jit(solution)/shard_map/pallas_call | solution.py:47
  97.5 2.9 %collective-permute-done.16.refs_3_ = bf16[128,1024]{1,0:T(8,128)(2,1)S(1)} collective-permute-done((bf16[128,1024]{1,0:T(8,128)(2,1)S(1)}, bf16[128,1024]{1,0:T(8,128)(2,1)S(1)}, u32[]{:S(2)}, u32[]{:S(2)}) %collective-permute-start.16) | collective-permute-done | bytes 262176 | tf_op jit(solution)/shard_map/ppermute | solution.py:527
  100.4 3.0 %shard_map.237 = (f32[160,768]{1,0:T(8,128)S(1)}, bf16[160,768]{1,0:T(8,128)(2,1)S(1)}, bf16[2,256,768]{2,1,0:T(8,128)(2,1)S(1)}, bf16[2,256,768]{2,1,0:T(8,128)(2,1)S(1)}) custom-call(s32[3]{0:T(128)S(1)} %pad_add_fusion.s, bf16[128,1024]{1,0:T(8,128)(2,1)S(1)} %collective-permute-done.13.refs_0_, bf16[128,1024]{1,0:T(8,128)(2,1)S(1)} %collective-permute-done.14.refs_1_, ...), custom_call_target="tpu_custom_call" | custom-call | flops 805306368 | bytes 12216832 | tf_op jit(solution)/shard_map/pallas_call | solution.py:47
  103.5 1.5 collective-permute-done.21
  105.1 1.5 collective-permute-start.22
  106.5 4.0 %collective-permute-done.22.received = bf16[80,768]{1,0:T(8,128)(2,1)S(1)} collective-permute-done((bf16[80,768]{1,0:T(8,128)(2,1)S(1)}, bf16[80,768]{1,0:T(8,128)(2,1)S(1)}, u32[]{:S(2)}, u32[]{:S(2)}) %collective-permute-start.22) | collective-permute-done | bytes 122912 | tf_op jit(solution)/shard_map/ppermute | solution.py:530
  111.7 1.8 collective-permute-start.23
  113.4 2.1 %collective-permute-start.25 = (bf16[80,768]{1,0:T(8,128)(2,1)S(1)}, bf16[80,768]{1,0:T(8,128)(2,1)S(1)}, u32[]{:S(2)}, u32[]{:S(2)}) collective-permute-start(bf16[80,768]{1,0:T(8,128)(2,1)S(1)} %shard_map.238.refs_0_), channel_id=1, source_target_pairs={{0,24},{4,28},{8,0},{12,4},{16,8},{20,12},{24,16},{28,20},{1,25},{... | collective-permute-start | bytes 368648 | tf_op jit(solution)/shard_map/ppermute | solution.py:523
  116.8 3.4 %shard_map.239 = (f32[80,1152]{1,0:T(8,128)S(1)}, f32[80,1152]{1,0:T(8,128)S(1)}, f32[1,768]{1,0:T(1,128)S(1)}) custom-call(s32[3]{0:T(128)S(1)} %pad_add_fusion.s, bf16[80,768]{1,0:T(8,128)(2,1)S(1)} %shard_map.238.refs_0_, bf16[1,1152,6144]{2,1,0:T(8,128)(2,1)} %refs_6_.8, bf16[1,1152,6144]{2,1,0:T(8,128)(2,1)} %refs_7_.7, ...), custom_call_target="tpu_custom_call" | custom-call | flops 283115520 | bytes 29215744 | tf_op jit(solution)/shard_map/pallas_call | solution.py:47
  120.2 2.0 %collective-permute-done.27.refs_3_ = bf16[80,768]{1,0:T(8,128)(2,1)S(1)} collective-permute-done((bf16[80,768]{1,0:T(8,128)(2,1)S(1)}, bf16[80,768]{1,0:T(8,128)(2,1)S(1)}, u32[]{:S(2)}, u32[]{:S(2)}) %collective-permute-start.27) | collective-permute-done | bytes 122912 | tf_op jit(solution)/shard_map/ppermute | solution.py:523
  122.2 1.5 collective-permute-start.28
  124.2 1.5 collective-permute-start.26
  125.7 7.0 %shard_map.240 = (f32[80,1152]{1,0:T(8,128)S(1)}, f32[80,1152]{1,0:T(8,128)S(1)}, f32[1,768]{1,0:T(1,128)S(1)}) custom-call(s32[3]{0:T(128)S(1)} %pad_add_fusion.s, bf16[80,768]{1,0:T(8,128)(2,1)S(1)} %collective-permute-done.29.refs_0_, bf16[80,768]{1,0:T(8,128)(2,1)S(1)} %collective-permute-done.23.refs_1_, ...), custom_call_target="tpu_custom_call" | custom-call | flops 1132462080 | bytes 30324736 | tf_op jit(solution)/shard_map/pallas_call | solution.py:47
  132.7 5.9 %shard_map.241 = (bf16[80,1152]{1,0:T(8,128)(2,1)S(1)}, f32[80,128]{1,0:T(8,128)S(1)}) custom-call(s32[3]{0:T(128)S(1)} %pad_add_fusion.s, bf16[80,768]{1,0:T(8,128)(2,1)S(1)} %collective-permute-done.24.refs_0_, bf16[80,768]{1,0:T(8,128)(2,1)S(1)} %collective-permute-done.26.refs_1_, bf16[80,768]{1,0:T(8,128)(2,1)S(1)} %collective-permute-done.28.refs_2_, ...), custom_call_target="tpu_custom_call" | custom-call | flops 849346560 | bytes 29686784 | tf_op jit(solution)/shard_map/pallas_call | solution.py:47
  138.6 2.8 %collective-permute-start.34 = (bf16[80,1152]{1,0:T(8,128)(2,1)S(1)}, bf16[80,1152]{1,0:T(8,128)(2,1)S(1)}, u32[]{:S(2)}, u32[]{:S(2)}) collective-permute-start(bf16[80,1152]{1,0:T(8,128)(2,1)S(1)} %get-tuple-element.70.refs_0_), channel_id=1, source_target_pairs={{0,16},{4,20},{8,24},{12,28},{16,0},{20,4},{24,8},{28,12},{1,17},{... | collective-permute-start | bytes 552968 | tf_op jit(solution)/shard_map/ppermute | solution.py:523
  141.4 3.8 %collective-permute-start.32 = (bf16[80,1152]{1,0:T(8,128)(2,1)S(1)}, bf16[80,1152]{1,0:T(8,128)(2,1)S(1)}, u32[]{:S(2)}, u32[]{:S(2)}) collective-permute-start(bf16[80,1152]{1,0:T(8,128)(2,1)S(1)} %get-tuple-element.70.refs_0_), channel_id=1, source_target_pairs={{0,24},{4,28},{8,0},{12,4},{16,8},{20,12},{24,16},{28,20},{1,25},{... | collective-permute-start | bytes 552968 | tf_op jit(solution)/shard_map/ppermute | solution.py:523
  146.3 1.4 collective-permute-start.41
  149.0 3.9 %shard_map.242 = (f32[80,768]{1,0:T(8,128)S(1)}, bf16[3,1152,768]{2,1,0:T(8,128)(2,1)S(1)}) custom-call(s32[3]{0:T(128)S(1)} %pad_add_fusion.s, bf16[80,1152]{1,0:T(8,128)(2,1)S(1)} %get-tuple-element.70.refs_0_, bf16[1,9216,768]{2,1,0:T(8,128)(2,1)} %refs_5_.4), custom_call_target="tpu_custom_call" | custom-call | flops 141557760 | bytes 19894272 | tf_op jit(solution)/shard_map/pallas_call | solution.py:47
  152.9 2.4 %copy-done.1 = bf16[3,1152,768]{2,1,0:T(8,128)(2,1)} copy-done((bf16[3,1152,768]{2,1,0:T(8,128)(2,1)}, bf16[3,1152,768]{2,1,0:T(8,128)(2,1)S(1)}, u32[]{:S(2)}) %copy-start.1) | copy-done | bytes 5308440
  158.1 1.4 collective-permute-start.42
  159.5 4.4 %shard_map.243.refs_3_ = f32[80,768]{1,0:T(8,128)S(1)} custom-call(s32[3]{0:T(128)S(1)} %pad_add_fusion.s, bf16[80,1152]{1,0:T(8,128)(2,1)S(1)} %collective-permute-done.36.refs_0_, bf16[80,1152]{1,0:T(8,128)(2,1)S(1)} %collective-permute-done.30.refs_1_, bf16[80,1152]{1,0:T(8,128)(2,1)S(1)} %collective-permute-done.32.refs_2_, ...), custom_call_target="tpu_custom_call" | custom-call | flops 566231040 | bytes 15384576 | tf_op jit(solution)/shard_map/pallas_call | solution.py:47
  163.9 2.7 %collective-permute-done.31.refs_0_ = bf16[80,1152]{1,0:T(8,128)(2,1)S(1)} collective-permute-done((bf16[80,1152]{1,0:T(8,128)(2,1)S(1)}, bf16[80,1152]{1,0:T(8,128)(2,1)S(1)}, u32[]{:S(2)}, u32[]{:S(2)}) %collective-permute-start.31) | collective-permute-done | bytes 184352 | tf_op jit(solution)/shard_map/ppermute | solution.py:527
  166.5 2.0 %collective-permute-done.33.refs_1_ = bf16[80,1152]{1,0:T(8,128)(2,1)S(1)} collective-permute-done((bf16[80,1152]{1,0:T(8,128)(2,1)S(1)}, bf16[80,1152]{1,0:T(8,128)(2,1)S(1)}, u32[]{:S(2)}, u32[]{:S(2)}) %collective-permute-start.33) | collective-permute-done | bytes 184352 | tf_op jit(solution)/shard_map/ppermute | solution.py:527
  168.6 1.8 %shard_map.244 = (bf16[32,768]{1,0:T(8,128)(2,1)S(1)}, bf16[32,768]{1,0:T(8,128)(2,1)S(1)}, bf16[32,768]{1,0:T(8,128)(2,1)S(1)}, bf16[32,768]{1,0:T(8,128)(2,1)S(1)}) custom-call(s32[3]{0:T(128)S(1)} %pad_add_fusion.s, bf16[80,1152]{1,0:T(8,128)(2,1)S(1)} %collective-permute-done.31.refs_0_, bf16[80,1152]{1,0:T(8,128)(2,1)S(1)} %collective-permute-done.33.refs_1_, ...), custom_call_target="tpu_custom_call" | custom-call | flops 424673280 | bytes 6345152 | tf_op jit(solution)/shard_map/pallas_call | solution.py:47
  172.4 2.3 %collective-permute-done.38.refs_2_ = bf16[32,768]{1,0:T(8,128)(2,1)S(1)} collective-permute-done((bf16[32,768]{1,0:T(8,128)(2,1)S(1)}, bf16[32,768]{1,0:T(8,128)(2,1)S(1)}, u32[]{:S(2)}, u32[]{:S(2)}) %collective-permute-start.38) | collective-permute-done | bytes 49184 | tf_op jit(solution)/shard_map/ppermute | solution.py:530
  175.4 2.0 %shard_map.245 = bf16[256,768]{1,0:T(8,128)(2,1)} custom-call(s32[3]{0:T(128)S(1)} %pad_add_fusion.s, bf16[32,768]{1,0:T(8,128)(2,1)S(1)} %get-tuple-element.75.refs_0_, bf16[32,768]{1,0:T(8,128)(2,1)S(1)} %collective-permute-done.37.refs_1_, bf16[32,768]{1,0:T(8,128)(2,1)S(1)} %collective-permute-done.38.refs_2_, ...), custom_call_target="tpu_custom_call" | custom-call | bytes 1778688 | tf_op jit(solution)/shard_map/pallas_call | solution.py:47
  (110 shorter events, 20.5 us)
Async XLA Ops:
  0.7 41.1 %copy-start.4 = (bf16[128,2048]{1,0:T(8,128)(2,1)S(1)}, bf16[128,2048]{1,0:T(8,128)(2,1)}, u32[]{:S(2)}) copy-start(bf16[128,2048]{1,0:T(8,128)(2,1)} %refs_2_.2) | copy-start | bytes 1572868
  0.7 41.1 %copy-start.5 = (bf16[128,2048]{1,0:T(8,128)(2,1)S(1)}, bf16[128,2048]{1,0:T(8,128)(2,1)}, u32[]{:S(2)}) copy-start(bf16[128,2048]{1,0:T(8,128)(2,1)} %refs_3_.1) | copy-start | bytes 1572868
  2.8 15.3 %collective-permute-start = (bf16[2,128,1024]{2,1,0:T(8,128)(2,1)}, bf16[2,128,1024]{2,1,0:T(8,128)(2,1)S(1)}, u32[]{:S(2)}, u32[]{:S(2)}) collective-permute-start(bf16[2,128,1024]{2,1,0:T(8,128)(2,1)} %shard_map.230), channel_id=1, source_target_pairs={{0,4},{4,0},{8,12},{12,8},{16,20},{20,16},{24,28},{28,24},{1,5},{5... | collective-permute-start | bytes 1572872 | tf_op jit(solution)/shard_map/ppermute | solution.py:527
  5.8 4.8 %collective-permute-start.2 = (s32[2,256]{1,0:T(2,128)}, s32[2,256]{1,0:T(2,128)S(1)}, u32[]{:S(2)}, u32[]{:S(2)}) collective-permute-start(s32[2,256]{1,0:T(2,128)} %bitcast.17), channel_id=1, source_target_pairs={{0,1},{1,0},{2,3},{3,2},{4,5},{5,4},{6,7},{7,6},{8,9},{9,8},{10,11... | collective-permute-start | bytes 6152 | tf_op jit(solution)/shard_map/ppermute | solution.py:530
  5.8 4.8 %collective-permute-start.3 = (s32[2,256]{1,0:T(2,128)}, s32[2,256]{1,0:T(2,128)S(1)}, u32[]{:S(2)}, u32[]{:S(2)}) collective-permute-start(s32[2,256]{1,0:T(2,128)} %bitcast.18), channel_id=1, source_target_pairs={{0,2},{1,3},{2,0},{3,1},{4,6},{5,7},{6,4},{7,5},{8,10},{9,11},{10,... | collective-permute-start | bytes 6152 | tf_op jit(solution)/shard_map/ppermute | solution.py:530
  7.3 3.3 %collective-permute-start.4 = (s32[2,256]{1,0:T(2,128)}, s32[2,256]{1,0:T(2,128)S(1)}, u32[]{:S(2)}, u32[]{:S(2)}) collective-permute-start(s32[2,256]{1,0:T(2,128)} %bitcast.19), channel_id=1, source_target_pairs={{0,3},{1,2},{2,1},{3,0},{4,7},{5,6},{6,5},{7,4},{8,11},{9,10},{10,... | collective-permute-start | bytes 6152 | tf_op jit(solution)/shard_map/ppermute | solution.py:530
  7.6 10.4 %collective-permute-start.1 = (f32[16,128]{1,0:T(8,128)}, f32[16,128]{1,0:T(8,128)S(1)}, u32[]{:S(2)}, u32[]{:S(2)}) collective-permute-start(f32[16,128]{1,0:T(8,128)} %bitcast.14), channel_id=1, source_target_pairs={{0,4},{4,0},{8,12},{12,8},{16,20},{20,16},{24,28},{28,24},{1,5},{5... | collective-permute-start | bytes 24584 | tf_op jit(solution)/shard_map/ppermute | solution.py:527
  18.1 23.7 %collective-permute-start.5 = (bf16[2,128,1024]{2,1,0:T(8,128)(2,1)}, bf16[2,128,1024]{2,1,0:T(8,128)(2,1)S(1)}, u32[]{:S(2)}, u32[]{:S(2)}) collective-permute-start(bf16[2,128,1024]{2,1,0:T(8,128)(2,1)} %shard_map.231), channel_id=1, source_target_pairs={{0,4},{4,0},{8,12},{12,8},{16,20},{20,16},{24,28},{28,24},{1,5},{5... | collective-permute-start | bytes 1572872 | tf_op jit(solution)/shard_map/ppermute | solution.py:527
  22.9 70.5 %copy-start = (bf16[2048,768]{1,0:T(8,128)(2,1)S(1)}, bf16[2048,768]{1,0:T(8,128)(2,1)}, u32[]{:S(2)}) copy-start(bf16[2048,768]{1,0:T(8,128)(2,1)} %refs_5_.3) | copy-start | bytes 9437188
  22.9 70.5 %copy-start.8 = (s32[320,1]{1,0:T(8,128)S(1)}, s32[320,1]{1,0:T(8,128)}, u32[]{:S(2)}) copy-start(s32[320,1]{1,0:T(8,128)} %constant.73.clone.refs_8_.refs_6_) | copy-start | bytes 3844
  22.9 70.5 %copy-start.9 = (s32[320,1]{1,0:T(8,128)S(1)}, s32[320,1]{1,0:T(8,128)}, u32[]{:S(2)}) copy-start(s32[320,1]{1,0:T(8,128)} %constant.74.clone.refs_9_.refs_7_) | copy-start | bytes 3844
  22.9 6.8 %collective-permute-start.6 = (bf16[272,128]{1,0:T(8,128)(2,1)S(1)}, bf16[272,128]{1,0:T(8,128)(2,1)S(1)}, u32[]{:S(2)}, u32[]{:S(2)}) collective-permute-start(bf16[272,128]{1,0:T(8,128)(2,1)S(1)} %get-tuple-element.49), channel_id=1, source_target_pairs={{0,8},{4,12},{8,16},{12,20},{16,24},{20,28},{24,0},{28,4},{1,9},{5... | collective-permute-start | bytes 208904 | tf_op jit(solution)/shard_map/ppermute | solution.py:523
  24.5 6.9 %collective-permute-start.7 = (bf16[272,128]{1,0:T(8,128)(2,1)S(1)}, bf16[272,128]{1,0:T(8,128)(2,1)S(1)}, u32[]{:S(2)}, u32[]{:S(2)}) collective-permute-start(bf16[272,128]{1,0:T(8,128)(2,1)S(1)} %get-tuple-element.50), channel_id=1, source_target_pairs={{0,16},{4,20},{8,24},{12,28},{16,0},{20,4},{24,8},{28,12},{1,17},{... | collective-permute-start | bytes 208904 | tf_op jit(solution)/shard_map/ppermute | solution.py:523
  27.1 4.8 %collective-permute-start.8 = (bf16[272,128]{1,0:T(8,128)(2,1)S(1)}, bf16[272,128]{1,0:T(8,128)(2,1)S(1)}, u32[]{:S(2)}, u32[]{:S(2)}) collective-permute-start(bf16[272,128]{1,0:T(8,128)(2,1)S(1)} %get-tuple-element.51), channel_id=1, source_target_pairs={{0,24},{4,28},{8,0},{12,4},{16,8},{20,12},{24,16},{28,20},{1,25},{... | collective-permute-start | bytes 208904 | tf_op jit(solution)/shard_map/ppermute | solution.py:523
  32.6 6.0 %collective-permute-start.10 = (bf16[256,128]{1,0:T(8,128)(2,1)S(1)}, bf16[256,128]{1,0:T(8,128)(2,1)S(1)}, u32[]{:S(2)}, u32[]{:S(2)}) collective-permute-start(bf16[256,128]{1,0:T(8,128)(2,1)S(1)} %get-tuple-element.54), channel_id=1, source_target_pairs={{0,16},{4,20},{8,24},{12,28},{16,0},{20,4},{24,8},{28,12},{1,17},{... | collective-permute-start | bytes 196616 | tf_op jit(solution)/shard_map/ppermute | solution.py:523
  33.1 5.5 %collective-permute-start.11 = (bf16[256,128]{1,0:T(8,128)(2,1)S(1)}, bf16[256,128]{1,0:T(8,128)(2,1)S(1)}, u32[]{:S(2)}, u32[]{:S(2)}) collective-permute-start(bf16[256,128]{1,0:T(8,128)(2,1)S(1)} %get-tuple-element.55), channel_id=1, source_target_pairs={{0,24},{4,28},{8,0},{12,4},{16,8},{20,12},{24,16},{28,20},{1,25},{... | collective-permute-start | bytes 196616 | tf_op jit(solution)/shard_map/ppermute | solution.py:523
  35.8 6.1 %collective-permute-start.9 = (bf16[256,128]{1,0:T(8,128)(2,1)S(1)}, bf16[256,128]{1,0:T(8,128)(2,1)S(1)}, u32[]{:S(2)}, u32[]{:S(2)}) collective-permute-start(bf16[256,128]{1,0:T(8,128)(2,1)S(1)} %get-tuple-element.53), channel_id=1, source_target_pairs={{0,8},{4,12},{8,16},{12,20},{16,24},{20,28},{24,0},{28,4},{1,9},{5... | collective-permute-start | bytes 196616 | tf_op jit(solution)/shard_map/ppermute | solution.py:523
  45.3 16.7 %collective-permute-start.12 = (bf16[256,1024]{1,0:T(8,128)(2,1)S(1)}, bf16[256,1024]{1,0:T(8,128)(2,1)S(1)}, u32[]{:S(2)}, u32[]{:S(2)}) collective-permute-start(bf16[256,1024]{1,0:T(8,128)(2,1)S(1)} %shard_map.235.refs_0_), channel_id=1, source_target_pairs={{0,8},{4,12},{8,16},{12,20},{16,24},{20,28},{24,0},{28,4},{1,9},{5... | collective-permute-start | bytes 1572872 | tf_op jit(solution)/shard_map/ppermute | solution.py:523
  45.3 23.1 %collective-permute-start.17 = (bf16[256,1024]{1,0:T(8,128)(2,1)S(1)}, bf16[256,1024]{1,0:T(8,128)(2,1)S(1)}, u32[]{:S(2)}, u32[]{:S(2)}) collective-permute-start(bf16[256,1024]{1,0:T(8,128)(2,1)S(1)} %shard_map.235.refs_0_), channel_id=1, source_target_pairs={{0,24},{4,28},{8,0},{12,4},{16,8},{20,12},{24,16},{28,20},{1,25},{... | collective-permute-start | bytes 1572872 | tf_op jit(solution)/shard_map/ppermute | solution.py:523
  49.2 44.2 %collective-permute-start.18 = (bf16[256,1024]{1,0:T(8,128)(2,1)S(1)}, bf16[256,1024]{1,0:T(8,128)(2,1)S(1)}, u32[]{:S(2)}, u32[]{:S(2)}) collective-permute-start(bf16[256,1024]{1,0:T(8,128)(2,1)S(1)} %shard_map.235.refs_0_), channel_id=1, source_target_pairs={{0,4},{4,0},{8,12},{12,8},{16,20},{20,16},{24,28},{28,24},{1,5},{5... | collective-permute-start | bytes 1572872 | tf_op jit(solution)/shard_map/ppermute | solution.py:527
  62.0 31.4 %collective-permute-start.19 = (bf16[256,1024]{1,0:T(8,128)(2,1)S(1)}, bf16[256,1024]{1,0:T(8,128)(2,1)S(1)}, u32[]{:S(2)}, u32[]{:S(2)}) collective-permute-start(bf16[256,1024]{1,0:T(8,128)(2,1)S(1)} %collective-permute-done.12.refs_1_), channel_id=1, source_target_pairs={{0,4},{4,0},{8,12},{12,8},{16,20},{20,16},{24,28},{28,24},{1,5},{5... | collective-permute-start | bytes 1572872 | tf_op jit(solution)/shard_map/ppermute | solution.py:527
  68.4 25.0 %collective-permute-start.20 = (bf16[256,1024]{1,0:T(8,128)(2,1)S(1)}, bf16[256,1024]{1,0:T(8,128)(2,1)S(1)}, u32[]{:S(2)}, u32[]{:S(2)}) collective-permute-start(bf16[256,1024]{1,0:T(8,128)(2,1)S(1)} %collective-permute-done.17.refs_2_), channel_id=1, source_target_pairs={{0,4},{4,0},{8,12},{12,8},{16,20},{20,16},{24,28},{28,24},{1,5},{5... | collective-permute-start | bytes 1572872 | tf_op jit(solution)/shard_map/ppermute | solution.py:527
  69.0 18.2 %collective-permute-start.13 = (bf16[128,1024]{1,0:T(8,128)(2,1)S(1)}, bf16[128,1024]{1,0:T(8,128)(2,1)S(1)}, u32[]{:S(2)}, u32[]{:S(2)}) collective-permute-start(bf16[128,1024]{1,0:T(8,128)(2,1)S(1)} %get-tuple-element.89), channel_id=1, source_target_pairs={{0,16},{4,20},{8,24},{12,28},{16,0},{20,4},{24,8},{28,12},{1,17},{... | collective-permute-start | bytes 786440 | tf_op jit(solution)/shard_map/ppermute | solution.py:523
  71.6 20.8 %collective-permute-start.14 = (bf16[128,1024]{1,0:T(8,128)(2,1)S(1)}, bf16[128,1024]{1,0:T(8,128)(2,1)S(1)}, u32[]{:S(2)}, u32[]{:S(2)}) collective-permute-start(bf16[128,1024]{1,0:T(8,128)(2,1)S(1)} %get-tuple-element.88), channel_id=1, source_target_pairs={{0,16},{4,20},{8,24},{12,28},{16,0},{20,4},{24,8},{28,12},{1,17},{... | collective-permute-start | bytes 786440 | tf_op jit(solution)/shard_map/ppermute | solution.py:523
  87.2 10.4 %collective-permute-start.15 = (bf16[128,1024]{1,0:T(8,128)(2,1)S(1)}, bf16[128,1024]{1,0:T(8,128)(2,1)S(1)}, u32[]{:S(2)}, u32[]{:S(2)}) collective-permute-start(bf16[128,1024]{1,0:T(8,128)(2,1)S(1)} %collective-permute-done.13.refs_0_), channel_id=1, source_target_pairs={{0,4},{4,0},{8,12},{12,8},{16,20},{20,16},{24,28},{28,24},{1,5},{5... | collective-permute-start | bytes 786440 | tf_op jit(solution)/shard_map/ppermute | solution.py:527
  92.4 8.0 %collective-permute-start.16 = (bf16[128,1024]{1,0:T(8,128)(2,1)S(1)}, bf16[128,1024]{1,0:T(8,128)(2,1)S(1)}, u32[]{:S(2)}, u32[]{:S(2)}) collective-permute-start(bf16[128,1024]{1,0:T(8,128)(2,1)S(1)} %collective-permute-done.14.refs_1_), channel_id=1, source_target_pairs={{0,4},{4,0},{8,12},{12,8},{16,20},{20,16},{24,28},{28,24},{1,5},{5... | collective-permute-start | bytes 786440 | tf_op jit(solution)/shard_map/ppermute | solution.py:527
  103.4 1.6 collective-permute-start.21
  105.1 5.4 %collective-permute-start.22 = (bf16[80,768]{1,0:T(8,128)(2,1)S(1)}, bf16[80,768]{1,0:T(8,128)(2,1)S(1)}, u32[]{:S(2)}, u32[]{:S(2)}) collective-permute-start(bf16[80,768]{1,0:T(8,128)(2,1)S(1)} %get-tuple-element.86), channel_id=1, source_target_pairs={{0,2},{1,3},{2,0},{3,1},{4,6},{5,7},{6,4},{7,5},{8,10},{9,11},{10,... | collective-permute-start | bytes 368648 | tf_op jit(solution)/shard_map/ppermute | solution.py:530
  111.5 33.7 %collective-permute-start.40 = (bf16[2,256,768]{2,1,0:T(8,128)(2,1)S(1)}, bf16[2,256,768]{2,1,0:T(8,128)(2,1)S(1)}, u32[]{:S(2)}, u32[]{:S(2)}) collective-permute-start(bf16[2,256,768]{2,1,0:T(8,128)(2,1)S(1)} %get-tuple-element.81), channel_id=1, source_target_pairs={{0,1},{1,0},{2,3},{3,2},{4,5},{5,4},{6,7},{7,6},{8,9},{9,8},{10,11... | collective-permute-start | bytes 2359304 | tf_op jit(solution)/shard_map/ppermute | solution.py:530
  111.6 10.6 %collective-permute-start.27 = (bf16[80,768]{1,0:T(8,128)(2,1)S(1)}, bf16[80,768]{1,0:T(8,128)(2,1)S(1)}, u32[]{:S(2)}, u32[]{:S(2)}) collective-permute-start(bf16[80,768]{1,0:T(8,128)(2,1)S(1)} %shard_map.238.refs_0_), channel_id=1, source_target_pairs={{0,16},{4,20},{8,24},{12,28},{16,0},{20,4},{24,8},{28,12},{1,17},{... | collective-permute-start | bytes 368648 | tf_op jit(solution)/shard_map/ppermute | solution.py:523
  111.7 12.0 %collective-permute-start.23 = (bf16[80,768]{1,0:T(8,128)(2,1)S(1)}, bf16[80,768]{1,0:T(8,128)(2,1)S(1)}, u32[]{:S(2)}, u32[]{:S(2)}) collective-permute-start(bf16[80,768]{1,0:T(8,128)(2,1)S(1)} %shard_map.238.refs_0_), channel_id=1, source_target_pairs={{0,8},{4,12},{8,16},{12,20},{16,24},{20,28},{24,0},{28,4},{1,9},{5... | collective-permute-start | bytes 368648 | tf_op jit(solution)/shard_map/ppermute | solution.py:523
  113.4 10.8 %collective-permute-start.25 = (bf16[80,768]{1,0:T(8,128)(2,1)S(1)}, bf16[80,768]{1,0:T(8,128)(2,1)S(1)}, u32[]{:S(2)}, u32[]{:S(2)}) collective-permute-start(bf16[80,768]{1,0:T(8,128)(2,1)S(1)} %shard_map.238.refs_0_), channel_id=1, source_target_pairs={{0,24},{4,28},{8,0},{12,4},{16,8},{20,12},{24,16},{28,20},{1,25},{... | collective-permute-start | bytes 368648 | tf_op jit(solution)/shard_map/ppermute | solution.py:523
  115.6 10.1 %collective-permute-start.29 = (bf16[80,768]{1,0:T(8,128)(2,1)S(1)}, bf16[80,768]{1,0:T(8,128)(2,1)S(1)}, u32[]{:S(2)}, u32[]{:S(2)}) collective-permute-start(bf16[80,768]{1,0:T(8,128)(2,1)S(1)} %shard_map.238.refs_0_), channel_id=1, source_target_pairs={{0,4},{4,0},{8,12},{12,8},{16,20},{20,16},{24,28},{28,24},{1,5},{5... | collective-permute-start | bytes 368648 | tf_op jit(solution)/shard_map/ppermute | solution.py:527
  122.2 10.5 %collective-permute-start.28 = (bf16[80,768]{1,0:T(8,128)(2,1)S(1)}, bf16[80,768]{1,0:T(8,128)(2,1)S(1)}, u32[]{:S(2)}, u32[]{:S(2)}) collective-permute-start(bf16[80,768]{1,0:T(8,128)(2,1)S(1)} %collective-permute-done.27.refs_3_), channel_id=1, source_target_pairs={{0,4},{4,0},{8,12},{12,8},{16,20},{20,16},{24,28},{28,24},{1,5},{5... | collective-permute-start | bytes 368648 | tf_op jit(solution)/shard_map/ppermute | solution.py:527
  123.7 9.1 %collective-permute-start.24 = (bf16[80,768]{1,0:T(8,128)(2,1)S(1)}, bf16[80,768]{1,0:T(8,128)(2,1)S(1)}, u32[]{:S(2)}, u32[]{:S(2)}) collective-permute-start(bf16[80,768]{1,0:T(8,128)(2,1)S(1)} %collective-permute-done.23.refs_1_), channel_id=1, source_target_pairs={{0,4},{4,0},{8,12},{12,8},{16,20},{20,16},{24,28},{28,24},{1,5},{5... | collective-permute-start | bytes 368648 | tf_op jit(solution)/shard_map/ppermute | solution.py:527
  124.2 8.5 %collective-permute-start.26 = (bf16[80,768]{1,0:T(8,128)(2,1)S(1)}, bf16[80,768]{1,0:T(8,128)(2,1)S(1)}, u32[]{:S(2)}, u32[]{:S(2)}) collective-permute-start(bf16[80,768]{1,0:T(8,128)(2,1)S(1)} %collective-permute-done.25.refs_2_), channel_id=1, source_target_pairs={{0,4},{4,0},{8,12},{12,8},{16,20},{20,16},{24,28},{28,24},{1,5},{5... | collective-permute-start | bytes 368648 | tf_op jit(solution)/shard_map/ppermute | solution.py:527
  138.6 16.6 %collective-permute-start.34 = (bf16[80,1152]{1,0:T(8,128)(2,1)S(1)}, bf16[80,1152]{1,0:T(8,128)(2,1)S(1)}, u32[]{:S(2)}, u32[]{:S(2)}) collective-permute-start(bf16[80,1152]{1,0:T(8,128)(2,1)S(1)} %get-tuple-element.70.refs_0_), channel_id=1, source_target_pairs={{0,16},{4,20},{8,24},{12,28},{16,0},{20,4},{24,8},{28,12},{1,17},{... | collective-permute-start | bytes 552968 | tf_op jit(solution)/shard_map/ppermute | solution.py:523
  141.4 14.5 %collective-permute-start.30 = (bf16[80,1152]{1,0:T(8,128)(2,1)S(1)}, bf16[80,1152]{1,0:T(8,128)(2,1)S(1)}, u32[]{:S(2)}, u32[]{:S(2)}) collective-permute-start(bf16[80,1152]{1,0:T(8,128)(2,1)S(1)} %get-tuple-element.70.refs_0_), channel_id=1, source_target_pairs={{0,8},{4,12},{8,16},{12,20},{16,24},{20,28},{24,0},{28,4},{1,9},{5... | collective-permute-start | bytes 552968 | tf_op jit(solution)/shard_map/ppermute | solution.py:523
  141.4 15.8 %collective-permute-start.32 = (bf16[80,1152]{1,0:T(8,128)(2,1)S(1)}, bf16[80,1152]{1,0:T(8,128)(2,1)S(1)}, u32[]{:S(2)}, u32[]{:S(2)}) collective-permute-start(bf16[80,1152]{1,0:T(8,128)(2,1)S(1)} %get-tuple-element.70.refs_0_), channel_id=1, source_target_pairs={{0,24},{4,28},{8,0},{12,4},{16,8},{20,12},{24,16},{28,20},{1,25},{... | collective-permute-start | bytes 552968 | tf_op jit(solution)/shard_map/ppermute | solution.py:523
  146.3 29.1 %collective-permute-start.41 = (bf16[1,256,768]{2,1,0:T(8,128)(2,1)}, bf16[1,256,768]{2,1,0:T(8,128)(2,1)S(1)}, u32[]{:S(2)}, u32[]{:S(2)}) collective-permute-start(bf16[1,256,768]{2,1,0:T(8,128)(2,1)} %get-tuple-element.84), channel_id=1, source_target_pairs={{0,2},{1,3},{2,0},{3,1},{4,6},{5,7},{6,4},{7,5},{8,10},{9,11},{10,... | collective-permute-start | bytes 1179656 | tf_op jit(solution)/shard_map/ppermute | solution.py:530
  147.7 10.4 %collective-permute-start.36 = (bf16[80,1152]{1,0:T(8,128)(2,1)S(1)}, bf16[80,1152]{1,0:T(8,128)(2,1)S(1)}, u32[]{:S(2)}, u32[]{:S(2)}) collective-permute-start(bf16[80,1152]{1,0:T(8,128)(2,1)S(1)} %get-tuple-element.70.refs_0_), channel_id=1, source_target_pairs={{0,4},{4,0},{8,12},{12,8},{16,20},{20,16},{24,28},{28,24},{1,5},{5... | collective-permute-start | bytes 552968 | tf_op jit(solution)/shard_map/ppermute | solution.py:527
  155.2 8.6 %collective-permute-start.35 = (bf16[80,1152]{1,0:T(8,128)(2,1)S(1)}, bf16[80,1152]{1,0:T(8,128)(2,1)S(1)}, u32[]{:S(2)}, u32[]{:S(2)}) collective-permute-start(bf16[80,1152]{1,0:T(8,128)(2,1)S(1)} %collective-permute-done.34.refs_3_), channel_id=1, source_target_pairs={{0,4},{4,0},{8,12},{12,8},{16,20},{20,16},{24,28},{28,24},{1,5},{5... | collective-permute-start | bytes 552968 | tf_op jit(solution)/shard_map/ppermute | solution.py:527
  156.0 10.6 %collective-permute-start.31 = (bf16[80,1152]{1,0:T(8,128)(2,1)S(1)}, bf16[80,1152]{1,0:T(8,128)(2,1)S(1)}, u32[]{:S(2)}, u32[]{:S(2)}) collective-permute-start(bf16[80,1152]{1,0:T(8,128)(2,1)S(1)} %collective-permute-done.30.refs_1_), channel_id=1, source_target_pairs={{0,4},{4,0},{8,12},{12,8},{16,20},{20,16},{24,28},{28,24},{1,5},{5... | collective-permute-start | bytes 552968 | tf_op jit(solution)/shard_map/ppermute | solution.py:527
  157.3 11.2 %collective-permute-start.33 = (bf16[80,1152]{1,0:T(8,128)(2,1)S(1)}, bf16[80,1152]{1,0:T(8,128)(2,1)S(1)}, u32[]{:S(2)}, u32[]{:S(2)}) collective-permute-start(bf16[80,1152]{1,0:T(8,128)(2,1)S(1)} %collective-permute-done.32.refs_2_), channel_id=1, source_target_pairs={{0,4},{4,0},{8,12},{12,8},{16,20},{20,16},{24,28},{28,24},{1,5},{5... | collective-permute-start | bytes 552968 | tf_op jit(solution)/shard_map/ppermute | solution.py:527
  158.1 14.2 %collective-permute-start.42 = (f32[8,16,128]{2,1,0:T(8,128)S(1)}, f32[8,16,128]{2,1,0:T(8,128)S(1)}, u32[]{:S(2)}, u32[]{:S(2)}) collective-permute-start(f32[8,16,128]{2,1,0:T(8,128)S(1)} %get-tuple-element.90), channel_id=1, source_target_pairs={{0,4},{4,0},{8,12},{12,8},{16,20},{20,16},{24,28},{28,24},{1,5},{5... | collective-permute-start | bytes 196616 | tf_op jit(solution)/shard_map/ppermute | solution.py:527
  170.4 2.0 %collective-permute-start.37 = (bf16[32,768]{1,0:T(8,128)(2,1)S(1)}, bf16[32,768]{1,0:T(8,128)(2,1)S(1)}, u32[]{:S(2)}, u32[]{:S(2)}) collective-permute-start(bf16[32,768]{1,0:T(8,128)(2,1)S(1)} %get-tuple-element.76), channel_id=1, source_target_pairs={{0,1},{1,0},{2,3},{3,2},{4,5},{5,4},{6,7},{7,6},{8,9},{9,8},{10,11... | collective-permute-start | bytes 147464 | tf_op jit(solution)/shard_map/ppermute | solution.py:530
  170.5 4.2 %collective-permute-start.38 = (bf16[32,768]{1,0:T(8,128)(2,1)S(1)}, bf16[32,768]{1,0:T(8,128)(2,1)S(1)}, u32[]{:S(2)}, u32[]{:S(2)}) collective-permute-start(bf16[32,768]{1,0:T(8,128)(2,1)S(1)} %get-tuple-element.77), channel_id=1, source_target_pairs={{0,2},{1,3},{2,0},{3,1},{4,6},{5,7},{6,4},{7,5},{8,10},{9,11},{10,... | collective-permute-start | bytes 147464 | tf_op jit(solution)/shard_map/ppermute | solution.py:530
  171.7 3.7 %collective-permute-start.39 = (bf16[32,768]{1,0:T(8,128)(2,1)S(1)}, bf16[32,768]{1,0:T(8,128)(2,1)S(1)}, u32[]{:S(2)}, u32[]{:S(2)}) collective-permute-start(bf16[32,768]{1,0:T(8,128)(2,1)S(1)} %get-tuple-element.78), channel_id=1, source_target_pairs={{0,3},{1,2},{2,1},{3,0},{4,7},{5,6},{6,5},{7,4},{8,11},{9,10},{10,... | collective-permute-start | bytes 147464 | tf_op jit(solution)/shard_map/ppermute | solution.py:530
  (18 other events, 231.6 us)

commit v7 on v6

--- a/solution.py
+++ b/solution.py
@@ -396,17 +396,17 @@
         for m in range(2):
             source = weights[m].at[0, :, lanes]
             copies.append(pltpu.make_async_copy(source, buffers[m].at[n], sem.at[len(copies)]))
-    throttled(copies, -1, 4)
+    throttled(copies, -1, 6)
     gate, up, stats = (None, None, None) if first else (b[...] for b in before)
     for n in range(count):
         rows = blocks[n][...].astype(F32)
         part = jnp.sum(jnp.where(is_spare, rows, 0.0), axis=0, keepdims=True)
         stats = part if stats is None else stats + part
         rows = jnp.where(is_spare, 0.0, rows).astype(BF16)
-        throttled(copies, 2 * n, 4)
+        throttled(copies, 2 * n, 6)
         part = mm(rows, buffers[0][n], NT)
         gate = part if gate is None else gate + part
-        throttled(copies, 2 * n + 1, 4)
+        throttled(copies, 2 * n + 1, 6)
         part = mm(rows, buffers[1][n], NT)
         up = part if up is None else up + part
     if not last:
@@ -447,17 +447,17 @@
             at = pl.ds(pl.multiple_of(source_of(s, nz, ny, p) * depth, depth), depth)
             source = w_down.at[0, at, :]
             copies.append(pltpu.make_async_copy(source, to.at[n], sem.at[len(copies)]))
-        throttled(copies, -1, 3)
+        throttled(copies, -1, 5)
     total = None if first else before[...]
     for n in range(count):
         if not last:
-            throttled(copies, n, 3)
+            throttled(copies, n, 5)
         part = mm(blocks[n][...], buf[n])
         total = part if total is None else total + part
     if not last:
         outs[0][...] = total
         for n in range(count, len(copies)):
-            throttled(copies, n, 3)
+            throttled(copies, n, 5)
         return
     result = (total * weight[:, 0:1]).astype(BF16)
     for r, out in enumerate(outs):
@@ -548,17 +548,20 @@
     def gather_y(held, events):
         for d in z_order:
             x = held[d, 0]
-            if d == z_order[-1]:
+            if d == z_order[-1] and events:
                 x = held[d, 0] = behind([x], events)[0]
             for e in range(1, ny):
                 held[d, e] = y_turn(x, e)
 
-    def stages(run, a):
+    def stages(run, a, groups):
         arrived = gather_z(a)
         state = []
+        if len(groups) == 2:
+            gather_y(arrived, [])
         for n, group in enumerate(groups):
-            state = run(n, group, [arrived[p] for p in group], state)
-            if n == 0:
+            blocks = [arrived[p] for p in group]
+            state = run(group, blocks, state, n == 0, n == len(groups) - 1)
+            if n == 0 and len(groups) == 3:
                 gather_y(arrived, state)
         return state
 
@@ -738,8 +741,7 @@
 
     in_vmem = pl.BlockSpec(memory_space=pltpu.VMEM)
 
-    def up(n, group, blocks, state):
-        first, last = n == 0, n == len(groups) - 1
+    def up(group, blocks, state, first, last):
         outs = [sds((slots, units), F32)] * 2 + [sds((1, cols), F32)]
         if last:
             outs = [sds((slots, units), BF16), sds((slots, 128), F32)]
@@ -754,8 +756,7 @@
             flops=4 * len(group) * slots * units * cols,
         )
 
-    def down(n, group, blocks, state):
-        first, last = n == 0, n == len(groups) - 1
+    def down(group, blocks, state, first, last):
         ahead = groups[-1] if first else []
         outs = [sds((slots, cols), F32)]
         outs += [sds((len(ahead), units, cols), BF16)] if ahead else []
@@ -797,8 +798,8 @@
         weight = sigmoid(jnp.sum(stats[:, 3:6], axis=1)[:, None] * inverse)
         weight = jnp.broadcast_to(weight, (slots, 128))
     else:
-        hidden, weight = stages(up, rows_out)
-    state = stages(down, hidden)
+        hidden, weight = stages(up, rows_out, groups)
+    state = stages(down, hidden, [groups[0] + groups[1], groups[2]])
     returned = [state[0]] + [swap(state[r], r) for r in range(1, nz)]
     (layer_out,) = call(
         functools.partial(combine_kernel, nz, cap),

time: 178 us -> 176 us (0.989)
  waiting for transfers between devices: 70 us -> 73.7 us
  Pallas kernels: 49.1 us -> 46.4 us
  local copies, waits for them, and re-layouts: 5.26 us -> 2.89 us
    ppermute x16, waiting for transfers between devices: 49.2 us -> 57.4 us  [z_turn(): return lax.ppermute(a, 'seq', pairs)]
    ppermute x17, waiting for transfers between devices: 12.2 us -> 7.62 us  [y_turn(): return lax.ppermute(a, 'seq', pairs)]
    pallas_call x14 -> x13, Pallas kernels: 45.2 us -> 42.6 us  [call(): pl.pallas_call(kernel, out_shape=list(outs), grid_spec=pltpu.PrefetchScal...]
    unnamed x46 -> x40, local copies, waits for them, and re-layouts: 3.7 us -> 1.33 us
  transfers between devices with their start and end apart: 43 -> 43, of which waited for: 18 -> 19; matrix products, arithmetic and copies ran while one was open for 1% -> 1% of each run, Pallas kernels for 21% -> 20%
where the time goes in v7:
time: 176 us; the launch traced here: 175 us
  waiting for transfers between devices  73.7 us (42%)
  starting transfers between devices  50.6 us (29%)
  Pallas kernels  46.4 us (26%)
  local copies, waits for them, and re-layouts  2.89 us (2%)
    ppermute x16, waiting for transfers between devices, z_turn(): return lax.ppermute(a, 'seq', pairs)  57.4 us
    pallas_call x13, Pallas kernels, call(): pl.pallas_call(kernel, out_shape=list(outs), grid_spec=pltpu.PrefetchScal...  42.6 us
    ppermute x16, starting transfers between devices, z_turn(): return lax.ppermute(a, 'seq', pairs)  24.6 us
    ppermute x17, starting transfers between devices, y_turn(): return lax.ppermute(a, 'seq', pairs)  19 us
    ppermute x10, waiting for transfers between devices, swap(): return lax.ppermute(a, 'exp', [(p, p ^ r) for p in range(nz)])  8.75 us
    ppermute x17, waiting for transfers between devices, y_turn(): return lax.ppermute(a, 'seq', pairs)  7.62 us
    ppermute x10, starting transfers between devices, swap(): return lax.ppermute(a, 'exp', [(p, p ^ r) for p in range(nz)])  7.01 us
  transfers between devices with their start and end apart: 43, of which 19 were waited for; matrix products, arithmetic and copies ran while one was open for 1% of the time, Pallas kernels for 20%

profile of v7, /device:TPU:0, one launch (start us, length us, event | category | flops | bytes accessed | tf_op | source)
XLA Modules:
  0.0 175.3 jit_solution(7907698026025036525)
XLA Ops:
  0.7 2.0 %shard_map.230 = bf16[2,128,1024]{2,1,0:T(8,128)(2,1)} custom-call(bf16[128,2048]{1,0:T(8,128)(2,1)} %refs_0_.5, bf16[128,2048]{1,0:T(8,128)(2,1)} %refs_1_.4), custom_call_target="tpu_custom_call" | custom-call | tf_op jit(solution)/shard_map/pallas_call | solution.py:592
  2.7 3.0 %collective-permute-start = (bf16[2,128,1024]{2,1,0:T(8,128)(2,1)}, bf16[2,128,1024]{2,1,0:T(8,128)(2,1)S(1)}, u32[]{:S(2)}, u32[]{:S(2)}) collective-permute-start(bf16[2,128,1024]{2,1,0:T(8,128)(2,1)} %shard_map.230), channel_id=1, source_target_pairs={{0,4},{4,0},{8,12},{12,8},{16,20},{20,16},{24,28},{28,24},{1,5},{5... | collective-permute-start | bytes 1572872 | tf_op jit(solution)/shard_map/ppermute | solution.py:527
  5.8 1.5 collective-permute-start.3
  8.7 1.9 %shard_map.231 = bf16[2,128,1024]{2,1,0:T(8,128)(2,1)} custom-call(bf16[128,2048]{1,0:T(8,128)(2,1)} %refs_2_.2, bf16[128,2048]{1,0:T(8,128)(2,1)} %refs_3_.1), custom_call_target="tpu_custom_call" | custom-call | tf_op jit(solution)/shard_map/pallas_call | solution.py:594
  10.6 1.2 copy-done.6
  11.8 1.6 shard_map.232
  13.4 4.7 %collective-permute-done.1.refs_4_ = f32[16,128]{1,0:T(8,128)S(1)} collective-permute-done((f32[16,128]{1,0:T(8,128)}, f32[16,128]{1,0:T(8,128)S(1)}, u32[]{:S(2)}, u32[]{:S(2)}) %collective-permute-start.1) | collective-permute-done | bytes 8224 | tf_op jit(solution)/shard_map/ppermute | solution.py:527
  18.1 1.7 collective-permute-start.5
  19.8 3.0 %shard_map.233 = (bf16[272,128]{1,0:T(8,128)(2,1)S(1)}, bf16[272,128]{1,0:T(8,128)(2,1)S(1)}, bf16[272,128]{1,0:T(8,128)(2,1)S(1)}, bf16[272,128]{1,0:T(8,128)(2...) custom-call(s32[3]{0:T(128)S(1)} %pad_add_fusion.s, bf16[128,2048]{1,0:T(8,128)(2,1)S(1)} %copy-done.1, ...), custom_call_target="tpu_custom_call" | custom-call | flops 67108864 | bytes 1884160 | tf_op jit(solution)/shard_map/pallas_call | solution.py:47
  22.9 1.6 collective-permute-start.6
  24.5 2.6 %collective-permute-start.7 = (bf16[272,128]{1,0:T(8,128)(2,1)S(1)}, bf16[272,128]{1,0:T(8,128)(2,1)S(1)}, u32[]{:S(2)}, u32[]{:S(2)}) collective-permute-start(bf16[272,128]{1,0:T(8,128)(2,1)S(1)} %get-tuple-element.49), channel_id=1, source_target_pairs={{0,16},{4,20},{8,24},{12,28},{16,0},{20,4},{24,8},{28,12},{1,17},{... | collective-permute-start | bytes 208904 | tf_op jit(solution)/shard_map/ppermute | solution.py:523
  27.1 1.3 collective-permute-start.8
  29.7 1.7 collective-permute-done.7.refs_2_
  33.1 2.7 %collective-permute-start.11 = (bf16[256,128]{1,0:T(8,128)(2,1)S(1)}, bf16[256,128]{1,0:T(8,128)(2,1)S(1)}, u32[]{:S(2)}, u32[]{:S(2)}) collective-permute-start(bf16[256,128]{1,0:T(8,128)(2,1)S(1)} %get-tuple-element.54), channel_id=1, source_target_pairs={{0,24},{4,28},{8,0},{12,4},{16,8},{20,12},{24,16},{28,20},{1,25},{... | collective-permute-start | bytes 196616 | tf_op jit(solution)/shard_map/ppermute | solution.py:523
  35.9 2.7 %collective-permute-done.10.refs_8_ = bf16[256,128]{1,0:T(8,128)(2,1)S(1)} collective-permute-done((bf16[256,128]{1,0:T(8,128)(2,1)S(1)}, bf16[256,128]{1,0:T(8,128)(2,1)S(1)}, u32[]{:S(2)}, u32[]{:S(2)}) %collective-permute-start.10) | collective-permute-done | bytes 65568 | tf_op jit(solution)/shard_map/ppermute | solution.py:523
  38.6 3.2 %collective-permute-done.9.refs_7_ = bf16[256,128]{1,0:T(8,128)(2,1)S(1)} collective-permute-done((bf16[256,128]{1,0:T(8,128)(2,1)S(1)}, bf16[256,128]{1,0:T(8,128)(2,1)S(1)}, u32[]{:S(2)}, u32[]{:S(2)}) %collective-permute-start.9) | collective-permute-done | bytes 65568 | tf_op jit(solution)/shard_map/ppermute | solution.py:523
  41.8 3.4 %shard_map.235.refs_0_ = bf16[256,1024]{1,0:T(8,128)(2,1)S(1)} custom-call(s32[3]{0:T(128)S(1)} %pad_add_fusion.s, bf16[128,2048]{1,0:T(8,128)(2,1)S(1)} %copy-done.1, bf16[128,2048]{1,0:T(8,128)(2,1)S(1)} %copy-done.2, bf16[128,2048]{1,0:T(8,128)(2,1)S(1)} %copy-done.3, bf16[128,2048]{1,0:T(8,128)(2,1)S(1)} %copy-done.4, ...), custom_call_target="tpu_custom_call" | custom-call | flops 268435456 | bytes 3956736 | tf_op jit(solution)/shard_map/pallas_call | solution.py:47
  45.3 3.8 %collective-permute-start.17 = (bf16[256,1024]{1,0:T(8,128)(2,1)S(1)}, bf16[256,1024]{1,0:T(8,128)(2,1)S(1)}, u32[]{:S(2)}, u32[]{:S(2)}) collective-permute-start(bf16[256,1024]{1,0:T(8,128)(2,1)S(1)} %shard_map.235.refs_0_), channel_id=1, source_target_pairs={{0,24},{4,28},{8,0},{12,4},{16,8},{20,12},{24,16},{28,20},{1,25},{... | collective-permute-start | bytes 1572872 | tf_op jit(solution)/shard_map/ppermute | solution.py:523
  49.7 12.3 %collective-permute-done.12.refs_1_ = bf16[256,1024]{1,0:T(8,128)(2,1)S(1)} collective-permute-done((bf16[256,1024]{1,0:T(8,128)(2,1)S(1)}, bf16[256,1024]{1,0:T(8,128)(2,1)S(1)}, u32[]{:S(2)}, u32[]{:S(2)}) %collective-permute-start.12) | collective-permute-done | bytes 524320 | tf_op jit(solution)/shard_map/ppermute | solution.py:523
  62.5 5.9 %collective-permute-done.17.refs_2_ = bf16[256,1024]{1,0:T(8,128)(2,1)S(1)} collective-permute-done((bf16[256,1024]{1,0:T(8,128)(2,1)S(1)}, bf16[256,1024]{1,0:T(8,128)(2,1)S(1)}, u32[]{:S(2)}, u32[]{:S(2)}) %collective-permute-start.17) | collective-permute-done | bytes 524320 | tf_op jit(solution)/shard_map/ppermute | solution.py:523
  69.0 2.6 %collective-permute-start.13 = (bf16[128,1024]{1,0:T(8,128)(2,1)S(1)}, bf16[128,1024]{1,0:T(8,128)(2,1)S(1)}, u32[]{:S(2)}, u32[]{:S(2)}) collective-permute-start(bf16[128,1024]{1,0:T(8,128)(2,1)S(1)} %get-tuple-element.87), channel_id=1, source_target_pairs={{0,16},{4,20},{8,24},{12,28},{16,0},{20,4},{24,8},{28,12},{1,17},{... | collective-permute-start | bytes 786440 | tf_op jit(solution)/shard_map/ppermute | solution.py:523
  72.0 15.2 %collective-permute-done.13.refs_0_ = bf16[128,1024]{1,0:T(8,128)(2,1)S(1)} collective-permute-done((bf16[128,1024]{1,0:T(8,128)(2,1)S(1)}, bf16[128,1024]{1,0:T(8,128)(2,1)S(1)}, u32[]{:S(2)}, u32[]{:S(2)}) %collective-permute-start.13) | collective-permute-done | bytes 262176 | tf_op jit(solution)/shard_map/ppermute | solution.py:523
  87.9 4.6 %collective-permute-done.14.refs_1_ = bf16[128,1024]{1,0:T(8,128)(2,1)S(1)} collective-permute-done((bf16[128,1024]{1,0:T(8,128)(2,1)S(1)}, bf16[128,1024]{1,0:T(8,128)(2,1)S(1)}, u32[]{:S(2)}, u32[]{:S(2)}) %collective-permute-start.14) | collective-permute-done | bytes 262176 | tf_op jit(solution)/shard_map/ppermute | solution.py:523
  93.4 4.1 %shard_map.236 = (bf16[3,256,768]{2,1,0:T(8,128)(2,1)S(1)}, f32[320,768]{1,0:T(8,128)S(1)}) custom-call(s32[3]{0:T(128)S(1)} %pad_add_fusion.s, bf16[256,1024]{1,0:T(8,128)(2,1)S(1)} %shard_map.235.refs_0_, bf16[256,1024]{1,0:T(8,128)(2,1)S(1)} %collective-permute-done.12.refs_1_, bf16[256,1024]{1,0:T(8,128)(2,1)S(1)} %collective-permute-done.17.refs_2_, ...), custom_call_target="tpu_custom_call" | custom-call | flops 2415919104 | bytes 11610624 | tf_op jit(solution)/shard_map/pallas_call | solution.py:47
  97.5 2.9 %collective-permute-done.16.refs_3_ = bf16[128,1024]{1,0:T(8,128)(2,1)S(1)} collective-permute-done((bf16[128,1024]{1,0:T(8,128)(2,1)S(1)}, bf16[128,1024]{1,0:T(8,128)(2,1)S(1)}, u32[]{:S(2)}, u32[]{:S(2)}) %collective-permute-start.16) | collective-permute-done | bytes 262176 | tf_op jit(solution)/shard_map/ppermute | solution.py:527
  100.4 3.0 %shard_map.237 = (f32[160,768]{1,0:T(8,128)S(1)}, bf16[160,768]{1,0:T(8,128)(2,1)S(1)}, bf16[2,256,768]{2,1,0:T(8,128)(2,1)S(1)}, bf16[2,256,768]{2,1,0:T(8,128)(2,1)S(1)}) custom-call(s32[3]{0:T(128)S(1)} %pad_add_fusion.s, bf16[128,1024]{1,0:T(8,128)(2,1)S(1)} %collective-permute-done.13.refs_0_, bf16[128,1024]{1,0:T(8,128)(2,1)S(1)} %collective-permute-done.14.refs_1_, ...), custom_call_target="tpu_custom_call" | custom-call | flops 805306368 | bytes 12216832 | tf_op jit(solution)/shard_map/pallas_call | solution.py:47
  103.5 1.5 collective-permute-done.21
  105.1 1.6 collective-permute-start.22
  106.6 3.9 %collective-permute-done.22.received = bf16[80,768]{1,0:T(8,128)(2,1)S(1)} collective-permute-done((bf16[80,768]{1,0:T(8,128)(2,1)S(1)}, bf16[80,768]{1,0:T(8,128)(2,1)S(1)}, u32[]{:S(2)}, u32[]{:S(2)}) %collective-permute-start.22) | collective-permute-done | bytes 122912 | tf_op jit(solution)/shard_map/ppermute | solution.py:530
  111.7 1.7 collective-permute-start.23
  113.4 2.2 %collective-permute-start.25 = (bf16[80,768]{1,0:T(8,128)(2,1)S(1)}, bf16[80,768]{1,0:T(8,128)(2,1)S(1)}, u32[]{:S(2)}, u32[]{:S(2)}) collective-permute-start(bf16[80,768]{1,0:T(8,128)(2,1)S(1)} %shard_map.238.refs_0_), channel_id=1, source_target_pairs={{0,24},{4,28},{8,0},{12,4},{16,8},{20,12},{24,16},{28,20},{1,25},{... | collective-permute-start | bytes 368648 | tf_op jit(solution)/shard_map/ppermute | solution.py:523
  116.8 3.4 %shard_map.239 = (f32[80,1152]{1,0:T(8,128)S(1)}, f32[80,1152]{1,0:T(8,128)S(1)}, f32[1,768]{1,0:T(1,128)S(1)}) custom-call(s32[3]{0:T(128)S(1)} %pad_add_fusion.s, bf16[80,768]{1,0:T(8,128)(2,1)S(1)} %shard_map.238.refs_0_, bf16[1,1152,6144]{2,1,0:T(8,128)(2,1)} %refs_6_.8, bf16[1,1152,6144]{2,1,0:T(8,128)(2,1)} %refs_7_.7, ...), custom_call_target="tpu_custom_call" | custom-call | flops 283115520 | bytes 29215744 | tf_op jit(solution)/shard_map/pallas_call | solution.py:47
  120.2 1.9 %collective-permute-done.27.refs_3_ = bf16[80,768]{1,0:T(8,128)(2,1)S(1)} collective-permute-done((bf16[80,768]{1,0:T(8,128)(2,1)S(1)}, bf16[80,768]{1,0:T(8,128)(2,1)S(1)}, u32[]{:S(2)}, u32[]{:S(2)}) %collective-permute-start.27) | collective-permute-done | bytes 122912 | tf_op jit(solution)/shard_map/ppermute | solution.py:523
  122.1 1.5 collective-permute-start.28
  124.1 1.5 collective-permute-start.26
  125.7 6.9 %shard_map.240 = (f32[80,1152]{1,0:T(8,128)S(1)}, f32[80,1152]{1,0:T(8,128)S(1)}, f32[1,768]{1,0:T(1,128)S(1)}) custom-call(s32[3]{0:T(128)S(1)} %pad_add_fusion.s, bf16[80,768]{1,0:T(8,128)(2,1)S(1)} %collective-permute-done.29.refs_0_, bf16[80,768]{1,0:T(8,128)(2,1)S(1)} %collective-permute-done.23.refs_1_, ...), custom_call_target="tpu_custom_call" | custom-call | flops 1132462080 | bytes 30324736 | tf_op jit(solution)/shard_map/pallas_call | solution.py:47
  132.6 5.7 %shard_map.241 = (bf16[80,1152]{1,0:T(8,128)(2,1)S(1)}, f32[80,128]{1,0:T(8,128)S(1)}) custom-call(s32[3]{0:T(128)S(1)} %pad_add_fusion.s, bf16[80,768]{1,0:T(8,128)(2,1)S(1)} %collective-permute-done.24.refs_0_, bf16[80,768]{1,0:T(8,128)(2,1)S(1)} %collective-permute-done.26.refs_1_, bf16[80,768]{1,0:T(8,128)(2,1)S(1)} %collective-permute-done.28.refs_2_, ...), custom_call_target="tpu_custom_call" | custom-call | flops 849346560 | bytes 29686784 | tf_op jit(solution)/shard_map/pallas_call | solution.py:47
  138.3 1.3 collective-permute-start.30
  139.6 2.6 %collective-permute-start.32 = (bf16[80,1152]{1,0:T(8,128)(2,1)S(1)}, bf16[80,1152]{1,0:T(8,128)(2,1)S(1)}, u32[]{:S(2)}, u32[]{:S(2)}) collective-permute-start(bf16[80,1152]{1,0:T(8,128)(2,1)S(1)} %get-tuple-element.69.refs_0_), channel_id=1, source_target_pairs={{0,24},{4,28},{8,0},{12,4},{16,8},{20,12},{24,16},{28,20},{1,25},{... | collective-permute-start | bytes 552968 | tf_op jit(solution)/shard_map/ppermute | solution.py:523
  145.4 1.5 collective-permute-start.41
  147.8 1.5 collective-permute-start.31
  150.9 6.9 %collective-permute-done.34.refs_4_ = bf16[80,1152]{1,0:T(8,128)(2,1)S(1)} collective-permute-done((bf16[80,1152]{1,0:T(8,128)(2,1)S(1)}, bf16[80,1152]{1,0:T(8,128)(2,1)S(1)}, u32[]{:S(2)}, u32[]{:S(2)}) %collective-permute-start.34) | collective-permute-done | bytes 184352 | tf_op jit(solution)/shard_map/ppermute | solution.py:523
  157.8 1.4 collective-permute-start.35
  160.0 5.9 %shard_map.242 = (f32[80,768]{1,0:T(8,128)S(1)}, bf16[3,1152,768]{2,1,0:T(8,128)(2,1)S(1)}) custom-call(s32[3]{0:T(128)S(1)} %pad_add_fusion.s, bf16[80,1152]{1,0:T(8,128)(2,1)S(1)} %get-tuple-element.69.refs_0_, bf16[80,1152]{1,0:T(8,128)(2,1)S(1)} %collective-permute-done.36.refs_1_, bf16[80,1152]{1,0:T(8,128)(2,1)S(1)} %collective-permute-done.30.refs_2_, ...), custom_call_target="tpu_custom_call" | custom-call | flops 707788800 | bytes 20631552 | tf_op jit(solution)/shard_map/pallas_call | solution.py:47
  165.9 1.8 %shard_map.243 = (bf16[32,768]{1,0:T(8,128)(2,1)S(1)}, bf16[32,768]{1,0:T(8,128)(2,1)S(1)}, bf16[32,768]{1,0:T(8,128)(2,1)S(1)}, bf16[32,768]{1,0:T(8,128)(2,1)S(1)}) custom-call(s32[3]{0:T(128)S(1)} %pad_add_fusion.s, bf16[80,1152]{1,0:T(8,128)(2,1)S(1)} %collective-permute-done.31.refs_0_, bf16[80,1152]{1,0:T(8,128)(2,1)S(1)} %collective-permute-done.33.refs_1_, ...), custom_call_target="tpu_custom_call" | custom-call | flops 424673280 | bytes 6345152 | tf_op jit(solution)/shard_map/pallas_call | solution.py:47
  167.8 1.6 collective-permute-start.38
  169.7 2.3 %collective-permute-done.38.refs_2_ = bf16[32,768]{1,0:T(8,128)(2,1)S(1)} collective-permute-done((bf16[32,768]{1,0:T(8,128)(2,1)S(1)}, bf16[32,768]{1,0:T(8,128)(2,1)S(1)}, u32[]{:S(2)}, u32[]{:S(2)}) %collective-permute-start.38) | collective-permute-done | bytes 49184 | tf_op jit(solution)/shard_map/ppermute | solution.py:530
  173.1 2.0 %shard_map.244 = bf16[256,768]{1,0:T(8,128)(2,1)} custom-call(s32[3]{0:T(128)S(1)} %pad_add_fusion.s, bf16[32,768]{1,0:T(8,128)(2,1)S(1)} %get-tuple-element.73.refs_0_, bf16[32,768]{1,0:T(8,128)(2,1)S(1)} %collective-permute-done.37.refs_1_, bf16[32,768]{1,0:T(8,128)(2,1)S(1)} %collective-permute-done.38.refs_2_, ...), custom_call_target="tpu_custom_call" | custom-call | bytes 1778688 | tf_op jit(solution)/shard_map/pallas_call | solution.py:47
  (102 shorter events, 19.1 us)
Async XLA Ops:
  0.7 41.1 %copy-start.3 = (bf16[128,2048]{1,0:T(8,128)(2,1)S(1)}, bf16[128,2048]{1,0:T(8,128)(2,1)}, u32[]{:S(2)}) copy-start(bf16[128,2048]{1,0:T(8,128)(2,1)} %refs_2_.2) | copy-start | bytes 1572868
  0.7 41.1 %copy-start.4 = (bf16[128,2048]{1,0:T(8,128)(2,1)S(1)}, bf16[128,2048]{1,0:T(8,128)(2,1)}, u32[]{:S(2)}) copy-start(bf16[128,2048]{1,0:T(8,128)(2,1)} %refs_3_.1) | copy-start | bytes 1572868
  2.7 15.3 %collective-permute-start = (bf16[2,128,1024]{2,1,0:T(8,128)(2,1)}, bf16[2,128,1024]{2,1,0:T(8,128)(2,1)S(1)}, u32[]{:S(2)}, u32[]{:S(2)}) collective-permute-start(bf16[2,128,1024]{2,1,0:T(8,128)(2,1)} %shard_map.230), channel_id=1, source_target_pairs={{0,4},{4,0},{8,12},{12,8},{16,20},{20,16},{24,28},{28,24},{1,5},{5... | collective-permute-start | bytes 1572872 | tf_op jit(solution)/shard_map/ppermute | solution.py:527
  5.8 4.8 %collective-permute-start.2 = (s32[2,256]{1,0:T(2,128)}, s32[2,256]{1,0:T(2,128)S(1)}, u32[]{:S(2)}, u32[]{:S(2)}) collective-permute-start(s32[2,256]{1,0:T(2,128)} %bitcast.15), channel_id=1, source_target_pairs={{0,1},{1,0},{2,3},{3,2},{4,5},{5,4},{6,7},{7,6},{8,9},{9,8},{10,11... | collective-permute-start | bytes 6152 | tf_op jit(solution)/shard_map/ppermute | solution.py:530
  5.8 4.8 %collective-permute-start.3 = (s32[2,256]{1,0:T(2,128)}, s32[2,256]{1,0:T(2,128)S(1)}, u32[]{:S(2)}, u32[]{:S(2)}) collective-permute-start(s32[2,256]{1,0:T(2,128)} %bitcast.16), channel_id=1, source_target_pairs={{0,2},{1,3},{2,0},{3,1},{4,6},{5,7},{6,4},{7,5},{8,10},{9,11},{10,... | collective-permute-start | bytes 6152 | tf_op jit(solution)/shard_map/ppermute | solution.py:530
  7.3 3.3 %collective-permute-start.4 = (s32[2,256]{1,0:T(2,128)}, s32[2,256]{1,0:T(2,128)S(1)}, u32[]{:S(2)}, u32[]{:S(2)}) collective-permute-start(s32[2,256]{1,0:T(2,128)} %bitcast.17), channel_id=1, source_target_pairs={{0,3},{1,2},{2,1},{3,0},{4,7},{5,6},{6,5},{7,4},{8,11},{9,10},{10,... | collective-permute-start | bytes 6152 | tf_op jit(solution)/shard_map/ppermute | solution.py:530
  7.6 10.4 %collective-permute-start.1 = (f32[16,128]{1,0:T(8,128)}, f32[16,128]{1,0:T(8,128)S(1)}, u32[]{:S(2)}, u32[]{:S(2)}) collective-permute-start(f32[16,128]{1,0:T(8,128)} %bitcast.12), channel_id=1, source_target_pairs={{0,4},{4,0},{8,12},{12,8},{16,20},{20,16},{24,28},{28,24},{1,5},{5... | collective-permute-start | bytes 24584 | tf_op jit(solution)/shard_map/ppermute | solution.py:527
  18.1 23.7 %collective-permute-start.5 = (bf16[2,128,1024]{2,1,0:T(8,128)(2,1)}, bf16[2,128,1024]{2,1,0:T(8,128)(2,1)S(1)}, u32[]{:S(2)}, u32[]{:S(2)}) collective-permute-start(bf16[2,128,1024]{2,1,0:T(8,128)(2,1)} %shard_map.231), channel_id=1, source_target_pairs={{0,4},{4,0},{8,12},{12,8},{16,20},{20,16},{24,28},{28,24},{1,5},{5... | collective-permute-start | bytes 1572872 | tf_op jit(solution)/shard_map/ppermute | solution.py:527
  22.9 70.5 %copy-start = (bf16[2048,768]{1,0:T(8,128)(2,1)S(1)}, bf16[2048,768]{1,0:T(8,128)(2,1)}, u32[]{:S(2)}) copy-start(bf16[2048,768]{1,0:T(8,128)(2,1)} %refs_5_.3) | copy-start | bytes 9437188
  22.9 70.5 %copy-start.7 = (s32[320,1]{1,0:T(8,128)S(1)}, s32[320,1]{1,0:T(8,128)}, u32[]{:S(2)}) copy-start(s32[320,1]{1,0:T(8,128)} %constant.73.clone.refs_8_.refs_6_) | copy-start | bytes 3844
  22.9 70.5 %copy-start.8 = (s32[320,1]{1,0:T(8,128)S(1)}, s32[320,1]{1,0:T(8,128)}, u32[]{:S(2)}) copy-start(s32[320,1]{1,0:T(8,128)} %constant.74.clone.refs_9_.refs_7_) | copy-start | bytes 3844
  22.9 6.8 %collective-permute-start.6 = (bf16[272,128]{1,0:T(8,128)(2,1)S(1)}, bf16[272,128]{1,0:T(8,128)(2,1)S(1)}, u32[]{:S(2)}, u32[]{:S(2)}) collective-permute-start(bf16[272,128]{1,0:T(8,128)(2,1)S(1)} %get-tuple-element.48), channel_id=1, source_target_pairs={{0,8},{4,12},{8,16},{12,20},{16,24},{20,28},{24,0},{28,4},{1,9},{5... | collective-permute-start | bytes 208904 | tf_op jit(solution)/shard_map/ppermute | solution.py:523
  24.5 6.9 %collective-permute-start.7 = (bf16[272,128]{1,0:T(8,128)(2,1)S(1)}, bf16[272,128]{1,0:T(8,128)(2,1)S(1)}, u32[]{:S(2)}, u32[]{:S(2)}) collective-permute-start(bf16[272,128]{1,0:T(8,128)(2,1)S(1)} %get-tuple-element.49), channel_id=1, source_target_pairs={{0,16},{4,20},{8,24},{12,28},{16,0},{20,4},{24,8},{28,12},{1,17},{... | collective-permute-start | bytes 208904 | tf_op jit(solution)/shard_map/ppermute | solution.py:523
  27.1 4.8 %collective-permute-start.8 = (bf16[272,128]{1,0:T(8,128)(2,1)S(1)}, bf16[272,128]{1,0:T(8,128)(2,1)S(1)}, u32[]{:S(2)}, u32[]{:S(2)}) collective-permute-start(bf16[272,128]{1,0:T(8,128)(2,1)S(1)} %get-tuple-element.50), channel_id=1, source_target_pairs={{0,24},{4,28},{8,0},{12,4},{16,8},{20,12},{24,16},{28,20},{1,25},{... | collective-permute-start | bytes 208904 | tf_op jit(solution)/shard_map/ppermute | solution.py:523
  32.6 6.0 %collective-permute-start.10 = (bf16[256,128]{1,0:T(8,128)(2,1)S(1)}, bf16[256,128]{1,0:T(8,128)(2,1)S(1)}, u32[]{:S(2)}, u32[]{:S(2)}) collective-permute-start(bf16[256,128]{1,0:T(8,128)(2,1)S(1)} %get-tuple-element.53), channel_id=1, source_target_pairs={{0,16},{4,20},{8,24},{12,28},{16,0},{20,4},{24,8},{28,12},{1,17},{... | collective-permute-start | bytes 196616 | tf_op jit(solution)/shard_map/ppermute | solution.py:523
  33.1 5.5 %collective-permute-start.11 = (bf16[256,128]{1,0:T(8,128)(2,1)S(1)}, bf16[256,128]{1,0:T(8,128)(2,1)S(1)}, u32[]{:S(2)}, u32[]{:S(2)}) collective-permute-start(bf16[256,128]{1,0:T(8,128)(2,1)S(1)} %get-tuple-element.54), channel_id=1, source_target_pairs={{0,24},{4,28},{8,0},{12,4},{16,8},{20,12},{24,16},{28,20},{1,25},{... | collective-permute-start | bytes 196616 | tf_op jit(solution)/shard_map/ppermute | solution.py:523
  35.8 6.1 %collective-permute-start.9 = (bf16[256,128]{1,0:T(8,128)(2,1)S(1)}, bf16[256,128]{1,0:T(8,128)(2,1)S(1)}, u32[]{:S(2)}, u32[]{:S(2)}) collective-permute-start(bf16[256,128]{1,0:T(8,128)(2,1)S(1)} %get-tuple-element.52), channel_id=1, source_target_pairs={{0,8},{4,12},{8,16},{12,20},{16,24},{20,28},{24,0},{28,4},{1,9},{5... | collective-permute-start | bytes 196616 | tf_op jit(solution)/shard_map/ppermute | solution.py:523
  45.3 16.7 %collective-permute-start.12 = (bf16[256,1024]{1,0:T(8,128)(2,1)S(1)}, bf16[256,1024]{1,0:T(8,128)(2,1)S(1)}, u32[]{:S(2)}, u32[]{:S(2)}) collective-permute-start(bf16[256,1024]{1,0:T(8,128)(2,1)S(1)} %shard_map.235.refs_0_), channel_id=1, source_target_pairs={{0,8},{4,12},{8,16},{12,20},{16,24},{20,28},{24,0},{28,4},{1,9},{5... | collective-permute-start | bytes 1572872 | tf_op jit(solution)/shard_map/ppermute | solution.py:523
  45.3 23.1 %collective-permute-start.17 = (bf16[256,1024]{1,0:T(8,128)(2,1)S(1)}, bf16[256,1024]{1,0:T(8,128)(2,1)S(1)}, u32[]{:S(2)}, u32[]{:S(2)}) collective-permute-start(bf16[256,1024]{1,0:T(8,128)(2,1)S(1)} %shard_map.235.refs_0_), channel_id=1, source_target_pairs={{0,24},{4,28},{8,0},{12,4},{16,8},{20,12},{24,16},{28,20},{1,25},{... | collective-permute-start | bytes 1572872 | tf_op jit(solution)/shard_map/ppermute | solution.py:523
  49.2 44.2 %collective-permute-start.18 = (bf16[256,1024]{1,0:T(8,128)(2,1)S(1)}, bf16[256,1024]{1,0:T(8,128)(2,1)S(1)}, u32[]{:S(2)}, u32[]{:S(2)}) collective-permute-start(bf16[256,1024]{1,0:T(8,128)(2,1)S(1)} %shard_map.235.refs_0_), channel_id=1, source_target_pairs={{0,4},{4,0},{8,12},{12,8},{16,20},{20,16},{24,28},{28,24},{1,5},{5... | collective-permute-start | bytes 1572872 | tf_op jit(solution)/shard_map/ppermute | solution.py:527
  62.0 31.4 %collective-permute-start.19 = (bf16[256,1024]{1,0:T(8,128)(2,1)S(1)}, bf16[256,1024]{1,0:T(8,128)(2,1)S(1)}, u32[]{:S(2)}, u32[]{:S(2)}) collective-permute-start(bf16[256,1024]{1,0:T(8,128)(2,1)S(1)} %collective-permute-done.12.refs_1_), channel_id=1, source_target_pairs={{0,4},{4,0},{8,12},{12,8},{16,20},{20,16},{24,28},{28,24},{1,5},{5... | collective-permute-start | bytes 1572872 | tf_op jit(solution)/shard_map/ppermute | solution.py:527
  68.4 25.0 %collective-permute-start.20 = (bf16[256,1024]{1,0:T(8,128)(2,1)S(1)}, bf16[256,1024]{1,0:T(8,128)(2,1)S(1)}, u32[]{:S(2)}, u32[]{:S(2)}) collective-permute-start(bf16[256,1024]{1,0:T(8,128)(2,1)S(1)} %collective-permute-done.17.refs_2_), channel_id=1, source_target_pairs={{0,4},{4,0},{8,12},{12,8},{16,20},{20,16},{24,28},{28,24},{1,5},{5... | collective-permute-start | bytes 1572872 | tf_op jit(solution)/shard_map/ppermute | solution.py:527
  69.0 18.2 %collective-permute-start.13 = (bf16[128,1024]{1,0:T(8,128)(2,1)S(1)}, bf16[128,1024]{1,0:T(8,128)(2,1)S(1)}, u32[]{:S(2)}, u32[]{:S(2)}) collective-permute-start(bf16[128,1024]{1,0:T(8,128)(2,1)S(1)} %get-tuple-element.87), channel_id=1, source_target_pairs={{0,16},{4,20},{8,24},{12,28},{16,0},{20,4},{24,8},{28,12},{1,17},{... | collective-permute-start | bytes 786440 | tf_op jit(solution)/shard_map/ppermute | solution.py:523
  71.6 20.9 %collective-permute-start.14 = (bf16[128,1024]{1,0:T(8,128)(2,1)S(1)}, bf16[128,1024]{1,0:T(8,128)(2,1)S(1)}, u32[]{:S(2)}, u32[]{:S(2)}) collective-permute-start(bf16[128,1024]{1,0:T(8,128)(2,1)S(1)} %get-tuple-element.86), channel_id=1, source_target_pairs={{0,16},{4,20},{8,24},{12,28},{16,0},{20,4},{24,8},{28,12},{1,17},{... | collective-permute-start | bytes 786440 | tf_op jit(solution)/shard_map/ppermute | solution.py:523
  87.1 10.3 %collective-permute-start.15 = (bf16[128,1024]{1,0:T(8,128)(2,1)S(1)}, bf16[128,1024]{1,0:T(8,128)(2,1)S(1)}, u32[]{:S(2)}, u32[]{:S(2)}) collective-permute-start(bf16[128,1024]{1,0:T(8,128)(2,1)S(1)} %collective-permute-done.13.refs_0_), channel_id=1, source_target_pairs={{0,4},{4,0},{8,12},{12,8},{16,20},{20,16},{24,28},{28,24},{1,5},{5... | collective-permute-start | bytes 786440 | tf_op jit(solution)/shard_map/ppermute | solution.py:527
  92.4 8.0 %collective-permute-start.16 = (bf16[128,1024]{1,0:T(8,128)(2,1)S(1)}, bf16[128,1024]{1,0:T(8,128)(2,1)S(1)}, u32[]{:S(2)}, u32[]{:S(2)}) collective-permute-start(bf16[128,1024]{1,0:T(8,128)(2,1)S(1)} %collective-permute-done.14.refs_1_), channel_id=1, source_target_pairs={{0,4},{4,0},{8,12},{12,8},{16,20},{20,16},{24,28},{28,24},{1,5},{5... | collective-permute-start | bytes 786440 | tf_op jit(solution)/shard_map/ppermute | solution.py:527
  103.5 1.6 collective-permute-start.21
  105.1 5.4 %collective-permute-start.22 = (bf16[80,768]{1,0:T(8,128)(2,1)S(1)}, bf16[80,768]{1,0:T(8,128)(2,1)S(1)}, u32[]{:S(2)}, u32[]{:S(2)}) collective-permute-start(bf16[80,768]{1,0:T(8,128)(2,1)S(1)} %get-tuple-element.84), channel_id=1, source_target_pairs={{0,2},{1,3},{2,0},{3,1},{4,6},{5,7},{6,4},{7,5},{8,10},{9,11},{10,... | collective-permute-start | bytes 368648 | tf_op jit(solution)/shard_map/ppermute | solution.py:530
  111.5 32.9 %collective-permute-start.40 = (bf16[2,256,768]{2,1,0:T(8,128)(2,1)S(1)}, bf16[2,256,768]{2,1,0:T(8,128)(2,1)S(1)}, u32[]{:S(2)}, u32[]{:S(2)}) collective-permute-start(bf16[2,256,768]{2,1,0:T(8,128)(2,1)S(1)} %get-tuple-element.79), channel_id=1, source_target_pairs={{0,1},{1,0},{2,3},{3,2},{4,5},{5,4},{6,7},{7,6},{8,9},{9,8},{10,11... | collective-permute-start | bytes 2359304 | tf_op jit(solution)/shard_map/ppermute | solution.py:530
  111.6 10.5 %collective-permute-start.27 = (bf16[80,768]{1,0:T(8,128)(2,1)S(1)}, bf16[80,768]{1,0:T(8,128)(2,1)S(1)}, u32[]{:S(2)}, u32[]{:S(2)}) collective-permute-start(bf16[80,768]{1,0:T(8,128)(2,1)S(1)} %shard_map.238.refs_0_), channel_id=1, source_target_pairs={{0,16},{4,20},{8,24},{12,28},{16,0},{20,4},{24,8},{28,12},{1,17},{... | collective-permute-start | bytes 368648 | tf_op jit(solution)/shard_map/ppermute | solution.py:523
  111.7 12.0 %collective-permute-start.23 = (bf16[80,768]{1,0:T(8,128)(2,1)S(1)}, bf16[80,768]{1,0:T(8,128)(2,1)S(1)}, u32[]{:S(2)}, u32[]{:S(2)}) collective-permute-start(bf16[80,768]{1,0:T(8,128)(2,1)S(1)} %shard_map.238.refs_0_), channel_id=1, source_target_pairs={{0,8},{4,12},{8,16},{12,20},{16,24},{20,28},{24,0},{28,4},{1,9},{5... | collective-permute-start | bytes 368648 | tf_op jit(solution)/shard_map/ppermute | solution.py:523
  113.4 10.7 %collective-permute-start.25 = (bf16[80,768]{1,0:T(8,128)(2,1)S(1)}, bf16[80,768]{1,0:T(8,128)(2,1)S(1)}, u32[]{:S(2)}, u32[]{:S(2)}) collective-permute-start(bf16[80,768]{1,0:T(8,128)(2,1)S(1)} %shard_map.238.refs_0_), channel_id=1, source_target_pairs={{0,24},{4,28},{8,0},{12,4},{16,8},{20,12},{24,16},{28,20},{1,25},{... | collective-permute-start | bytes 368648 | tf_op jit(solution)/shard_map/ppermute | solution.py:523
  115.6 10.1 %collective-permute-start.29 = (bf16[80,768]{1,0:T(8,128)(2,1)S(1)}, bf16[80,768]{1,0:T(8,128)(2,1)S(1)}, u32[]{:S(2)}, u32[]{:S(2)}) collective-permute-start(bf16[80,768]{1,0:T(8,128)(2,1)S(1)} %shard_map.238.refs_0_), channel_id=1, source_target_pairs={{0,4},{4,0},{8,12},{12,8},{16,20},{20,16},{24,28},{28,24},{1,5},{5... | collective-permute-start | bytes 368648 | tf_op jit(solution)/shard_map/ppermute | solution.py:527
  122.1 10.5 %collective-permute-start.28 = (bf16[80,768]{1,0:T(8,128)(2,1)S(1)}, bf16[80,768]{1,0:T(8,128)(2,1)S(1)}, u32[]{:S(2)}, u32[]{:S(2)}) collective-permute-start(bf16[80,768]{1,0:T(8,128)(2,1)S(1)} %collective-permute-done.27.refs_3_), channel_id=1, source_target_pairs={{0,4},{4,0},{8,12},{12,8},{16,20},{20,16},{24,28},{28,24},{1,5},{5... | collective-permute-start | bytes 368648 | tf_op jit(solution)/shard_map/ppermute | solution.py:527
  123.6 9.0 %collective-permute-start.24 = (bf16[80,768]{1,0:T(8,128)(2,1)S(1)}, bf16[80,768]{1,0:T(8,128)(2,1)S(1)}, u32[]{:S(2)}, u32[]{:S(2)}) collective-permute-start(bf16[80,768]{1,0:T(8,128)(2,1)S(1)} %collective-permute-done.23.refs_1_), channel_id=1, source_target_pairs={{0,4},{4,0},{8,12},{12,8},{16,20},{20,16},{24,28},{28,24},{1,5},{5... | collective-permute-start | bytes 368648 | tf_op jit(solution)/shard_map/ppermute | solution.py:527
  124.1 8.5 %collective-permute-start.26 = (bf16[80,768]{1,0:T(8,128)(2,1)S(1)}, bf16[80,768]{1,0:T(8,128)(2,1)S(1)}, u32[]{:S(2)}, u32[]{:S(2)}) collective-permute-start(bf16[80,768]{1,0:T(8,128)(2,1)S(1)} %collective-permute-done.25.refs_2_), channel_id=1, source_target_pairs={{0,4},{4,0},{8,12},{12,8},{16,20},{20,16},{24,28},{28,24},{1,5},{5... | collective-permute-start | bytes 368648 | tf_op jit(solution)/shard_map/ppermute | solution.py:527
  138.3 9.4 %collective-permute-start.30 = (bf16[80,1152]{1,0:T(8,128)(2,1)S(1)}, bf16[80,1152]{1,0:T(8,128)(2,1)S(1)}, u32[]{:S(2)}, u32[]{:S(2)}) collective-permute-start(bf16[80,1152]{1,0:T(8,128)(2,1)S(1)} %get-tuple-element.69.refs_0_), channel_id=1, source_target_pairs={{0,8},{4,12},{8,16},{12,20},{16,24},{20,28},{24,0},{28,4},{1,9},{5... | collective-permute-start | bytes 552968 | tf_op jit(solution)/shard_map/ppermute | solution.py:523
  139.6 10.2 %collective-permute-start.32 = (bf16[80,1152]{1,0:T(8,128)(2,1)S(1)}, bf16[80,1152]{1,0:T(8,128)(2,1)S(1)}, u32[]{:S(2)}, u32[]{:S(2)}) collective-permute-start(bf16[80,1152]{1,0:T(8,128)(2,1)S(1)} %get-tuple-element.69.refs_0_), channel_id=1, source_target_pairs={{0,24},{4,28},{8,0},{12,4},{16,8},{20,12},{24,16},{28,20},{1,25},{... | collective-permute-start | bytes 552968 | tf_op jit(solution)/shard_map/ppermute | solution.py:523
  142.2 15.6 %collective-permute-start.34 = (bf16[80,1152]{1,0:T(8,128)(2,1)S(1)}, bf16[80,1152]{1,0:T(8,128)(2,1)S(1)}, u32[]{:S(2)}, u32[]{:S(2)}) collective-permute-start(bf16[80,1152]{1,0:T(8,128)(2,1)S(1)} %get-tuple-element.69.refs_0_), channel_id=1, source_target_pairs={{0,16},{4,20},{8,24},{12,28},{16,0},{20,4},{24,8},{28,12},{1,17},{... | collective-permute-start | bytes 552968 | tf_op jit(solution)/shard_map/ppermute | solution.py:523
  143.2 16.1 %collective-permute-start.36 = (bf16[80,1152]{1,0:T(8,128)(2,1)S(1)}, bf16[80,1152]{1,0:T(8,128)(2,1)S(1)}, u32[]{:S(2)}, u32[]{:S(2)}) collective-permute-start(bf16[80,1152]{1,0:T(8,128)(2,1)S(1)} %get-tuple-element.69.refs_0_), channel_id=1, source_target_pairs={{0,4},{4,0},{8,12},{12,8},{16,20},{20,16},{24,28},{28,24},{1,5},{5... | collective-permute-start | bytes 552968 | tf_op jit(solution)/shard_map/ppermute | solution.py:527
  145.4 27.7 %collective-permute-start.41 = (bf16[1,256,768]{2,1,0:T(8,128)(2,1)}, bf16[1,256,768]{2,1,0:T(8,128)(2,1)S(1)}, u32[]{:S(2)}, u32[]{:S(2)}) collective-permute-start(bf16[1,256,768]{2,1,0:T(8,128)(2,1)} %get-tuple-element.82), channel_id=1, source_target_pairs={{0,2},{1,3},{2,0},{3,1},{4,6},{5,7},{6,4},{7,5},{8,10},{9,11},{10,... | collective-permute-start | bytes 1179656 | tf_op jit(solution)/shard_map/ppermute | solution.py:530
  147.8 18.1 %collective-permute-start.31 = (bf16[80,1152]{1,0:T(8,128)(2,1)S(1)}, bf16[80,1152]{1,0:T(8,128)(2,1)S(1)}, u32[]{:S(2)}, u32[]{:S(2)}) collective-permute-start(bf16[80,1152]{1,0:T(8,128)(2,1)S(1)} %collective-permute-done.30.refs_2_), channel_id=1, source_target_pairs={{0,4},{4,0},{8,12},{12,8},{16,20},{20,16},{24,28},{28,24},{1,5},{5... | collective-permute-start | bytes 552968 | tf_op jit(solution)/shard_map/ppermute | solution.py:527
  149.7 16.1 %collective-permute-start.33 = (bf16[80,1152]{1,0:T(8,128)(2,1)S(1)}, bf16[80,1152]{1,0:T(8,128)(2,1)S(1)}, u32[]{:S(2)}, u32[]{:S(2)}) collective-permute-start(bf16[80,1152]{1,0:T(8,128)(2,1)S(1)} %collective-permute-done.32.refs_3_), channel_id=1, source_target_pairs={{0,4},{4,0},{8,12},{12,8},{16,20},{20,16},{24,28},{28,24},{1,5},{5... | collective-permute-start | bytes 552968 | tf_op jit(solution)/shard_map/ppermute | solution.py:527
  157.8 8.1 %collective-permute-start.35 = (bf16[80,1152]{1,0:T(8,128)(2,1)S(1)}, bf16[80,1152]{1,0:T(8,128)(2,1)S(1)}, u32[]{:S(2)}, u32[]{:S(2)}) collective-permute-start(bf16[80,1152]{1,0:T(8,128)(2,1)S(1)} %collective-permute-done.34.refs_4_), channel_id=1, source_target_pairs={{0,4},{4,0},{8,12},{12,8},{16,20},{20,16},{24,28},{28,24},{1,5},{5... | collective-permute-start | bytes 552968 | tf_op jit(solution)/shard_map/ppermute | solution.py:527
  159.3 10.4 %collective-permute-start.42 = (f32[8,16,128]{2,1,0:T(8,128)S(1)}, f32[8,16,128]{2,1,0:T(8,128)S(1)}, u32[]{:S(2)}, u32[]{:S(2)}) collective-permute-start(f32[8,16,128]{2,1,0:T(8,128)S(1)} %get-tuple-element.88), channel_id=1, source_target_pairs={{0,4},{4,0},{8,12},{12,8},{16,20},{20,16},{24,28},{28,24},{1,5},{5... | collective-permute-start | bytes 196616 | tf_op jit(solution)/shard_map/ppermute | solution.py:527
  167.8 2.0 %collective-permute-start.37 = (bf16[32,768]{1,0:T(8,128)(2,1)S(1)}, bf16[32,768]{1,0:T(8,128)(2,1)S(1)}, u32[]{:S(2)}, u32[]{:S(2)}) collective-permute-start(bf16[32,768]{1,0:T(8,128)(2,1)S(1)} %get-tuple-element.74), channel_id=1, source_target_pairs={{0,1},{1,0},{2,3},{3,2},{4,5},{5,4},{6,7},{7,6},{8,9},{9,8},{10,11... | collective-permute-start | bytes 147464 | tf_op jit(solution)/shard_map/ppermute | solution.py:530
  167.8 4.2 %collective-permute-start.38 = (bf16[32,768]{1,0:T(8,128)(2,1)S(1)}, bf16[32,768]{1,0:T(8,128)(2,1)S(1)}, u32[]{:S(2)}, u32[]{:S(2)}) collective-permute-start(bf16[32,768]{1,0:T(8,128)(2,1)S(1)} %get-tuple-element.75), channel_id=1, source_target_pairs={{0,2},{1,3},{2,0},{3,1},{4,6},{5,7},{6,4},{7,5},{8,10},{9,11},{10,... | collective-permute-start | bytes 147464 | tf_op jit(solution)/shard_map/ppermute | solution.py:530
  169.4 3.7 %collective-permute-start.39 = (bf16[32,768]{1,0:T(8,128)(2,1)S(1)}, bf16[32,768]{1,0:T(8,128)(2,1)S(1)}, u32[]{:S(2)}, u32[]{:S(2)}) collective-permute-start(bf16[32,768]{1,0:T(8,128)(2,1)S(1)} %get-tuple-element.76), channel_id=1, source_target_pairs={{0,3},{1,2},{2,1},{3,0},{4,7},{5,6},{6,5},{7,4},{8,11},{9,10},{10,... | collective-permute-start | bytes 147464 | tf_op jit(solution)/shard_map/ppermute | solution.py:530
  (15 other events, 201.6 us)

commit v8 on v7

--- a/solution.py
+++ b/solution.py
@@ -465,20 +465,21 @@
         out[...] = mm(one_hot(wanted == row_base[...]), result).astype(BF16)
 
 
-def combine_kernel(nz, cap, s, *refs):
+def stream_kernel(cap, s, keep, received, residual, codes, ret_r, ret_base, out, pick):
+    nz = codes.shape[0]
     j = s[2]
+    out[...] = residual[...].astype(F32) + (keep[...].astype(F32) + received[...].astype(F32))
+    ids = (lax.bitwise_xor(ret_r[...], j) * nz + j) * cap + ret_base[...]
+    pick[...] = one_hot((ids == codes[j, 0:1, :]) | (ids == codes[j, 1:2, :]))
+
+
+def combine_kernel(nz, s, *refs):
     returned = refs[:nz]
-    keep, received, residual, codes, ret_r, ret_base, out, stacked, own, sem = refs[nz:]
-    copies = run_copies([(residual, own)], sem)
+    before, pick, out, stacked = refs[nz:]
     rows = returned[0].shape[0]
     for n in range(nz):
         stacked[n * rows : (n + 1) * rows, :] = returned[n][...]
-    ids = lax.bitwise_xor(ret_r[...], j) * (nz * cap) + ret_base[...] + j * cap
-    pick = (ids == codes[j, 0:1, :]) | (ids == codes[j, 1:2, :])
-    added = mm(one_hot(pick), stacked[...], TN)
-    copies[0].wait()
-    total = own[...].astype(F32) + (keep[...].astype(F32) + received[...].astype(F32))
-    out[...] = (total + added).astype(BF16)
+    out[...] = (before[...] + mm(pick[...], stacked[...], TN)).astype(BF16)
 
 
 def local(
@@ -800,17 +801,19 @@
     else:
         hidden, weight = stages(up, rows_out, groups)
     state = stages(down, hidden, [groups[0] + groups[1], groups[2]])
+    stream, picks = call(
+        functools.partial(stream_kernel, cap),
+        place,
+        [keep_all[0], received_all[0], residual, codes, ret_r, ret_base],
+        [sds((block, cols), F32), sds((nz * ret_rows, block), BF16)],
+    )
     returned = [state[0]] + [swap(state[r], r) for r in range(1, nz)]
     (layer_out,) = call(
-        functools.partial(combine_kernel, nz, cap),
+        functools.partial(combine_kernel, nz),
         place,
-        returned + [keep_all[0], received_all[0], hbm(residual), codes, ret_r, ret_base],
+        returned + [stream, picks],
         [sds((block, cols), BF16)],
-        [
-            pltpu.VMEM((nz * ret_rows, cols), BF16),
-            pltpu.VMEM((block, cols), BF16),
-            pltpu.SemaphoreType.DMA((1,)),
-        ],
+        [pltpu.VMEM((nz * ret_rows, cols), BF16)],
     )
     return layer_out, final_rows
 

time: 176 us -> 175 us (level)
    pallas_call x13 -> x14, Pallas kernels: 42.6 us -> 43 us  [call(): pl.pallas_call(kernel, out_shape=list(outs), grid_spec=pltpu.PrefetchScal...]
where the time goes in v8:
time: 175 us
  waiting for transfers between devices  73.6 us (42%)
  starting transfers between devices  50.5 us (29%)
  Pallas kernels  46.8 us (27%)
  local copies, waits for them, and re-layouts  2.15 us (1%)
    ppermute x16, waiting for transfers between devices, z_turn(): return lax.ppermute(a, 'seq', pairs)  58.1 us
    pallas_call x14, Pallas kernels, call(): pl.pallas_call(kernel, out_shape=list(outs), grid_spec=pltpu.PrefetchScal...  43 us
    ppermute x16, starting transfers between devices, z_turn(): return lax.ppermute(a, 'seq', pairs)  24.6 us
    ppermute x17, starting transfers between devices, y_turn(): return lax.ppermute(a, 'seq', pairs)  19 us
    ppermute x10, waiting for transfers between devices, swap(): return lax.ppermute(a, 'exp', [(p, p ^ r) for p in range(nz)])  7.93 us
    ppermute x17, waiting for transfers between devices, y_turn(): return lax.ppermute(a, 'seq', pairs)  7.57 us
    ppermute x10, starting transfers between devices, swap(): return lax.ppermute(a, 'exp', [(p, p ^ r) for p in range(nz)])  6.96 us
  transfers between devices with their start and end apart: 43, of which 19 were waited for; matrix products, arithmetic and copies ran while one was open for 1% of the time, Pallas kernels for 20%

profile of v8, /device:TPU:0, one launch (start us, length us, event | category | flops | bytes accessed | tf_op | source)
XLA Modules:
  0.0 174.6 jit_solution(5388760398323616087)
XLA Ops:
  0.7 2.0 %shard_map.230 = bf16[2,128,1024]{2,1,0:T(8,128)(2,1)} custom-call(bf16[128,2048]{1,0:T(8,128)(2,1)} %refs_0_.5, bf16[128,2048]{1,0:T(8,128)(2,1)} %refs_1_.4), custom_call_target="tpu_custom_call" | custom-call | tf_op jit(solution)/shard_map/pallas_call | solution.py:593
  2.8 3.0 %collective-permute-start = (bf16[2,128,1024]{2,1,0:T(8,128)(2,1)}, bf16[2,128,1024]{2,1,0:T(8,128)(2,1)S(1)}, u32[]{:S(2)}, u32[]{:S(2)}) collective-permute-start(bf16[2,128,1024]{2,1,0:T(8,128)(2,1)} %shard_map.230), channel_id=1, source_target_pairs={{0,4},{4,0},{8,12},{12,8},{16,20},{20,16},{24,28},{28,24},{1,5},{5... | collective-permute-start | bytes 1572872 | tf_op jit(solution)/shard_map/ppermute | solution.py:528
  5.8 1.5 collective-permute-start.3
  8.7 1.8 %shard_map.231 = bf16[2,128,1024]{2,1,0:T(8,128)(2,1)} custom-call(bf16[128,2048]{1,0:T(8,128)(2,1)} %refs_2_.2, bf16[128,2048]{1,0:T(8,128)(2,1)} %refs_3_.1), custom_call_target="tpu_custom_call" | custom-call | tf_op jit(solution)/shard_map/pallas_call | solution.py:595
  11.9 1.6 shard_map.232
  13.4 4.7 %collective-permute-done.1.refs_4_ = f32[16,128]{1,0:T(8,128)S(1)} collective-permute-done((f32[16,128]{1,0:T(8,128)}, f32[16,128]{1,0:T(8,128)S(1)}, u32[]{:S(2)}, u32[]{:S(2)}) %collective-permute-start.1) | collective-permute-done | bytes 8224 | tf_op jit(solution)/shard_map/ppermute | solution.py:528
  18.1 1.7 collective-permute-start.5
  19.9 3.0 %shard_map.233 = (bf16[272,128]{1,0:T(8,128)(2,1)S(1)}, bf16[272,128]{1,0:T(8,128)(2,1)S(1)}, bf16[272,128]{1,0:T(8,128)(2,1)S(1)}, bf16[272,128]{1,0:T(8,128)(2...) custom-call(s32[3]{0:T(128)S(1)} %pad_add_fusion.s, bf16[128,2048]{1,0:T(8,128)(2,1)S(1)} %copy-done.1, ...), custom_call_target="tpu_custom_call" | custom-call | flops 67108864 | bytes 1884160 | tf_op jit(solution)/shard_map/pallas_call | solution.py:47
  22.9 1.6 collective-permute-start.6
  24.5 2.6 %collective-permute-start.7 = (bf16[272,128]{1,0:T(8,128)(2,1)S(1)}, bf16[272,128]{1,0:T(8,128)(2,1)S(1)}, u32[]{:S(2)}, u32[]{:S(2)}) collective-permute-start(bf16[272,128]{1,0:T(8,128)(2,1)S(1)} %get-tuple-element.51), channel_id=1, source_target_pairs={{0,16},{4,20},{8,24},{12,28},{16,0},{20,4},{24,8},{28,12},{1,17},{... | collective-permute-start | bytes 208904 | tf_op jit(solution)/shard_map/ppermute | solution.py:524
  27.1 1.3 collective-permute-start.8
  29.7 1.7 collective-permute-done.7.refs_2_
  33.1 2.7 %collective-permute-start.11 = (bf16[256,128]{1,0:T(8,128)(2,1)S(1)}, bf16[256,128]{1,0:T(8,128)(2,1)S(1)}, u32[]{:S(2)}, u32[]{:S(2)}) collective-permute-start(bf16[256,128]{1,0:T(8,128)(2,1)S(1)} %get-tuple-element.56), channel_id=1, source_target_pairs={{0,24},{4,28},{8,0},{12,4},{16,8},{20,12},{24,16},{28,20},{1,25},{... | collective-permute-start | bytes 196616 | tf_op jit(solution)/shard_map/ppermute | solution.py:524
  35.9 2.7 %collective-permute-done.10.refs_8_ = bf16[256,128]{1,0:T(8,128)(2,1)S(1)} collective-permute-done((bf16[256,128]{1,0:T(8,128)(2,1)S(1)}, bf16[256,128]{1,0:T(8,128)(2,1)S(1)}, u32[]{:S(2)}, u32[]{:S(2)}) %collective-permute-start.10) | collective-permute-done | bytes 65568 | tf_op jit(solution)/shard_map/ppermute | solution.py:524
  38.6 3.2 %collective-permute-done.9.refs_7_ = bf16[256,128]{1,0:T(8,128)(2,1)S(1)} collective-permute-done((bf16[256,128]{1,0:T(8,128)(2,1)S(1)}, bf16[256,128]{1,0:T(8,128)(2,1)S(1)}, u32[]{:S(2)}, u32[]{:S(2)}) %collective-permute-start.9) | collective-permute-done | bytes 65568 | tf_op jit(solution)/shard_map/ppermute | solution.py:524
  41.9 3.4 %shard_map.235.refs_0_ = bf16[256,1024]{1,0:T(8,128)(2,1)S(1)} custom-call(s32[3]{0:T(128)S(1)} %pad_add_fusion.s, bf16[128,2048]{1,0:T(8,128)(2,1)S(1)} %copy-done.1, bf16[128,2048]{1,0:T(8,128)(2,1)S(1)} %copy-done.2, bf16[128,2048]{1,0:T(8,128)(2,1)S(1)} %copy-done.3, bf16[128,2048]{1,0:T(8,128)(2,1)S(1)} %copy-done.4, ...), custom_call_target="tpu_custom_call" | custom-call | flops 268435456 | bytes 3956736 | tf_op jit(solution)/shard_map/pallas_call | solution.py:47
  45.3 3.8 %collective-permute-start.17 = (bf16[256,1024]{1,0:T(8,128)(2,1)S(1)}, bf16[256,1024]{1,0:T(8,128)(2,1)S(1)}, u32[]{:S(2)}, u32[]{:S(2)}) collective-permute-start(bf16[256,1024]{1,0:T(8,128)(2,1)S(1)} %shard_map.235.refs_0_), channel_id=1, source_target_pairs={{0,24},{4,28},{8,0},{12,4},{16,8},{20,12},{24,16},{28,20},{1,25},{... | collective-permute-start | bytes 1572872 | tf_op jit(solution)/shard_map/ppermute | solution.py:524
  49.7 12.3 %collective-permute-done.12.refs_1_ = bf16[256,1024]{1,0:T(8,128)(2,1)S(1)} collective-permute-done((bf16[256,1024]{1,0:T(8,128)(2,1)S(1)}, bf16[256,1024]{1,0:T(8,128)(2,1)S(1)}, u32[]{:S(2)}, u32[]{:S(2)}) %collective-permute-start.12) | collective-permute-done | bytes 524320 | tf_op jit(solution)/shard_map/ppermute | solution.py:524
  62.5 5.9 %collective-permute-done.17.refs_2_ = bf16[256,1024]{1,0:T(8,128)(2,1)S(1)} collective-permute-done((bf16[256,1024]{1,0:T(8,128)(2,1)S(1)}, bf16[256,1024]{1,0:T(8,128)(2,1)S(1)}, u32[]{:S(2)}, u32[]{:S(2)}) %collective-permute-start.17) | collective-permute-done | bytes 524320 | tf_op jit(solution)/shard_map/ppermute | solution.py:524
  69.0 2.6 %collective-permute-start.13 = (bf16[128,1024]{1,0:T(8,128)(2,1)S(1)}, bf16[128,1024]{1,0:T(8,128)(2,1)S(1)}, u32[]{:S(2)}, u32[]{:S(2)}) collective-permute-start(bf16[128,1024]{1,0:T(8,128)(2,1)S(1)} %get-tuple-element.91), channel_id=1, source_target_pairs={{0,16},{4,20},{8,24},{12,28},{16,0},{20,4},{24,8},{28,12},{1,17},{... | collective-permute-start | bytes 786440 | tf_op jit(solution)/shard_map/ppermute | solution.py:524
  72.0 15.2 %collective-permute-done.13.refs_0_ = bf16[128,1024]{1,0:T(8,128)(2,1)S(1)} collective-permute-done((bf16[128,1024]{1,0:T(8,128)(2,1)S(1)}, bf16[128,1024]{1,0:T(8,128)(2,1)S(1)}, u32[]{:S(2)}, u32[]{:S(2)}) %collective-permute-start.13) | collective-permute-done | bytes 262176 | tf_op jit(solution)/shard_map/ppermute | solution.py:524
  87.9 4.6 %collective-permute-done.14.refs_1_ = bf16[128,1024]{1,0:T(8,128)(2,1)S(1)} collective-permute-done((bf16[128,1024]{1,0:T(8,128)(2,1)S(1)}, bf16[128,1024]{1,0:T(8,128)(2,1)S(1)}, u32[]{:S(2)}, u32[]{:S(2)}) %collective-permute-start.14) | collective-permute-done | bytes 262176 | tf_op jit(solution)/shard_map/ppermute | solution.py:524
  93.4 4.1 %shard_map.236 = (bf16[3,256,768]{2,1,0:T(8,128)(2,1)S(1)}, f32[320,768]{1,0:T(8,128)S(1)}) custom-call(s32[3]{0:T(128)S(1)} %pad_add_fusion.s, bf16[256,1024]{1,0:T(8,128)(2,1)S(1)} %shard_map.235.refs_0_, bf16[256,1024]{1,0:T(8,128)(2,1)S(1)} %collective-permute-done.12.refs_1_, bf16[256,1024]{1,0:T(8,128)(2,1)S(1)} %collective-permute-done.17.refs_2_, ...), custom_call_target="tpu_custom_call" | custom-call | flops 2415919104 | bytes 11610624 | tf_op jit(solution)/shard_map/pallas_call | solution.py:47
  97.6 2.8 %collective-permute-done.16.refs_3_ = bf16[128,1024]{1,0:T(8,128)(2,1)S(1)} collective-permute-done((bf16[128,1024]{1,0:T(8,128)(2,1)S(1)}, bf16[128,1024]{1,0:T(8,128)(2,1)S(1)}, u32[]{:S(2)}, u32[]{:S(2)}) %collective-permute-start.16) | collective-permute-done | bytes 262176 | tf_op jit(solution)/shard_map/ppermute | solution.py:528
  100.4 3.0 %shard_map.237 = (f32[160,768]{1,0:T(8,128)S(1)}, bf16[160,768]{1,0:T(8,128)(2,1)S(1)}, bf16[2,256,768]{2,1,0:T(8,128)(2,1)S(1)}, bf16[2,256,768]{2,1,0:T(8,128)(2,1)S(1)}) custom-call(s32[3]{0:T(128)S(1)} %pad_add_fusion.s, bf16[128,1024]{1,0:T(8,128)(2,1)S(1)} %collective-permute-done.13.refs_0_, bf16[128,1024]{1,0:T(8,128)(2,1)S(1)} %collective-permute-done.14.refs_1_, ...), custom_call_target="tpu_custom_call" | custom-call | flops 805306368 | bytes 12216832 | tf_op jit(solution)/shard_map/pallas_call | solution.py:47
  103.6 1.5 collective-permute-done.21
  105.1 1.4 collective-permute-start.22
  106.5 4.0 %collective-permute-done.22.received = bf16[80,768]{1,0:T(8,128)(2,1)S(1)} collective-permute-done((bf16[80,768]{1,0:T(8,128)(2,1)S(1)}, bf16[80,768]{1,0:T(8,128)(2,1)S(1)}, u32[]{:S(2)}, u32[]{:S(2)}) %collective-permute-start.22) | collective-permute-done | bytes 122912 | tf_op jit(solution)/shard_map/ppermute | solution.py:531
  111.7 1.8 %collective-permute-start.23 = (bf16[80,768]{1,0:T(8,128)(2,1)S(1)}, bf16[80,768]{1,0:T(8,128)(2,1)S(1)}, u32[]{:S(2)}, u32[]{:S(2)}) collective-permute-start(bf16[80,768]{1,0:T(8,128)(2,1)S(1)} %shard_map.238.refs_0_), channel_id=1, source_target_pairs={{0,8},{4,12},{8,16},{12,20},{16,24},{20,28},{24,0},{28,4},{1,9},{5... | collective-permute-start | bytes 368648 | tf_op jit(solution)/shard_map/ppermute | solution.py:524
  113.5 2.1 %collective-permute-start.25 = (bf16[80,768]{1,0:T(8,128)(2,1)S(1)}, bf16[80,768]{1,0:T(8,128)(2,1)S(1)}, u32[]{:S(2)}, u32[]{:S(2)}) collective-permute-start(bf16[80,768]{1,0:T(8,128)(2,1)S(1)} %shard_map.238.refs_0_), channel_id=1, source_target_pairs={{0,24},{4,28},{8,0},{12,4},{16,8},{20,12},{24,16},{28,20},{1,25},{... | collective-permute-start | bytes 368648 | tf_op jit(solution)/shard_map/ppermute | solution.py:524
  116.8 3.4 %shard_map.239 = (f32[80,1152]{1,0:T(8,128)S(1)}, f32[80,1152]{1,0:T(8,128)S(1)}, f32[1,768]{1,0:T(1,128)S(1)}) custom-call(s32[3]{0:T(128)S(1)} %pad_add_fusion.s, bf16[80,768]{1,0:T(8,128)(2,1)S(1)} %shard_map.238.refs_0_, bf16[1,1152,6144]{2,1,0:T(8,128)(2,1)} %refs_6_.7, bf16[1,1152,6144]{2,1,0:T(8,128)(2,1)} %refs_7_.7, ...), custom_call_target="tpu_custom_call" | custom-call | flops 283115520 | bytes 29215744 | tf_op jit(solution)/shard_map/pallas_call | solution.py:47
  120.2 2.0 %collective-permute-done.27.refs_3_ = bf16[80,768]{1,0:T(8,128)(2,1)S(1)} collective-permute-done((bf16[80,768]{1,0:T(8,128)(2,1)S(1)}, bf16[80,768]{1,0:T(8,128)(2,1)S(1)}, u32[]{:S(2)}, u32[]{:S(2)}) %collective-permute-start.27) | collective-permute-done | bytes 122912 | tf_op jit(solution)/shard_map/ppermute | solution.py:524
  122.2 1.5 collective-permute-start.28
  124.2 1.5 collective-permute-start.26
  125.7 6.9 %shard_map.240 = (f32[80,1152]{1,0:T(8,128)S(1)}, f32[80,1152]{1,0:T(8,128)S(1)}, f32[1,768]{1,0:T(1,128)S(1)}) custom-call(s32[3]{0:T(128)S(1)} %pad_add_fusion.s, bf16[80,768]{1,0:T(8,128)(2,1)S(1)} %collective-permute-done.29.refs_0_, bf16[80,768]{1,0:T(8,128)(2,1)S(1)} %collective-permute-done.23.refs_1_, ...), custom_call_target="tpu_custom_call" | custom-call | flops 1132462080 | bytes 30324736 | tf_op jit(solution)/shard_map/pallas_call | solution.py:47
  132.7 5.7 %shard_map.241 = (bf16[80,1152]{1,0:T(8,128)(2,1)S(1)}, f32[80,128]{1,0:T(8,128)S(1)}) custom-call(s32[3]{0:T(128)S(1)} %pad_add_fusion.s, bf16[80,768]{1,0:T(8,128)(2,1)S(1)} %collective-permute-done.24.refs_0_, bf16[80,768]{1,0:T(8,128)(2,1)S(1)} %collective-permute-done.26.refs_1_, bf16[80,768]{1,0:T(8,128)(2,1)S(1)} %collective-permute-done.28.refs_2_, ...), custom_call_target="tpu_custom_call" | custom-call | flops 849346560 | bytes 29686784 | tf_op jit(solution)/shard_map/pallas_call | solution.py:47
  138.4 1.2 collective-permute-start.30
  139.6 2.6 %collective-permute-start.32 = (bf16[80,1152]{1,0:T(8,128)(2,1)S(1)}, bf16[80,1152]{1,0:T(8,128)(2,1)S(1)}, u32[]{:S(2)}, u32[]{:S(2)}) collective-permute-start(bf16[80,1152]{1,0:T(8,128)(2,1)S(1)} %get-tuple-element.71.refs_0_), channel_id=1, source_target_pairs={{0,24},{4,28},{8,0},{12,4},{16,8},{20,12},{24,16},{28,20},{1,25},{... | collective-permute-start | bytes 552968 | tf_op jit(solution)/shard_map/ppermute | solution.py:524
  144.7 1.6 collective-permute-start.41
  146.3 1.5 collective-permute-done.30.refs_2_
  147.8 1.5 collective-permute-start.31
  150.9 6.9 %collective-permute-done.34.refs_4_ = bf16[80,1152]{1,0:T(8,128)(2,1)S(1)} collective-permute-done((bf16[80,1152]{1,0:T(8,128)(2,1)S(1)}, bf16[80,1152]{1,0:T(8,128)(2,1)S(1)}, u32[]{:S(2)}, u32[]{:S(2)}) %collective-permute-start.34) | collective-permute-done | bytes 184352 | tf_op jit(solution)/shard_map/ppermute | solution.py:524
  157.8 1.4 collective-permute-start.35
  160.0 5.9 %shard_map.242 = (f32[80,768]{1,0:T(8,128)S(1)}, bf16[3,1152,768]{2,1,0:T(8,128)(2,1)S(1)}) custom-call(s32[3]{0:T(128)S(1)} %pad_add_fusion.s, bf16[80,1152]{1,0:T(8,128)(2,1)S(1)} %get-tuple-element.71.refs_0_, bf16[80,1152]{1,0:T(8,128)(2,1)S(1)} %collective-permute-done.36.refs_1_, bf16[80,1152]{1,0:T(8,128)(2,1)S(1)} %collective-permute-done.30.refs_2_, ...), custom_call_target="tpu_custom_call" | custom-call | flops 707788800 | bytes 20631552 | tf_op jit(solution)/shard_map/pallas_call | solution.py:47
  166.0 1.8 %shard_map.243 = (bf16[32,768]{1,0:T(8,128)(2,1)S(1)}, bf16[32,768]{1,0:T(8,128)(2,1)S(1)}, bf16[32,768]{1,0:T(8,128)(2,1)S(1)}, bf16[32,768]{1,0:T(8,128)(2,1)S(1)}) custom-call(s32[3]{0:T(128)S(1)} %pad_add_fusion.s, bf16[80,1152]{1,0:T(8,128)(2,1)S(1)} %collective-permute-done.31.refs_0_, bf16[80,1152]{1,0:T(8,128)(2,1)S(1)} %collective-permute-done.33.refs_1_, ...), custom_call_target="tpu_custom_call" | custom-call | flops 424673280 | bytes 6345152 | tf_op jit(solution)/shard_map/pallas_call | solution.py:47
  167.9 1.5 collective-permute-start.38
  170.6 1.4 collective-permute-done.38.refs_2_
  173.1 1.6 shard_map.245
  (103 shorter events, 19.7 us)
Async XLA Ops:
  0.7 41.2 %copy-start.3 = (bf16[128,2048]{1,0:T(8,128)(2,1)S(1)}, bf16[128,2048]{1,0:T(8,128)(2,1)}, u32[]{:S(2)}) copy-start(bf16[128,2048]{1,0:T(8,128)(2,1)} %refs_2_.2) | copy-start | bytes 1572868
  0.7 41.1 %copy-start.4 = (bf16[128,2048]{1,0:T(8,128)(2,1)S(1)}, bf16[128,2048]{1,0:T(8,128)(2,1)}, u32[]{:S(2)}) copy-start(bf16[128,2048]{1,0:T(8,128)(2,1)} %refs_3_.1) | copy-start | bytes 1572868
  2.8 15.3 %collective-permute-start = (bf16[2,128,1024]{2,1,0:T(8,128)(2,1)}, bf16[2,128,1024]{2,1,0:T(8,128)(2,1)S(1)}, u32[]{:S(2)}, u32[]{:S(2)}) collective-permute-start(bf16[2,128,1024]{2,1,0:T(8,128)(2,1)} %shard_map.230), channel_id=1, source_target_pairs={{0,4},{4,0},{8,12},{12,8},{16,20},{20,16},{24,28},{28,24},{1,5},{5... | collective-permute-start | bytes 1572872 | tf_op jit(solution)/shard_map/ppermute | solution.py:528
  5.8 4.8 %collective-permute-start.2 = (s32[2,256]{1,0:T(2,128)}, s32[2,256]{1,0:T(2,128)S(1)}, u32[]{:S(2)}, u32[]{:S(2)}) collective-permute-start(s32[2,256]{1,0:T(2,128)} %bitcast.15), channel_id=1, source_target_pairs={{0,1},{1,0},{2,3},{3,2},{4,5},{5,4},{6,7},{7,6},{8,9},{9,8},{10,11... | collective-permute-start | bytes 6152 | tf_op jit(solution)/shard_map/ppermute | solution.py:531
  5.8 4.8 %collective-permute-start.3 = (s32[2,256]{1,0:T(2,128)}, s32[2,256]{1,0:T(2,128)S(1)}, u32[]{:S(2)}, u32[]{:S(2)}) collective-permute-start(s32[2,256]{1,0:T(2,128)} %bitcast.16), channel_id=1, source_target_pairs={{0,2},{1,3},{2,0},{3,1},{4,6},{5,7},{6,4},{7,5},{8,10},{9,11},{10,... | collective-permute-start | bytes 6152 | tf_op jit(solution)/shard_map/ppermute | solution.py:531
  7.3 3.3 %collective-permute-start.4 = (s32[2,256]{1,0:T(2,128)}, s32[2,256]{1,0:T(2,128)S(1)}, u32[]{:S(2)}, u32[]{:S(2)}) collective-permute-start(s32[2,256]{1,0:T(2,128)} %bitcast.17), channel_id=1, source_target_pairs={{0,3},{1,2},{2,1},{3,0},{4,7},{5,6},{6,5},{7,4},{8,11},{9,10},{10,... | collective-permute-start | bytes 6152 | tf_op jit(solution)/shard_map/ppermute | solution.py:531
  7.7 10.4 %collective-permute-start.1 = (f32[16,128]{1,0:T(8,128)}, f32[16,128]{1,0:T(8,128)S(1)}, u32[]{:S(2)}, u32[]{:S(2)}) collective-permute-start(f32[16,128]{1,0:T(8,128)} %bitcast.12), channel_id=1, source_target_pairs={{0,4},{4,0},{8,12},{12,8},{16,20},{20,16},{24,28},{28,24},{1,5},{5... | collective-permute-start | bytes 24584 | tf_op jit(solution)/shard_map/ppermute | solution.py:528
  18.1 23.7 %collective-permute-start.5 = (bf16[2,128,1024]{2,1,0:T(8,128)(2,1)}, bf16[2,128,1024]{2,1,0:T(8,128)(2,1)S(1)}, u32[]{:S(2)}, u32[]{:S(2)}) collective-permute-start(bf16[2,128,1024]{2,1,0:T(8,128)(2,1)} %shard_map.231), channel_id=1, source_target_pairs={{0,4},{4,0},{8,12},{12,8},{16,20},{20,16},{24,28},{28,24},{1,5},{5... | collective-permute-start | bytes 1572872 | tf_op jit(solution)/shard_map/ppermute | solution.py:528
  22.9 70.5 %copy-start = (bf16[2048,768]{1,0:T(8,128)(2,1)S(1)}, bf16[2048,768]{1,0:T(8,128)(2,1)}, u32[]{:S(2)}) copy-start(bf16[2048,768]{1,0:T(8,128)(2,1)} %refs_5_.3) | copy-start | bytes 9437188
  22.9 70.5 %copy-start.7 = (s32[320,1]{1,0:T(8,128)S(1)}, s32[320,1]{1,0:T(8,128)}, u32[]{:S(2)}) copy-start(s32[320,1]{1,0:T(8,128)} %constant.73.clone.refs_8_.refs_6_) | copy-start | bytes 3844
  22.9 70.5 %copy-start.8 = (s32[320,1]{1,0:T(8,128)S(1)}, s32[320,1]{1,0:T(8,128)}, u32[]{:S(2)}) copy-start(s32[320,1]{1,0:T(8,128)} %constant.74.clone.refs_9_.refs_7_) | copy-start | bytes 3844
  22.9 6.8 %collective-permute-start.6 = (bf16[272,128]{1,0:T(8,128)(2,1)S(1)}, bf16[272,128]{1,0:T(8,128)(2,1)S(1)}, u32[]{:S(2)}, u32[]{:S(2)}) collective-permute-start(bf16[272,128]{1,0:T(8,128)(2,1)S(1)} %get-tuple-element.50), channel_id=1, source_target_pairs={{0,8},{4,12},{8,16},{12,20},{16,24},{20,28},{24,0},{28,4},{1,9},{5... | collective-permute-start | bytes 208904 | tf_op jit(solution)/shard_map/ppermute | solution.py:524
  24.5 6.9 %collective-permute-start.7 = (bf16[272,128]{1,0:T(8,128)(2,1)S(1)}, bf16[272,128]{1,0:T(8,128)(2,1)S(1)}, u32[]{:S(2)}, u32[]{:S(2)}) collective-permute-start(bf16[272,128]{1,0:T(8,128)(2,1)S(1)} %get-tuple-element.51), channel_id=1, source_target_pairs={{0,16},{4,20},{8,24},{12,28},{16,0},{20,4},{24,8},{28,12},{1,17},{... | collective-permute-start | bytes 208904 | tf_op jit(solution)/shard_map/ppermute | solution.py:524
  27.1 4.8 %collective-permute-start.8 = (bf16[272,128]{1,0:T(8,128)(2,1)S(1)}, bf16[272,128]{1,0:T(8,128)(2,1)S(1)}, u32[]{:S(2)}, u32[]{:S(2)}) collective-permute-start(bf16[272,128]{1,0:T(8,128)(2,1)S(1)} %get-tuple-element.52), channel_id=1, source_target_pairs={{0,24},{4,28},{8,0},{12,4},{16,8},{20,12},{24,16},{28,20},{1,25},{... | collective-permute-start | bytes 208904 | tf_op jit(solution)/shard_map/ppermute | solution.py:524
  32.6 6.0 %collective-permute-start.10 = (bf16[256,128]{1,0:T(8,128)(2,1)S(1)}, bf16[256,128]{1,0:T(8,128)(2,1)S(1)}, u32[]{:S(2)}, u32[]{:S(2)}) collective-permute-start(bf16[256,128]{1,0:T(8,128)(2,1)S(1)} %get-tuple-element.55), channel_id=1, source_target_pairs={{0,16},{4,20},{8,24},{12,28},{16,0},{20,4},{24,8},{28,12},{1,17},{... | collective-permute-start | bytes 196616 | tf_op jit(solution)/shard_map/ppermute | solution.py:524
  33.1 5.5 %collective-permute-start.11 = (bf16[256,128]{1,0:T(8,128)(2,1)S(1)}, bf16[256,128]{1,0:T(8,128)(2,1)S(1)}, u32[]{:S(2)}, u32[]{:S(2)}) collective-permute-start(bf16[256,128]{1,0:T(8,128)(2,1)S(1)} %get-tuple-element.56), channel_id=1, source_target_pairs={{0,24},{4,28},{8,0},{12,4},{16,8},{20,12},{24,16},{28,20},{1,25},{... | collective-permute-start | bytes 196616 | tf_op jit(solution)/shard_map/ppermute | solution.py:524
  35.8 6.1 %collective-permute-start.9 = (bf16[256,128]{1,0:T(8,128)(2,1)S(1)}, bf16[256,128]{1,0:T(8,128)(2,1)S(1)}, u32[]{:S(2)}, u32[]{:S(2)}) collective-permute-start(bf16[256,128]{1,0:T(8,128)(2,1)S(1)} %get-tuple-element.54), channel_id=1, source_target_pairs={{0,8},{4,12},{8,16},{12,20},{16,24},{20,28},{24,0},{28,4},{1,9},{5... | collective-permute-start | bytes 196616 | tf_op jit(solution)/shard_map/ppermute | solution.py:524
  45.3 16.7 %collective-permute-start.12 = (bf16[256,1024]{1,0:T(8,128)(2,1)S(1)}, bf16[256,1024]{1,0:T(8,128)(2,1)S(1)}, u32[]{:S(2)}, u32[]{:S(2)}) collective-permute-start(bf16[256,1024]{1,0:T(8,128)(2,1)S(1)} %shard_map.235.refs_0_), channel_id=1, source_target_pairs={{0,8},{4,12},{8,16},{12,20},{16,24},{20,28},{24,0},{28,4},{1,9},{5... | collective-permute-start | bytes 1572872 | tf_op jit(solution)/shard_map/ppermute | solution.py:524
  45.3 23.1 %collective-permute-start.17 = (bf16[256,1024]{1,0:T(8,128)(2,1)S(1)}, bf16[256,1024]{1,0:T(8,128)(2,1)S(1)}, u32[]{:S(2)}, u32[]{:S(2)}) collective-permute-start(bf16[256,1024]{1,0:T(8,128)(2,1)S(1)} %shard_map.235.refs_0_), channel_id=1, source_target_pairs={{0,24},{4,28},{8,0},{12,4},{16,8},{20,12},{24,16},{28,20},{1,25},{... | collective-permute-start | bytes 1572872 | tf_op jit(solution)/shard_map/ppermute | solution.py:524
  49.2 44.2 %collective-permute-start.18 = (bf16[256,1024]{1,0:T(8,128)(2,1)S(1)}, bf16[256,1024]{1,0:T(8,128)(2,1)S(1)}, u32[]{:S(2)}, u32[]{:S(2)}) collective-permute-start(bf16[256,1024]{1,0:T(8,128)(2,1)S(1)} %shard_map.235.refs_0_), channel_id=1, source_target_pairs={{0,4},{4,0},{8,12},{12,8},{16,20},{20,16},{24,28},{28,24},{1,5},{5... | collective-permute-start | bytes 1572872 | tf_op jit(solution)/shard_map/ppermute | solution.py:528
  62.0 31.4 %collective-permute-start.19 = (bf16[256,1024]{1,0:T(8,128)(2,1)S(1)}, bf16[256,1024]{1,0:T(8,128)(2,1)S(1)}, u32[]{:S(2)}, u32[]{:S(2)}) collective-permute-start(bf16[256,1024]{1,0:T(8,128)(2,1)S(1)} %collective-permute-done.12.refs_1_), channel_id=1, source_target_pairs={{0,4},{4,0},{8,12},{12,8},{16,20},{20,16},{24,28},{28,24},{1,5},{5... | collective-permute-start | bytes 1572872 | tf_op jit(solution)/shard_map/ppermute | solution.py:528
  68.4 25.0 %collective-permute-start.20 = (bf16[256,1024]{1,0:T(8,128)(2,1)S(1)}, bf16[256,1024]{1,0:T(8,128)(2,1)S(1)}, u32[]{:S(2)}, u32[]{:S(2)}) collective-permute-start(bf16[256,1024]{1,0:T(8,128)(2,1)S(1)} %collective-permute-done.17.refs_2_), channel_id=1, source_target_pairs={{0,4},{4,0},{8,12},{12,8},{16,20},{20,16},{24,28},{28,24},{1,5},{5... | collective-permute-start | bytes 1572872 | tf_op jit(solution)/shard_map/ppermute | solution.py:528
  69.0 18.1 %collective-permute-start.13 = (bf16[128,1024]{1,0:T(8,128)(2,1)S(1)}, bf16[128,1024]{1,0:T(8,128)(2,1)S(1)}, u32[]{:S(2)}, u32[]{:S(2)}) collective-permute-start(bf16[128,1024]{1,0:T(8,128)(2,1)S(1)} %get-tuple-element.91), channel_id=1, source_target_pairs={{0,16},{4,20},{8,24},{12,28},{16,0},{20,4},{24,8},{28,12},{1,17},{... | collective-permute-start | bytes 786440 | tf_op jit(solution)/shard_map/ppermute | solution.py:524
  71.6 20.8 %collective-permute-start.14 = (bf16[128,1024]{1,0:T(8,128)(2,1)S(1)}, bf16[128,1024]{1,0:T(8,128)(2,1)S(1)}, u32[]{:S(2)}, u32[]{:S(2)}) collective-permute-start(bf16[128,1024]{1,0:T(8,128)(2,1)S(1)} %get-tuple-element.90), channel_id=1, source_target_pairs={{0,16},{4,20},{8,24},{12,28},{16,0},{20,4},{24,8},{28,12},{1,17},{... | collective-permute-start | bytes 786440 | tf_op jit(solution)/shard_map/ppermute | solution.py:524
  87.2 10.4 %collective-permute-start.15 = (bf16[128,1024]{1,0:T(8,128)(2,1)S(1)}, bf16[128,1024]{1,0:T(8,128)(2,1)S(1)}, u32[]{:S(2)}, u32[]{:S(2)}) collective-permute-start(bf16[128,1024]{1,0:T(8,128)(2,1)S(1)} %collective-permute-done.13.refs_0_), channel_id=1, source_target_pairs={{0,4},{4,0},{8,12},{12,8},{16,20},{20,16},{24,28},{28,24},{1,5},{5... | collective-permute-start | bytes 786440 | tf_op jit(solution)/shard_map/ppermute | solution.py:528
  92.4 8.0 %collective-permute-start.16 = (bf16[128,1024]{1,0:T(8,128)(2,1)S(1)}, bf16[128,1024]{1,0:T(8,128)(2,1)S(1)}, u32[]{:S(2)}, u32[]{:S(2)}) collective-permute-start(bf16[128,1024]{1,0:T(8,128)(2,1)S(1)} %collective-permute-done.14.refs_1_), channel_id=1, source_target_pairs={{0,4},{4,0},{8,12},{12,8},{16,20},{20,16},{24,28},{28,24},{1,5},{5... | collective-permute-start | bytes 786440 | tf_op jit(solution)/shard_map/ppermute | solution.py:528
  103.5 1.6 collective-permute-start.21
  105.1 5.4 %collective-permute-start.22 = (bf16[80,768]{1,0:T(8,128)(2,1)S(1)}, bf16[80,768]{1,0:T(8,128)(2,1)S(1)}, u32[]{:S(2)}, u32[]{:S(2)}) collective-permute-start(bf16[80,768]{1,0:T(8,128)(2,1)S(1)} %get-tuple-element.88), channel_id=1, source_target_pairs={{0,2},{1,3},{2,0},{3,1},{4,6},{5,7},{6,4},{7,5},{8,10},{9,11},{10,... | collective-permute-start | bytes 368648 | tf_op jit(solution)/shard_map/ppermute | solution.py:531
  111.6 32.9 %collective-permute-start.40 = (bf16[2,256,768]{2,1,0:T(8,128)(2,1)S(1)}, bf16[2,256,768]{2,1,0:T(8,128)(2,1)S(1)}, u32[]{:S(2)}, u32[]{:S(2)}) collective-permute-start(bf16[2,256,768]{2,1,0:T(8,128)(2,1)S(1)} %get-tuple-element.81), channel_id=1, source_target_pairs={{0,1},{1,0},{2,3},{3,2},{4,5},{5,4},{6,7},{7,6},{8,9},{9,8},{10,11... | collective-permute-start | bytes 2359304 | tf_op jit(solution)/shard_map/ppermute | solution.py:531
  111.6 10.6 %collective-permute-start.27 = (bf16[80,768]{1,0:T(8,128)(2,1)S(1)}, bf16[80,768]{1,0:T(8,128)(2,1)S(1)}, u32[]{:S(2)}, u32[]{:S(2)}) collective-permute-start(bf16[80,768]{1,0:T(8,128)(2,1)S(1)} %shard_map.238.refs_0_), channel_id=1, source_target_pairs={{0,16},{4,20},{8,24},{12,28},{16,0},{20,4},{24,8},{28,12},{1,17},{... | collective-permute-start | bytes 368648 | tf_op jit(solution)/shard_map/ppermute | solution.py:524
  111.7 12.0 %collective-permute-start.23 = (bf16[80,768]{1,0:T(8,128)(2,1)S(1)}, bf16[80,768]{1,0:T(8,128)(2,1)S(1)}, u32[]{:S(2)}, u32[]{:S(2)}) collective-permute-start(bf16[80,768]{1,0:T(8,128)(2,1)S(1)} %shard_map.238.refs_0_), channel_id=1, source_target_pairs={{0,8},{4,12},{8,16},{12,20},{16,24},{20,28},{24,0},{28,4},{1,9},{5... | collective-permute-start | bytes 368648 | tf_op jit(solution)/shard_map/ppermute | solution.py:524
  113.5 10.8 %collective-permute-start.25 = (bf16[80,768]{1,0:T(8,128)(2,1)S(1)}, bf16[80,768]{1,0:T(8,128)(2,1)S(1)}, u32[]{:S(2)}, u32[]{:S(2)}) collective-permute-start(bf16[80,768]{1,0:T(8,128)(2,1)S(1)} %shard_map.238.refs_0_), channel_id=1, source_target_pairs={{0,24},{4,28},{8,0},{12,4},{16,8},{20,12},{24,16},{28,20},{1,25},{... | collective-permute-start | bytes 368648 | tf_op jit(solution)/shard_map/ppermute | solution.py:524
  115.6 10.1 %collective-permute-start.29 = (bf16[80,768]{1,0:T(8,128)(2,1)S(1)}, bf16[80,768]{1,0:T(8,128)(2,1)S(1)}, u32[]{:S(2)}, u32[]{:S(2)}) collective-permute-start(bf16[80,768]{1,0:T(8,128)(2,1)S(1)} %shard_map.238.refs_0_), channel_id=1, source_target_pairs={{0,4},{4,0},{8,12},{12,8},{16,20},{20,16},{24,28},{28,24},{1,5},{5... | collective-permute-start | bytes 368648 | tf_op jit(solution)/shard_map/ppermute | solution.py:528
  122.2 10.5 %collective-permute-start.28 = (bf16[80,768]{1,0:T(8,128)(2,1)S(1)}, bf16[80,768]{1,0:T(8,128)(2,1)S(1)}, u32[]{:S(2)}, u32[]{:S(2)}) collective-permute-start(bf16[80,768]{1,0:T(8,128)(2,1)S(1)} %collective-permute-done.27.refs_3_), channel_id=1, source_target_pairs={{0,4},{4,0},{8,12},{12,8},{16,20},{20,16},{24,28},{28,24},{1,5},{5... | collective-permute-start | bytes 368648 | tf_op jit(solution)/shard_map/ppermute | solution.py:528
  123.7 9.0 %collective-permute-start.24 = (bf16[80,768]{1,0:T(8,128)(2,1)S(1)}, bf16[80,768]{1,0:T(8,128)(2,1)S(1)}, u32[]{:S(2)}, u32[]{:S(2)}) collective-permute-start(bf16[80,768]{1,0:T(8,128)(2,1)S(1)} %collective-permute-done.23.refs_1_), channel_id=1, source_target_pairs={{0,4},{4,0},{8,12},{12,8},{16,20},{20,16},{24,28},{28,24},{1,5},{5... | collective-permute-start | bytes 368648 | tf_op jit(solution)/shard_map/ppermute | solution.py:528
  124.2 8.5 %collective-permute-start.26 = (bf16[80,768]{1,0:T(8,128)(2,1)S(1)}, bf16[80,768]{1,0:T(8,128)(2,1)S(1)}, u32[]{:S(2)}, u32[]{:S(2)}) collective-permute-start(bf16[80,768]{1,0:T(8,128)(2,1)S(1)} %collective-permute-done.25.refs_2_), channel_id=1, source_target_pairs={{0,4},{4,0},{8,12},{12,8},{16,20},{20,16},{24,28},{28,24},{1,5},{5... | collective-permute-start | bytes 368648 | tf_op jit(solution)/shard_map/ppermute | solution.py:528
  138.4 9.4 %collective-permute-start.30 = (bf16[80,1152]{1,0:T(8,128)(2,1)S(1)}, bf16[80,1152]{1,0:T(8,128)(2,1)S(1)}, u32[]{:S(2)}, u32[]{:S(2)}) collective-permute-start(bf16[80,1152]{1,0:T(8,128)(2,1)S(1)} %get-tuple-element.71.refs_0_), channel_id=1, source_target_pairs={{0,8},{4,12},{8,16},{12,20},{16,24},{20,28},{24,0},{28,4},{1,9},{5... | collective-permute-start | bytes 552968 | tf_op jit(solution)/shard_map/ppermute | solution.py:524
  139.6 10.1 %collective-permute-start.32 = (bf16[80,1152]{1,0:T(8,128)(2,1)S(1)}, bf16[80,1152]{1,0:T(8,128)(2,1)S(1)}, u32[]{:S(2)}, u32[]{:S(2)}) collective-permute-start(bf16[80,1152]{1,0:T(8,128)(2,1)S(1)} %get-tuple-element.71.refs_0_), channel_id=1, source_target_pairs={{0,24},{4,28},{8,0},{12,4},{16,8},{20,12},{24,16},{28,20},{1,25},{... | collective-permute-start | bytes 552968 | tf_op jit(solution)/shard_map/ppermute | solution.py:524
  142.3 15.6 %collective-permute-start.34 = (bf16[80,1152]{1,0:T(8,128)(2,1)S(1)}, bf16[80,1152]{1,0:T(8,128)(2,1)S(1)}, u32[]{:S(2)}, u32[]{:S(2)}) collective-permute-start(bf16[80,1152]{1,0:T(8,128)(2,1)S(1)} %get-tuple-element.71.refs_0_), channel_id=1, source_target_pairs={{0,16},{4,20},{8,24},{12,28},{16,0},{20,4},{24,8},{28,12},{1,17},{... | collective-permute-start | bytes 552968 | tf_op jit(solution)/shard_map/ppermute | solution.py:524
  143.2 16.1 %collective-permute-start.36 = (bf16[80,1152]{1,0:T(8,128)(2,1)S(1)}, bf16[80,1152]{1,0:T(8,128)(2,1)S(1)}, u32[]{:S(2)}, u32[]{:S(2)}) collective-permute-start(bf16[80,1152]{1,0:T(8,128)(2,1)S(1)} %get-tuple-element.71.refs_0_), channel_id=1, source_target_pairs={{0,4},{4,0},{8,12},{12,8},{16,20},{20,16},{24,28},{28,24},{1,5},{5... | collective-permute-start | bytes 552968 | tf_op jit(solution)/shard_map/ppermute | solution.py:528
  144.7 25.1 %collective-permute-start.41 = (bf16[1,256,768]{2,1,0:T(8,128)(2,1)S(1)}, bf16[1,256,768]{2,1,0:T(8,128)(2,1)S(1)}, u32[]{:S(2)}, u32[]{:S(2)}) collective-permute-start(bf16[1,256,768]{2,1,0:T(8,128)(2,1)S(1)} %get-tuple-element.86), channel_id=1, source_target_pairs={{0,2},{1,3},{2,0},{3,1},{4,6},{5,7},{6,4},{7,5},{8,10},{9,11},{10,... | collective-permute-start | bytes 1179656 | tf_op jit(solution)/shard_map/ppermute | solution.py:531
  147.8 18.1 %collective-permute-start.31 = (bf16[80,1152]{1,0:T(8,128)(2,1)S(1)}, bf16[80,1152]{1,0:T(8,128)(2,1)S(1)}, u32[]{:S(2)}, u32[]{:S(2)}) collective-permute-start(bf16[80,1152]{1,0:T(8,128)(2,1)S(1)} %collective-permute-done.30.refs_2_), channel_id=1, source_target_pairs={{0,4},{4,0},{8,12},{12,8},{16,20},{20,16},{24,28},{28,24},{1,5},{5... | collective-permute-start | bytes 552968 | tf_op jit(solution)/shard_map/ppermute | solution.py:528
  149.8 16.2 %collective-permute-start.33 = (bf16[80,1152]{1,0:T(8,128)(2,1)S(1)}, bf16[80,1152]{1,0:T(8,128)(2,1)S(1)}, u32[]{:S(2)}, u32[]{:S(2)}) collective-permute-start(bf16[80,1152]{1,0:T(8,128)(2,1)S(1)} %collective-permute-done.32.refs_3_), channel_id=1, source_target_pairs={{0,4},{4,0},{8,12},{12,8},{16,20},{20,16},{24,28},{28,24},{1,5},{5... | collective-permute-start | bytes 552968 | tf_op jit(solution)/shard_map/ppermute | solution.py:528
  157.8 8.1 %collective-permute-start.35 = (bf16[80,1152]{1,0:T(8,128)(2,1)S(1)}, bf16[80,1152]{1,0:T(8,128)(2,1)S(1)}, u32[]{:S(2)}, u32[]{:S(2)}) collective-permute-start(bf16[80,1152]{1,0:T(8,128)(2,1)S(1)} %collective-permute-done.34.refs_4_), channel_id=1, source_target_pairs={{0,4},{4,0},{8,12},{12,8},{16,20},{20,16},{24,28},{28,24},{1,5},{5... | collective-permute-start | bytes 552968 | tf_op jit(solution)/shard_map/ppermute | solution.py:528
  159.4 10.4 %collective-permute-start.42 = (f32[8,16,128]{2,1,0:T(8,128)S(1)}, f32[8,16,128]{2,1,0:T(8,128)S(1)}, u32[]{:S(2)}, u32[]{:S(2)}) collective-permute-start(f32[8,16,128]{2,1,0:T(8,128)S(1)} %get-tuple-element.92), channel_id=1, source_target_pairs={{0,4},{4,0},{8,12},{12,8},{16,20},{20,16},{24,28},{28,24},{1,5},{5... | collective-permute-start | bytes 196616 | tf_op jit(solution)/shard_map/ppermute | solution.py:528
  167.8 2.8 %collective-permute-start.37 = (bf16[32,768]{1,0:T(8,128)(2,1)S(1)}, bf16[32,768]{1,0:T(8,128)(2,1)S(1)}, u32[]{:S(2)}, u32[]{:S(2)}) collective-permute-start(bf16[32,768]{1,0:T(8,128)(2,1)S(1)} %get-tuple-element.76), channel_id=1, source_target_pairs={{0,1},{1,0},{2,3},{3,2},{4,5},{5,4},{6,7},{7,6},{8,9},{9,8},{10,11... | collective-permute-start | bytes 147464 | tf_op jit(solution)/shard_map/ppermute | solution.py:531
  167.9 4.2 %collective-permute-start.38 = (bf16[32,768]{1,0:T(8,128)(2,1)S(1)}, bf16[32,768]{1,0:T(8,128)(2,1)S(1)}, u32[]{:S(2)}, u32[]{:S(2)}) collective-permute-start(bf16[32,768]{1,0:T(8,128)(2,1)S(1)} %get-tuple-element.77), channel_id=1, source_target_pairs={{0,2},{1,3},{2,0},{3,1},{4,6},{5,7},{6,4},{7,5},{8,10},{9,11},{10,... | collective-permute-start | bytes 147464 | tf_op jit(solution)/shard_map/ppermute | solution.py:531
  169.4 3.7 %collective-permute-start.39 = (bf16[32,768]{1,0:T(8,128)(2,1)S(1)}, bf16[32,768]{1,0:T(8,128)(2,1)S(1)}, u32[]{:S(2)}, u32[]{:S(2)}) collective-permute-start(bf16[32,768]{1,0:T(8,128)(2,1)S(1)} %get-tuple-element.78), channel_id=1, source_target_pairs={{0,3},{1,2},{2,1},{3,0},{4,7},{5,6},{6,5},{7,4},{8,11},{9,10},{10,... | collective-permute-start | bytes 147464 | tf_op jit(solution)/shard_map/ppermute | solution.py:531
  (15 other events, 194.4 us)

commit v9 on v8

--- a/solution.py
+++ b/solution.py
@@ -75,6 +75,17 @@
     for c in copies:
         c.start()
     return copies
+
+
+CUTS = 4
+
+
+def cut_rows(pairs):
+    cut = []
+    for a, b in pairs:
+        rows = a.shape[0] // CUTS
+        cut += [(a.at[pl.ds(n * rows, rows)], b.at[pl.ds(n * rows, rows)]) for n in range(CUTS)]
+    return cut
 
 
 def one_hot(mask):
@@ -146,7 +157,7 @@
     width = out.shape[2]
     share = lax.rem(lax.rem(lax.axis_index("seq"), ny) + away, ny)
     at = pl.ds(pl.multiple_of(share * width, 128), width)
-    for c in run_copies([(a.at[:, at], out.at[0]), (b.at[:, at], out.at[1])], sem):
+    for c in run_copies(cut_rows([(a.at[:, at], out.at[0]), (b.at[:, at], out.at[1])]), sem):
         c.wait()
 
 
@@ -162,7 +173,8 @@
     total_tok = tok * ny
     share = hd // nz
     mine = pl.ds(pl.multiple_of(y * heads * hd, 128), heads * hd)
-    copies = run_copies([(x.at[:, mine], own.at[m]) for m, x in enumerate((k_arg, v_arg))], sem)
+    pairs = [(x.at[:, mine], own.at[m]) for m, x in enumerate((k_arg, v_arg))]
+    copies = run_copies(cut_rows(pairs), sem)
     for d in range(ny):
         at = pl.multiple_of(lax.rem(y + ny - d, ny) * tok, tok)
         log_all[:, pl.ds(at, tok)] = logs[d][pl.ds(y * heads, heads), :]
@@ -587,7 +599,7 @@
             out_shape=sds((2, tok, width), BF16),
             in_specs=[pl.BlockSpec(memory_space=pltpu.HBM)] * 2,
             out_specs=pl.BlockSpec(memory_space=pltpu.VMEM),
-            scratch_shapes=[pltpu.SemaphoreType.DMA((2,))],
+            scratch_shapes=[pltpu.SemaphoreType.DMA((2 * CUTS,))],
             compiler_params=pltpu.CompilerParams(vmem_limit_bytes=60 * 1024 * 1024),
         )
         kvs.append(y_turn(pack(key_in, value_in), d))
@@ -626,7 +638,7 @@
             pltpu.VMEM((heads, hd, hd), BF16),
             pltpu.VMEM((16, hd), F32),
             pltpu.VMEM((2, tok, width), BF16),
-            pltpu.SemaphoreType.DMA((2,)),
+            pltpu.SemaphoreType.DMA((2 * CUTS,)),
         ],
         limit=40,
             flops=2 * long * hd * hd * heads,

time: 175 us -> 175 us (level)
  transfers between devices with their start and end apart: 43 -> 43, of which waited for: 19 -> 19; matrix products, arithmetic and copies ran while one was open for 1% -> 1% of each run, Pallas kernels for 20% -> 21%
where the time goes in v9:
time: 175 us
  waiting for transfers between devices  73.5 us (42%)
  starting transfers between devices  50.6 us (29%)
  Pallas kernels  47.2 us (27%)
  local copies, waits for them, and re-layouts  2.15 us (1%)
    ppermute x16, waiting for transfers between devices, z_turn(): return lax.ppermute(a, 'seq', pairs)  58 us
    pallas_call x14, Pallas kernels, call(): pl.pallas_call(kernel, out_shape=list(outs), grid_spec=pltpu.PrefetchScal...  43.2 us
    ppermute x16, starting transfers between devices, z_turn(): return lax.ppermute(a, 'seq', pairs)  24.6 us
    ppermute x17, starting transfers between devices, y_turn(): return lax.ppermute(a, 'seq', pairs)  19.1 us
    ppermute x10, waiting for transfers between devices, swap(): return lax.ppermute(a, 'exp', [(p, p ^ r) for p in range(nz)])  8.02 us
    ppermute x17, waiting for transfers between devices, y_turn(): return lax.ppermute(a, 'seq', pairs)  7.47 us
    ppermute x10, starting transfers between devices, swap(): return lax.ppermute(a, 'exp', [(p, p ^ r) for p in range(nz)])  6.93 us
  transfers between devices with their start and end apart: 43, of which 19 were waited for; matrix products, arithmetic and copies ran while one was open for 1% of the time, Pallas kernels for 21%

profile of v9, /device:TPU:0, one launch (start us, length us, event | category | flops | bytes accessed | tf_op | source)
XLA Modules:
  0.0 175.0 jit_solution(17136593543778266632)
XLA Ops:
  0.7 2.1 %shard_map.230 = bf16[2,128,1024]{2,1,0:T(8,128)(2,1)} custom-call(bf16[128,2048]{1,0:T(8,128)(2,1)} %refs_0_.5, bf16[128,2048]{1,0:T(8,128)(2,1)} %refs_1_.4), custom_call_target="tpu_custom_call" | custom-call | tf_op jit(solution)/shard_map/pallas_call | solution.py:605
  2.8 3.0 %collective-permute-start = (bf16[2,128,1024]{2,1,0:T(8,128)(2,1)}, bf16[2,128,1024]{2,1,0:T(8,128)(2,1)S(1)}, u32[]{:S(2)}, u32[]{:S(2)}) collective-permute-start(bf16[2,128,1024]{2,1,0:T(8,128)(2,1)} %shard_map.230), channel_id=1, source_target_pairs={{0,4},{4,0},{8,12},{12,8},{16,20},{20,16},{24,28},{28,24},{1,5},{5... | collective-permute-start | bytes 1572872 | tf_op jit(solution)/shard_map/ppermute | solution.py:540
  5.9 1.5 collective-permute-start.3
  8.8 1.9 %shard_map.231 = bf16[2,128,1024]{2,1,0:T(8,128)(2,1)} custom-call(bf16[128,2048]{1,0:T(8,128)(2,1)} %refs_2_.2, bf16[128,2048]{1,0:T(8,128)(2,1)} %refs_3_.1), custom_call_target="tpu_custom_call" | custom-call | tf_op jit(solution)/shard_map/pallas_call | solution.py:607
  12.0 1.6 shard_map.232
  13.6 4.6 %collective-permute-done.1.refs_4_ = f32[16,128]{1,0:T(8,128)S(1)} collective-permute-done((f32[16,128]{1,0:T(8,128)}, f32[16,128]{1,0:T(8,128)S(1)}, u32[]{:S(2)}, u32[]{:S(2)}) %collective-permute-start.1) | collective-permute-done | bytes 8224 | tf_op jit(solution)/shard_map/ppermute | solution.py:540
  18.2 1.7 collective-permute-start.5
  19.9 3.2 %shard_map.233 = (bf16[272,128]{1,0:T(8,128)(2,1)S(1)}, bf16[272,128]{1,0:T(8,128)(2,1)S(1)}, bf16[272,128]{1,0:T(8,128)(2,1)S(1)}, bf16[272,128]{1,0:T(8,128)(2...) custom-call(s32[3]{0:T(128)S(1)} %pad_add_fusion.s, bf16[128,2048]{1,0:T(8,128)(2,1)S(1)} %copy-done.1, ...), custom_call_target="tpu_custom_call" | custom-call | flops 67108864 | bytes 1884160 | tf_op jit(solution)/shard_map/pallas_call | solution.py:47
  23.2 1.6 collective-permute-start.6
  24.8 2.6 %collective-permute-start.7 = (bf16[272,128]{1,0:T(8,128)(2,1)S(1)}, bf16[272,128]{1,0:T(8,128)(2,1)S(1)}, u32[]{:S(2)}, u32[]{:S(2)}) collective-permute-start(bf16[272,128]{1,0:T(8,128)(2,1)S(1)} %get-tuple-element.51), channel_id=1, source_target_pairs={{0,16},{4,20},{8,24},{12,28},{16,0},{20,4},{24,8},{28,12},{1,17},{... | collective-permute-start | bytes 208904 | tf_op jit(solution)/shard_map/ppermute | solution.py:536
  27.4 1.3 collective-permute-start.8
  30.0 1.7 collective-permute-done.7.refs_2_
  33.4 2.7 %collective-permute-start.11 = (bf16[256,128]{1,0:T(8,128)(2,1)S(1)}, bf16[256,128]{1,0:T(8,128)(2,1)S(1)}, u32[]{:S(2)}, u32[]{:S(2)}) collective-permute-start(bf16[256,128]{1,0:T(8,128)(2,1)S(1)} %get-tuple-element.56), channel_id=1, source_target_pairs={{0,24},{4,28},{8,0},{12,4},{16,8},{20,12},{24,16},{28,20},{1,25},{... | collective-permute-start | bytes 196616 | tf_op jit(solution)/shard_map/ppermute | solution.py:536
  36.2 2.7 %collective-permute-done.10.refs_8_ = bf16[256,128]{1,0:T(8,128)(2,1)S(1)} collective-permute-done((bf16[256,128]{1,0:T(8,128)(2,1)S(1)}, bf16[256,128]{1,0:T(8,128)(2,1)S(1)}, u32[]{:S(2)}, u32[]{:S(2)}) %collective-permute-start.10) | collective-permute-done | bytes 65568 | tf_op jit(solution)/shard_map/ppermute | solution.py:536
  38.9 3.2 %collective-permute-done.9.refs_7_ = bf16[256,128]{1,0:T(8,128)(2,1)S(1)} collective-permute-done((bf16[256,128]{1,0:T(8,128)(2,1)S(1)}, bf16[256,128]{1,0:T(8,128)(2,1)S(1)}, u32[]{:S(2)}, u32[]{:S(2)}) %collective-permute-start.9) | collective-permute-done | bytes 65568 | tf_op jit(solution)/shard_map/ppermute | solution.py:536
  42.1 3.4 %shard_map.235.refs_0_ = bf16[256,1024]{1,0:T(8,128)(2,1)S(1)} custom-call(s32[3]{0:T(128)S(1)} %pad_add_fusion.s, bf16[128,2048]{1,0:T(8,128)(2,1)S(1)} %copy-done.1, bf16[128,2048]{1,0:T(8,128)(2,1)S(1)} %copy-done.2, bf16[128,2048]{1,0:T(8,128)(2,1)S(1)} %copy-done.3, bf16[128,2048]{1,0:T(8,128)(2,1)S(1)} %copy-done.4, ...), custom_call_target="tpu_custom_call" | custom-call | flops 268435456 | bytes 3956736 | tf_op jit(solution)/shard_map/pallas_call | solution.py:47
  45.6 3.8 %collective-permute-start.17 = (bf16[256,1024]{1,0:T(8,128)(2,1)S(1)}, bf16[256,1024]{1,0:T(8,128)(2,1)S(1)}, u32[]{:S(2)}, u32[]{:S(2)}) collective-permute-start(bf16[256,1024]{1,0:T(8,128)(2,1)S(1)} %shard_map.235.refs_0_), channel_id=1, source_target_pairs={{0,24},{4,28},{8,0},{12,4},{16,8},{20,12},{24,16},{28,20},{1,25},{... | collective-permute-start | bytes 1572872 | tf_op jit(solution)/shard_map/ppermute | solution.py:536
  50.0 12.3 %collective-permute-done.12.refs_1_ = bf16[256,1024]{1,0:T(8,128)(2,1)S(1)} collective-permute-done((bf16[256,1024]{1,0:T(8,128)(2,1)S(1)}, bf16[256,1024]{1,0:T(8,128)(2,1)S(1)}, u32[]{:S(2)}, u32[]{:S(2)}) %collective-permute-start.12) | collective-permute-done | bytes 524320 | tf_op jit(solution)/shard_map/ppermute | solution.py:536
  62.8 5.9 %collective-permute-done.17.refs_2_ = bf16[256,1024]{1,0:T(8,128)(2,1)S(1)} collective-permute-done((bf16[256,1024]{1,0:T(8,128)(2,1)S(1)}, bf16[256,1024]{1,0:T(8,128)(2,1)S(1)}, u32[]{:S(2)}, u32[]{:S(2)}) %collective-permute-start.17) | collective-permute-done | bytes 524320 | tf_op jit(solution)/shard_map/ppermute | solution.py:536
  69.3 2.6 %collective-permute-start.13 = (bf16[128,1024]{1,0:T(8,128)(2,1)S(1)}, bf16[128,1024]{1,0:T(8,128)(2,1)S(1)}, u32[]{:S(2)}, u32[]{:S(2)}) collective-permute-start(bf16[128,1024]{1,0:T(8,128)(2,1)S(1)} %get-tuple-element.91), channel_id=1, source_target_pairs={{0,16},{4,20},{8,24},{12,28},{16,0},{20,4},{24,8},{28,12},{1,17},{... | collective-permute-start | bytes 786440 | tf_op jit(solution)/shard_map/ppermute | solution.py:536
  72.3 15.2 %collective-permute-done.13.refs_0_ = bf16[128,1024]{1,0:T(8,128)(2,1)S(1)} collective-permute-done((bf16[128,1024]{1,0:T(8,128)(2,1)S(1)}, bf16[128,1024]{1,0:T(8,128)(2,1)S(1)}, u32[]{:S(2)}, u32[]{:S(2)}) %collective-permute-start.13) | collective-permute-done | bytes 262176 | tf_op jit(solution)/shard_map/ppermute | solution.py:536
  88.2 4.6 %collective-permute-done.14.refs_1_ = bf16[128,1024]{1,0:T(8,128)(2,1)S(1)} collective-permute-done((bf16[128,1024]{1,0:T(8,128)(2,1)S(1)}, bf16[128,1024]{1,0:T(8,128)(2,1)S(1)}, u32[]{:S(2)}, u32[]{:S(2)}) %collective-permute-start.14) | collective-permute-done | bytes 262176 | tf_op jit(solution)/shard_map/ppermute | solution.py:536
  93.7 4.1 %shard_map.236 = (bf16[3,256,768]{2,1,0:T(8,128)(2,1)S(1)}, f32[320,768]{1,0:T(8,128)S(1)}) custom-call(s32[3]{0:T(128)S(1)} %pad_add_fusion.s, bf16[256,1024]{1,0:T(8,128)(2,1)S(1)} %shard_map.235.refs_0_, bf16[256,1024]{1,0:T(8,128)(2,1)S(1)} %collective-permute-done.12.refs_1_, bf16[256,1024]{1,0:T(8,128)(2,1)S(1)} %collective-permute-done.17.refs_2_, ...), custom_call_target="tpu_custom_call" | custom-call | flops 2415919104 | bytes 11610624 | tf_op jit(solution)/shard_map/pallas_call | solution.py:47
  97.9 2.8 %collective-permute-done.16.refs_3_ = bf16[128,1024]{1,0:T(8,128)(2,1)S(1)} collective-permute-done((bf16[128,1024]{1,0:T(8,128)(2,1)S(1)}, bf16[128,1024]{1,0:T(8,128)(2,1)S(1)}, u32[]{:S(2)}, u32[]{:S(2)}) %collective-permute-start.16) | collective-permute-done | bytes 262176 | tf_op jit(solution)/shard_map/ppermute | solution.py:540
  100.7 3.0 %shard_map.237 = (f32[160,768]{1,0:T(8,128)S(1)}, bf16[160,768]{1,0:T(8,128)(2,1)S(1)}, bf16[2,256,768]{2,1,0:T(8,128)(2,1)S(1)}, bf16[2,256,768]{2,1,0:T(8,128)(2,1)S(1)}) custom-call(s32[3]{0:T(128)S(1)} %pad_add_fusion.s, bf16[128,1024]{1,0:T(8,128)(2,1)S(1)} %collective-permute-done.13.refs_0_, bf16[128,1024]{1,0:T(8,128)(2,1)S(1)} %collective-permute-done.14.refs_1_, ...), custom_call_target="tpu_custom_call" | custom-call | flops 805306368 | bytes 12216832 | tf_op jit(solution)/shard_map/pallas_call | solution.py:47
  103.8 1.5 collective-permute-done.21
  105.4 1.4 collective-permute-start.22
  106.8 4.0 %collective-permute-done.22.received = bf16[80,768]{1,0:T(8,128)(2,1)S(1)} collective-permute-done((bf16[80,768]{1,0:T(8,128)(2,1)S(1)}, bf16[80,768]{1,0:T(8,128)(2,1)S(1)}, u32[]{:S(2)}, u32[]{:S(2)}) %collective-permute-start.22) | collective-permute-done | bytes 122912 | tf_op jit(solution)/shard_map/ppermute | solution.py:543
  112.0 1.7 collective-permute-start.23
  113.7 2.2 %collective-permute-start.25 = (bf16[80,768]{1,0:T(8,128)(2,1)S(1)}, bf16[80,768]{1,0:T(8,128)(2,1)S(1)}, u32[]{:S(2)}, u32[]{:S(2)}) collective-permute-start(bf16[80,768]{1,0:T(8,128)(2,1)S(1)} %shard_map.238.refs_0_), channel_id=1, source_target_pairs={{0,24},{4,28},{8,0},{12,4},{16,8},{20,12},{24,16},{28,20},{1,25},{... | collective-permute-start | bytes 368648 | tf_op jit(solution)/shard_map/ppermute | solution.py:536
  117.1 3.4 %shard_map.239 = (f32[80,1152]{1,0:T(8,128)S(1)}, f32[80,1152]{1,0:T(8,128)S(1)}, f32[1,768]{1,0:T(1,128)S(1)}) custom-call(s32[3]{0:T(128)S(1)} %pad_add_fusion.s, bf16[80,768]{1,0:T(8,128)(2,1)S(1)} %shard_map.238.refs_0_, bf16[1,1152,6144]{2,1,0:T(8,128)(2,1)} %refs_6_.7, bf16[1,1152,6144]{2,1,0:T(8,128)(2,1)} %refs_7_.7, ...), custom_call_target="tpu_custom_call" | custom-call | flops 283115520 | bytes 29215744 | tf_op jit(solution)/shard_map/pallas_call | solution.py:47
  120.5 1.9 %collective-permute-done.27.refs_3_ = bf16[80,768]{1,0:T(8,128)(2,1)S(1)} collective-permute-done((bf16[80,768]{1,0:T(8,128)(2,1)S(1)}, bf16[80,768]{1,0:T(8,128)(2,1)S(1)}, u32[]{:S(2)}, u32[]{:S(2)}) %collective-permute-start.27) | collective-permute-done | bytes 122912 | tf_op jit(solution)/shard_map/ppermute | solution.py:536
  122.4 1.5 collective-permute-start.28
  124.5 1.5 collective-permute-start.26
  126.0 6.9 %shard_map.240 = (f32[80,1152]{1,0:T(8,128)S(1)}, f32[80,1152]{1,0:T(8,128)S(1)}, f32[1,768]{1,0:T(1,128)S(1)}) custom-call(s32[3]{0:T(128)S(1)} %pad_add_fusion.s, bf16[80,768]{1,0:T(8,128)(2,1)S(1)} %collective-permute-done.29.refs_0_, bf16[80,768]{1,0:T(8,128)(2,1)S(1)} %collective-permute-done.23.refs_1_, ...), custom_call_target="tpu_custom_call" | custom-call | flops 1132462080 | bytes 30324736 | tf_op jit(solution)/shard_map/pallas_call | solution.py:47
  132.9 5.7 %shard_map.241 = (bf16[80,1152]{1,0:T(8,128)(2,1)S(1)}, f32[80,128]{1,0:T(8,128)S(1)}) custom-call(s32[3]{0:T(128)S(1)} %pad_add_fusion.s, bf16[80,768]{1,0:T(8,128)(2,1)S(1)} %collective-permute-done.24.refs_0_, bf16[80,768]{1,0:T(8,128)(2,1)S(1)} %collective-permute-done.26.refs_1_, bf16[80,768]{1,0:T(8,128)(2,1)S(1)} %collective-permute-done.28.refs_2_, ...), custom_call_target="tpu_custom_call" | custom-call | flops 849346560 | bytes 29686784 | tf_op jit(solution)/shard_map/pallas_call | solution.py:47
  138.7 1.2 collective-permute-start.30
  139.9 2.6 %collective-permute-start.32 = (bf16[80,1152]{1,0:T(8,128)(2,1)S(1)}, bf16[80,1152]{1,0:T(8,128)(2,1)S(1)}, u32[]{:S(2)}, u32[]{:S(2)}) collective-permute-start(bf16[80,1152]{1,0:T(8,128)(2,1)S(1)} %get-tuple-element.71.refs_0_), channel_id=1, source_target_pairs={{0,24},{4,28},{8,0},{12,4},{16,8},{20,12},{24,16},{28,20},{1,25},{... | collective-permute-start | bytes 552968 | tf_op jit(solution)/shard_map/ppermute | solution.py:536
  145.0 1.6 collective-permute-start.41
  146.6 1.5 collective-permute-done.30.refs_2_
  148.1 1.5 collective-permute-start.31
  151.2 6.9 %collective-permute-done.34.refs_4_ = bf16[80,1152]{1,0:T(8,128)(2,1)S(1)} collective-permute-done((bf16[80,1152]{1,0:T(8,128)(2,1)S(1)}, bf16[80,1152]{1,0:T(8,128)(2,1)S(1)}, u32[]{:S(2)}, u32[]{:S(2)}) %collective-permute-start.34) | collective-permute-done | bytes 184352 | tf_op jit(solution)/shard_map/ppermute | solution.py:536
  158.1 1.5 collective-permute-start.35
  160.3 5.9 %shard_map.242 = (f32[80,768]{1,0:T(8,128)S(1)}, bf16[3,1152,768]{2,1,0:T(8,128)(2,1)S(1)}) custom-call(s32[3]{0:T(128)S(1)} %pad_add_fusion.s, bf16[80,1152]{1,0:T(8,128)(2,1)S(1)} %get-tuple-element.71.refs_0_, bf16[80,1152]{1,0:T(8,128)(2,1)S(1)} %collective-permute-done.36.refs_1_, bf16[80,1152]{1,0:T(8,128)(2,1)S(1)} %collective-permute-done.30.refs_2_, ...), custom_call_target="tpu_custom_call" | custom-call | flops 707788800 | bytes 20631552 | tf_op jit(solution)/shard_map/pallas_call | solution.py:47
  166.2 1.8 %shard_map.243 = (bf16[32,768]{1,0:T(8,128)(2,1)S(1)}, bf16[32,768]{1,0:T(8,128)(2,1)S(1)}, bf16[32,768]{1,0:T(8,128)(2,1)S(1)}, bf16[32,768]{1,0:T(8,128)(2,1)S(1)}) custom-call(s32[3]{0:T(128)S(1)} %pad_add_fusion.s, bf16[80,1152]{1,0:T(8,128)(2,1)S(1)} %collective-permute-done.31.refs_0_, bf16[80,1152]{1,0:T(8,128)(2,1)S(1)} %collective-permute-done.33.refs_1_, ...), custom_call_target="tpu_custom_call" | custom-call | flops 424673280 | bytes 6345152 | tf_op jit(solution)/shard_map/pallas_call | solution.py:47
  168.1 1.6 collective-permute-start.38
  170.9 1.4 collective-permute-done.38.refs_2_
  173.4 1.6 shard_map.245
  (103 shorter events, 19.7 us)
Async XLA Ops:
  0.7 41.4 %copy-start.3 = (bf16[128,2048]{1,0:T(8,128)(2,1)S(1)}, bf16[128,2048]{1,0:T(8,128)(2,1)}, u32[]{:S(2)}) copy-start(bf16[128,2048]{1,0:T(8,128)(2,1)} %refs_2_.2) | copy-start | bytes 1572868
  0.7 41.4 %copy-start.4 = (bf16[128,2048]{1,0:T(8,128)(2,1)S(1)}, bf16[128,2048]{1,0:T(8,128)(2,1)}, u32[]{:S(2)}) copy-start(bf16[128,2048]{1,0:T(8,128)(2,1)} %refs_3_.1) | copy-start | bytes 1572868
  2.8 15.3 %collective-permute-start = (bf16[2,128,1024]{2,1,0:T(8,128)(2,1)}, bf16[2,128,1024]{2,1,0:T(8,128)(2,1)S(1)}, u32[]{:S(2)}, u32[]{:S(2)}) collective-permute-start(bf16[2,128,1024]{2,1,0:T(8,128)(2,1)} %shard_map.230), channel_id=1, source_target_pairs={{0,4},{4,0},{8,12},{12,8},{16,20},{20,16},{24,28},{28,24},{1,5},{5... | collective-permute-start | bytes 1572872 | tf_op jit(solution)/shard_map/ppermute | solution.py:540
  5.9 4.9 %collective-permute-start.2 = (s32[2,256]{1,0:T(2,128)}, s32[2,256]{1,0:T(2,128)S(1)}, u32[]{:S(2)}, u32[]{:S(2)}) collective-permute-start(s32[2,256]{1,0:T(2,128)} %bitcast.15), channel_id=1, source_target_pairs={{0,1},{1,0},{2,3},{3,2},{4,5},{5,4},{6,7},{7,6},{8,9},{9,8},{10,11... | collective-permute-start | bytes 6152 | tf_op jit(solution)/shard_map/ppermute | solution.py:543
  5.9 4.9 %collective-permute-start.3 = (s32[2,256]{1,0:T(2,128)}, s32[2,256]{1,0:T(2,128)S(1)}, u32[]{:S(2)}, u32[]{:S(2)}) collective-permute-start(s32[2,256]{1,0:T(2,128)} %bitcast.16), channel_id=1, source_target_pairs={{0,2},{1,3},{2,0},{3,1},{4,6},{5,7},{6,4},{7,5},{8,10},{9,11},{10,... | collective-permute-start | bytes 6152 | tf_op jit(solution)/shard_map/ppermute | solution.py:543
  7.4 3.4 %collective-permute-start.4 = (s32[2,256]{1,0:T(2,128)}, s32[2,256]{1,0:T(2,128)S(1)}, u32[]{:S(2)}, u32[]{:S(2)}) collective-permute-start(s32[2,256]{1,0:T(2,128)} %bitcast.17), channel_id=1, source_target_pairs={{0,3},{1,2},{2,1},{3,0},{4,7},{5,6},{6,5},{7,4},{8,11},{9,10},{10,... | collective-permute-start | bytes 6152 | tf_op jit(solution)/shard_map/ppermute | solution.py:543
  7.7 10.4 %collective-permute-start.1 = (f32[16,128]{1,0:T(8,128)}, f32[16,128]{1,0:T(8,128)S(1)}, u32[]{:S(2)}, u32[]{:S(2)}) collective-permute-start(f32[16,128]{1,0:T(8,128)} %bitcast.12), channel_id=1, source_target_pairs={{0,4},{4,0},{8,12},{12,8},{16,20},{20,16},{24,28},{28,24},{1,5},{5... | collective-permute-start | bytes 24584 | tf_op jit(solution)/shard_map/ppermute | solution.py:540
  18.2 23.9 %collective-permute-start.5 = (bf16[2,128,1024]{2,1,0:T(8,128)(2,1)}, bf16[2,128,1024]{2,1,0:T(8,128)(2,1)S(1)}, u32[]{:S(2)}, u32[]{:S(2)}) collective-permute-start(bf16[2,128,1024]{2,1,0:T(8,128)(2,1)} %shard_map.231), channel_id=1, source_target_pairs={{0,4},{4,0},{8,12},{12,8},{16,20},{20,16},{24,28},{28,24},{1,5},{5... | collective-permute-start | bytes 1572872 | tf_op jit(solution)/shard_map/ppermute | solution.py:540
  23.1 70.5 %copy-start = (bf16[2048,768]{1,0:T(8,128)(2,1)S(1)}, bf16[2048,768]{1,0:T(8,128)(2,1)}, u32[]{:S(2)}) copy-start(bf16[2048,768]{1,0:T(8,128)(2,1)} %refs_5_.3) | copy-start | bytes 9437188
  23.2 70.5 %copy-start.7 = (s32[320,1]{1,0:T(8,128)S(1)}, s32[320,1]{1,0:T(8,128)}, u32[]{:S(2)}) copy-start(s32[320,1]{1,0:T(8,128)} %constant.73.clone.refs_8_.refs_6_) | copy-start | bytes 3844
  23.2 70.5 %copy-start.8 = (s32[320,1]{1,0:T(8,128)S(1)}, s32[320,1]{1,0:T(8,128)}, u32[]{:S(2)}) copy-start(s32[320,1]{1,0:T(8,128)} %constant.74.clone.refs_9_.refs_7_) | copy-start | bytes 3844
  23.2 6.8 %collective-permute-start.6 = (bf16[272,128]{1,0:T(8,128)(2,1)S(1)}, bf16[272,128]{1,0:T(8,128)(2,1)S(1)}, u32[]{:S(2)}, u32[]{:S(2)}) collective-permute-start(bf16[272,128]{1,0:T(8,128)(2,1)S(1)} %get-tuple-element.50), channel_id=1, source_target_pairs={{0,8},{4,12},{8,16},{12,20},{16,24},{20,28},{24,0},{28,4},{1,9},{5... | collective-permute-start | bytes 208904 | tf_op jit(solution)/shard_map/ppermute | solution.py:536
  24.8 6.9 %collective-permute-start.7 = (bf16[272,128]{1,0:T(8,128)(2,1)S(1)}, bf16[272,128]{1,0:T(8,128)(2,1)S(1)}, u32[]{:S(2)}, u32[]{:S(2)}) collective-permute-start(bf16[272,128]{1,0:T(8,128)(2,1)S(1)} %get-tuple-element.51), channel_id=1, source_target_pairs={{0,16},{4,20},{8,24},{12,28},{16,0},{20,4},{24,8},{28,12},{1,17},{... | collective-permute-start | bytes 208904 | tf_op jit(solution)/shard_map/ppermute | solution.py:536
  27.4 4.8 %collective-permute-start.8 = (bf16[272,128]{1,0:T(8,128)(2,1)S(1)}, bf16[272,128]{1,0:T(8,128)(2,1)S(1)}, u32[]{:S(2)}, u32[]{:S(2)}) collective-permute-start(bf16[272,128]{1,0:T(8,128)(2,1)S(1)} %get-tuple-element.52), channel_id=1, source_target_pairs={{0,24},{4,28},{8,0},{12,4},{16,8},{20,12},{24,16},{28,20},{1,25},{... | collective-permute-start | bytes 208904 | tf_op jit(solution)/shard_map/ppermute | solution.py:536
  32.9 6.0 %collective-permute-start.10 = (bf16[256,128]{1,0:T(8,128)(2,1)S(1)}, bf16[256,128]{1,0:T(8,128)(2,1)S(1)}, u32[]{:S(2)}, u32[]{:S(2)}) collective-permute-start(bf16[256,128]{1,0:T(8,128)(2,1)S(1)} %get-tuple-element.55), channel_id=1, source_target_pairs={{0,16},{4,20},{8,24},{12,28},{16,0},{20,4},{24,8},{28,12},{1,17},{... | collective-permute-start | bytes 196616 | tf_op jit(solution)/shard_map/ppermute | solution.py:536
  33.4 5.5 %collective-permute-start.11 = (bf16[256,128]{1,0:T(8,128)(2,1)S(1)}, bf16[256,128]{1,0:T(8,128)(2,1)S(1)}, u32[]{:S(2)}, u32[]{:S(2)}) collective-permute-start(bf16[256,128]{1,0:T(8,128)(2,1)S(1)} %get-tuple-element.56), channel_id=1, source_target_pairs={{0,24},{4,28},{8,0},{12,4},{16,8},{20,12},{24,16},{28,20},{1,25},{... | collective-permute-start | bytes 196616 | tf_op jit(solution)/shard_map/ppermute | solution.py:536
  36.1 6.1 %collective-permute-start.9 = (bf16[256,128]{1,0:T(8,128)(2,1)S(1)}, bf16[256,128]{1,0:T(8,128)(2,1)S(1)}, u32[]{:S(2)}, u32[]{:S(2)}) collective-permute-start(bf16[256,128]{1,0:T(8,128)(2,1)S(1)} %get-tuple-element.54), channel_id=1, source_target_pairs={{0,8},{4,12},{8,16},{12,20},{16,24},{20,28},{24,0},{28,4},{1,9},{5... | collective-permute-start | bytes 196616 | tf_op jit(solution)/shard_map/ppermute | solution.py:536
  45.6 16.7 %collective-permute-start.12 = (bf16[256,1024]{1,0:T(8,128)(2,1)S(1)}, bf16[256,1024]{1,0:T(8,128)(2,1)S(1)}, u32[]{:S(2)}, u32[]{:S(2)}) collective-permute-start(bf16[256,1024]{1,0:T(8,128)(2,1)S(1)} %shard_map.235.refs_0_), channel_id=1, source_target_pairs={{0,8},{4,12},{8,16},{12,20},{16,24},{20,28},{24,0},{28,4},{1,9},{5... | collective-permute-start | bytes 1572872 | tf_op jit(solution)/shard_map/ppermute | solution.py:536
  45.6 23.1 %collective-permute-start.17 = (bf16[256,1024]{1,0:T(8,128)(2,1)S(1)}, bf16[256,1024]{1,0:T(8,128)(2,1)S(1)}, u32[]{:S(2)}, u32[]{:S(2)}) collective-permute-start(bf16[256,1024]{1,0:T(8,128)(2,1)S(1)} %shard_map.235.refs_0_), channel_id=1, source_target_pairs={{0,24},{4,28},{8,0},{12,4},{16,8},{20,12},{24,16},{28,20},{1,25},{... | collective-permute-start | bytes 1572872 | tf_op jit(solution)/shard_map/ppermute | solution.py:536
  49.4 44.2 %collective-permute-start.18 = (bf16[256,1024]{1,0:T(8,128)(2,1)S(1)}, bf16[256,1024]{1,0:T(8,128)(2,1)S(1)}, u32[]{:S(2)}, u32[]{:S(2)}) collective-permute-start(bf16[256,1024]{1,0:T(8,128)(2,1)S(1)} %shard_map.235.refs_0_), channel_id=1, source_target_pairs={{0,4},{4,0},{8,12},{12,8},{16,20},{20,16},{24,28},{28,24},{1,5},{5... | collective-permute-start | bytes 1572872 | tf_op jit(solution)/shard_map/ppermute | solution.py:540
  62.3 31.4 %collective-permute-start.19 = (bf16[256,1024]{1,0:T(8,128)(2,1)S(1)}, bf16[256,1024]{1,0:T(8,128)(2,1)S(1)}, u32[]{:S(2)}, u32[]{:S(2)}) collective-permute-start(bf16[256,1024]{1,0:T(8,128)(2,1)S(1)} %collective-permute-done.12.refs_1_), channel_id=1, source_target_pairs={{0,4},{4,0},{8,12},{12,8},{16,20},{20,16},{24,28},{28,24},{1,5},{5... | collective-permute-start | bytes 1572872 | tf_op jit(solution)/shard_map/ppermute | solution.py:540
  68.7 25.0 %collective-permute-start.20 = (bf16[256,1024]{1,0:T(8,128)(2,1)S(1)}, bf16[256,1024]{1,0:T(8,128)(2,1)S(1)}, u32[]{:S(2)}, u32[]{:S(2)}) collective-permute-start(bf16[256,1024]{1,0:T(8,128)(2,1)S(1)} %collective-permute-done.17.refs_2_), channel_id=1, source_target_pairs={{0,4},{4,0},{8,12},{12,8},{16,20},{20,16},{24,28},{28,24},{1,5},{5... | collective-permute-start | bytes 1572872 | tf_op jit(solution)/shard_map/ppermute | solution.py:540
  69.3 18.2 %collective-permute-start.13 = (bf16[128,1024]{1,0:T(8,128)(2,1)S(1)}, bf16[128,1024]{1,0:T(8,128)(2,1)S(1)}, u32[]{:S(2)}, u32[]{:S(2)}) collective-permute-start(bf16[128,1024]{1,0:T(8,128)(2,1)S(1)} %get-tuple-element.91), channel_id=1, source_target_pairs={{0,16},{4,20},{8,24},{12,28},{16,0},{20,4},{24,8},{28,12},{1,17},{... | collective-permute-start | bytes 786440 | tf_op jit(solution)/shard_map/ppermute | solution.py:536
  71.9 20.9 %collective-permute-start.14 = (bf16[128,1024]{1,0:T(8,128)(2,1)S(1)}, bf16[128,1024]{1,0:T(8,128)(2,1)S(1)}, u32[]{:S(2)}, u32[]{:S(2)}) collective-permute-start(bf16[128,1024]{1,0:T(8,128)(2,1)S(1)} %get-tuple-element.90), channel_id=1, source_target_pairs={{0,16},{4,20},{8,24},{12,28},{16,0},{20,4},{24,8},{28,12},{1,17},{... | collective-permute-start | bytes 786440 | tf_op jit(solution)/shard_map/ppermute | solution.py:536
  87.4 10.4 %collective-permute-start.15 = (bf16[128,1024]{1,0:T(8,128)(2,1)S(1)}, bf16[128,1024]{1,0:T(8,128)(2,1)S(1)}, u32[]{:S(2)}, u32[]{:S(2)}) collective-permute-start(bf16[128,1024]{1,0:T(8,128)(2,1)S(1)} %collective-permute-done.13.refs_0_), channel_id=1, source_target_pairs={{0,4},{4,0},{8,12},{12,8},{16,20},{20,16},{24,28},{28,24},{1,5},{5... | collective-permute-start | bytes 786440 | tf_op jit(solution)/shard_map/ppermute | solution.py:540
  92.7 8.0 %collective-permute-start.16 = (bf16[128,1024]{1,0:T(8,128)(2,1)S(1)}, bf16[128,1024]{1,0:T(8,128)(2,1)S(1)}, u32[]{:S(2)}, u32[]{:S(2)}) collective-permute-start(bf16[128,1024]{1,0:T(8,128)(2,1)S(1)} %collective-permute-done.14.refs_1_), channel_id=1, source_target_pairs={{0,4},{4,0},{8,12},{12,8},{16,20},{20,16},{24,28},{28,24},{1,5},{5... | collective-permute-start | bytes 786440 | tf_op jit(solution)/shard_map/ppermute | solution.py:540
  103.8 1.6 collective-permute-start.21
  105.4 5.4 %collective-permute-start.22 = (bf16[80,768]{1,0:T(8,128)(2,1)S(1)}, bf16[80,768]{1,0:T(8,128)(2,1)S(1)}, u32[]{:S(2)}, u32[]{:S(2)}) collective-permute-start(bf16[80,768]{1,0:T(8,128)(2,1)S(1)} %get-tuple-element.88), channel_id=1, source_target_pairs={{0,2},{1,3},{2,0},{3,1},{4,6},{5,7},{6,4},{7,5},{8,10},{9,11},{10,... | collective-permute-start | bytes 368648 | tf_op jit(solution)/shard_map/ppermute | solution.py:543
  111.9 32.9 %collective-permute-start.40 = (bf16[2,256,768]{2,1,0:T(8,128)(2,1)S(1)}, bf16[2,256,768]{2,1,0:T(8,128)(2,1)S(1)}, u32[]{:S(2)}, u32[]{:S(2)}) collective-permute-start(bf16[2,256,768]{2,1,0:T(8,128)(2,1)S(1)} %get-tuple-element.81), channel_id=1, source_target_pairs={{0,1},{1,0},{2,3},{3,2},{4,5},{5,4},{6,7},{7,6},{8,9},{9,8},{10,11... | collective-permute-start | bytes 2359304 | tf_op jit(solution)/shard_map/ppermute | solution.py:543
  111.9 10.5 %collective-permute-start.27 = (bf16[80,768]{1,0:T(8,128)(2,1)S(1)}, bf16[80,768]{1,0:T(8,128)(2,1)S(1)}, u32[]{:S(2)}, u32[]{:S(2)}) collective-permute-start(bf16[80,768]{1,0:T(8,128)(2,1)S(1)} %shard_map.238.refs_0_), channel_id=1, source_target_pairs={{0,16},{4,20},{8,24},{12,28},{16,0},{20,4},{24,8},{28,12},{1,17},{... | collective-permute-start | bytes 368648 | tf_op jit(solution)/shard_map/ppermute | solution.py:536
  112.0 12.0 %collective-permute-start.23 = (bf16[80,768]{1,0:T(8,128)(2,1)S(1)}, bf16[80,768]{1,0:T(8,128)(2,1)S(1)}, u32[]{:S(2)}, u32[]{:S(2)}) collective-permute-start(bf16[80,768]{1,0:T(8,128)(2,1)S(1)} %shard_map.238.refs_0_), channel_id=1, source_target_pairs={{0,8},{4,12},{8,16},{12,20},{16,24},{20,28},{24,0},{28,4},{1,9},{5... | collective-permute-start | bytes 368648 | tf_op jit(solution)/shard_map/ppermute | solution.py:536
  113.7 10.7 %collective-permute-start.25 = (bf16[80,768]{1,0:T(8,128)(2,1)S(1)}, bf16[80,768]{1,0:T(8,128)(2,1)S(1)}, u32[]{:S(2)}, u32[]{:S(2)}) collective-permute-start(bf16[80,768]{1,0:T(8,128)(2,1)S(1)} %shard_map.238.refs_0_), channel_id=1, source_target_pairs={{0,24},{4,28},{8,0},{12,4},{16,8},{20,12},{24,16},{28,20},{1,25},{... | collective-permute-start | bytes 368648 | tf_op jit(solution)/shard_map/ppermute | solution.py:536
  115.9 10.1 %collective-permute-start.29 = (bf16[80,768]{1,0:T(8,128)(2,1)S(1)}, bf16[80,768]{1,0:T(8,128)(2,1)S(1)}, u32[]{:S(2)}, u32[]{:S(2)}) collective-permute-start(bf16[80,768]{1,0:T(8,128)(2,1)S(1)} %shard_map.238.refs_0_), channel_id=1, source_target_pairs={{0,4},{4,0},{8,12},{12,8},{16,20},{20,16},{24,28},{28,24},{1,5},{5... | collective-permute-start | bytes 368648 | tf_op jit(solution)/shard_map/ppermute | solution.py:540
  122.4 10.5 %collective-permute-start.28 = (bf16[80,768]{1,0:T(8,128)(2,1)S(1)}, bf16[80,768]{1,0:T(8,128)(2,1)S(1)}, u32[]{:S(2)}, u32[]{:S(2)}) collective-permute-start(bf16[80,768]{1,0:T(8,128)(2,1)S(1)} %collective-permute-done.27.refs_3_), channel_id=1, source_target_pairs={{0,4},{4,0},{8,12},{12,8},{16,20},{20,16},{24,28},{28,24},{1,5},{5... | collective-permute-start | bytes 368648 | tf_op jit(solution)/shard_map/ppermute | solution.py:540
  124.0 9.0 %collective-permute-start.24 = (bf16[80,768]{1,0:T(8,128)(2,1)S(1)}, bf16[80,768]{1,0:T(8,128)(2,1)S(1)}, u32[]{:S(2)}, u32[]{:S(2)}) collective-permute-start(bf16[80,768]{1,0:T(8,128)(2,1)S(1)} %collective-permute-done.23.refs_1_), channel_id=1, source_target_pairs={{0,4},{4,0},{8,12},{12,8},{16,20},{20,16},{24,28},{28,24},{1,5},{5... | collective-permute-start | bytes 368648 | tf_op jit(solution)/shard_map/ppermute | solution.py:540
  124.5 8.5 %collective-permute-start.26 = (bf16[80,768]{1,0:T(8,128)(2,1)S(1)}, bf16[80,768]{1,0:T(8,128)(2,1)S(1)}, u32[]{:S(2)}, u32[]{:S(2)}) collective-permute-start(bf16[80,768]{1,0:T(8,128)(2,1)S(1)} %collective-permute-done.25.refs_2_), channel_id=1, source_target_pairs={{0,4},{4,0},{8,12},{12,8},{16,20},{20,16},{24,28},{28,24},{1,5},{5... | collective-permute-start | bytes 368648 | tf_op jit(solution)/shard_map/ppermute | solution.py:540
  138.7 9.4 %collective-permute-start.30 = (bf16[80,1152]{1,0:T(8,128)(2,1)S(1)}, bf16[80,1152]{1,0:T(8,128)(2,1)S(1)}, u32[]{:S(2)}, u32[]{:S(2)}) collective-permute-start(bf16[80,1152]{1,0:T(8,128)(2,1)S(1)} %get-tuple-element.71.refs_0_), channel_id=1, source_target_pairs={{0,8},{4,12},{8,16},{12,20},{16,24},{20,28},{24,0},{28,4},{1,9},{5... | collective-permute-start | bytes 552968 | tf_op jit(solution)/shard_map/ppermute | solution.py:536
  139.9 10.2 %collective-permute-start.32 = (bf16[80,1152]{1,0:T(8,128)(2,1)S(1)}, bf16[80,1152]{1,0:T(8,128)(2,1)S(1)}, u32[]{:S(2)}, u32[]{:S(2)}) collective-permute-start(bf16[80,1152]{1,0:T(8,128)(2,1)S(1)} %get-tuple-element.71.refs_0_), channel_id=1, source_target_pairs={{0,24},{4,28},{8,0},{12,4},{16,8},{20,12},{24,16},{28,20},{1,25},{... | collective-permute-start | bytes 552968 | tf_op jit(solution)/shard_map/ppermute | solution.py:536
  142.5 15.6 %collective-permute-start.34 = (bf16[80,1152]{1,0:T(8,128)(2,1)S(1)}, bf16[80,1152]{1,0:T(8,128)(2,1)S(1)}, u32[]{:S(2)}, u32[]{:S(2)}) collective-permute-start(bf16[80,1152]{1,0:T(8,128)(2,1)S(1)} %get-tuple-element.71.refs_0_), channel_id=1, source_target_pairs={{0,16},{4,20},{8,24},{12,28},{16,0},{20,4},{24,8},{28,12},{1,17},{... | collective-permute-start | bytes 552968 | tf_op jit(solution)/shard_map/ppermute | solution.py:536
  143.5 16.0 %collective-permute-start.36 = (bf16[80,1152]{1,0:T(8,128)(2,1)S(1)}, bf16[80,1152]{1,0:T(8,128)(2,1)S(1)}, u32[]{:S(2)}, u32[]{:S(2)}) collective-permute-start(bf16[80,1152]{1,0:T(8,128)(2,1)S(1)} %get-tuple-element.71.refs_0_), channel_id=1, source_target_pairs={{0,4},{4,0},{8,12},{12,8},{16,20},{20,16},{24,28},{28,24},{1,5},{5... | collective-permute-start | bytes 552968 | tf_op jit(solution)/shard_map/ppermute | solution.py:540
  145.0 25.0 %collective-permute-start.41 = (bf16[1,256,768]{2,1,0:T(8,128)(2,1)S(1)}, bf16[1,256,768]{2,1,0:T(8,128)(2,1)S(1)}, u32[]{:S(2)}, u32[]{:S(2)}) collective-permute-start(bf16[1,256,768]{2,1,0:T(8,128)(2,1)S(1)} %get-tuple-element.86), channel_id=1, source_target_pairs={{0,2},{1,3},{2,0},{3,1},{4,6},{5,7},{6,4},{7,5},{8,10},{9,11},{10,... | collective-permute-start | bytes 1179656 | tf_op jit(solution)/shard_map/ppermute | solution.py:543
  148.1 18.1 %collective-permute-start.31 = (bf16[80,1152]{1,0:T(8,128)(2,1)S(1)}, bf16[80,1152]{1,0:T(8,128)(2,1)S(1)}, u32[]{:S(2)}, u32[]{:S(2)}) collective-permute-start(bf16[80,1152]{1,0:T(8,128)(2,1)S(1)} %collective-permute-done.30.refs_2_), channel_id=1, source_target_pairs={{0,4},{4,0},{8,12},{12,8},{16,20},{20,16},{24,28},{28,24},{1,5},{5... | collective-permute-start | bytes 552968 | tf_op jit(solution)/shard_map/ppermute | solution.py:540
  150.0 16.1 %collective-permute-start.33 = (bf16[80,1152]{1,0:T(8,128)(2,1)S(1)}, bf16[80,1152]{1,0:T(8,128)(2,1)S(1)}, u32[]{:S(2)}, u32[]{:S(2)}) collective-permute-start(bf16[80,1152]{1,0:T(8,128)(2,1)S(1)} %collective-permute-done.32.refs_3_), channel_id=1, source_target_pairs={{0,4},{4,0},{8,12},{12,8},{16,20},{20,16},{24,28},{28,24},{1,5},{5... | collective-permute-start | bytes 552968 | tf_op jit(solution)/shard_map/ppermute | solution.py:540
  158.1 8.1 %collective-permute-start.35 = (bf16[80,1152]{1,0:T(8,128)(2,1)S(1)}, bf16[80,1152]{1,0:T(8,128)(2,1)S(1)}, u32[]{:S(2)}, u32[]{:S(2)}) collective-permute-start(bf16[80,1152]{1,0:T(8,128)(2,1)S(1)} %collective-permute-done.34.refs_4_), channel_id=1, source_target_pairs={{0,4},{4,0},{8,12},{12,8},{16,20},{20,16},{24,28},{28,24},{1,5},{5... | collective-permute-start | bytes 552968 | tf_op jit(solution)/shard_map/ppermute | solution.py:540
  159.6 10.4 %collective-permute-start.42 = (f32[8,16,128]{2,1,0:T(8,128)S(1)}, f32[8,16,128]{2,1,0:T(8,128)S(1)}, u32[]{:S(2)}, u32[]{:S(2)}) collective-permute-start(f32[8,16,128]{2,1,0:T(8,128)S(1)} %get-tuple-element.92), channel_id=1, source_target_pairs={{0,4},{4,0},{8,12},{12,8},{16,20},{20,16},{24,28},{28,24},{1,5},{5... | collective-permute-start | bytes 196616 | tf_op jit(solution)/shard_map/ppermute | solution.py:540
  168.1 2.8 %collective-permute-start.37 = (bf16[32,768]{1,0:T(8,128)(2,1)S(1)}, bf16[32,768]{1,0:T(8,128)(2,1)S(1)}, u32[]{:S(2)}, u32[]{:S(2)}) collective-permute-start(bf16[32,768]{1,0:T(8,128)(2,1)S(1)} %get-tuple-element.76), channel_id=1, source_target_pairs={{0,1},{1,0},{2,3},{3,2},{4,5},{5,4},{6,7},{7,6},{8,9},{9,8},{10,11... | collective-permute-start | bytes 147464 | tf_op jit(solution)/shard_map/ppermute | solution.py:543
  168.1 4.2 %collective-permute-start.38 = (bf16[32,768]{1,0:T(8,128)(2,1)S(1)}, bf16[32,768]{1,0:T(8,128)(2,1)S(1)}, u32[]{:S(2)}, u32[]{:S(2)}) collective-permute-start(bf16[32,768]{1,0:T(8,128)(2,1)S(1)} %get-tuple-element.77), channel_id=1, source_target_pairs={{0,2},{1,3},{2,0},{3,1},{4,6},{5,7},{6,4},{7,5},{8,10},{9,11},{10,... | collective-permute-start | bytes 147464 | tf_op jit(solution)/shard_map/ppermute | solution.py:543
  169.7 3.7 %collective-permute-start.39 = (bf16[32,768]{1,0:T(8,128)(2,1)S(1)}, bf16[32,768]{1,0:T(8,128)(2,1)S(1)}, u32[]{:S(2)}, u32[]{:S(2)}) collective-permute-start(bf16[32,768]{1,0:T(8,128)(2,1)S(1)} %get-tuple-element.78), channel_id=1, source_target_pairs={{0,3},{1,2},{2,1},{3,0},{4,7},{5,6},{6,5},{7,4},{8,11},{9,10},{10,... | collective-permute-start | bytes 147464 | tf_op jit(solution)/shard_map/ppermute | solution.py:543
  (15 other events, 195.5 us)
